TPU v7x, 128 devices: a whole 4x4x4 slice. The times are simulated.
128 devices in a mesh: req: 8 (over y, core), exp: 16 (over x, z).
Axes of the slice: x: 4, y: 4, z: 4, core: 2. Of those that a mesh axis runs over, the one named last changes fastest.
Arguments:
- residual: bfloat16 [8320, 2048], P(('req', 'exp')), may hold values from -6 to 6
- prefill_qkv: bfloat16 [16, 3, 512, 2048], P('req', None, None, 'exp'), may hold values from -4.5 to 4.5
- decode_qkv: bfloat16 [128, 3, 2048], P('req', None, 'exp'), may hold values from -4.5 to 4.5
- cache_pool: bfloat16 [2, 992, 128, 2048], P(None, 'req', None, 'exp'), may hold values from -4.5 to 4.5
- page_table: int32 [128, 64], P('req'), may hold values from 0 to 123, as said below
- cache_len: int32 [128], P('req'), may hold values from 2 to 8192
- out_weight: bfloat16 [2048, 2048], P('exp'), may hold values from -0.125 to 0.125
- norm_gain: float32 [2048], replicated, may hold values from 0.1 to 1.9
- shared_gate_up: bfloat16 [2, 2048, 5632], P(None, None, 'exp'), may hold values from -0.125 to 0.125
- shared_down: bfloat16 [5632, 2048], P('exp'), may hold values from -0.078125 to 0.078125
- shared_gate: bfloat16 [2048], replicated, may hold values from -0.25 to 0.25
- routes: int32 [8320, 4], P(('req', 'exp')), may hold values from 0 to 63, all different within a row; in each aligned block of 65 rows (0 to 64, 65 to 129, ...) at most 8 rows name the same one
- route_weight: float32 [8320, 4], P(('req', 'exp')), may hold values from 0.1 to 0.5
- expert_gate_up: bfloat16 [128, 2, 2048, 704], P(('req', 'exp')), may hold values from -0.125 to 0.125
- expert_down: bfloat16 [128, 704, 2048], P(('req', 'exp')), may hold values from -0.15625 to 0.15625
Outputs:
- layer_out: bfloat16 [8320, 2048], P(('req', 'exp'))
Inputs may be any that keep to these rules, and one draw needn't show every extreme that they name: `page_table`: for decode request i the first ceil(cache_len[i] / 128) entries name distinct pages among the requests of one req index and hold its cache in order; later entries name pages but are not read. `routes`: in the rows of one device (aligned blocks of 65 rows) no expert is named more than 8 times; a row names 4 different experts.
All inputs are finite; a program needn't handle non-finite values.
Results may differ from a plain program's by a relative error of at most 0.015.
Values may be sent and summed in bfloat16 or wider, within the bound.
No kernel may reach another device: no remote copies, remote signals or barrier semaphores. Data moves between devices by JAX's collectives and lax.ppermute only.
A program may use at most 128 MiB of HBM per device.

v0:
```python
import jax
import jax.numpy as jnp
from jax import lax
from jax.sharding import PartitionSpec as P

HD = 128
EXP_COL = 4


NEG_FILL = -1e30


def masked_weights(scores, allowed):
    masked = jnp.where(allowed, scores, NEG_FILL)
    highest = jnp.max(masked, axis=-1, keepdims=True)
    raised = jnp.where(allowed, jnp.exp(masked - highest), 0.0)
    return (raised / jnp.sum(raised, axis=-1, keepdims=True)).astype(jnp.bfloat16)


def prefill_heads(prefill_qkv):
    spans, three_rows, span_len, width_here = prefill_qkv.shape
    heads_here = width_here // HD
    split_qkv = prefill_qkv.reshape(spans, three_rows, span_len, heads_here, HD)
    scores = jnp.einsum(
        "pqhd,pkhd->phqk", split_qkv[:, 0], split_qkv[:, 1], preferred_element_type=jnp.float32
    ) * HD ** (-0.5)
    causal = jnp.arange(span_len)[:, None] >= jnp.arange(span_len)[None, :]
    weights = masked_weights(scores, causal[None, None])
    mixed_rows = jnp.einsum(
        "phqk,pkhd->pqhd", weights, split_qkv[:, 2], preferred_element_type=jnp.float32
    )
    return mixed_rows.astype(jnp.bfloat16).reshape(spans * span_len, width_here)


def decode_heads(decode_qkv, cache_pool, page_table, cache_len):
    requests, three_rows, width_here = decode_qkv.shape
    heads_here = width_here // HD
    pool_pages, page_len = (cache_pool.shape[1], cache_pool.shape[2])
    max_pages = page_table.shape[1]
    used_pages = (cache_len + page_len - 1) // page_len
    columns = jnp.broadcast_to(
        jnp.arange(max_pages, dtype=jnp.int32)[None, :], (requests, max_pages)
    )
    live_entry = columns < used_pages[:, None]
    target = jnp.where(live_entry, page_table, pool_pages).reshape(-1)
    request_ids = jnp.broadcast_to(
        jnp.arange(requests, dtype=jnp.int32)[:, None], (requests, max_pages)
    ).reshape(-1)
    owners = jnp.full((pool_pages,), -1, jnp.int32).at[target].set(request_ids, mode="drop")
    page_order = (
        jnp.zeros((pool_pages,), jnp.int32).at[target].set(columns.reshape(-1), mode="drop")
    )
    token_owner = jnp.repeat(owners, page_len)
    token_place = (
        page_order[:, None] * page_len + jnp.arange(page_len, dtype=jnp.int32)[None, :]
    ).reshape(-1)
    allowed = (token_owner[None, :] == jnp.arange(requests, dtype=jnp.int32)[:, None]) & (
        token_place[None, :] < cache_len[:, None]
    )
    pool_rows = cache_pool.reshape(2, pool_pages * page_len, heads_here, HD)
    query_rows = decode_qkv[:, 0].reshape(requests, heads_here, HD)
    own_keys = decode_qkv[:, 1].reshape(requests, heads_here, HD)
    own_values = decode_qkv[:, 2].reshape(requests, heads_here, HD)
    cached = jnp.einsum(
        "ihd,thd->iht", query_rows, pool_rows[0], preferred_element_type=jnp.float32
    ) * HD ** (-0.5)
    own_scores = jnp.einsum(
        "ihd,ihd->ih", query_rows, own_keys, preferred_element_type=jnp.float32
    )[..., None] * HD ** (-0.5)
    joined = jnp.concatenate([cached, own_scores], axis=-1)
    allowed_all = jnp.concatenate(
        [allowed[:, None, :], jnp.ones((requests, heads_here, 1), bool)], axis=-1
    )
    weights = masked_weights(joined, allowed_all)
    mixed_rows = jnp.einsum(
        "iht,thd->ihd", weights[..., :-1], pool_rows[1], preferred_element_type=jnp.float32
    )
    mixed_rows = mixed_rows + weights[..., -1:].astype(jnp.float32) * own_values.astype(jnp.float32)
    return mixed_rows.astype(jnp.bfloat16).reshape(requests, width_here)


def on_device(
    residual,
    prefill_qkv,
    decode_qkv,
    cache_pool,
    page_table,
    cache_len,
    out_weight,
    norm_gain,
    shared_gate_up,
    shared_down,
    shared_gate,
    routes,
    route_weight,
    expert_gate_up,
    expert_down,
):
    attended = jnp.concatenate(
        [prefill_heads(prefill_qkv), decode_heads(decode_qkv, cache_pool, page_table, cache_len)],
        axis=0,
    )
    groups = lax.axis_size("exp")
    tok_rows = residual.shape[0]
    model_width = out_weight.shape[1]
    projected = lax.psum_scatter(
        jnp.dot(attended, out_weight, preferred_element_type=jnp.float32).astype(jnp.bfloat16),
        "exp",
        scatter_dimension=0,
        tiled=True,
    ).astype(jnp.float32)
    stream = lax.optimization_barrier(
        (residual.astype(jnp.float32) + projected).astype(jnp.bfloat16)
    )
    stream_wide = stream.astype(jnp.float32)
    normed = (
        stream_wide
        * lax.rsqrt(jnp.mean(stream_wide * stream_wide, axis=-1, keepdims=True) + 1e-06)
        * norm_gain
    ).astype(jnp.bfloat16)
    block_rows = lax.all_gather(normed, "exp", axis=0, tiled=True)
    gate_part = jnp.dot(block_rows, shared_gate_up[0], preferred_element_type=jnp.float32)
    up_part = jnp.dot(block_rows, shared_gate_up[1], preferred_element_type=jnp.float32)
    hidden = (jax.nn.silu(gate_part) * up_part).astype(jnp.bfloat16)
    partials = jnp.dot(hidden, shared_down, preferred_element_type=jnp.float32)
    shared = lax.psum_scatter(
        partials.astype(jnp.bfloat16), "exp", scatter_dimension=0, tiled=True
    ).astype(jnp.float32)
    shared_scale = jax.nn.sigmoid(jnp.dot(normed, shared_gate, preferred_element_type=jnp.float32))
    experts_all = EXP_COL * groups
    halves = lax.axis_size("req") // EXP_COL
    route_count = routes.shape[1]
    capacity = max(2, tok_rows * route_count * 2 // experts_all)
    flat_routes = routes.reshape(-1)
    onehot = (flat_routes[:, None] == jnp.arange(experts_all, dtype=jnp.int32)[None, :]).astype(
        jnp.int32
    )
    slot_rank = jnp.sum(onehot * (jnp.cumsum(onehot, axis=0) - 1), axis=1)
    slot_of = flat_routes * capacity + slot_rank
    select = jnp.any(
        jnp.arange(experts_all * capacity, dtype=jnp.int32)[:, None, None]
        == slot_of.reshape(tok_rows, route_count)[None],
        axis=-1,
    ).astype(jnp.bfloat16)
    packed = jnp.dot(select, normed, preferred_element_type=jnp.float32).astype(jnp.bfloat16)
    outgoing = jnp.broadcast_to(
        packed.reshape(experts_all, 1, capacity, model_width),
        (experts_all, halves, capacity, model_width),
    ).reshape(experts_all * halves, capacity, model_width)
    arrived = lax.all_to_all(outgoing, ("req", "exp"), split_axis=0, concat_axis=0, tiled=True)
    senders, slot_total, width_here = arrived.shape
    flat_rows = arrived.reshape(senders * slot_total, width_here)
    expert_gate = jnp.dot(flat_rows, expert_gate_up[0, 0], preferred_element_type=jnp.float32)
    expert_up = jnp.dot(flat_rows, expert_gate_up[0, 1], preferred_element_type=jnp.float32)
    hidden = (jax.nn.silu(expert_gate) * expert_up).astype(jnp.bfloat16)
    answer = jnp.dot(hidden, expert_down[0], preferred_element_type=jnp.float32).astype(
        jnp.bfloat16
    )
    returned = lax.all_to_all(
        answer.reshape(senders, slot_total, width_here),
        ("req", "exp"),
        split_axis=0,
        concat_axis=0,
        tiled=True,
    )
    summed = jnp.sum(
        returned.reshape(experts_all, halves, capacity, model_width).astype(jnp.float32), axis=1
    ).reshape(experts_all * capacity, model_width)
    picked = summed[slot_of].reshape(tok_rows, route_count, model_width)
    routed = jnp.sum(picked * route_weight[..., None], axis=1)
    result_rows = stream_wide + routed + shared_scale[:, None] * shared
    return result_rows.astype(jnp.bfloat16)


def solution(mesh):
    placed = (
        P(("req", "exp"), None),
        P("req", None, None, "exp"),
        P("req", None, "exp"),
        P(None, "req", None, "exp"),
        P("req", None),
        P("req"),
        P("exp", None),
        P(),
        P(None, None, "exp"),
        P("exp", None),
        P(),
        P(("req", "exp"), None),
        P(("req", "exp"), None),
        P(("req", "exp"), None, None, None),
        P(("req", "exp"), None, None),
    )
    return jax.shard_map(
        on_device, mesh=mesh, in_specs=placed, out_specs=P(("req", "exp"), None), check_vma=False
    )
```

profile of v0, /device:TPU:66, one launch (start us, length us, event | category | flops | bytes accessed | tf_op | source)
XLA Modules:
  0.0 391.5 jit_solution(4719682502850788841)
XLA Ops:
  6.6 6.0 %fusion.75 = (bf16[1,124,128,128]{3,2,1,0:T(8,128)(2,1)}, bf16[1,124,128,128]{3,2,1,0:T(8,128)(2,1)}) fusion(bf16[2,124,128,128]{3,2,1,0:T(8,128)(2,1)} %param.18), kind=kLoop, calls=%fused_computation.118 | loop fusion | bytes 16252928 | tf_op jit(solution)/shard_map/slice | solution.py:65
  12.9 4.4 %fusion.3 = f32[16,1,15872]{2,0,1:T(8,128)} fusion(bf16[15872,128]{1,0:T(8,128)(2,1)} %bitcast.149, bf16[16,3,128]{2,0,1:T(8,128)(2,1)S(1)} %copy-done.7), kind=kOutput, calls=%fused_computation.5 | convolution fusion | flops 65265664 | bytes 5083136 | tf_op jit(solution)/shard_map/ihd,thd->iht/dot_general | solution.py:64
  17.5 4.3 %scatter_custom_fusion.1 = s32[124]{0:T(128)S(1)} fusion(s32[1024]{0:T(1024)S(1)} %bitcast.156, s32[1024]{0:T(1024)S(1)} %reshape.356, s32[]{:T(128)} %constant.25.clone.1), kind=kCustom, calls=%fused_computation.107 | custom fusion | bytes 500 | tf_op jit(solution)/shard_map/scatter | solution.py:51
  21.9 4.3 %scatter_custom_fusion = s32[124]{0:T(128)S(1)} fusion(s32[1024]{0:T(1024)S(1)} %bitcast.157, s32[1024]{0:T(1024)S(1)} %reshape.348, s32[]{:T(128)} %constant.22.clone.1), kind=kCustom, calls=%fused_computation.109 | custom fusion | bytes 500 | tf_op jit(solution)/shard_map/scatter | solution.py:49
  26.3 0.3 fusion.39
  26.6 1.6 fusion.43
  28.2 1.7 fusion.54
  29.9 0.3 divide_convert_fusion.2
  30.4 0.9 copy.56
  31.3 0.7 fusion.31
  32.0 3.5 fusion.76
  35.5 2.2 convolution_convert_fusion.3
  37.7 3.2 convolution_convert_fusion.1
  40.9 66.5 %fusion = bf16[80,2048]{1,0:T(8,128)(2,1)S(1)} fusion(bf16[1040,2048]{1,0:T(8,128)(2,1)} %convolution_convert_fusion.1), kind=kCustom, calls=%all-reduce-scatter | all-reduce-scatter fusion | flops 2621441 | bytes 4588032
  107.5 3.0 collective-permute-start.1
  110.5 4.2 %collective-permute-start = (bf16[80,2048]{1,0:T(8,128)(2,1)S(1)}, bf16[80,2048]{1,0:T(8,128)(2,1)}, u32[]{:S(2)}, u32[]{:S(2)}) collective-permute-start(bf16[80,2048]{1,0:T(8,128)(2,1)S(1)} %fusion), channel_id=1, source_target_pairs={{0,1},{1,2},{2,3},{3,4},{4,5},{5,6},{6,7},{7,8},{8,9},{9,10},{10,1... | collective-permute-start | bytes 983048
  114.8 0.8 slice.79
  115.5 3.2 collective-permute-start.2
  119.1 0.9 reduce-window.6
  120.3 0.7 dynamic-slice.6
  121.6 10.2 %collective-permute-done.2 = bf16[65,2048]{1,0:T(8,128)(2,1)} collective-permute-done((bf16[65,2048]{1,0:T(8,128)(2,1)}, bf16[65,2048]{1,0:T(8,128)(2,1)}, u32[]{:S(2)}, u32[]{:S(2)}) %collective-permute-start.2) | collective-permute-done | bytes 266272
  131.9 11.8 %concatenate.12 = bf16[305,2048]{1,0:T(8,128)(2,1)} concatenate(bf16[65,2048]{1,0:T(8,128)(2,1)} %collective-permute-done.2, bf16[80,2048]{1,0:T(8,128)(2,1)} %collective-permute-done.1, bf16[80,2048]{1,0:T(8,128)(2,1)} %collective-permute-done, bf16[80,2048]{1,0:T(8,128)(2,1)S(1)} %fusion), dimensions={0} | concatenate | bytes 2498560
  143.6 1.2 add_convert_fusion
  145.0 0.9 fusion.72
  146.1 0.4 fusion.49
  146.6 0.8 fusion.14
  147.4 2.5 broadcast_in_dim.97
  149.9 9.7 %all-to-all-start = ((bf16[128,8,2048]{2,1,0:T(8,128)(2,1)}), bf16[128,8,2048]{2,1,0:T(8,128)(2,1)}, u32[]{:S(2)}, u32[]{:S(2)}) async-start(bf16[128,8,2048]{2,1,0:T(8,128)(2,1)} %bitcast.150), calls=%async_computation | async-start | bytes 8388608 | tf_op jit(solution)/shard_map/all_to_all | solution.py:150
  159.7 52.4 %all-to-all-done = bf16[128,8,2048]{2,1,0:T(8,128)(2,1)} async-done(((bf16[128,8,2048]{2,1,0:T(8,128)(2,1)}), bf16[128,8,2048]{2,1,0:T(8,128)(2,1)}, u32[]{:S(2)}, u32[]{:S(2)}) %all-to-all-start) | async-done | bytes 4194336 | tf_op jit(solution)/shard_map/all_to_all | solution.py:150
  212.1 7.8 %fusion.6 = f32[1024,704]{0,1:T(8,128)} fusion(bf16[128,8,2048]{2,1,0:T(8,128)(2,1)} %all-to-all-done, bf16[1,2,2048,704]{2,3,1,0:T(8,128)(2,1)} %param.28), kind=kOutput, calls=%fused_computation.11 | convolution fusion | flops 2952790016 | bytes 9961472 | tf_op jit(solution)/shard_map/dot_general | solution.py:153
  219.9 11.2 %convert_bitcast_fusion = bf16[128,8,2048]{2,1,0:T(8,128)(2,1)} fusion(bf16[1,704,2048]{2,1,0:T(8,128)(2,1)S(1)} %copy-done, f32[1024,704]{0,1:T(8,128)} %fusion.6, bf16[1,2,2048,704]{2,3,1,0:T(8,128)(2,1)} %param.28, bf16[128,8,2048]{2,1,0:T(8,128)(2,1)} %all-to-all-done), kind=kOutput, calls=%fused_computation.13 | convolution fusion | flops 5912002560 | bytes 17039360 | tf_op jit(solution)/shard_map/dot_general | solution.py:156
  231.1 8.2 %all-to-all-start.1 = ((bf16[128,8,2048]{2,1,0:T(8,128)(2,1)}), bf16[128,8,2048]{2,1,0:T(8,128)(2,1)}, u32[]{:S(2)}, u32[]{:S(2)}) async-start(bf16[128,8,2048]{2,1,0:T(8,128)(2,1)} %convert_bitcast_fusion), calls=%async_computation.1 | async-start | bytes 8388608 | tf_op jit(solution)/shard_map/all_to_all | solution.py:159
  239.3 0.3 all-gather.3.cloned.1.call-done
  239.6 4.6 %reshape.361 = bf16[1040,2048]{1,0:T(8,128)(2,1)} reshape(bf16[16,65,2048]{2,1,0:T(8,128)(2,1)} %all-gather.3.cloned.1.call-done) | data formatting | bytes 8519680
  244.2 5.8 %fusion.21 = f32[1040,352]{1,0:T(8,128)} fusion(bf16[1040,2048]{1,0:T(8,128)(2,1)} %reshape.361, bf16[2,2048,352]{1,2,0:T(8,128)(2,1)S(1)} %copy-done.14), kind=kOutput, calls=%fused_computation.30 | convolution fusion | flops 1499463680 | bytes 7165952 | tf_op jit(solution)/shard_map/dot_general | solution.py:122
  250.0 8.4 %convolution_convert_fusion = bf16[1040,2048]{1,0:T(8,128)(2,1)} fusion(bf16[352,2048]{1,0:T(8,128)(2,1)} %param.24, bf16[1040,2048]{1,0:T(8,128)(2,1)} %reshape.361, f32[1040,352]{1,0:T(8,128)} %fusion.21, bf16[2,2048,352]{1,2,0:T(8,128)(2,1)S(1)} %copy-done.14), kind=kOutput, calls=%fused_computation.7 | convolution fusion | flops 3003253760 | bytes 12867584 | tf_op jit(solution)/shard_map/dot_general | solution.py:125
  258.4 69.6 %fusion.1 = bf16[80,2048]{1,0:T(8,128)(2,1)S(1)} fusion(bf16[1040,2048]{1,0:T(8,128)(2,1)} %convolution_convert_fusion), kind=kCustom, calls=%all-reduce-scatter.1 | all-reduce-scatter fusion | flops 2621441 | bytes 4588032
  328.0 4.5 %collective-permute-start.4 = (bf16[80,2048]{1,0:T(8,128)(2,1)S(1)}, bf16[80,2048]{1,0:T(8,128)(2,1)S(1)}, u32[]{:S(2)}, u32[]{:S(2)}) collective-permute-start(bf16[80,2048]{1,0:T(8,128)(2,1)S(1)} %fusion.1), channel_id=1, source_target_pairs={{0,2},{1,3},{2,4},{3,5},{4,6},{5,7},{6,8},{7,9},{8,10},{9,11},{10,... | collective-permute-start | bytes 983048
  332.6 3.1 collective-permute-start.3
  335.7 3.9 %collective-permute-start.5 = (bf16[65,2048]{1,0:T(8,128)(2,1)S(1)}, bf16[65,2048]{1,0:T(8,128)(2,1)S(1)}, u32[]{:S(2)}, u32[]{:S(2)}) collective-permute-start(bf16[65,2048]{1,0:T(8,128)(2,1)S(1)} %slice.80), channel_id=1, source_target_pairs={{0,3},{1,4},{2,5},{3,6},{4,7},{5,8},{6,9},{7,10},{8,11},{9,12},{10... | collective-permute-start | bytes 798728
  339.8 0.3 fusion.35
  340.1 13.9 %collective-permute-done.5 = bf16[65,2048]{1,0:T(8,128)(2,1)S(1)} collective-permute-done((bf16[65,2048]{1,0:T(8,128)(2,1)S(1)}, bf16[65,2048]{1,0:T(8,128)(2,1)S(1)}, u32[]{:S(2)}, u32[]{:S(2)}) %collective-permute-start.5) | collective-permute-done | bytes 266272
  354.0 9.9 %concatenate.13 = bf16[305,2048]{1,0:T(8,128)(2,1)} concatenate(bf16[65,2048]{1,0:T(8,128)(2,1)S(1)} %collective-permute-done.5, bf16[80,2048]{1,0:T(8,128)(2,1)S(1)} %collective-permute-done.4, bf16[80,2048]{1,0:T(8,128)(2,1)S(1)} %collective-permute-done.3, bf16[80,2048]{1,0:T(8,128)(2,1)S(1)} %fusion.1), dimensions={0} | concatenate | bytes 2498560
  363.8 5.5 %convert_reduce_fusion = f32[64,8,2048]{2,1,0:T(8,128)} fusion(bf16[128,8,2048]{2,1,0:T(8,128)(2,1)} %all-to-all-done.1), kind=kLoop, calls=%fused_computation.6 | loop fusion | flops 3145728 | bytes 8388608 | tf_op jit(solution)/shard_map/reduce_sum | solution.py:166
  369.3 6.9 %gather_fusion = f32[260,2048]{1,0:T(8,128)} fusion(f32[512,2048]{1,0:T(8,128)} %bitcast.148, s32[1024]{0:T(1024)S(1)} %pad_clamp_fusion), kind=kCustom, calls=%fused_computation | custom fusion | bytes 4260880 | tf_op jit(solution)/shard_map/gather | solution.py:169
  376.2 3.3 reshape.332
  379.5 3.2 multiply_reduce_fusion
  382.7 1.9 fusion.48
  (70 shorter events, 2.1 us)
Async XLA Ops:
  6.5 213.4 %copy-start = (bf16[1,704,2048]{2,1,0:T(8,128)(2,1)S(1)}, bf16[1,704,2048]{2,1,0:T(8,128)(2,1)}, u32[]{:S(2)}) copy-start(bf16[1,704,2048]{2,1,0:T(8,128)(2,1)} %param.29) | copy-start | bytes 8650756
  6.5 233.1 %all-gather.3.cloned.1.call-start = ((), (), s32[]{:S(2)}) async-start(), calls=%async_computation.2 | async-start | bytes 5013504 | tf_op jit(solution)/shard_map/all_gather | solution.py:121
  6.6 6.0 %copy-start.7 = (bf16[16,3,128]{2,0,1:T(8,128)(2,1)S(1)}, bf16[16,3,128]{2,0,1:T(8,128)(2,1)}, u32[]{:S(2)}) copy-start(bf16[16,3,128]{2,0,1:T(8,128)(2,1)} %param.17) | copy-start | bytes 36868
  12.9 4.4 %copy-start.12 = (s32[16]{0:T(128)S(1)}, s32[16]{0:T(128)}, u32[]{:S(2)}) copy-start(s32[16]{0:T(128)} %param.20) | copy-start | bytes 196
  12.9 4.4 %copy-start.8 = (s32[16,64]{1,0:T(8,128)S(1)}, s32[16,64]{1,0:T(8,128)}, u32[]{:S(2)}) copy-start(s32[16,64]{1,0:T(8,128)} %param.19) | copy-start | bytes 12292
  26.2 3.7 copy-start.2
  26.2 4.1 %copy-start.4 = (bf16[2,3,512,128]{3,2,1,0:T(8,128)(2,1)S(1)}, bf16[2,3,512,128]{3,2,1,0:T(8,128)(2,1)}, u32[]{:S(2)}) copy-start(bf16[2,3,512,128]{3,2,1,0:T(8,128)(2,1)} %param.16) | copy-start | bytes 2359300
  26.6 4.7 %copy-start.3 = (bf16[1,124,128,128]{3,2,1,0:T(8,128)(2,1)S(1)}, bf16[1,124,128,128]{3,2,1,0:T(8,128)(2,1)}, u32[]{:S(2)}) copy-start(bf16[1,124,128,128]{3,2,1,0:T(8,128)(2,1)} %get-tuple-element.6) | copy-start | bytes 12189700
  35.5 2.2 copy-start.5
  40.9 77.9 %copy-start.10 = (s32[65,4]{0,1:T(4,128)S(1)}, s32[65,4]{0,1:T(4,128)}, u32[]{:S(2)}) copy-start(s32[65,4]{0,1:T(4,128)} %param.26) | copy-start | bytes 3124
  40.9 79.3 %copy-start.13 = (u32[128]{0:T(128)S(1)}, u32[128]{0:T(128)}, u32[]{:S(2)}) copy-start(u32[128]{0:T(128)} %constant.80) | copy-start | bytes 1540
  107.5 37.5 %copy-start.6 = (f32[2048]{0:T(1024)S(1)}, f32[2048]{0:T(1024)}, u32[]{:S(2)}) copy-start(f32[2048]{0:T(1024)} %param.22) | copy-start | bytes 24580
  107.5 24.4 %collective-permute-start.1 = (bf16[80,2048]{1,0:T(8,128)(2,1)S(1)}, bf16[80,2048]{1,0:T(8,128)(2,1)}, u32[]{:S(2)}, u32[]{:S(2)}) collective-permute-start(bf16[80,2048]{1,0:T(8,128)(2,1)S(1)} %fusion), channel_id=1, source_target_pairs={{0,2},{1,3},{2,4},{3,5},{4,6},{5,7},{6,8},{7,9},{8,10},{9,11},{10,... | collective-permute-start | bytes 983048
  110.5 21.3 %collective-permute-start = (bf16[80,2048]{1,0:T(8,128)(2,1)S(1)}, bf16[80,2048]{1,0:T(8,128)(2,1)}, u32[]{:S(2)}, u32[]{:S(2)}) collective-permute-start(bf16[80,2048]{1,0:T(8,128)(2,1)S(1)} %fusion), channel_id=1, source_target_pairs={{0,1},{1,2},{2,3},{3,4},{4,5},{5,6},{6,7},{7,8},{8,9},{9,10},{10,1... | collective-permute-start | bytes 983048
  115.5 16.3 %collective-permute-start.2 = (bf16[65,2048]{1,0:T(8,128)(2,1)}, bf16[65,2048]{1,0:T(8,128)(2,1)}, u32[]{:S(2)}, u32[]{:S(2)}) collective-permute-start(bf16[65,2048]{1,0:T(8,128)(2,1)} %slice.79), channel_id=1, source_target_pairs={{0,3},{1,4},{2,5},{3,6},{4,7},{5,8},{6,9},{7,10},{8,11},{9,12},{10... | collective-permute-start | bytes 798728
  149.9 62.2 %all-to-all-start = ((bf16[128,8,2048]{2,1,0:T(8,128)(2,1)}), bf16[128,8,2048]{2,1,0:T(8,128)(2,1)}, u32[]{:S(2)}, u32[]{:S(2)}) async-start(bf16[128,8,2048]{2,1,0:T(8,128)(2,1)} %bitcast.150), calls=%async_computation | async-start | bytes 8388608 | tf_op jit(solution)/shard_map/all_to_all | solution.py:150
  231.1 132.7 %all-to-all-start.1 = ((bf16[128,8,2048]{2,1,0:T(8,128)(2,1)}), bf16[128,8,2048]{2,1,0:T(8,128)(2,1)}, u32[]{:S(2)}, u32[]{:S(2)}) async-start(bf16[128,8,2048]{2,1,0:T(8,128)(2,1)} %convert_bitcast_fusion), calls=%async_computation.1 | async-start | bytes 8388608 | tf_op jit(solution)/shard_map/all_to_all | solution.py:159
  239.3 4.9 %copy-start.14 = (bf16[2,2048,352]{1,2,0:T(8,128)(2,1)S(1)}, bf16[2,2048,352]{1,2,0:T(8,128)(2,1)}, u32[]{:S(2)}) copy-start(bf16[2,2048,352]{1,2,0:T(8,128)(2,1)} %param.23) | copy-start | bytes 8650756
  258.4 81.3 %copy-start.11 = (f32[65,4]{0,1:T(4,128)S(1)}, f32[65,4]{0,1:T(4,128)}, u32[]{:S(2)}) copy-start(f32[65,4]{0,1:T(4,128)} %param.27) | copy-start | bytes 3124
  258.4 81.4 %copy-start.9 = (bf16[2048]{0:T(1024)(128)(2,1)S(1)}, bf16[2048]{0:T(1024)(128)(2,1)}, u32[]{:S(2)}) copy-start(bf16[2048]{0:T(1024)(128)(2,1)} %param.25) | copy-start | bytes 12292
  328.0 25.9 %collective-permute-start.4 = (bf16[80,2048]{1,0:T(8,128)(2,1)S(1)}, bf16[80,2048]{1,0:T(8,128)(2,1)S(1)}, u32[]{:S(2)}, u32[]{:S(2)}) collective-permute-start(bf16[80,2048]{1,0:T(8,128)(2,1)S(1)} %fusion.1), channel_id=1, source_target_pairs={{0,2},{1,3},{2,4},{3,5},{4,6},{5,7},{6,8},{7,9},{8,10},{9,11},{10,... | collective-permute-start | bytes 983048
  332.6 21.4 %collective-permute-start.3 = (bf16[80,2048]{1,0:T(8,128)(2,1)S(1)}, bf16[80,2048]{1,0:T(8,128)(2,1)S(1)}, u32[]{:S(2)}, u32[]{:S(2)}) collective-permute-start(bf16[80,2048]{1,0:T(8,128)(2,1)S(1)} %fusion.1), channel_id=1, source_target_pairs={{0,1},{1,2},{2,3},{3,4},{4,5},{5,6},{6,7},{7,8},{8,9},{9,10},{10,1... | collective-permute-start | bytes 983048
  335.7 18.3 %collective-permute-start.5 = (bf16[65,2048]{1,0:T(8,128)(2,1)S(1)}, bf16[65,2048]{1,0:T(8,128)(2,1)S(1)}, u32[]{:S(2)}, u32[]{:S(2)}) collective-permute-start(bf16[65,2048]{1,0:T(8,128)(2,1)S(1)} %slice.80), channel_id=1, source_target_pairs={{0,3},{1,4},{2,5},{3,6},{4,7},{5,8},{6,9},{7,10},{8,11},{9,12},{10... | collective-permute-start | bytes 798728
  376.2 8.4 %copy-start.1 = (bf16[1,704,2048]{2,1,0:T(8,128)(2,1)S(1)}, bf16[1,704,2048]{2,1,0:T(8,128)(2,1)}, u32[]{:S(2)}) copy-start(bf16[1,704,2048]{2,1,0:T(8,128)(2,1)} %param.29) | copy-start | bytes 8650756
Sparse Core Ops, SparseCore 0:
  146.0 93.5 all-gather.2
where the time goes:
time: 393 us; the launch traced here: 391 us
  blocking collectives  136 us (35%)
  waiting for transfers between devices  76.8 us (20%)
  local copies, waits for them, and re-layouts  57.2 us (15%)
  matrix products  48.2 us (12%)
  starting transfers between devices  40 us (10%)
  other arithmetic  18.7 us (5%)
  between operations  14.4 us (4%)
    unnamed x2, blocking collectives  136 us
    all_to_all x1, waiting for transfers between devices, on_device(): lax.all_to_all(outgoing, ('req', 'exp'), split_axis=0, concat_axis=0, til...  52.4 us
    unnamed x40, local copies, waits for them, and re-layouts  29 us
    unnamed x7, waiting for transfers between devices  24.1 us
    unnamed x6, starting transfers between devices  22.1 us
    dot_general x1, matrix products, on_device(): jnp.dot(hidden, expert_down[0], preferred_element_type=jnp.float32)  11.2 us
    all_to_all x1, starting transfers between devices, on_device(): lax.all_to_all(outgoing, ('req', 'exp'), split_axis=0, concat_axis=0, til...  9.69 us
    dot_general x1, matrix products, on_device(): partials = jnp.dot(hidden, shared_down, preferred_element_type=jnp.float32)  8.4 us
  transfers between devices with their start and end apart: 9, of which 4 were waited for; matrix products, arithmetic and copies ran while one was open for 32% of the time, Pallas kernels for 0%

commit v1 on v0

v1 whole, which is shorter than its diff:
```python
import functools

import jax
import jax.numpy as jnp
from jax import lax
from jax.experimental import pallas as pl
from jax.experimental.pallas import tpu as pltpu
from jax.sharding import PartitionSpec as P

HD = 128
SIDE = 4
ROWS = 72
NEG_FILL = -1e30
MIB = 1 << 20
BF = jnp.bfloat16
F32 = jnp.float32
NT = (((1,), (1,)), ((), ()))


def vmem(limit):
    return pltpu.CompilerParams(vmem_limit_bytes=limit * MIB)


def dot(a, b):
    return jnp.dot(a, b, preferred_element_type=F32)


def attention_kernel(lens, table, pre, dec, pool, out, keys, values, scores, sems):
    scale = HD ** (-0.5)
    copies = [
        pltpu.make_async_copy(pool.at[i], buf, sems.at[i]) for i, buf in enumerate((keys, values))
    ]
    for c in copies:
        c.start()
    spans, _, span, _ = pre.shape
    part = span // 2
    for r in range(spans):
        for h in range(2):
            width = part * (h + 1)
            q = pre[r, 0, h * part : (h + 1) * part, :]
            k = pre[r, 1, :width, :]
            v = pre[r, 2, :width, :]
            s = lax.dot_general(q, k, NT, preferred_element_type=F32) * scale
            row = lax.broadcasted_iota(jnp.int32, s.shape, 0) + h * part
            col = lax.broadcasted_iota(jnp.int32, s.shape, 1)
            s = jnp.where(col <= row, s, NEG_FILL)
            p = jnp.exp(s - jnp.max(s, axis=-1, keepdims=True))
            w = (p / jnp.sum(p, axis=-1, keepdims=True)).astype(BF)
            out[r * span + h * part : r * span + (h + 1) * part, :] = dot(w, v).astype(BF)
    requests, entries = table.shape
    pages, page = keys.shape[0], keys.shape[1]
    held = jnp.clip(
        lens[...] - page * lax.broadcasted_iota(jnp.int32, (requests, entries), 1), 0, page
    )
    ids = table[...]
    lane = lax.broadcasted_iota(jnp.int32, (requests, page), 1)
    limit = jnp.zeros((requests, page), jnp.int32)
    for j in range(entries):
        limit = limit + jnp.where(ids[:, j : j + 1] == lane, held[:, j : j + 1], 0)
    q = dec[0]
    own = jnp.sum(q.astype(F32) * dec[1].astype(F32), axis=-1, keepdims=True) * scale
    group = 4
    wide = group * page
    copies[0].wait()
    top = jnp.full((requests, wide), NEG_FILL, F32)
    for c in range(pages // group):
        k = keys[c * group : (c + 1) * group].reshape(wide, HD)
        s = lax.dot_general(q, k, NT, preferred_element_type=F32) * scale
        s = jnp.concatenate(
            [
                jnp.where(
                    lane < limit[:, c * group + g : c * group + g + 1],
                    s[:, g * page : (g + 1) * page],
                    NEG_FILL,
                )
                for g in range(group)
            ],
            axis=1,
        )
        scores[:, c * wide : (c + 1) * wide] = s
        top = jnp.maximum(top, s)
    top = jnp.maximum(jnp.max(top, axis=-1, keepdims=True), own)
    total = jnp.zeros((requests, wide), F32)
    for c in range(pages // group):
        p = jnp.exp(scores[:, c * wide : (c + 1) * wide] - top)
        scores[:, c * wide : (c + 1) * wide] = p
        total = total + p
    own = jnp.exp(own - top)
    total = jnp.sum(total, axis=-1, keepdims=True) + own
    copies[1].wait()
    mixed = (own / total).astype(BF).astype(F32) * dec[2].astype(F32)
    for c in range(pages // group):
        w = (scores[:, c * wide : (c + 1) * wide] / total).astype(BF)
        mixed = mixed + dot(w, values[c * group : (c + 1) * group].reshape(wide, HD))
    out[spans * span : spans * span + requests, :] = mixed.astype(BF)


def attention(prefill_qkv, decode_qkv, cache_pool, page_table, cache_len):
    requests = decode_qkv.shape[0]
    pages, page = cache_pool.shape[1:3]
    rows = prefill_qkv.shape[0] * prefill_qkv.shape[2] + requests
    whole = pl.BlockSpec(memory_space=pltpu.VMEM)
    return pl.pallas_call(
        attention_kernel,
        out_shape=jax.ShapeDtypeStruct((rows, HD), BF),
        in_specs=[whole, whole, whole, whole, pl.BlockSpec(memory_space=pl.ANY)],
        out_specs=whole,
        scratch_shapes=[
            pltpu.VMEM((pages, page, HD), BF),
            pltpu.VMEM((pages, page, HD), BF),
            pltpu.VMEM((requests, pages * page), F32),
            pltpu.SemaphoreType.DMA((2,)),
        ],
        compiler_params=vmem(48),
        name="attention",
    )(cache_len[:, None], page_table, prefill_qkv, decode_qkv.transpose(1, 0, 2), cache_pool)


def project_kernel(mine, blocks, weight, *outs):
    half = weight.shape[1] // 2
    at_x, at_z = mine[0] // SIDE, mine[0] % SIDE

    def rows(picked):
        return jnp.concatenate([blocks[i].astype(F32) for i in picked], axis=0).astype(BF)

    xs = [jnp.bitwise_xor(at_x, d) * SIDE for d in range(SIDE)]
    zs = [jnp.bitwise_xor(at_z, d) for d in range(SIDE)]
    for d in range(SIDE):
        outs[d][...] = dot(rows([xs[d] + z for z in zs]), weight[:, :half]).astype(BF)
        outs[SIDE + d][...] = dot(rows([x + zs[d] for x in xs]), weight[:, half:]).astype(BF)


def project(attended, out_weight, mine):
    blocks = attended.reshape(SIDE * SIDE, -1, HD)
    blocks = jnp.pad(blocks, ((0, 0), (0, ROWS - blocks.shape[1]), (0, 0)))
    half = out_weight.shape[1] // 2
    whole = pl.BlockSpec(memory_space=pltpu.VMEM)
    return pl.pallas_call(
        project_kernel,
        out_shape=[jax.ShapeDtypeStruct((SIDE * ROWS, half), BF)] * (2 * SIDE),
        in_specs=[pl.BlockSpec(memory_space=pltpu.SMEM), whole, whole],
        out_specs=[whole] * (2 * SIDE),
        compiler_params=vmem(32),
        name="project",
    )(mine, blocks, out_weight)


def along_x(a, d):
    return lax.ppermute(a, "exp", [(i, i ^ (d * SIDE)) for i in range(SIDE * SIDE)])


def along_z(a, d):
    return lax.ppermute(a, "exp", [(i, i ^ d) for i in range(SIDE * SIDE)])


def add_up(parts):
    total = parts[0].astype(F32)
    for p in parts[1:]:
        total = total + p.astype(F32)
    return total


def reduce_scatter(parts):
    parts_a, parts_b = parts[:SIDE], parts[SIDE:]
    got_a, got_b = [parts_a[0]], [parts_b[0]]
    for d in (2, 1, 3):
        got_a.append(along_x(parts_a[d], d))
        got_b.append(along_z(parts_b[d], d))
    sum_a = add_up(got_a).astype(BF).reshape(SIDE, ROWS, -1)
    sum_b = add_up(got_b).astype(BF).reshape(SIDE, ROWS, -1)
    sum_a, sum_b = lax.optimization_barrier((sum_a, sum_b))
    got_a, got_b = [sum_a[0]], [sum_b[0]]
    for d in (2, 1, 3):
        got_a.append(along_z(sum_a[d], d))
        got_b.append(along_x(sum_b[d], d))
    return got_a, got_b


def token_kernel(a0, a1, a2, a3, b0, b1, b2, b3, residual, gain, select, stream, normed, outgoing):
    f = lambda r: r[...].astype(F32)
    projected = jnp.concatenate(
        [f(a0) + f(a1) + f(a2) + f(a3), f(b0) + f(b1) + f(b2) + f(b3)], axis=1
    )
    held = (f(residual) + projected).astype(BF)
    stream[...] = held
    wide = held.astype(F32)
    mean = jnp.mean(wide * wide, axis=-1, keepdims=True)
    rows = (wide * lax.rsqrt(mean + 1e-06) * gain[...]).astype(BF)
    normed[...] = rows
    experts, _, capacity, width = outgoing.shape
    group = 8
    for g in range(experts // group):
        n = group * capacity
        picked = dot(select[g * n : (g + 1) * n, :], rows).reshape(group, capacity, width).astype(BF)
        outgoing[g * group : (g + 1) * group, 0] = picked
        outgoing[g * group : (g + 1) * group, 1] = picked


def expert_kernel(rows, gate_up, down, out):
    x = rows[...]
    gate = dot(x, gate_up[0, 0])
    up = dot(x, gate_up[0, 1])
    hidden = (gate / (1.0 + jnp.exp(-gate)) * up).astype(BF)
    out[...] = dot(hidden, down[0]).astype(BF)


def experts(rows, gate_up, down):
    count, width = rows.shape
    step = 256
    return pl.pallas_call(
        expert_kernel,
        grid=(count // step,),
        out_shape=jax.ShapeDtypeStruct((count, width), BF),
        in_specs=[
            pl.BlockSpec((step, width), lambda i: (i, 0)),
            pl.BlockSpec(gate_up.shape, lambda i: (0, 0, 0, 0)),
            pl.BlockSpec(down.shape, lambda i: (0, 0, 0)),
        ],
        out_specs=pl.BlockSpec((step, width), lambda i: (i, 0)),
        compiler_params=vmem(40),
        cost_estimate=pl.CostEstimate(
            flops=6 * count * width * down.shape[1],
            bytes_accessed=2 * (2 * count * width + 3 * width * down.shape[1]),
            transcendentals=count * down.shape[1],
        ),
        name="experts",
    )(rows, gate_up, down)


def shared_kernel(mine, rows, gate_up, down, *rest):
    outs, hidden = rest[:-1], rest[-1]
    half = down.shape[1] // 2
    for g in range(SIDE):
        x = rows[g * SIDE * ROWS : (g + 1) * SIDE * ROWS, :]
        gate = dot(x, gate_up[0])
        up = dot(x, gate_up[1])
        hidden[g] = (gate / (1.0 + jnp.exp(-gate)) * up).reshape(SIDE, ROWS, -1)
    at_x, at_z = mine[0] // SIDE, mine[0] % SIDE
    for d in range(SIDE):
        x_row = jnp.bitwise_xor(at_x, d)
        z_row = jnp.bitwise_xor(at_z, d)
        part = jnp.concatenate([hidden[x_row, jnp.bitwise_xor(at_z, j)] for j in range(SIDE)], axis=0)
        outs[d][...] = dot(part.astype(BF), down[:, :half]).astype(BF)
        part = jnp.concatenate([hidden[jnp.bitwise_xor(at_x, j), z_row] for j in range(SIDE)], axis=0)
        outs[SIDE + d][...] = dot(part.astype(BF), down[:, half:]).astype(BF)


def shared_expert(mine, rows, gate_up, down):
    whole = pl.BlockSpec(memory_space=pltpu.VMEM)
    half = down.shape[1] // 2
    count, width = rows.shape
    return pl.pallas_call(
        shared_kernel,
        out_shape=[jax.ShapeDtypeStruct((SIDE * ROWS, half), BF)] * (2 * SIDE),
        in_specs=[pl.BlockSpec(memory_space=pltpu.SMEM), whole, whole, whole],
        out_specs=[whole] * (2 * SIDE),
        scratch_shapes=[pltpu.VMEM((SIDE, SIDE, ROWS, down.shape[0]), F32)],
        compiler_params=vmem(48),
        cost_estimate=pl.CostEstimate(
            flops=6 * count * width * down.shape[0],
            bytes_accessed=2 * (2 * count * width + 3 * width * down.shape[0]),
            transcendentals=count * down.shape[0],
        ),
        name="shared_expert",
    )(mine, rows, gate_up, down)


def on_device(
    residual,
    prefill_qkv,
    decode_qkv,
    cache_pool,
    page_table,
    cache_len,
    out_weight,
    norm_gain,
    shared_gate_up,
    shared_down,
    shared_gate,
    routes,
    route_weight,
    expert_gate_up,
    expert_down,
):
    mine = lax.axis_index("exp")
    groups = lax.axis_size("exp")
    tok_rows, width = residual.shape
    devices = groups * lax.axis_size("req")
    experts_all = devices // 2
    route_count = routes.shape[1]
    capacity = 8

    flat = routes.reshape(-1)
    place = jnp.arange(flat.shape[0], dtype=jnp.int32)
    same = (flat[:, None] == flat[None, :]) & (place[None, :] < place[:, None])
    rank = jnp.sum(same.astype(jnp.int32), axis=1)
    slot_of = (flat * capacity + rank).reshape(tok_rows, route_count)
    slot_of = jnp.pad(slot_of, ((0, ROWS - tok_rows), (0, 0)), constant_values=-1)
    weight = jnp.pad(route_weight, ((0, ROWS - tok_rows), (0, 0)))
    slots = jnp.arange(experts_all * capacity, dtype=jnp.int32)
    select = jnp.any(slots[:, None, None] == slot_of[None], axis=-1).astype(BF)
    columns = jnp.arange(devices * capacity, dtype=jnp.int32)
    columns = columns // (2 * capacity) * capacity + columns % capacity
    mix = jnp.sum(
        jnp.where(slot_of[:, :, None] == columns[None, None, :], weight[:, :, None], 0.0), axis=1
    )
    mix_high = mix.astype(BF)
    mix_low = (mix - mix_high.astype(F32)).astype(BF)
    mix = jnp.concatenate([mix_high, mix_low], axis=0)

    attended = attention(prefill_qkv, decode_qkv, cache_pool, page_table, cache_len)
    got_a, got_b = reduce_scatter(project(attended, out_weight, mine[None]))
    stream, normed, outgoing = pl.pallas_call(
        token_kernel,
        out_shape=[
            jax.ShapeDtypeStruct((ROWS, width), BF),
            jax.ShapeDtypeStruct((ROWS, width), BF),
            jax.ShapeDtypeStruct((experts_all, 2, capacity, width), BF),
        ],
        compiler_params=vmem(32),
        name="token_rows",
    )(
        *got_a,
        *got_b,
        jnp.pad(residual, ((0, ROWS - tok_rows), (0, 0))),
        norm_gain[None, :],
        select,
    )
    block_rows = lax.all_gather(normed, "exp", axis=0, tiled=True)
    arrived = lax.all_to_all(
        outgoing.reshape(devices, capacity, width),
        ("req", "exp"),
        split_axis=0,
        concat_axis=0,
        tiled=True,
    )
    answer = experts(arrived.reshape(devices * capacity, width), expert_gate_up, expert_down)
    returned = lax.all_to_all(
        answer.reshape(devices, capacity, width),
        ("req", "exp"),
        split_axis=0,
        concat_axis=0,
        tiled=True,
    )
    parts = shared_expert(mine[None], block_rows, shared_gate_up, shared_down)
    got_a, got_b = reduce_scatter(parts)
    shared = jnp.concatenate([add_up(got_a), add_up(got_b)], axis=1)
    shared_scale = jax.nn.sigmoid(dot(normed, shared_gate))
    routed = dot(mix, returned.reshape(devices * capacity, width))
    routed = routed[:ROWS] + routed[ROWS:]
    result = stream.astype(F32) + routed + shared_scale[:, None] * shared
    return result[:tok_rows].astype(BF)


def solution(mesh):
    placed = (
        P(("req", "exp"), None),
        P("req", None, None, "exp"),
        P("req", None, "exp"),
        P(None, "req", None, "exp"),
        P("req", None),
        P("req"),
        P("exp", None),
        P(),
        P(None, None, "exp"),
        P("exp", None),
        P(),
        P(("req", "exp"), None),
        P(("req", "exp"), None),
        P(("req", "exp"), None, None, None),
        P(("req", "exp"), None, None),
    )
    return jax.shard_map(
        on_device, mesh=mesh, in_specs=placed, out_specs=P(("req", "exp"), None), check_vma=False
    )
```

time: 393 us -> 281 us (0.72)
  the two profiles are of different devices: /device:TPU:66 before, /device:TPU:8 now
where the time goes in v1:
time: 281 us; the launch traced here: 278 us
  waiting for transfers between devices  130 us (46%)
  starting transfers between devices  59.1 us (21%)
  Pallas kernels  33.2 us (12%)
  local copies, waits for them, and re-layouts  29.5 us (10%)
  between operations  13.7 us (5%)
  other arithmetic  7.73 us (3%)
  matrix products  4.35 us (2%)
    all_to_all x1, waiting for transfers between devices, on_device(): lax.all_to_all(outgoing.reshape(devices, capacity, width), ('req', 'exp')...  46.9 us
    all_gather x1, waiting for transfers between devices, on_device(): block_rows = lax.all_gather(normed, 'exp', axis=0, tiled=True)  38.8 us
    ppermute x12, waiting for transfers between devices, along_x(): lax.ppermute(a, 'exp', [(i, i ^ d * SIDE) for i in range(SIDE * SIDE)])  33.1 us
    unnamed x40, local copies, waits for them, and re-layouts  25.8 us
    ppermute x12, starting transfers between devices, along_z(): return lax.ppermute(a, 'exp', [(i, i ^ d) for i in range(SIDE * SIDE)])  22.9 us
    ppermute x12, starting transfers between devices, along_x(): lax.ppermute(a, 'exp', [(i, i ^ d * SIDE) for i in range(SIDE * SIDE)])  20.4 us
    pallas_call x1, Pallas kernels, experts(): pl.pallas_call(expert_kernel, grid=(count // step,), out_shape=jax.ShapeD...  13.6 us
    pallas_call x1, Pallas kernels, shared_expert(): pl.pallas_call(shared_kernel, out_shape=[jax.ShapeDtypeStruct((SIDE * ROW...  11.7 us
  transfers between devices with their start and end apart: 27, of which 17 were waited for; matrix products, arithmetic and copies ran while one was open for 9% of the time, Pallas kernels for 9%

profile of v1, /device:TPU:8, one launch (start us, length us, event | category | flops | bytes accessed | tf_op | source)
XLA Modules:
  0.0 277.8 jit_solution(3237040550336567751)
XLA Ops:
  7.3 1.1 copy-done.2
  9.8 4.3 %attention.1 = bf16[1040,128]{1,0:T(8,128)(2,1)S(1)} custom-call(s32[16,1]{1,0:T(8,128)S(1)} %copy.38.lens, s32[16,64]{1,0:T(8,128)S(1)} %copy-done.5, bf16[2,3,512,128]{3,2,1,0:T(8,128)(2,1)S(1)} %copy-done.2, bf16[3,16,128]{2,1,0:T(8,128)(2,1)S(1)} %bitcast.63, bf16[2,124,128,128]{3,2,1,0:T(8,128)(2,1)} %pool.1), custom_call_target="tpu_custom_call" | custom-call | tf_op jit(solution)/shard_map/attention/pallas_call | solution.py:103
  14.3 0.9 copy-done.3
  15.1 2.0 project.1
  17.2 3.0 %collective-permute-start = (bf16[288,1024]{1,0:T(8,128)(2,1)S(1)}, bf16[288,1024]{1,0:T(8,128)(2,1)S(1)}, u32[]{:S(2)}, u32[]{:S(2)}) collective-permute-start(bf16[288,1024]{1,0:T(8,128)(2,1)S(1)} %get-tuple-element.29), channel_id=1, source_target_pairs={{0,8},{1,9},{2,10},{3,11},{4,12},{5,13},{6,14},{7,15},{8,0},{9,1},... | collective-permute-start | bytes 1769480 | tf_op jit(solution)/shard_map/ppermute | solution.py:149
  21.4 3.9 %collective-permute-start.3 = (bf16[288,1024]{1,0:T(8,128)(2,1)S(1)}, bf16[288,1024]{1,0:T(8,128)(2,1)S(1)}, u32[]{:S(2)}, u32[]{:S(2)}) collective-permute-start(bf16[288,1024]{1,0:T(8,128)(2,1)S(1)} %get-tuple-element.33), channel_id=1, source_target_pairs={{0,2},{1,3},{2,0},{3,1},{4,6},{5,7},{6,4},{7,5},{8,10},{9,11},{10,... | collective-permute-start | bytes 1769480 | tf_op jit(solution)/shard_map/ppermute | solution.py:153
  25.2 1.0 collective-permute-start.4
  26.3 8.7 %collective-permute-done = bf16[288,1024]{1,0:T(8,128)(2,1)S(1)} collective-permute-done((bf16[288,1024]{1,0:T(8,128)(2,1)S(1)}, bf16[288,1024]{1,0:T(8,128)(2,1)S(1)}, u32[]{:S(2)}, u32[]{:S(2)}) %collective-permute-start) | collective-permute-done | bytes 589856 | tf_op jit(solution)/shard_map/ppermute | solution.py:149
  35.8 4.0 %collective-permute-start.5 = (bf16[288,1024]{1,0:T(8,128)(2,1)S(1)}, bf16[288,1024]{1,0:T(8,128)(2,1)}, u32[]{:S(2)}, u32[]{:S(2)}) collective-permute-start(bf16[288,1024]{1,0:T(8,128)(2,1)S(1)} %get-tuple-element.35), channel_id=1, source_target_pairs={{0,3},{1,2},{2,1},{3,0},{4,7},{5,6},{6,5},{7,4},{8,11},{9,10},{10,... | collective-permute-start | bytes 1769480 | tf_op jit(solution)/shard_map/ppermute | solution.py:153
  43.2 3.4 %collective-permute-done.1 = bf16[288,1024]{1,0:T(8,128)(2,1)} collective-permute-done((bf16[288,1024]{1,0:T(8,128)(2,1)}, bf16[288,1024]{1,0:T(8,128)(2,1)}, u32[]{:S(2)}, u32[]{:S(2)}) %collective-permute-start.1) | collective-permute-done | bytes 589856 | tf_op jit(solution)/shard_map/ppermute | solution.py:149
  46.6 1.8 add_convert_fusion.3
  48.5 3.0 %collective-permute-done.4 = bf16[288,1024]{1,0:T(8,128)(2,1)} collective-permute-done((bf16[288,1024]{1,0:T(8,128)(2,1)S(1)}, bf16[288,1024]{1,0:T(8,128)(2,1)}, u32[]{:S(2)}, u32[]{:S(2)}) %collective-permute-start.4) | collective-permute-done | bytes 589856 | tf_op jit(solution)/shard_map/ppermute | solution.py:153
  51.7 1.7 add_convert_fusion.2
  53.5 3.4 %collective-permute-start.8 = (bf16[72,1024]{1,0:T(8,128)(2,1)S(1)}, bf16[72,1024]{1,0:T(8,128)(2,1)S(1)}, u32[]{:S(2)}, u32[]{:S(2)}) collective-permute-start(bf16[72,1024]{1,0:T(8,128)(2,1)S(1)} %get-tuple-element.65), channel_id=1, source_target_pairs={{0,3},{1,2},{2,1},{3,0},{4,7},{5,6},{6,5},{7,4},{8,11},{9,10},{10,... | collective-permute-start | bytes 442376 | tf_op jit(solution)/shard_map/ppermute | solution.py:153
  56.9 1.6 collective-permute-start.6
  58.5 2.8 %collective-permute-start.11 = (bf16[72,1024]{1,0:T(8,128)(2,1)S(1)}, bf16[72,1024]{1,0:T(8,128)(2,1)S(1)}, u32[]{:S(2)}, u32[]{:S(2)}) collective-permute-start(bf16[72,1024]{1,0:T(8,128)(2,1)S(1)} %get-tuple-element.61), channel_id=1, source_target_pairs={{0,12},{1,13},{2,14},{3,15},{4,8},{5,9},{6,10},{7,11},{8,4},{9,5},... | collective-permute-start | bytes 442376 | tf_op jit(solution)/shard_map/ppermute | solution.py:149
  61.6 3.0 %collective-permute-start.9 = (bf16[72,1024]{1,0:T(8,128)(2,1)S(1)}, bf16[72,1024]{1,0:T(8,128)(2,1)S(1)}, u32[]{:S(2)}, u32[]{:S(2)}) collective-permute-start(bf16[72,1024]{1,0:T(8,128)(2,1)S(1)} %get-tuple-element.63), channel_id=1, source_target_pairs={{0,8},{1,9},{2,10},{3,11},{4,12},{5,13},{6,14},{7,15},{8,0},{9,1},... | collective-permute-start | bytes 442376 | tf_op jit(solution)/shard_map/ppermute | solution.py:149
  65.5 0.9 collective-permute-done.10.b2
  66.4 1.8 collective-permute-done.9.b1
  68.2 1.6 token_rows.1
  69.8 2.0 copy-done.1
  71.8 9.6 %all-to-all-start = ((bf16[128,8,2048]{2,1,0:T(8,128)(2,1)}), bf16[128,8,2048]{2,1,0:T(8,128)(2,1)}, u32[]{:S(2)}, u32[]{:S(2)}) async-start(bf16[128,8,2048]{2,1,0:T(8,128)(2,1)} %bitcast.62), calls=%async_computation | async-start | bytes 8388608 | tf_op jit(solution)/shard_map/all_to_all | solution.py:330
  81.4 8.5 %copy.42.gate_up = bf16[1,2,2048,704]{3,2,1,0:T(8,128)(2,1)} copy(bf16[1,2,2048,704]{2,3,1,0:T(8,128)(2,1)} %param.28) | data formatting | bytes 11534336 | tf_op args[13]
  90.0 46.9 %all-to-all-done = bf16[128,8,2048]{2,1,0:T(8,128)(2,1)} async-done(((bf16[128,8,2048]{2,1,0:T(8,128)(2,1)}), bf16[128,8,2048]{2,1,0:T(8,128)(2,1)}, u32[]{:S(2)}, u32[]{:S(2)}) %all-to-all-start) | async-done | bytes 4194336 | tf_op jit(solution)/shard_map/all_to_all | solution.py:330
  136.8 1.8 copy-done.7
  138.6 13.6 %experts.1 = bf16[1024,2048]{1,0:T(8,128)(2,1)S(1)} custom-call(bf16[1024,2048]{1,0:T(8,128)(2,1)} %bitcast.15.rows, bf16[1,2,2048,704]{3,2,1,0:T(8,128)(2,1)} %copy.42.gate_up, bf16[1,704,2048]{2,1,0:T(8,128)(2,1)S(1)} %copy-done.7), custom_call_target="tpu_custom_call" | custom-call | flops 8858370048 | bytes 17039360 | tf_op jit(solution)/shard_map/experts/pallas_call | solution.py:210
  152.3 2.0 copy-done
  154.3 6.2 %all-to-all-start.1 = ((bf16[128,8,2048]{2,1,0:T(8,128)(2,1)}), bf16[128,8,2048]{2,1,0:T(8,128)(2,1)}, u32[]{:S(2)}, u32[]{:S(2)}) async-start(bf16[128,8,2048]{2,1,0:T(8,128)(2,1)} %bitcast.61), calls=%async_computation.1 | async-start | bytes 8388608 | tf_op jit(solution)/shard_map/all_to_all | solution.py:338
  160.6 4.7 %copy.43.gate_up = bf16[2,2048,352]{2,1,0:T(8,128)(2,1)} copy(bf16[2,2048,352]{1,2,0:T(8,128)(2,1)} %param.23) | data formatting | bytes 5767168 | tf_op args[8]
  166.3 38.8 %all-gather.2.cloned.1.call-done.rows = bf16[1152,2048]{1,0:T(8,128)(2,1)} async-done(((bf16[72,2048]{1,0:T(8,128)(2,1)}), bf16[1152,2048]{1,0:T(8,128)(2,1)}) %all-gather.2.cloned.1.call-update) | async-done | bytes 4718608 | tf_op jit(solution)/shard_map/all_gather | solution.py:329
  205.0 11.7 %shared_expert.1 = (bf16[288,1024]{1,0:T(8,128)(2,1)S(1)}, bf16[288,1024]{1,0:T(8,128)(2,1)}, bf16[288,1024]{1,0:T(8,128)(2,1)}, bf16[288,1024]{1,0:T(8,128)(2,1...) custom-call(s32[1]{0:T(128)} %bitcast.mine, ...), custom_call_target="tpu_custom_call" | custom-call | flops 4982833152 | bytes 13762560 | tf_op jit(solution)/shard_map/shared_expert/pallas_call | solution.py:252
  218.4 2.0 collective-permute-start.12
  220.4 1.1 fusion.5
  221.6 3.8 %collective-permute-start.13 = (bf16[288,1024]{1,0:T(8,128)(2,1)}, bf16[288,1024]{1,0:T(8,128)(2,1)S(1)}, u32[]{:S(2)}, u32[]{:S(2)}) collective-permute-start(bf16[288,1024]{1,0:T(8,128)(2,1)} %get-tuple-element.43), channel_id=1, source_target_pairs={{0,4},{1,5},{2,6},{3,7},{4,0},{5,1},{6,2},{7,3},{8,12},{9,13},{10,... | collective-permute-start | bytes 1769480 | tf_op jit(solution)/shard_map/ppermute | solution.py:149
  225.3 3.2 %fusion = f32[144,2048]{1,0:T(8,128)S(1)} fusion(bf16[128,8,2048]{2,1,0:T(8,128)(2,1)} %all-to-all-done.1, bf16[72,1024]{1,0:T(8,128)(2,1)} %get-tuple-element.51, bf16[72,1024]{1,0:T(8,128)(2,1)} %get-tuple-element.52), kind=kOutput, calls=%fused_computation | convolution fusion | flops 604569600 | bytes 5668864 | tf_op jit(solution)/shard_map/dot_general | solution.py:25
  228.6 1.1 collective-permute-start.15
  229.6 2.2 collective-permute-start.16
  231.8 4.2 %collective-permute-done.12 = bf16[288,1024]{1,0:T(8,128)(2,1)S(1)} collective-permute-done((bf16[288,1024]{1,0:T(8,128)(2,1)}, bf16[288,1024]{1,0:T(8,128)(2,1)S(1)}, u32[]{:S(2)}, u32[]{:S(2)}) %collective-permute-start.12) | collective-permute-done | bytes 589856 | tf_op jit(solution)/shard_map/ppermute | solution.py:149
  236.0 1.5 collective-permute-start.17
  237.6 9.9 %collective-permute-done.13 = bf16[288,1024]{1,0:T(8,128)(2,1)S(1)} collective-permute-done((bf16[288,1024]{1,0:T(8,128)(2,1)}, bf16[288,1024]{1,0:T(8,128)(2,1)S(1)}, u32[]{:S(2)}, u32[]{:S(2)}) %collective-permute-start.13) | collective-permute-done | bytes 589856 | tf_op jit(solution)/shard_map/ppermute | solution.py:149
  247.5 1.5 add_convert_fusion.1
  249.0 6.4 %collective-permute-done.16 = bf16[288,1024]{1,0:T(8,128)(2,1)S(1)} collective-permute-done((bf16[288,1024]{1,0:T(8,128)(2,1)S(1)}, bf16[288,1024]{1,0:T(8,128)(2,1)S(1)}, u32[]{:S(2)}, u32[]{:S(2)}) %collective-permute-start.16) | collective-permute-done | bytes 589856 | tf_op jit(solution)/shard_map/ppermute | solution.py:153
  255.8 3.0 %collective-permute-start.18 = (bf16[72,1024]{1,0:T(8,128)(2,1)S(1)}, bf16[72,1024]{1,0:T(8,128)(2,1)S(1)}, u32[]{:S(2)}, u32[]{:S(2)}) collective-permute-start(bf16[72,1024]{1,0:T(8,128)(2,1)S(1)} %get-tuple-element.55), channel_id=1, source_target_pairs={{0,2},{1,3},{2,0},{3,1},{4,6},{5,7},{6,4},{7,5},{8,10},{9,11},{10,... | collective-permute-start | bytes 442376 | tf_op jit(solution)/shard_map/ppermute | solution.py:153
  258.8 1.2 collective-permute-start.20
  260.1 3.3 %collective-permute-start.21 = (bf16[72,1024]{1,0:T(8,128)(2,1)S(1)}, bf16[72,1024]{1,0:T(8,128)(2,1)S(1)}, u32[]{:S(2)}, u32[]{:S(2)}) collective-permute-start(bf16[72,1024]{1,0:T(8,128)(2,1)S(1)} %get-tuple-element.58), channel_id=1, source_target_pairs={{0,8},{1,9},{2,10},{3,11},{4,12},{5,13},{6,14},{7,15},{8,0},{9,1},... | collective-permute-start | bytes 442376 | tf_op jit(solution)/shard_map/ppermute | solution.py:149
  263.4 0.9 collective-permute-start.23
  264.6 1.4 collective-permute-done.20
  266.9 3.1 %collective-permute-done.23 = bf16[72,1024]{1,0:T(8,128)(2,1)S(1)} collective-permute-done((bf16[72,1024]{1,0:T(8,128)(2,1)S(1)}, bf16[72,1024]{1,0:T(8,128)(2,1)S(1)}, u32[]{:S(2)}, u32[]{:S(2)}) %collective-permute-start.23) | collective-permute-done | bytes 147488 | tf_op jit(solution)/shard_map/ppermute | solution.py:149
  (83 shorter events, 14.5 us)
Async XLA Ops:
  6.5 198.5 %all-gather.2.cloned.1.call-start = ((), (), s32[]{:S(2)}) async-start(), calls=%async_computation.2 | async-start | bytes 5013504 | tf_op jit(solution)/shard_map/all_gather | solution.py:329
  7.3 1.1 copy-start.2
  8.4 0.7 copy-start.4
  9.1 0.7 copy-start.5
  14.1 1.0 copy-start.3
  14.1 25.7 %copy-start.15 = (s32[65,4]{0,1:T(4,128)S(1)}, s32[65,4]{0,1:T(4,128)}, u32[]{:S(2)}) copy-start(s32[65,4]{0,1:T(4,128)} %param.26) | copy-start | bytes 3124
  17.2 17.8 %collective-permute-start = (bf16[288,1024]{1,0:T(8,128)(2,1)S(1)}, bf16[288,1024]{1,0:T(8,128)(2,1)S(1)}, u32[]{:S(2)}, u32[]{:S(2)}) collective-permute-start(bf16[288,1024]{1,0:T(8,128)(2,1)S(1)} %get-tuple-element.29), channel_id=1, source_target_pairs={{0,8},{1,9},{2,10},{3,11},{4,12},{5,13},{6,14},{7,15},{8,0},{9,1},... | collective-permute-start | bytes 1769480 | tf_op jit(solution)/shard_map/ppermute | solution.py:149
  20.2 26.4 %collective-permute-start.1 = (bf16[288,1024]{1,0:T(8,128)(2,1)}, bf16[288,1024]{1,0:T(8,128)(2,1)}, u32[]{:S(2)}, u32[]{:S(2)}) collective-permute-start(bf16[288,1024]{1,0:T(8,128)(2,1)} %get-tuple-element.30), channel_id=1, source_target_pairs={{0,4},{1,5},{2,6},{3,7},{4,0},{5,1},{6,2},{7,3},{8,12},{9,13},{10,... | collective-permute-start | bytes 1769480 | tf_op jit(solution)/shard_map/ppermute | solution.py:149
  20.8 25.8 %collective-permute-start.2 = (bf16[288,1024]{1,0:T(8,128)(2,1)}, bf16[288,1024]{1,0:T(8,128)(2,1)}, u32[]{:S(2)}, u32[]{:S(2)}) collective-permute-start(bf16[288,1024]{1,0:T(8,128)(2,1)} %get-tuple-element.31), channel_id=1, source_target_pairs={{0,12},{1,13},{2,14},{3,15},{4,8},{5,9},{6,10},{7,11},{8,4},{9,5},... | collective-permute-start | bytes 1769480 | tf_op jit(solution)/shard_map/ppermute | solution.py:149
  21.4 27.1 %collective-permute-start.3 = (bf16[288,1024]{1,0:T(8,128)(2,1)S(1)}, bf16[288,1024]{1,0:T(8,128)(2,1)S(1)}, u32[]{:S(2)}, u32[]{:S(2)}) collective-permute-start(bf16[288,1024]{1,0:T(8,128)(2,1)S(1)} %get-tuple-element.33), channel_id=1, source_target_pairs={{0,2},{1,3},{2,0},{3,1},{4,6},{5,7},{6,4},{7,5},{8,10},{9,11},{10,... | collective-permute-start | bytes 1769480 | tf_op jit(solution)/shard_map/ppermute | solution.py:153
  25.2 26.2 %collective-permute-start.4 = (bf16[288,1024]{1,0:T(8,128)(2,1)S(1)}, bf16[288,1024]{1,0:T(8,128)(2,1)}, u32[]{:S(2)}, u32[]{:S(2)}) collective-permute-start(bf16[288,1024]{1,0:T(8,128)(2,1)S(1)} %get-tuple-element.34), channel_id=1, source_target_pairs={{0,1},{1,0},{2,3},{3,2},{4,5},{5,4},{6,7},{7,6},{8,9},{9,8},{10,11... | collective-permute-start | bytes 1769480 | tf_op jit(solution)/shard_map/ppermute | solution.py:153
  35.0 0.8 copy-start.13
  35.8 15.9 %collective-permute-start.5 = (bf16[288,1024]{1,0:T(8,128)(2,1)S(1)}, bf16[288,1024]{1,0:T(8,128)(2,1)}, u32[]{:S(2)}, u32[]{:S(2)}) collective-permute-start(bf16[288,1024]{1,0:T(8,128)(2,1)S(1)} %get-tuple-element.35), channel_id=1, source_target_pairs={{0,3},{1,2},{2,1},{3,0},{4,7},{5,6},{6,5},{7,4},{8,11},{9,10},{10,... | collective-permute-start | bytes 1769480 | tf_op jit(solution)/shard_map/ppermute | solution.py:153
  53.4 11.5 %copy-start.14 = (bf16[65,2048]{1,0:T(8,128)(2,1)S(1)}, bf16[65,2048]{1,0:T(8,128)(2,1)}, u32[]{:S(2)}) copy-start(bf16[65,2048]{1,0:T(8,128)(2,1)} %param.15) | copy-start | bytes 798724
  53.4 14.8 %copy-start.6 = (f32[2048]{0:T(1024)S(1)}, f32[2048]{0:T(1024)}, u32[]{:S(2)}) copy-start(f32[2048]{0:T(1024)} %param.22) | copy-start | bytes 24580
  53.5 8.1 %collective-permute-start.8 = (bf16[72,1024]{1,0:T(8,128)(2,1)S(1)}, bf16[72,1024]{1,0:T(8,128)(2,1)S(1)}, u32[]{:S(2)}, u32[]{:S(2)}) collective-permute-start(bf16[72,1024]{1,0:T(8,128)(2,1)S(1)} %get-tuple-element.65), channel_id=1, source_target_pairs={{0,3},{1,2},{2,1},{3,0},{4,7},{5,6},{6,5},{7,4},{8,11},{9,10},{10,... | collective-permute-start | bytes 442376 | tf_op jit(solution)/shard_map/ppermute | solution.py:153
  56.9 8.0 %collective-permute-start.7 = (bf16[72,1024]{1,0:T(8,128)(2,1)S(1)}, bf16[72,1024]{1,0:T(8,128)(2,1)S(1)}, u32[]{:S(2)}, u32[]{:S(2)}) collective-permute-start(bf16[72,1024]{1,0:T(8,128)(2,1)S(1)} %get-tuple-element.66), channel_id=1, source_target_pairs={{0,1},{1,0},{2,3},{3,2},{4,5},{5,4},{6,7},{7,6},{8,9},{9,8},{10,11... | collective-permute-start | bytes 442376 | tf_op jit(solution)/shard_map/ppermute | solution.py:153
  56.9 8.0 %collective-permute-start.6 = (bf16[72,1024]{1,0:T(8,128)(2,1)S(1)}, bf16[72,1024]{1,0:T(8,128)(2,1)S(1)}, u32[]{:S(2)}, u32[]{:S(2)}) collective-permute-start(bf16[72,1024]{1,0:T(8,128)(2,1)S(1)} %get-tuple-element.67), channel_id=1, source_target_pairs={{0,2},{1,3},{2,0},{3,1},{4,6},{5,7},{6,4},{7,5},{8,10},{9,11},{10,... | collective-permute-start | bytes 442376 | tf_op jit(solution)/shard_map/ppermute | solution.py:153
  58.5 7.0 %collective-permute-start.11 = (bf16[72,1024]{1,0:T(8,128)(2,1)S(1)}, bf16[72,1024]{1,0:T(8,128)(2,1)S(1)}, u32[]{:S(2)}, u32[]{:S(2)}) collective-permute-start(bf16[72,1024]{1,0:T(8,128)(2,1)S(1)} %get-tuple-element.61), channel_id=1, source_target_pairs={{0,12},{1,13},{2,14},{3,15},{4,8},{5,9},{6,10},{7,11},{8,4},{9,5},... | collective-permute-start | bytes 442376 | tf_op jit(solution)/shard_map/ppermute | solution.py:149
  61.3 5.1 %collective-permute-start.10 = (bf16[72,1024]{1,0:T(8,128)(2,1)S(1)}, bf16[72,1024]{1,0:T(8,128)(2,1)S(1)}, u32[]{:S(2)}, u32[]{:S(2)}) collective-permute-start(bf16[72,1024]{1,0:T(8,128)(2,1)S(1)} %get-tuple-element.62), channel_id=1, source_target_pairs={{0,4},{1,5},{2,6},{3,7},{4,0},{5,1},{6,2},{7,3},{8,12},{9,13},{10,... | collective-permute-start | bytes 442376 | tf_op jit(solution)/shard_map/ppermute | solution.py:149
  61.6 6.6 %collective-permute-start.9 = (bf16[72,1024]{1,0:T(8,128)(2,1)S(1)}, bf16[72,1024]{1,0:T(8,128)(2,1)S(1)}, u32[]{:S(2)}, u32[]{:S(2)}) collective-permute-start(bf16[72,1024]{1,0:T(8,128)(2,1)S(1)} %get-tuple-element.63), channel_id=1, source_target_pairs={{0,8},{1,9},{2,10},{3,11},{4,12},{5,13},{6,14},{7,15},{8,0},{9,1},... | collective-permute-start | bytes 442376 | tf_op jit(solution)/shard_map/ppermute | solution.py:149
  69.8 2.0 copy-start.1
  71.8 65.0 %all-to-all-start = ((bf16[128,8,2048]{2,1,0:T(8,128)(2,1)}), bf16[128,8,2048]{2,1,0:T(8,128)(2,1)}, u32[]{:S(2)}, u32[]{:S(2)}) async-start(bf16[128,8,2048]{2,1,0:T(8,128)(2,1)} %bitcast.62), calls=%async_computation | async-start | bytes 8388608 | tf_op jit(solution)/shard_map/all_to_all | solution.py:330
  136.8 1.8 copy-start.7
  152.3 2.0 copy-start
  154.3 6.2 %copy-start.16 = (bf16[2048]{0:T(1024)(128)(2,1)S(1)}, bf16[2048]{0:T(1024)(128)(2,1)}, u32[]{:S(2)}) copy-start(bf16[2048]{0:T(1024)(128)(2,1)} %param.25) | copy-start | bytes 12292
  154.3 71.0 %all-to-all-start.1 = ((bf16[128,8,2048]{2,1,0:T(8,128)(2,1)}), bf16[128,8,2048]{2,1,0:T(8,128)(2,1)}, u32[]{:S(2)}, u32[]{:S(2)}) async-start(bf16[128,8,2048]{2,1,0:T(8,128)(2,1)} %bitcast.61), calls=%async_computation.1 | async-start | bytes 8388608 | tf_op jit(solution)/shard_map/all_to_all | solution.py:338
  160.6 4.8 %copy-start.17 = (f32[65,4]{0,1:T(4,128)S(1)}, f32[65,4]{0,1:T(4,128)}, u32[]{:S(2)}) copy-start(f32[65,4]{0,1:T(4,128)} %param.27) | copy-start | bytes 3124
  160.6 44.5 %copy-start.8 = (bf16[352,2048]{1,0:T(8,128)(2,1)S(1)}, bf16[352,2048]{1,0:T(8,128)(2,1)}, u32[]{:S(2)}) copy-start(bf16[352,2048]{1,0:T(8,128)(2,1)} %down.3) | copy-start | bytes 4325380
  216.7 0.8 copy-start.9
  217.5 0.9 copy-start.11
  218.4 17.6 %collective-permute-start.12 = (bf16[288,1024]{1,0:T(8,128)(2,1)}, bf16[288,1024]{1,0:T(8,128)(2,1)S(1)}, u32[]{:S(2)}, u32[]{:S(2)}) collective-permute-start(bf16[288,1024]{1,0:T(8,128)(2,1)} %get-tuple-element.42), channel_id=1, source_target_pairs={{0,8},{1,9},{2,10},{3,11},{4,12},{5,13},{6,14},{7,15},{8,0},{9,1},... | collective-permute-start | bytes 1769480 | tf_op jit(solution)/shard_map/ppermute | solution.py:149
  221.6 26.0 %collective-permute-start.13 = (bf16[288,1024]{1,0:T(8,128)(2,1)}, bf16[288,1024]{1,0:T(8,128)(2,1)S(1)}, u32[]{:S(2)}, u32[]{:S(2)}) collective-permute-start(bf16[288,1024]{1,0:T(8,128)(2,1)} %get-tuple-element.43), channel_id=1, source_target_pairs={{0,4},{1,5},{2,6},{3,7},{4,0},{5,1},{6,2},{7,3},{8,12},{9,13},{10,... | collective-permute-start | bytes 1769480 | tf_op jit(solution)/shard_map/ppermute | solution.py:149
  225.3 22.2 %collective-permute-start.14 = (bf16[288,1024]{1,0:T(8,128)(2,1)}, bf16[288,1024]{1,0:T(8,128)(2,1)}, u32[]{:S(2)}, u32[]{:S(2)}) collective-permute-start(bf16[288,1024]{1,0:T(8,128)(2,1)} %get-tuple-element.44), channel_id=1, source_target_pairs={{0,12},{1,13},{2,14},{3,15},{4,8},{5,9},{6,10},{7,11},{8,4},{9,5},... | collective-permute-start | bytes 1769480 | tf_op jit(solution)/shard_map/ppermute | solution.py:149
  225.3 3.2 %copy-start.12 = (bf16[288,1024]{1,0:T(8,128)(2,1)S(1)}, bf16[288,1024]{1,0:T(8,128)(2,1)}, u32[]{:S(2)}) copy-start(bf16[288,1024]{1,0:T(8,128)(2,1)} %copy-done.11) | copy-start | bytes 1769476
  225.3 4.3 %copy-start.10 = (bf16[288,1024]{1,0:T(8,128)(2,1)S(1)}, bf16[288,1024]{1,0:T(8,128)(2,1)}, u32[]{:S(2)}) copy-start(bf16[288,1024]{1,0:T(8,128)(2,1)} %copy-done.9) | copy-start | bytes 1769476
  228.6 20.4 %collective-permute-start.15 = (bf16[288,1024]{1,0:T(8,128)(2,1)S(1)}, bf16[288,1024]{1,0:T(8,128)(2,1)S(1)}, u32[]{:S(2)}, u32[]{:S(2)}) collective-permute-start(bf16[288,1024]{1,0:T(8,128)(2,1)S(1)} %copy-done.12), channel_id=1, source_target_pairs={{0,2},{1,3},{2,0},{3,1},{4,6},{5,7},{6,4},{7,5},{8,10},{9,11},{10,... | collective-permute-start | bytes 1769480 | tf_op jit(solution)/shard_map/ppermute | solution.py:153
  229.6 25.7 %collective-permute-start.16 = (bf16[288,1024]{1,0:T(8,128)(2,1)S(1)}, bf16[288,1024]{1,0:T(8,128)(2,1)S(1)}, u32[]{:S(2)}, u32[]{:S(2)}) collective-permute-start(bf16[288,1024]{1,0:T(8,128)(2,1)S(1)} %copy-done.10), channel_id=1, source_target_pairs={{0,1},{1,0},{2,3},{3,2},{4,5},{5,4},{6,7},{7,6},{8,9},{9,8},{10,11... | collective-permute-start | bytes 1769480 | tf_op jit(solution)/shard_map/ppermute | solution.py:153
  236.0 19.4 %collective-permute-start.17 = (bf16[288,1024]{1,0:T(8,128)(2,1)S(1)}, bf16[288,1024]{1,0:T(8,128)(2,1)S(1)}, u32[]{:S(2)}, u32[]{:S(2)}) collective-permute-start(bf16[288,1024]{1,0:T(8,128)(2,1)S(1)} %get-tuple-element.48), channel_id=1, source_target_pairs={{0,3},{1,2},{2,1},{3,0},{4,7},{5,6},{6,5},{7,4},{8,11},{9,10},{10,... | collective-permute-start | bytes 1769480 | tf_op jit(solution)/shard_map/ppermute | solution.py:153
  255.8 8.5 %collective-permute-start.18 = (bf16[72,1024]{1,0:T(8,128)(2,1)S(1)}, bf16[72,1024]{1,0:T(8,128)(2,1)S(1)}, u32[]{:S(2)}, u32[]{:S(2)}) collective-permute-start(bf16[72,1024]{1,0:T(8,128)(2,1)S(1)} %get-tuple-element.55), channel_id=1, source_target_pairs={{0,2},{1,3},{2,0},{3,1},{4,6},{5,7},{6,4},{7,5},{8,10},{9,11},{10,... | collective-permute-start | bytes 442376 | tf_op jit(solution)/shard_map/ppermute | solution.py:153
  258.8 7.2 %collective-permute-start.20 = (bf16[72,1024]{1,0:T(8,128)(2,1)S(1)}, bf16[72,1024]{1,0:T(8,128)(2,1)S(1)}, u32[]{:S(2)}, u32[]{:S(2)}) collective-permute-start(bf16[72,1024]{1,0:T(8,128)(2,1)S(1)} %get-tuple-element.56), channel_id=1, source_target_pairs={{0,3},{1,2},{2,1},{3,0},{4,7},{5,6},{6,5},{7,4},{8,11},{9,10},{10,... | collective-permute-start | bytes 442376 | tf_op jit(solution)/shard_map/ppermute | solution.py:153
  260.1 6.2 %collective-permute-start.19 = (bf16[72,1024]{1,0:T(8,128)(2,1)S(1)}, bf16[72,1024]{1,0:T(8,128)(2,1)S(1)}, u32[]{:S(2)}, u32[]{:S(2)}) collective-permute-start(bf16[72,1024]{1,0:T(8,128)(2,1)S(1)} %get-tuple-element.57), channel_id=1, source_target_pairs={{0,1},{1,0},{2,3},{3,2},{4,5},{5,4},{6,7},{7,6},{8,9},{9,8},{10,11... | collective-permute-start | bytes 442376 | tf_op jit(solution)/shard_map/ppermute | solution.py:153
  260.1 6.8 %collective-permute-start.21 = (bf16[72,1024]{1,0:T(8,128)(2,1)S(1)}, bf16[72,1024]{1,0:T(8,128)(2,1)S(1)}, u32[]{:S(2)}, u32[]{:S(2)}) collective-permute-start(bf16[72,1024]{1,0:T(8,128)(2,1)S(1)} %get-tuple-element.58), channel_id=1, source_target_pairs={{0,8},{1,9},{2,10},{3,11},{4,12},{5,13},{6,14},{7,15},{8,0},{9,1},... | collective-permute-start | bytes 442376 | tf_op jit(solution)/shard_map/ppermute | solution.py:149
  263.4 6.6 %collective-permute-start.23 = (bf16[72,1024]{1,0:T(8,128)(2,1)S(1)}, bf16[72,1024]{1,0:T(8,128)(2,1)S(1)}, u32[]{:S(2)}, u32[]{:S(2)}) collective-permute-start(bf16[72,1024]{1,0:T(8,128)(2,1)S(1)} %get-tuple-element.59), channel_id=1, source_target_pairs={{0,12},{1,13},{2,14},{3,15},{4,8},{5,9},{6,10},{7,11},{8,4},{9,5},... | collective-permute-start | bytes 442376 | tf_op jit(solution)/shard_map/ppermute | solution.py:149
  264.3 5.7 %collective-permute-start.22 = (bf16[72,1024]{1,0:T(8,128)(2,1)S(1)}, bf16[72,1024]{1,0:T(8,128)(2,1)S(1)}, u32[]{:S(2)}, u32[]{:S(2)}) collective-permute-start(bf16[72,1024]{1,0:T(8,128)(2,1)S(1)} %get-tuple-element.60), channel_id=1, source_target_pairs={{0,4},{1,5},{2,6},{3,7},{4,0},{5,1},{6,2},{7,3},{8,12},{9,13},{10,... | collective-permute-start | bytes 442376 | tf_op jit(solution)/shard_map/ppermute | solution.py:149
Sparse Core Ops, SparseCore 0:
  72.0 133.0 all-gather.1

commit v2 on v1

--- a/solution.py
+++ b/solution.py
@@ -160,23 +160,43 @@
     return total
 
 
-def reduce_scatter(parts):
+def sum_first(parts):
     parts_a, parts_b = parts[:SIDE], parts[SIDE:]
     got_a, got_b = [parts_a[0]], [parts_b[0]]
-    for d in (2, 1, 3):
+    for d in (1, 3, 2):
         got_a.append(along_x(parts_a[d], d))
         got_b.append(along_z(parts_b[d], d))
     sum_a = add_up(got_a).astype(BF).reshape(SIDE, ROWS, -1)
     sum_b = add_up(got_b).astype(BF).reshape(SIDE, ROWS, -1)
-    sum_a, sum_b = lax.optimization_barrier((sum_a, sum_b))
+    return sum_a, sum_b
+
+
+def sum_second(sum_a, sum_b):
     got_a, got_b = [sum_a[0]], [sum_b[0]]
-    for d in (2, 1, 3):
+    for d in (1, 3, 2):
         got_a.append(along_z(sum_a[d], d))
         got_b.append(along_x(sum_b[d], d))
     return got_a, got_b
 
 
-def token_kernel(a0, a1, a2, a3, b0, b1, b2, b3, residual, gain, select, stream, normed, outgoing):
+def gather(rows):
+    half = rows.shape[1] // 2
+    rows_a, rows_b = rows[:, :half], rows[:, half:]
+    got_a, got_b = {0: rows_a}, {0: rows_b}
+    for d in (1, 3, 2):
+        got_a[d] = along_z(rows_a, d)
+        got_b[d] = along_x(rows_b, d)
+    rows_a = jnp.stack([got_a[d] for d in range(SIDE)])
+    rows_b = jnp.stack([got_b[d] for d in range(SIDE)])
+    rows_a, rows_b = lax.optimization_barrier((rows_a, rows_b))
+    got_a, got_b = {0: rows_a}, {0: rows_b}
+    for d in (1, 3, 2):
+        got_a[d] = along_x(rows_a, d)
+        got_b[d] = along_z(rows_b, d)
+    return [got_a[d] for d in range(SIDE)], [got_b[d] for d in range(SIDE)]
+
+
+def token_kernel(a0, a1, a2, a3, b0, b1, b2, b3, residual, gain, stream, normed):
     f = lambda r: r[...].astype(F32)
     projected = jnp.concatenate(
         [f(a0) + f(a1) + f(a2) + f(a3), f(b0) + f(b1) + f(b2) + f(b3)], axis=1
@@ -185,15 +205,36 @@
     stream[...] = held
     wide = held.astype(F32)
     mean = jnp.mean(wide * wide, axis=-1, keepdims=True)
-    rows = (wide * lax.rsqrt(mean + 1e-06) * gain[...]).astype(BF)
-    normed[...] = rows
-    experts, _, capacity, width = outgoing.shape
-    group = 8
-    for g in range(experts // group):
-        n = group * capacity
-        picked = dot(select[g * n : (g + 1) * n, :], rows).reshape(group, capacity, width).astype(BF)
-        outgoing[g * group : (g + 1) * group, 0] = picked
-        outgoing[g * group : (g + 1) * group, 1] = picked
+    normed[...] = (wide * lax.rsqrt(mean + 1e-06) * gain[...]).astype(BF)
+
+
+def pick_kernel(mine, *refs):
+    rows_a, rows_b, select, out = refs[:SIDE], refs[SIDE : 2 * SIDE], refs[-2], refs[-1]
+    columns, _, capacity, width = out.shape
+    half = width // 2
+    for x in range(SIDE):
+        for z in range(SIDE):
+            block = jnp.bitwise_xor(mine[0], x * SIDE + z)
+            chosen = select[block]
+            a = dot(chosen, rows_a[x][z]).reshape(columns, capacity, half).astype(BF)
+            b = dot(chosen, rows_b[z][x]).reshape(columns, capacity, half).astype(BF)
+            for r in range(columns):
+                out[r, block, :, :half] = a[r]
+                out[r, block, :, half:] = b[r]
+
+
+def pick(mine, rows_a, rows_b, select, capacity):
+    blocks, slots, _ = select.shape
+    width = 2 * rows_a[0].shape[-1]
+    whole = pl.BlockSpec(memory_space=pltpu.VMEM)
+    return pl.pallas_call(
+        pick_kernel,
+        out_shape=jax.ShapeDtypeStruct((slots // capacity, blocks, capacity, width), BF),
+        in_specs=[pl.BlockSpec(memory_space=pltpu.SMEM)] + [whole] * (2 * SIDE + 1),
+        out_specs=whole,
+        compiler_params=vmem(32),
+        name="pick",
+    )(mine, *rows_a, *rows_b, select)
 
 
 def expert_kernel(rows, gate_up, down, out):
@@ -227,33 +268,32 @@
     )(rows, gate_up, down)
 
 
-def shared_kernel(mine, rows, gate_up, down, *rest):
-    outs, hidden = rest[:-1], rest[-1]
+def shared_kernel(*refs):
+    rows_a, rows_b = refs[:SIDE], refs[SIDE : 2 * SIDE]
+    gate_up, down = refs[2 * SIDE : 2 * SIDE + 2]
+    outs, hidden = refs[2 * SIDE + 2 : -1], refs[-1]
     half = down.shape[1] // 2
-    for g in range(SIDE):
-        x = rows[g * SIDE * ROWS : (g + 1) * SIDE * ROWS, :]
-        gate = dot(x, gate_up[0])
-        up = dot(x, gate_up[1])
-        hidden[g] = (gate / (1.0 + jnp.exp(-gate)) * up).reshape(SIDE, ROWS, -1)
-    at_x, at_z = mine[0] // SIDE, mine[0] % SIDE
+    for x in range(SIDE):
+        a = rows_a[x][...]
+        b = jnp.concatenate(
+            [rows_b[z][x].astype(F32) for z in range(SIDE)], axis=0
+        ).astype(BF)
+        gate = dot(a, gate_up[0, :half]) + dot(b, gate_up[0, half:])
+        up = dot(a, gate_up[1, :half]) + dot(b, gate_up[1, half:])
+        hidden[x] = (gate / (1.0 + jnp.exp(-gate)) * up).reshape(SIDE, ROWS, -1)
     for d in range(SIDE):
-        x_row = jnp.bitwise_xor(at_x, d)
-        z_row = jnp.bitwise_xor(at_z, d)
-        part = jnp.concatenate([hidden[x_row, jnp.bitwise_xor(at_z, j)] for j in range(SIDE)], axis=0)
+        part = hidden[d].reshape(SIDE * ROWS, -1)
         outs[d][...] = dot(part.astype(BF), down[:, :half]).astype(BF)
-        part = jnp.concatenate([hidden[jnp.bitwise_xor(at_x, j), z_row] for j in range(SIDE)], axis=0)
+        part = hidden[:, d].reshape(SIDE * ROWS, -1)
         outs[SIDE + d][...] = dot(part.astype(BF), down[:, half:]).astype(BF)
 
 
-def shared_expert(mine, rows, gate_up, down):
-    whole = pl.BlockSpec(memory_space=pltpu.VMEM)
+def shared_expert(rows_a, rows_b, gate_up, down):
     half = down.shape[1] // 2
-    count, width = rows.shape
+    count, width = SIDE * SIDE * ROWS, down.shape[1]
     return pl.pallas_call(
         shared_kernel,
         out_shape=[jax.ShapeDtypeStruct((SIDE * ROWS, half), BF)] * (2 * SIDE),
-        in_specs=[pl.BlockSpec(memory_space=pltpu.SMEM), whole, whole, whole],
-        out_specs=[whole] * (2 * SIDE),
         scratch_shapes=[pltpu.VMEM((SIDE, SIDE, ROWS, down.shape[0]), F32)],
         compiler_params=vmem(48),
         cost_estimate=pl.CostEstimate(
@@ -262,7 +302,7 @@
             transcendentals=count * down.shape[0],
         ),
         name="shared_expert",
-    )(mine, rows, gate_up, down)
+    )(*[a.reshape(SIDE * ROWS, half) for a in rows_a], *rows_b, gate_up, down)
 
 
 def on_device(
@@ -297,8 +337,18 @@
     slot_of = (flat * capacity + rank).reshape(tok_rows, route_count)
     slot_of = jnp.pad(slot_of, ((0, ROWS - tok_rows), (0, 0)), constant_values=-1)
     weight = jnp.pad(route_weight, ((0, ROWS - tok_rows), (0, 0)))
-    slots = jnp.arange(experts_all * capacity, dtype=jnp.int32)
-    select = jnp.any(slots[:, None, None] == slot_of[None], axis=-1).astype(BF)
+    block_routes = jnp.pad(
+        lax.all_gather(routes, "exp", axis=0),
+        ((0, 0), (0, ROWS - tok_rows), (0, 0)),
+        constant_values=-1,
+    )
+    split = experts_all // lax.axis_size("req")
+    column = jnp.arange(lax.axis_size("req"), dtype=jnp.int32) * split + mine // 2
+    hit = jnp.any(block_routes[:, None] == column[None, :, None, None], axis=-1)
+    before = jnp.arange(ROWS)[:, None] < jnp.arange(ROWS)[None, :]
+    hit_rank = dot(hit.astype(BF), before.astype(BF)).astype(jnp.int32)
+    select = hit[:, :, None] & (hit_rank[:, :, None] == jnp.arange(capacity)[None, None, :, None])
+    select = select.astype(BF).reshape(groups, -1, ROWS)
     columns = jnp.arange(devices * capacity, dtype=jnp.int32)
     columns = columns // (2 * capacity) * capacity + columns % capacity
     mix = jnp.sum(
@@ -309,32 +359,28 @@
     mix = jnp.concatenate([mix_high, mix_low], axis=0)
 
     attended = attention(prefill_qkv, decode_qkv, cache_pool, page_table, cache_len)
-    got_a, got_b = reduce_scatter(project(attended, out_weight, mine[None]))
-    stream, normed, outgoing = pl.pallas_call(
+    sums = sum_first(project(attended, out_weight, mine[None]))
+    got_a, got_b = sum_second(*lax.optimization_barrier(sums))
+    stream, normed = pl.pallas_call(
         token_kernel,
-        out_shape=[
-            jax.ShapeDtypeStruct((ROWS, width), BF),
-            jax.ShapeDtypeStruct((ROWS, width), BF),
-            jax.ShapeDtypeStruct((experts_all, 2, capacity, width), BF),
-        ],
+        out_shape=[jax.ShapeDtypeStruct((ROWS, width), BF)] * 2,
         compiler_params=vmem(32),
         name="token_rows",
-    )(
-        *got_a,
-        *got_b,
-        jnp.pad(residual, ((0, ROWS - tok_rows), (0, 0))),
-        norm_gain[None, :],
-        select,
-    )
-    block_rows = lax.all_gather(normed, "exp", axis=0, tiled=True)
+    )(*got_a, *got_b, jnp.pad(residual, ((0, ROWS - tok_rows), (0, 0))), norm_gain[None, :])
+    rows_a, rows_b = gather(normed)
+    outgoing = pick(mine[None], rows_a, rows_b, select, capacity)
     arrived = lax.all_to_all(
-        outgoing.reshape(devices, capacity, width),
-        ("req", "exp"),
+        outgoing.reshape(lax.axis_size("req"), groups * capacity, width),
+        "req",
         split_axis=0,
         concat_axis=0,
         tiled=True,
     )
+    sums = sum_first(shared_expert(rows_a, rows_b, shared_gate_up, shared_down))
+    arrived, *sums = lax.optimization_barrier((arrived, *sums))
+    got_a, got_b = sum_second(*sums)
     answer = experts(arrived.reshape(devices * capacity, width), expert_gate_up, expert_down)
+    answer, got_a, got_b = lax.optimization_barrier((answer, got_a, got_b))
     returned = lax.all_to_all(
         answer.reshape(devices, capacity, width),
         ("req", "exp"),
@@ -342,8 +388,6 @@
         concat_axis=0,
         tiled=True,
     )
-    parts = shared_expert(mine[None], block_rows, shared_gate_up, shared_down)
-    got_a, got_b = reduce_scatter(parts)
     shared = jnp.concatenate([add_up(got_a), add_up(got_b)], axis=1)
     shared_scale = jax.nn.sigmoid(dot(normed, shared_gate))
     routed = dot(mix, returned.reshape(devices * capacity, width))

time: 281 us -> 283 us (level)
  blocking collectives: 0 us -> 31.7 us
  waiting for transfers between devices: 130 us -> 104 us
  between operations: 13.7 us -> 0.68 us
  starting transfers between devices: 59.1 us -> 67.2 us
    all_to_all x1, waiting for transfers between devices: 0.01 us -> 49.6 us  [on_device(): lax.all_to_all(answer.reshape(devices, capacity, width), ('req', 'exp'),...]
    all_to_all x1, waiting for transfers between devices: 46.9 us -> 0.01 us  [on_device(): lax.all_to_all(outgoing.reshape(lax.axis_size('req'), groups * capacity,...]
    all_gather x1 -> x0, waiting for transfers between devices: 38.8 us -> none  [on_device(): block_rows = lax.all_gather(normed, 'exp', axis=0, tiled=True)]
    all_gather x0 -> x1, blocking collectives: none -> 31.7 us  [on_device(): lax.all_gather(routes, 'exp', axis=0)]
    ppermute x12 -> x18, waiting for transfers between devices: 11.4 us -> 37.4 us  [along_z(): return lax.ppermute(a, 'exp', [(i, i ^ d) for i in range(SIDE * SIDE)])]
    ppermute x12 -> x18, waiting for transfers between devices: 33.1 us -> 16.6 us  [along_x(): lax.ppermute(a, 'exp', [(i, i ^ d * SIDE) for i in range(SIDE * SIDE)])]
    ppermute x12 -> x18, starting transfers between devices: 20.4 us -> 29 us  [along_x(): lax.ppermute(a, 'exp', [(i, i ^ d * SIDE) for i in range(SIDE * SIDE)])]
    all_to_all x1, starting transfers between devices: 9.6 us -> 4.92 us  [on_device(): lax.all_to_all(outgoing.reshape(lax.axis_size('req'), groups * capacity,...]
  transfers between devices with their start and end apart: 27 -> 38, of which waited for: 17 -> 16; matrix products, arithmetic and copies ran while one was open for 9% -> 9% of each run, Pallas kernels for 9% -> 9%
where the time goes in v2:
time: 283 us; the launch traced here: 280 us
  waiting for transfers between devices  104 us (37%)
  starting transfers between devices  67.2 us (24%)
  Pallas kernels  34.3 us (12%)
  blocking collectives  31.7 us (11%)
  local copies, waits for them, and re-layouts  30.5 us (11%)
  other arithmetic  9.06 us (3%)
  matrix products  3.29 us (1%)
    all_to_all x1, waiting for transfers between devices, on_device(): lax.all_to_all(answer.reshape(devices, capacity, width), ('req', 'exp'),...  49.6 us
    ppermute x18, waiting for transfers between devices, along_z(): return lax.ppermute(a, 'exp', [(i, i ^ d) for i in range(SIDE * SIDE)])  37.4 us
    all_gather x1, blocking collectives, on_device(): lax.all_gather(routes, 'exp', axis=0)  31.7 us
    ppermute x18, starting transfers between devices, along_x(): lax.ppermute(a, 'exp', [(i, i ^ d * SIDE) for i in range(SIDE * SIDE)])  29 us
    ppermute x18, starting transfers between devices, along_z(): return lax.ppermute(a, 'exp', [(i, i ^ d) for i in range(SIDE * SIDE)])  26.4 us
    unnamed x82, local copies, waits for them, and re-layouts  23.9 us
    ppermute x18, waiting for transfers between devices, along_x(): lax.ppermute(a, 'exp', [(i, i ^ d * SIDE) for i in range(SIDE * SIDE)])  16.6 us
    pallas_call x1, Pallas kernels, experts(): pl.pallas_call(expert_kernel, grid=(count // step,), out_shape=jax.ShapeD...  13.6 us
  transfers between devices with their start and end apart: 38, of which 16 were waited for; matrix products, arithmetic and copies ran while one was open for 9% of the time, Pallas kernels for 9%

profile of v2, /device:TPU:8, one launch (start us, length us, event | category | flops | bytes accessed | tf_op | source)
XLA Modules:
  0.0 280.4 jit_solution(10449727383046489883)
XLA Ops:
  3.3 4.3 %attention.1 = bf16[1040,128]{1,0:T(8,128)(2,1)S(1)} custom-call(s32[16,1]{1,0:T(8,128)S(1)} %copy.53.lens, s32[16,64]{1,0:T(8,128)S(1)} %copy-done.13, bf16[2,3,512,128]{3,2,1,0:T(8,128)(2,1)S(1)} %copy-done.3, bf16[3,16,128]{2,1,0:T(8,128)(2,1)S(1)} %bitcast.91, bf16[2,124,128,128]{3,2,1,0:T(8,128)(2,1)} %pool.1), custom_call_target="tpu_custom_call" | custom-call | tf_op jit(solution)/shard_map/attention/pallas_call | solution.py:103
  10.0 2.0 collective-permute-start.3
  12.0 2.5 collective-permute-start.4
  15.6 1.5 collective-permute-start
  17.1 2.1 collective-permute-start.1
  19.2 7.1 %collective-permute-done.3 = bf16[288,1024]{1,0:T(8,128)(2,1)S(1)} collective-permute-done((bf16[288,1024]{1,0:T(8,128)(2,1)S(1)}, bf16[288,1024]{1,0:T(8,128)(2,1)S(1)}, u32[]{:S(2)}, u32[]{:S(2)}) %collective-permute-start.3) | collective-permute-done | bytes 589856 | tf_op jit(solution)/shard_map/ppermute | solution.py:153
  26.3 3.0 %collective-permute-start.2 = (bf16[288,1024]{1,0:T(8,128)(2,1)S(1)}, bf16[288,1024]{1,0:T(8,128)(2,1)S(1)}, u32[]{:S(2)}, u32[]{:S(2)}) collective-permute-start(bf16[288,1024]{1,0:T(8,128)(2,1)S(1)} %get-tuple-element.42), channel_id=1, source_target_pairs={{0,8},{1,9},{2,10},{3,11},{4,12},{5,13},{6,14},{7,15},{8,0},{9,1},... | collective-permute-start | bytes 1769480 | tf_op jit(solution)/shard_map/ppermute | solution.py:149
  29.3 10.2 %collective-permute-done.4 = bf16[288,1024]{1,0:T(8,128)(2,1)S(1)} collective-permute-done((bf16[288,1024]{1,0:T(8,128)(2,1)S(1)}, bf16[288,1024]{1,0:T(8,128)(2,1)S(1)}, u32[]{:S(2)}, u32[]{:S(2)}) %collective-permute-start.4) | collective-permute-done | bytes 589856 | tf_op jit(solution)/shard_map/ppermute | solution.py:153
  39.5 1.8 collective-permute-done.5
  41.7 3.5 %collective-permute-done.1 = bf16[288,1024]{1,0:T(8,128)(2,1)S(1)} collective-permute-done((bf16[288,1024]{1,0:T(8,128)(2,1)S(1)}, bf16[288,1024]{1,0:T(8,128)(2,1)S(1)}, u32[]{:S(2)}, u32[]{:S(2)}) %collective-permute-start.1) | collective-permute-done | bytes 589856 | tf_op jit(solution)/shard_map/ppermute | solution.py:149
  45.6 2.2 collective-permute-start.10
  48.2 2.5 collective-permute-start.7
  52.4 1.6 collective-permute-start.9
  54.1 1.8 collective-permute-done.11.b3
  55.9 1.5 collective-permute-done.8.a3
  58.0 1.9 collective-permute-start.15
  59.9 4.4 %collective-permute-start.16 = (bf16[72,1024]{1,0:T(8,128)(2,1)S(1)}, bf16[72,1024]{1,0:T(8,128)(2,1)S(1)}, u32[]{:S(2)}, u32[]{:S(2)}) collective-permute-start(bf16[72,1024]{1,0:T(8,128)(2,1)S(1)} %get-tuple-element.95), channel_id=1, source_target_pairs={{0,8},{1,9},{2,10},{3,11},{4,12},{5,13},{6,14},{7,15},{8,0},{9,1},... | collective-permute-start | bytes 442376 | tf_op jit(solution)/shard_map/ppermute | solution.py:149
  64.6 3.6 %collective-permute-start.13 = (bf16[72,1024]{1,0:T(8,128)(2,1)S(1)}, bf16[72,1024]{1,0:T(8,128)(2,1)S(1)}, u32[]{:S(2)}, u32[]{:S(2)}) collective-permute-start(bf16[72,1024]{1,0:T(8,128)(2,1)S(1)} %get-tuple-element.96), channel_id=1, source_target_pairs={{0,2},{1,3},{2,0},{3,1},{4,6},{5,7},{6,4},{7,5},{8,10},{9,11},{10,... | collective-permute-start | bytes 442376 | tf_op jit(solution)/shard_map/ppermute | solution.py:153
  69.0 1.6 collective-permute-done.17
  70.8 2.2 collective-permute-done.13
  72.9 1.7 collective-permute-done.14
  74.8 4.7 %collective-permute-start.19 = (bf16[4,72,1024]{2,1,0:T(8,128)(2,1)S(1)}, bf16[4,72,1024]{2,1,0:T(8,128)(2,1)S(1)}, u32[]{:S(2)}, u32[]{:S(2)}) collective-permute-start(bf16[4,72,1024]{2,1,0:T(8,128)(2,1)S(1)} %pad_maximum_fusion.1.refs_0_), channel_id=1, source_target_pairs={{0,8},{1,9},{2,10},{3,11},{4,12},{5,13},{6,14},{7,15},{8,0},{9,1},... | collective-permute-start | bytes 1769480 | tf_op jit(solution)/shard_map/ppermute | solution.py:149
  79.5 2.3 collective-permute-start.22
  81.7 8.6 %collective-permute-done.18.refs_1_ = bf16[4,72,1024]{2,1,0:T(8,128)(2,1)S(1)} collective-permute-done((bf16[4,72,1024]{2,1,0:T(8,128)(2,1)S(1)}, bf16[4,72,1024]{2,1,0:T(8,128)(2,1)S(1)}, u32[]{:S(2)}, u32[]{:S(2)}) %collective-permute-start.18) | collective-permute-done | bytes 589856 | tf_op jit(solution)/shard_map/ppermute | solution.py:149
  91.8 31.7 %all-gather.1 = s32[16,65,4]{1,2,0:T(4,128)S(1)} all-gather(s32[1,65,4]{1,2,0:T(4,128)S(1)} %bitcast.103), channel_id=2, replica_groups=mesh['req'=8,'exp'=16] {'exp'}, dimensions={0}, use_global_device_ids=true | all-gather | bytes 17680 | tf_op jit(solution)/shard_map/all_gather | solution.py:341
  127.5 3.1 %pick.1 = bf16[8,16,8,2048]{3,2,1,0:T(8,128)(2,1)S(1)} custom-call(s32[1]{0:T(128)} %bitcast.mine, bf16[4,72,1024]{2,1,0:T(8,128)(2,1)S(1)} %pad_maximum_fusion.1.refs_0_, bf16[4,72,1024]{2,1,0:T(8,128)(2,1)S(1)} %collective-permute-done.18.refs_1_, bf16[4,72,1024]{2,1,0:T(8,128)(2,1)S(1)} %collective-permute-done.19.refs_2_, ...), custom_call_target="tpu_custom_call" | custom-call | tf_op jit(solution)/shard_map/pick/pallas_call | solution.py:230
  130.6 2.0 copy-done
  132.6 4.9 %all-to-all-start = ((bf16[8,128,2048]{2,1,0:T(8,128)(2,1)}), bf16[8,128,2048]{2,1,0:T(8,128)(2,1)}, u32[]{:S(2)}, u32[]{:S(2)}) async-start(bf16[8,128,2048]{2,1,0:T(8,128)(2,1)} %bitcast.85), calls=%async_computation | async-start | bytes 8388608 | tf_op jit(solution)/shard_map/all_to_all | solution.py:372
  137.5 4.6 %copy.58.refs_8_ = bf16[2,2048,352]{2,1,0:T(8,128)(2,1)} copy(bf16[2,2048,352]{1,2,0:T(8,128)(2,1)} %param.23) | data formatting | bytes 5767168 | tf_op args[8]
  142.2 11.7 %shared_expert.1 = (bf16[288,1024]{1,0:T(8,128)(2,1)S(1)}, bf16[288,1024]{1,0:T(8,128)(2,1)}, bf16[288,1024]{1,0:T(8,128)(2,1)S(1)}, bf16[288,1024]{1,0:T(8,128)...) custom-call(bf16[288,1024]{1,0:T(8,128)(2,1)S(1)} %bitcast.87, ...), custom_call_target="tpu_custom_call" | custom-call | flops 4982833152 | bytes 13762560 | tf_op jit(solution)/shard_map/shared_expert/pallas_call | solution.py:294
  154.4 1.5 collective-permute-start.28
  155.9 2.1 collective-permute-start.29
  158.5 1.5 collective-permute-start.25
  160.0 10.1 %collective-permute-done.27 = bf16[288,1024]{1,0:T(8,128)(2,1)S(1)} collective-permute-done((bf16[288,1024]{1,0:T(8,128)(2,1)S(1)}, bf16[288,1024]{1,0:T(8,128)(2,1)S(1)}, u32[]{:S(2)}, u32[]{:S(2)}) %collective-permute-start.27) | collective-permute-done | bytes 589856 | tf_op jit(solution)/shard_map/ppermute | solution.py:153
  172.3 8.4 %copy.59.gate_up = bf16[1,2,2048,704]{3,2,1,0:T(8,128)(2,1)} copy(bf16[1,2,2048,704]{2,3,1,0:T(8,128)(2,1)} %param.28) | data formatting | bytes 11534336 | tf_op args[13]
  180.7 3.0 %collective-permute-done.28 = bf16[288,1024]{1,0:T(8,128)(2,1)} collective-permute-done((bf16[288,1024]{1,0:T(8,128)(2,1)}, bf16[288,1024]{1,0:T(8,128)(2,1)}, u32[]{:S(2)}, u32[]{:S(2)}) %collective-permute-start.28) | collective-permute-done | bytes 589856 | tf_op jit(solution)/shard_map/ppermute | solution.py:153
  183.7 2.7 add_convert_fusion
  187.3 2.8 %add_convert_fusion.1 = bf16[288,1024]{1,0:T(8,128)(2,1)} fusion(bf16[288,1024]{1,0:T(8,128)(2,1)} %collective-permute-done.26, bf16[288,1024]{1,0:T(8,128)(2,1)} %copy-done.20, bf16[288,1024]{1,0:T(8,128)(2,1)} %copy-done.19, bf16[288,1024]{1,0:T(8,128)(2,1)S(1)} %get-tuple-element.53), kind=kLoop, calls=%fused_computation.3 | loop fusion | flops 2359296 | bytes 2949120 | tf_op jit(solution)/shard_map/convert_element_type | solution.py:169
  190.2 1.9 slice_bitcast_fusion.4
  192.3 1.8 collective-permute-start.31
  194.1 2.1 collective-permute-start.32
  197.1 1.8 collective-permute-start.34
  199.0 2.0 collective-permute-start.35
  201.0 13.6 %experts.1 = bf16[1024,2048]{1,0:T(8,128)(2,1)S(1)} custom-call(bf16[1024,2048]{1,0:T(8,128)(2,1)} %bitcast.33.rows, bf16[1,2,2048,704]{3,2,1,0:T(8,128)(2,1)} %copy.59.gate_up, bf16[1,704,2048]{2,1,0:T(8,128)(2,1)S(1)} %copy-done.15), custom_call_target="tpu_custom_call" | custom-call | flops 8858370048 | bytes 17039360 | tf_op jit(solution)/shard_map/experts/pallas_call | solution.py:251
  214.6 2.0 copy-done.1
  217.5 7.0 %all-to-all-start.1 = ((bf16[128,8,2048]{2,1,0:T(8,128)(2,1)}), bf16[128,8,2048]{2,1,0:T(8,128)(2,1)}, u32[]{:S(2)}, u32[]{:S(2)}) async-start(bf16[128,8,2048]{2,1,0:T(8,128)(2,1)} %bitcast.86), calls=%async_computation.1 | async-start | bytes 8388608 | tf_op jit(solution)/shard_map/all_to_all | solution.py:384
  226.0 49.6 %all-to-all-done.1 = bf16[128,8,2048]{2,1,0:T(8,128)(2,1)} async-done(((bf16[128,8,2048]{2,1,0:T(8,128)(2,1)}), bf16[128,8,2048]{2,1,0:T(8,128)(2,1)}, u32[]{:S(2)}, u32[]{:S(2)}) %all-to-all-start.1) | async-done | bytes 4194336 | tf_op jit(solution)/shard_map/all_to_all | solution.py:384
  275.6 3.0 %fusion = f32[144,2048]{1,0:T(8,128)S(1)} fusion(bf16[128,8,2048]{2,1,0:T(8,128)(2,1)} %all-to-all-done.1, bf16[72,1024]{1,0:T(8,128)(2,1)S(1)} %get-tuple-element.73, bf16[72,1024]{1,0:T(8,128)(2,1)S(1)} %get-tuple-element.74), kind=kOutput, calls=%fused_computation | convolution fusion | flops 604569600 | bytes 5668864 | tf_op jit(solution)/shard_map/dot_general | solution.py:25
  (155 shorter events, 26.7 us)
Async XLA Ops:
  10.0 16.3 %collective-permute-start.3 = (bf16[288,1024]{1,0:T(8,128)(2,1)S(1)}, bf16[288,1024]{1,0:T(8,128)(2,1)S(1)}, u32[]{:S(2)}, u32[]{:S(2)}) collective-permute-start(bf16[288,1024]{1,0:T(8,128)(2,1)S(1)} %get-tuple-element.44), channel_id=1, source_target_pairs={{0,1},{1,0},{2,3},{3,2},{4,5},{5,4},{6,7},{7,6},{8,9},{9,8},{10,11... | collective-permute-start | bytes 1769480 | tf_op jit(solution)/shard_map/ppermute | solution.py:153
  12.0 27.5 %collective-permute-start.4 = (bf16[288,1024]{1,0:T(8,128)(2,1)S(1)}, bf16[288,1024]{1,0:T(8,128)(2,1)S(1)}, u32[]{:S(2)}, u32[]{:S(2)}) collective-permute-start(bf16[288,1024]{1,0:T(8,128)(2,1)S(1)} %get-tuple-element.45), channel_id=1, source_target_pairs={{0,3},{1,2},{2,1},{3,0},{4,7},{5,6},{6,5},{7,4},{8,11},{9,10},{10,... | collective-permute-start | bytes 1769480 | tf_op jit(solution)/shard_map/ppermute | solution.py:153
  14.5 26.7 %collective-permute-start.5 = (bf16[288,1024]{1,0:T(8,128)(2,1)S(1)}, bf16[288,1024]{1,0:T(8,128)(2,1)S(1)}, u32[]{:S(2)}, u32[]{:S(2)}) collective-permute-start(bf16[288,1024]{1,0:T(8,128)(2,1)S(1)} %get-tuple-element.46), channel_id=1, source_target_pairs={{0,2},{1,3},{2,0},{3,1},{4,6},{5,7},{6,4},{7,5},{8,10},{9,11},{10,... | collective-permute-start | bytes 1769480 | tf_op jit(solution)/shard_map/ppermute | solution.py:153
  15.6 26.1 %collective-permute-start = (bf16[288,1024]{1,0:T(8,128)(2,1)S(1)}, bf16[288,1024]{1,0:T(8,128)(2,1)S(1)}, u32[]{:S(2)}, u32[]{:S(2)}) collective-permute-start(bf16[288,1024]{1,0:T(8,128)(2,1)S(1)} %get-tuple-element.40), channel_id=1, source_target_pairs={{0,4},{1,5},{2,6},{3,7},{4,0},{5,1},{6,2},{7,3},{8,12},{9,13},{10,... | collective-permute-start | bytes 1769480 | tf_op jit(solution)/shard_map/ppermute | solution.py:149
  17.1 28.1 %collective-permute-start.1 = (bf16[288,1024]{1,0:T(8,128)(2,1)S(1)}, bf16[288,1024]{1,0:T(8,128)(2,1)S(1)}, u32[]{:S(2)}, u32[]{:S(2)}) collective-permute-start(bf16[288,1024]{1,0:T(8,128)(2,1)S(1)} %get-tuple-element.41), channel_id=1, source_target_pairs={{0,12},{1,13},{2,14},{3,15},{4,8},{5,9},{6,10},{7,11},{8,4},{9,5},... | collective-permute-start | bytes 1769480 | tf_op jit(solution)/shard_map/ppermute | solution.py:149
  26.3 18.9 %collective-permute-start.2 = (bf16[288,1024]{1,0:T(8,128)(2,1)S(1)}, bf16[288,1024]{1,0:T(8,128)(2,1)S(1)}, u32[]{:S(2)}, u32[]{:S(2)}) collective-permute-start(bf16[288,1024]{1,0:T(8,128)(2,1)S(1)} %get-tuple-element.42), channel_id=1, source_target_pairs={{0,8},{1,9},{2,10},{3,11},{4,12},{5,13},{6,14},{7,15},{8,0},{9,1},... | collective-permute-start | bytes 1769480 | tf_op jit(solution)/shard_map/ppermute | solution.py:149
  45.6 8.5 %copy-start.22 = (bf16[65,2048]{1,0:T(8,128)(2,1)S(1)}, bf16[65,2048]{1,0:T(8,128)(2,1)}, u32[]{:S(2)}) copy-start(bf16[65,2048]{1,0:T(8,128)(2,1)} %param.15) | copy-start | bytes 798724
  45.6 12.0 %copy-start.14 = (f32[2048]{0:T(1024)S(1)}, f32[2048]{0:T(1024)}, u32[]{:S(2)}) copy-start(f32[2048]{0:T(1024)} %param.22) | copy-start | bytes 24580
  45.6 6.8 %collective-permute-start.10 = (bf16[72,1024]{1,0:T(8,128)(2,1)S(1)}, bf16[72,1024]{1,0:T(8,128)(2,1)S(1)}, u32[]{:S(2)}, u32[]{:S(2)}) collective-permute-start(bf16[72,1024]{1,0:T(8,128)(2,1)S(1)} %get-tuple-element.86), channel_id=1, source_target_pairs={{0,12},{1,13},{2,14},{3,15},{4,8},{5,9},{6,10},{7,11},{8,4},{9,5},... | collective-permute-start | bytes 442376 | tf_op jit(solution)/shard_map/ppermute | solution.py:149
  47.8 8.0 %collective-permute-start.11 = (bf16[72,1024]{1,0:T(8,128)(2,1)S(1)}, bf16[72,1024]{1,0:T(8,128)(2,1)S(1)}, u32[]{:S(2)}, u32[]{:S(2)}) collective-permute-start(bf16[72,1024]{1,0:T(8,128)(2,1)S(1)} %get-tuple-element.85), channel_id=1, source_target_pairs={{0,8},{1,9},{2,10},{3,11},{4,12},{5,13},{6,14},{7,15},{8,0},{9,1},... | collective-permute-start | bytes 442376 | tf_op jit(solution)/shard_map/ppermute | solution.py:149
  47.9 8.0 %collective-permute-start.6 = (bf16[72,1024]{1,0:T(8,128)(2,1)S(1)}, bf16[72,1024]{1,0:T(8,128)(2,1)S(1)}, u32[]{:S(2)}, u32[]{:S(2)}) collective-permute-start(bf16[72,1024]{1,0:T(8,128)(2,1)S(1)} %get-tuple-element.91), channel_id=1, source_target_pairs={{0,1},{1,0},{2,3},{3,2},{4,5},{5,4},{6,7},{7,6},{8,9},{9,8},{10,11... | collective-permute-start | bytes 442376 | tf_op jit(solution)/shard_map/ppermute | solution.py:153
  48.2 7.7 %collective-permute-start.7 = (bf16[72,1024]{1,0:T(8,128)(2,1)S(1)}, bf16[72,1024]{1,0:T(8,128)(2,1)S(1)}, u32[]{:S(2)}, u32[]{:S(2)}) collective-permute-start(bf16[72,1024]{1,0:T(8,128)(2,1)S(1)} %get-tuple-element.90), channel_id=1, source_target_pairs={{0,3},{1,2},{2,1},{3,0},{4,7},{5,6},{6,5},{7,4},{8,11},{9,10},{10,... | collective-permute-start | bytes 442376 | tf_op jit(solution)/shard_map/ppermute | solution.py:153
  50.7 6.6 %collective-permute-start.8 = (bf16[72,1024]{1,0:T(8,128)(2,1)S(1)}, bf16[72,1024]{1,0:T(8,128)(2,1)S(1)}, u32[]{:S(2)}, u32[]{:S(2)}) collective-permute-start(bf16[72,1024]{1,0:T(8,128)(2,1)S(1)} %get-tuple-element.89), channel_id=1, source_target_pairs={{0,2},{1,3},{2,0},{3,1},{4,6},{5,7},{6,4},{7,5},{8,10},{9,11},{10,... | collective-permute-start | bytes 442376 | tf_op jit(solution)/shard_map/ppermute | solution.py:153
  52.4 5.1 %collective-permute-start.9 = (bf16[72,1024]{1,0:T(8,128)(2,1)S(1)}, bf16[72,1024]{1,0:T(8,128)(2,1)S(1)}, u32[]{:S(2)}, u32[]{:S(2)}) collective-permute-start(bf16[72,1024]{1,0:T(8,128)(2,1)S(1)} %get-tuple-element.87), channel_id=1, source_target_pairs={{0,4},{1,5},{2,6},{3,7},{4,0},{5,1},{6,2},{7,3},{8,12},{9,13},{10,... | collective-permute-start | bytes 442376 | tf_op jit(solution)/shard_map/ppermute | solution.py:149
  57.9 16.7 %copy-start.8 = (bf16[72,2048]{1,0:T(8,128)(2,1)}, bf16[72,2048]{1,0:T(8,128)(2,1)S(1)}, u32[]{:S(2)}) copy-start(bf16[72,2048]{1,0:T(8,128)(2,1)S(1)} %get-tuple-element.49) | copy-start | bytes 884740
  57.9 16.7 %copy-start.10 = (bf16[72,2048]{1,0:T(8,128)(2,1)}, bf16[72,2048]{1,0:T(8,128)(2,1)S(1)}, u32[]{:S(2)}) copy-start(bf16[72,2048]{1,0:T(8,128)(2,1)S(1)} %get-tuple-element.50) | copy-start | bytes 884740
  58.0 10.2 %collective-permute-start.15 = (bf16[72,1024]{1,0:T(8,128)(2,1)S(1)}, bf16[72,1024]{1,0:T(8,128)(2,1)S(1)}, u32[]{:S(2)}, u32[]{:S(2)}) collective-permute-start(bf16[72,1024]{1,0:T(8,128)(2,1)S(1)} %get-tuple-element.95), channel_id=1, source_target_pairs={{0,4},{1,5},{2,6},{3,7},{4,0},{5,1},{6,2},{7,3},{8,12},{9,13},{10,... | collective-permute-start | bytes 442376 | tf_op jit(solution)/shard_map/ppermute | solution.py:149
  59.9 9.1 %collective-permute-start.16 = (bf16[72,1024]{1,0:T(8,128)(2,1)S(1)}, bf16[72,1024]{1,0:T(8,128)(2,1)S(1)}, u32[]{:S(2)}, u32[]{:S(2)}) collective-permute-start(bf16[72,1024]{1,0:T(8,128)(2,1)S(1)} %get-tuple-element.95), channel_id=1, source_target_pairs={{0,8},{1,9},{2,10},{3,11},{4,12},{5,13},{6,14},{7,15},{8,0},{9,1},... | collective-permute-start | bytes 442376 | tf_op jit(solution)/shard_map/ppermute | solution.py:149
  64.3 6.4 %collective-permute-start.17 = (bf16[72,1024]{1,0:T(8,128)(2,1)S(1)}, bf16[72,1024]{1,0:T(8,128)(2,1)S(1)}, u32[]{:S(2)}, u32[]{:S(2)}) collective-permute-start(bf16[72,1024]{1,0:T(8,128)(2,1)S(1)} %get-tuple-element.95), channel_id=1, source_target_pairs={{0,12},{1,13},{2,14},{3,15},{4,8},{5,9},{6,10},{7,11},{8,4},{9,5},... | collective-permute-start | bytes 442376 | tf_op jit(solution)/shard_map/ppermute | solution.py:149
  64.3 6.4 %collective-permute-start.12 = (bf16[72,1024]{1,0:T(8,128)(2,1)S(1)}, bf16[72,1024]{1,0:T(8,128)(2,1)S(1)}, u32[]{:S(2)}, u32[]{:S(2)}) collective-permute-start(bf16[72,1024]{1,0:T(8,128)(2,1)S(1)} %get-tuple-element.96), channel_id=1, source_target_pairs={{0,1},{1,0},{2,3},{3,2},{4,5},{5,4},{6,7},{7,6},{8,9},{9,8},{10,11... | collective-permute-start | bytes 442376 | tf_op jit(solution)/shard_map/ppermute | solution.py:153
  64.6 8.3 %collective-permute-start.13 = (bf16[72,1024]{1,0:T(8,128)(2,1)S(1)}, bf16[72,1024]{1,0:T(8,128)(2,1)S(1)}, u32[]{:S(2)}, u32[]{:S(2)}) collective-permute-start(bf16[72,1024]{1,0:T(8,128)(2,1)S(1)} %get-tuple-element.96), channel_id=1, source_target_pairs={{0,2},{1,3},{2,0},{3,1},{4,6},{5,7},{6,4},{7,5},{8,10},{9,11},{10,... | collective-permute-start | bytes 442376 | tf_op jit(solution)/shard_map/ppermute | solution.py:153
  68.2 6.4 %collective-permute-start.14 = (bf16[72,1024]{1,0:T(8,128)(2,1)S(1)}, bf16[72,1024]{1,0:T(8,128)(2,1)S(1)}, u32[]{:S(2)}, u32[]{:S(2)}) collective-permute-start(bf16[72,1024]{1,0:T(8,128)(2,1)S(1)} %get-tuple-element.96), channel_id=1, source_target_pairs={{0,3},{1,2},{2,1},{3,0},{4,7},{5,6},{6,5},{7,4},{8,11},{9,10},{10,... | collective-permute-start | bytes 442376 | tf_op jit(solution)/shard_map/ppermute | solution.py:153
  70.7 21.1 %copy-start.35 = (s32[65,4]{0,1:T(4,128)S(1)}, s32[65,4]{0,1:T(4,128)}, u32[]{:S(2)}) copy-start(s32[65,4]{0,1:T(4,128)} %param.26) | copy-start | bytes 3124
  70.7 59.8 %copy-start.2 = (bf16[4,72,1024]{2,1,0:T(8,128)(2,1)}, bf16[4,72,1024]{2,1,0:T(8,128)(2,1)S(1)}, u32[]{:S(2)}) copy-start(bf16[4,72,1024]{2,1,0:T(8,128)(2,1)S(1)} %pad_maximum_fusion.2.refs_4_) | copy-start | bytes 1769476
  74.7 15.7 %collective-permute-start.18 = (bf16[4,72,1024]{2,1,0:T(8,128)(2,1)S(1)}, bf16[4,72,1024]{2,1,0:T(8,128)(2,1)S(1)}, u32[]{:S(2)}, u32[]{:S(2)}) collective-permute-start(bf16[4,72,1024]{2,1,0:T(8,128)(2,1)S(1)} %pad_maximum_fusion.1.refs_0_), channel_id=1, source_target_pairs={{0,4},{1,5},{2,6},{3,7},{4,0},{5,1},{6,2},{7,3},{8,12},{9,13},{10,... | collective-permute-start | bytes 1769480 | tf_op jit(solution)/shard_map/ppermute | solution.py:149
  74.8 52.6 %collective-permute-start.19 = (bf16[4,72,1024]{2,1,0:T(8,128)(2,1)S(1)}, bf16[4,72,1024]{2,1,0:T(8,128)(2,1)S(1)}, u32[]{:S(2)}, u32[]{:S(2)}) collective-permute-start(bf16[4,72,1024]{2,1,0:T(8,128)(2,1)S(1)} %pad_maximum_fusion.1.refs_0_), channel_id=1, source_target_pairs={{0,8},{1,9},{2,10},{3,11},{4,12},{5,13},{6,14},{7,15},{8,0},{9,1},... | collective-permute-start | bytes 1769480 | tf_op jit(solution)/shard_map/ppermute | solution.py:149
  79.5 47.9 %collective-permute-start.20 = (bf16[4,72,1024]{2,1,0:T(8,128)(2,1)S(1)}, bf16[4,72,1024]{2,1,0:T(8,128)(2,1)S(1)}, u32[]{:S(2)}, u32[]{:S(2)}) collective-permute-start(bf16[4,72,1024]{2,1,0:T(8,128)(2,1)S(1)} %pad_maximum_fusion.1.refs_0_), channel_id=1, source_target_pairs={{0,12},{1,13},{2,14},{3,15},{4,8},{5,9},{6,10},{7,11},{8,4},{9,5},... | collective-permute-start | bytes 1769480 | tf_op jit(solution)/shard_map/ppermute | solution.py:149
  79.5 48.0 %collective-permute-start.21 = (bf16[4,72,1024]{2,1,0:T(8,128)(2,1)S(1)}, bf16[4,72,1024]{2,1,0:T(8,128)(2,1)S(1)}, u32[]{:S(2)}, u32[]{:S(2)}) collective-permute-start(bf16[4,72,1024]{2,1,0:T(8,128)(2,1)S(1)} %pad_maximum_fusion.2.refs_4_), channel_id=1, source_target_pairs={{0,1},{1,0},{2,3},{3,2},{4,5},{5,4},{6,7},{7,6},{8,9},{9,8},{10,11... | collective-permute-start | bytes 1769480 | tf_op jit(solution)/shard_map/ppermute | solution.py:153
  79.5 48.0 %collective-permute-start.22 = (bf16[4,72,1024]{2,1,0:T(8,128)(2,1)S(1)}, bf16[4,72,1024]{2,1,0:T(8,128)(2,1)}, u32[]{:S(2)}, u32[]{:S(2)}) collective-permute-start(bf16[4,72,1024]{2,1,0:T(8,128)(2,1)S(1)} %pad_maximum_fusion.2.refs_4_), channel_id=1, source_target_pairs={{0,2},{1,3},{2,0},{3,1},{4,6},{5,7},{6,4},{7,5},{8,10},{9,11},{10,... | collective-permute-start | bytes 1769480 | tf_op jit(solution)/shard_map/ppermute | solution.py:153
  90.3 37.1 %collective-permute-start.23 = (bf16[4,72,1024]{2,1,0:T(8,128)(2,1)S(1)}, bf16[4,72,1024]{2,1,0:T(8,128)(2,1)}, u32[]{:S(2)}, u32[]{:S(2)}) collective-permute-start(bf16[4,72,1024]{2,1,0:T(8,128)(2,1)S(1)} %pad_maximum_fusion.2.refs_4_), channel_id=1, source_target_pairs={{0,3},{1,2},{2,1},{3,0},{4,7},{5,6},{6,5},{7,4},{8,11},{9,10},{10,... | collective-permute-start | bytes 1769480 | tf_op jit(solution)/shard_map/ppermute | solution.py:153
  132.6 57.6 %all-to-all-start = ((bf16[8,128,2048]{2,1,0:T(8,128)(2,1)}), bf16[8,128,2048]{2,1,0:T(8,128)(2,1)}, u32[]{:S(2)}, u32[]{:S(2)}) async-start(bf16[8,128,2048]{2,1,0:T(8,128)(2,1)} %bitcast.85), calls=%async_computation | async-start | bytes 8388608 | tf_op jit(solution)/shard_map/all_to_all | solution.py:372
  153.8 16.2 %collective-permute-start.27 = (bf16[288,1024]{1,0:T(8,128)(2,1)S(1)}, bf16[288,1024]{1,0:T(8,128)(2,1)S(1)}, u32[]{:S(2)}, u32[]{:S(2)}) collective-permute-start(bf16[288,1024]{1,0:T(8,128)(2,1)S(1)} %get-tuple-element.58), channel_id=1, source_target_pairs={{0,1},{1,0},{2,3},{3,2},{4,5},{5,4},{6,7},{7,6},{8,9},{9,8},{10,11... | collective-permute-start | bytes 1769480 | tf_op jit(solution)/shard_map/ppermute | solution.py:153
  154.4 29.3 %collective-permute-start.28 = (bf16[288,1024]{1,0:T(8,128)(2,1)}, bf16[288,1024]{1,0:T(8,128)(2,1)}, u32[]{:S(2)}, u32[]{:S(2)}) collective-permute-start(bf16[288,1024]{1,0:T(8,128)(2,1)} %get-tuple-element.59), channel_id=1, source_target_pairs={{0,3},{1,2},{2,1},{3,0},{4,7},{5,6},{6,5},{7,4},{8,11},{9,10},{10,... | collective-permute-start | bytes 1769480 | tf_op jit(solution)/shard_map/ppermute | solution.py:153
  155.9 27.8 %collective-permute-start.29 = (bf16[288,1024]{1,0:T(8,128)(2,1)}, bf16[288,1024]{1,0:T(8,128)(2,1)}, u32[]{:S(2)}, u32[]{:S(2)}) collective-permute-start(bf16[288,1024]{1,0:T(8,128)(2,1)} %get-tuple-element.60), channel_id=1, source_target_pairs={{0,2},{1,3},{2,0},{3,1},{4,6},{5,7},{6,4},{7,5},{8,10},{9,11},{10,... | collective-permute-start | bytes 1769480 | tf_op jit(solution)/shard_map/ppermute | solution.py:153
  157.9 28.4 %collective-permute-start.24 = (bf16[288,1024]{1,0:T(8,128)(2,1)}, bf16[288,1024]{1,0:T(8,128)(2,1)S(1)}, u32[]{:S(2)}, u32[]{:S(2)}) collective-permute-start(bf16[288,1024]{1,0:T(8,128)(2,1)} %get-tuple-element.54), channel_id=1, source_target_pairs={{0,4},{1,5},{2,6},{3,7},{4,0},{5,1},{6,2},{7,3},{8,12},{9,13},{10,... | collective-permute-start | bytes 1769480 | tf_op jit(solution)/shard_map/ppermute | solution.py:149
  158.5 27.8 %collective-permute-start.25 = (bf16[288,1024]{1,0:T(8,128)(2,1)S(1)}, bf16[288,1024]{1,0:T(8,128)(2,1)S(1)}, u32[]{:S(2)}, u32[]{:S(2)}) collective-permute-start(bf16[288,1024]{1,0:T(8,128)(2,1)S(1)} %get-tuple-element.55), channel_id=1, source_target_pairs={{0,12},{1,13},{2,14},{3,15},{4,8},{5,9},{6,10},{7,11},{8,4},{9,5},... | collective-permute-start | bytes 1769480 | tf_op jit(solution)/shard_map/ppermute | solution.py:149
  170.8 15.9 %collective-permute-start.26 = (bf16[288,1024]{1,0:T(8,128)(2,1)S(1)}, bf16[288,1024]{1,0:T(8,128)(2,1)}, u32[]{:S(2)}, u32[]{:S(2)}) collective-permute-start(bf16[288,1024]{1,0:T(8,128)(2,1)S(1)} %get-tuple-element.56), channel_id=1, source_target_pairs={{0,8},{1,9},{2,10},{3,11},{4,12},{5,13},{6,14},{7,15},{8,0},{9,1},... | collective-permute-start | bytes 1769480 | tf_op jit(solution)/shard_map/ppermute | solution.py:149
  187.3 13.6 %copy-start.15 = (bf16[1,704,2048]{2,1,0:T(8,128)(2,1)S(1)}, bf16[1,704,2048]{2,1,0:T(8,128)(2,1)}, u32[]{:S(2)}) copy-start(bf16[1,704,2048]{2,1,0:T(8,128)(2,1)} %down.1) | copy-start | bytes 8650756
  192.1 6.9 %collective-permute-start.30 = (bf16[72,1024]{1,0:T(8,128)(2,1)S(1)}, bf16[72,1024]{1,0:T(8,128)(2,1)S(1)}, u32[]{:S(2)}, u32[]{:S(2)}) collective-permute-start(bf16[72,1024]{1,0:T(8,128)(2,1)S(1)} %get-tuple-element.83), channel_id=1, source_target_pairs={{0,1},{1,0},{2,3},{3,2},{4,5},{5,4},{6,7},{7,6},{8,9},{9,8},{10,11... | collective-permute-start | bytes 442376 | tf_op jit(solution)/shard_map/ppermute | solution.py:153
  192.3 24.2 %collective-permute-start.31 = (bf16[72,1024]{1,0:T(8,128)(2,1)S(1)}, bf16[72,1024]{1,0:T(8,128)(2,1)S(1)}, u32[]{:S(2)}, u32[]{:S(2)}) collective-permute-start(bf16[72,1024]{1,0:T(8,128)(2,1)S(1)} %get-tuple-element.82), channel_id=1, source_target_pairs={{0,3},{1,2},{2,1},{3,0},{4,7},{5,6},{6,5},{7,4},{8,11},{9,10},{10,... | collective-permute-start | bytes 442376 | tf_op jit(solution)/shard_map/ppermute | solution.py:153
  194.1 22.5 %collective-permute-start.32 = (bf16[72,1024]{1,0:T(8,128)(2,1)S(1)}, bf16[72,1024]{1,0:T(8,128)(2,1)S(1)}, u32[]{:S(2)}, u32[]{:S(2)}) collective-permute-start(bf16[72,1024]{1,0:T(8,128)(2,1)S(1)} %get-tuple-element.81), channel_id=1, source_target_pairs={{0,2},{1,3},{2,0},{3,1},{4,6},{5,7},{6,4},{7,5},{8,10},{9,11},{10,... | collective-permute-start | bytes 442376 | tf_op jit(solution)/shard_map/ppermute | solution.py:153
  196.9 19.7 %collective-permute-start.33 = (bf16[72,1024]{1,0:T(8,128)(2,1)S(1)}, bf16[72,1024]{1,0:T(8,128)(2,1)S(1)}, u32[]{:S(2)}, u32[]{:S(2)}) collective-permute-start(bf16[72,1024]{1,0:T(8,128)(2,1)S(1)} %get-tuple-element.79), channel_id=1, source_target_pairs={{0,4},{1,5},{2,6},{3,7},{4,0},{5,1},{6,2},{7,3},{8,12},{9,13},{10,... | collective-permute-start | bytes 442376 | tf_op jit(solution)/shard_map/ppermute | solution.py:149
  197.1 19.5 %collective-permute-start.34 = (bf16[72,1024]{1,0:T(8,128)(2,1)S(1)}, bf16[72,1024]{1,0:T(8,128)(2,1)S(1)}, u32[]{:S(2)}, u32[]{:S(2)}) collective-permute-start(bf16[72,1024]{1,0:T(8,128)(2,1)S(1)} %get-tuple-element.78), channel_id=1, source_target_pairs={{0,12},{1,13},{2,14},{3,15},{4,8},{5,9},{6,10},{7,11},{8,4},{9,5},... | collective-permute-start | bytes 442376 | tf_op jit(solution)/shard_map/ppermute | solution.py:149
  199.0 17.7 %collective-permute-start.35 = (bf16[72,1024]{1,0:T(8,128)(2,1)S(1)}, bf16[72,1024]{1,0:T(8,128)(2,1)S(1)}, u32[]{:S(2)}, u32[]{:S(2)}) collective-permute-start(bf16[72,1024]{1,0:T(8,128)(2,1)S(1)} %get-tuple-element.77), channel_id=1, source_target_pairs={{0,8},{1,9},{2,10},{3,11},{4,12},{5,13},{6,14},{7,15},{8,0},{9,1},... | collective-permute-start | bytes 442376 | tf_op jit(solution)/shard_map/ppermute | solution.py:149
  217.4 7.7 %copy-start.37 = (bf16[2048]{0:T(1024)(128)(2,1)S(1)}, bf16[2048]{0:T(1024)(128)(2,1)}, u32[]{:S(2)}) copy-start(bf16[2048]{0:T(1024)(128)(2,1)} %param.25) | copy-start | bytes 12292
  217.4 7.7 %copy-start.38 = (f32[65,4]{0,1:T(4,128)S(1)}, f32[65,4]{0,1:T(4,128)}, u32[]{:S(2)}) copy-start(f32[65,4]{0,1:T(4,128)} %param.27) | copy-start | bytes 3124
  217.4 8.0 %copy-start.11 = (bf16[72,2048]{1,0:T(8,128)(2,1)S(1)}, bf16[72,2048]{1,0:T(8,128)(2,1)}, u32[]{:S(2)}) copy-start(bf16[72,2048]{1,0:T(8,128)(2,1)} %copy-done.10) | copy-start | bytes 884740
  217.5 58.1 %all-to-all-start.1 = ((bf16[128,8,2048]{2,1,0:T(8,128)(2,1)}), bf16[128,8,2048]{2,1,0:T(8,128)(2,1)}, u32[]{:S(2)}, u32[]{:S(2)}) async-start(bf16[128,8,2048]{2,1,0:T(8,128)(2,1)} %bitcast.86), calls=%async_computation.1 | async-start | bytes 8388608 | tf_op jit(solution)/shard_map/all_to_all | solution.py:384
  (29 other events, 49.1 us)

commit v3 on v2

--- a/solution.py
+++ b/solution.py
@@ -9,7 +9,10 @@
 
 HD = 128
 SIDE = 4
+TOKENS = 65
 ROWS = 72
+LANES = 128
+ROUTES = 4
 NEG_FILL = -1e30
 MIB = 1 << 20
 BF = jnp.bfloat16
@@ -23,6 +26,10 @@
 
 def dot(a, b):
     return jnp.dot(a, b, preferred_element_type=F32)
+
+
+def dot_nt(a, b):
+    return lax.dot_general(a, b, NT, preferred_element_type=F32)
 
 
 def attention_kernel(lens, table, pre, dec, pool, out, keys, values, scores, sems):
@@ -196,7 +203,7 @@
     return [got_a[d] for d in range(SIDE)], [got_b[d] for d in range(SIDE)]
 
 
-def token_kernel(a0, a1, a2, a3, b0, b1, b2, b3, residual, gain, stream, normed):
+def token_kernel(a0, a1, a2, a3, b0, b1, b2, b3, residual, gain, tags, stream, normed):
     f = lambda r: r[...].astype(F32)
     projected = jnp.concatenate(
         [f(a0) + f(a1) + f(a2) + f(a3), f(b0) + f(b1) + f(b2) + f(b3)], axis=1
@@ -205,42 +212,75 @@
     stream[...] = held
     wide = held.astype(F32)
     mean = jnp.mean(wide * wide, axis=-1, keepdims=True)
-    normed[...] = (wide * lax.rsqrt(mean + 1e-06) * gain[...]).astype(BF)
+    rows = wide * lax.rsqrt(mean + 1e-06) * gain[...]
+    normed[...] = rows.astype(BF)
+    count, lanes = tags.shape
+    is_tag = lax.broadcasted_iota(jnp.int32, (count, lanes), 0) >= TOKENS
+    normed[:, :lanes] = jnp.where(is_tag, tags[...], rows[:, :lanes]).astype(BF)
+
+
+def chosen_rows(mine, rows_a, columns, capacity):
+    shape = (columns, LANES)
+    expert = lax.broadcasted_iota(jnp.int32, shape, 0) * (SIDE * SIDE // 2) + mine // 2
+    expert = expert.astype(F32)
+    hits = []
+    for x in range(SIDE):
+        for z in range(SIDE):
+            tags = rows_a[x][z][:, :LANES].astype(F32)
+            hit = jnp.zeros(shape, F32)
+            for k in range(ROUTES):
+                named = jnp.broadcast_to(tags[TOKENS + k : TOKENS + k + 1, :], shape)
+                hit = jnp.where(named == expert, 1.0, hit)
+            hits.append(hit)
+    hits = jnp.concatenate(hits, axis=0)
+    before = lax.broadcasted_iota(jnp.int32, (LANES, LANES), 0) < lax.broadcasted_iota(
+        jnp.int32, (LANES, LANES), 1
+    )
+    rank = dot(hits.astype(BF), before.astype(F32).astype(BF))
+    rank = jnp.where(hits > 0.0, rank, -1.0)
+    slot = lax.broadcasted_iota(jnp.int32, (columns, capacity, LANES), 1).astype(F32)
+    chosen = []
+    for i in range(SIDE * SIDE):
+        here = rank[i * columns : (i + 1) * columns, :]
+        here = jnp.broadcast_to(here[:, None, :], (columns, capacity, LANES))
+        here = jnp.where(here == slot, 1.0, 0.0).reshape(columns * capacity, LANES)
+        chosen.append(here[:, :ROWS].astype(BF))
+    return chosen
 
 
 def pick_kernel(mine, *refs):
-    rows_a, rows_b, select, out = refs[:SIDE], refs[SIDE : 2 * SIDE], refs[-2], refs[-1]
+    rows_a, rows_b, out = refs[:SIDE], refs[SIDE : 2 * SIDE], refs[-1]
     columns, _, capacity, width = out.shape
     half = width // 2
+    chosen = chosen_rows(mine[0], rows_a, columns, capacity)
     for x in range(SIDE):
         for z in range(SIDE):
             block = jnp.bitwise_xor(mine[0], x * SIDE + z)
-            chosen = select[block]
-            a = dot(chosen, rows_a[x][z]).reshape(columns, capacity, half).astype(BF)
-            b = dot(chosen, rows_b[z][x]).reshape(columns, capacity, half).astype(BF)
+            pick = chosen[x * SIDE + z]
+            a = dot(pick, rows_a[x][z]).reshape(columns, capacity, half).astype(BF)
+            b = dot(pick, rows_b[z][x]).reshape(columns, capacity, half).astype(BF)
             for r in range(columns):
                 out[r, block, :, :half] = a[r]
                 out[r, block, :, half:] = b[r]
 
 
-def pick(mine, rows_a, rows_b, select, capacity):
-    blocks, slots, _ = select.shape
+def pick(mine, rows_a, rows_b, columns, capacity):
     width = 2 * rows_a[0].shape[-1]
     whole = pl.BlockSpec(memory_space=pltpu.VMEM)
     return pl.pallas_call(
         pick_kernel,
-        out_shape=jax.ShapeDtypeStruct((slots // capacity, blocks, capacity, width), BF),
-        in_specs=[pl.BlockSpec(memory_space=pltpu.SMEM)] + [whole] * (2 * SIDE + 1),
+        out_shape=jax.ShapeDtypeStruct((columns, SIDE * SIDE, capacity, width), BF),
+        in_specs=[pl.BlockSpec(memory_space=pltpu.SMEM)] + [whole] * (2 * SIDE),
         out_specs=whole,
-        compiler_params=vmem(32),
+        compiler_params=vmem(56),
         name="pick",
-    )(mine, *rows_a, *rows_b, select)
+    )(mine, *rows_a, *rows_b)
 
 
 def expert_kernel(rows, gate_up, down, out):
     x = rows[...]
-    gate = dot(x, gate_up[0, 0])
-    up = dot(x, gate_up[0, 1])
+    gate = dot_nt(x, gate_up[0, 0])
+    up = dot_nt(x, gate_up[0, 1])
     hidden = (gate / (1.0 + jnp.exp(-gate)) * up).astype(BF)
     out[...] = dot(hidden, down[0]).astype(BF)
 
@@ -258,7 +298,7 @@
             pl.BlockSpec(down.shape, lambda i: (0, 0, 0)),
         ],
         out_specs=pl.BlockSpec((step, width), lambda i: (i, 0)),
-        compiler_params=vmem(40),
+        compiler_params=vmem(50),
         cost_estimate=pl.CostEstimate(
             flops=6 * count * width * down.shape[1],
             bytes_accessed=2 * (2 * count * width + 3 * width * down.shape[1]),
@@ -278,8 +318,8 @@
         b = jnp.concatenate(
             [rows_b[z][x].astype(F32) for z in range(SIDE)], axis=0
         ).astype(BF)
-        gate = dot(a, gate_up[0, :half]) + dot(b, gate_up[0, half:])
-        up = dot(a, gate_up[1, :half]) + dot(b, gate_up[1, half:])
+        gate = dot_nt(a, gate_up[0, :, :half]) + dot_nt(b, gate_up[0, :, half:])
+        up = dot_nt(a, gate_up[1, :, :half]) + dot_nt(b, gate_up[1, :, half:])
         hidden[x] = (gate / (1.0 + jnp.exp(-gate)) * up).reshape(SIDE, ROWS, -1)
     for d in range(SIDE):
         part = hidden[d].reshape(SIDE * ROWS, -1)
@@ -337,18 +377,11 @@
     slot_of = (flat * capacity + rank).reshape(tok_rows, route_count)
     slot_of = jnp.pad(slot_of, ((0, ROWS - tok_rows), (0, 0)), constant_values=-1)
     weight = jnp.pad(route_weight, ((0, ROWS - tok_rows), (0, 0)))
-    block_routes = jnp.pad(
-        lax.all_gather(routes, "exp", axis=0),
-        ((0, 0), (0, ROWS - tok_rows), (0, 0)),
-        constant_values=-1,
-    )
-    split = experts_all // lax.axis_size("req")
-    column = jnp.arange(lax.axis_size("req"), dtype=jnp.int32) * split + mine // 2
-    hit = jnp.any(block_routes[:, None] == column[None, :, None, None], axis=-1)
-    before = jnp.arange(ROWS)[:, None] < jnp.arange(ROWS)[None, :]
-    hit_rank = dot(hit.astype(BF), before.astype(BF)).astype(jnp.int32)
-    select = hit[:, :, None] & (hit_rank[:, :, None] == jnp.arange(capacity)[None, None, :, None])
-    select = select.astype(BF).reshape(groups, -1, ROWS)
+    tags = jnp.pad(
+        routes.T.astype(F32),
+        ((tok_rows, ROWS - tok_rows - route_count), (0, LANES - tok_rows)),
+        constant_values=-1.0,
+    )
     columns = jnp.arange(devices * capacity, dtype=jnp.int32)
     columns = columns // (2 * capacity) * capacity + columns % capacity
     mix = jnp.sum(
@@ -366,9 +399,15 @@
         out_shape=[jax.ShapeDtypeStruct((ROWS, width), BF)] * 2,
         compiler_params=vmem(32),
         name="token_rows",
-    )(*got_a, *got_b, jnp.pad(residual, ((0, ROWS - tok_rows), (0, 0))), norm_gain[None, :])
+    )(
+        *got_a,
+        *got_b,
+        jnp.pad(residual, ((0, ROWS - tok_rows), (0, 0))),
+        norm_gain[None, :],
+        tags,
+    )
     rows_a, rows_b = gather(normed)
-    outgoing = pick(mine[None], rows_a, rows_b, select, capacity)
+    outgoing = pick(mine[None], rows_a, rows_b, lax.axis_size("req"), capacity)
     arrived = lax.all_to_all(
         outgoing.reshape(lax.axis_size("req"), groups * capacity, width),
         "req",
@@ -376,11 +415,10 @@
         concat_axis=0,
         tiled=True,
     )
-    sums = sum_first(shared_expert(rows_a, rows_b, shared_gate_up, shared_down))
-    arrived, *sums = lax.optimization_barrier((arrived, *sums))
-    got_a, got_b = sum_second(*sums)
-    answer = experts(arrived.reshape(devices * capacity, width), expert_gate_up, expert_down)
-    answer, got_a, got_b = lax.optimization_barrier((answer, got_a, got_b))
+    sums = sum_first(shared_expert(rows_a, rows_b, shared_gate_up.transpose(0, 2, 1), shared_down))
+    got_a, got_b = sum_second(*lax.optimization_barrier(sums))
+    arrived, got_a, got_b = lax.optimization_barrier((arrived, got_a, got_b))
+    answer = experts(arrived.reshape(devices * capacity, width), expert_gate_up.transpose(0, 1, 3, 2), expert_down)
     returned = lax.all_to_all(
         answer.reshape(devices, capacity, width),
         ("req", "exp"),

time: 283 us -> 260 us (0.919)
  blocking collectives: 31.7 us -> 0 us
  waiting for transfers between devices: 104 us -> 133 us
  local copies, waits for them, and re-layouts: 30.5 us -> 12.3 us
  Pallas kernels: 34.3 us -> 38 us
  other arithmetic: 9.06 us -> 5.98 us
  starting transfers between devices: 67.2 us -> 64.3 us
    all_gather x1 -> x0, blocking collectives: 31.7 us -> none  [on_device(): lax.all_gather(routes, 'exp', axis=0)]
    unnamed x82 -> x42, local copies, waits for them, and re-layouts: 23.9 us -> 7.68 us
    ppermute x18, waiting for transfers between devices: 37.4 us -> 52.1 us  [along_z(): return lax.ppermute(a, 'exp', [(i, i ^ d) for i in range(SIDE * SIDE)])]
    ppermute x18, waiting for transfers between devices: 16.6 us -> 30.3 us  [along_x(): lax.ppermute(a, 'exp', [(i, i ^ d * SIDE) for i in range(SIDE * SIDE)])]
    ppermute x18, starting transfers between devices: 29 us -> 25.8 us  [along_x(): lax.ppermute(a, 'exp', [(i, i ^ d * SIDE) for i in range(SIDE * SIDE)])]
  transfers between devices with their start and end apart: 38 -> 38, of which waited for: 16 -> 24; matrix products, arithmetic and copies ran while one was open for 9% -> 3% of each run, Pallas kernels for 9% -> 4%
where the time goes in v3:
time: 260 us; the launch traced here: 257 us
  waiting for transfers between devices  133 us (51%)
  starting transfers between devices  64.3 us (25%)
  Pallas kernels  38 us (15%)
  local copies, waits for them, and re-layouts  12.3 us (5%)
  other arithmetic  5.98 us (2%)
  matrix products  3.15 us (1%)
    ppermute x18, waiting for transfers between devices, along_z(): return lax.ppermute(a, 'exp', [(i, i ^ d) for i in range(SIDE * SIDE)])  52.1 us
    all_to_all x1, waiting for transfers between devices, on_device(): lax.all_to_all(answer.reshape(devices, capacity, width), ('req', 'exp'),...  50.4 us
    ppermute x18, waiting for transfers between devices, along_x(): lax.ppermute(a, 'exp', [(i, i ^ d * SIDE) for i in range(SIDE * SIDE)])  30.3 us
    ppermute x18, starting transfers between devices, along_z(): return lax.ppermute(a, 'exp', [(i, i ^ d) for i in range(SIDE * SIDE)])  25.9 us
    ppermute x18, starting transfers between devices, along_x(): lax.ppermute(a, 'exp', [(i, i ^ d * SIDE) for i in range(SIDE * SIDE)])  25.8 us
    pallas_call x1, Pallas kernels, experts(): pl.pallas_call(expert_kernel, grid=(count // step,), out_shape=jax.ShapeD...  14.6 us
    pallas_call x1, Pallas kernels, shared_expert(): pl.pallas_call(shared_kernel, out_shape=[jax.ShapeDtypeStruct((SIDE * ROW...  10.8 us
    unnamed x42, local copies, waits for them, and re-layouts  7.68 us
  transfers between devices with their start and end apart: 38, of which 24 were waited for; matrix products, arithmetic and copies ran while one was open for 3% of the time, Pallas kernels for 4%

profile of v3, /device:TPU:8, one launch (start us, length us, event | category | flops | bytes accessed | tf_op | source)
XLA Modules:
  0.0 257.0 jit_solution(5774382652252594884)
XLA Ops:
  3.3 4.3 %attention.1 = bf16[1040,128]{1,0:T(8,128)(2,1)S(1)} custom-call(s32[16,1]{1,0:T(8,128)S(1)} %copy.29.lens, s32[16,64]{1,0:T(8,128)S(1)} %copy-done.7, bf16[2,3,512,128]{3,2,1,0:T(8,128)(2,1)S(1)} %copy-done.2, bf16[3,16,128]{2,1,0:T(8,128)(2,1)S(1)} %bitcast.79, bf16[2,124,128,128]{3,2,1,0:T(8,128)(2,1)} %pool.1), custom_call_target="tpu_custom_call" | custom-call | tf_op jit(solution)/shard_map/attention/pallas_call | solution.py:110
  8.6 2.2 project.1
  10.9 1.9 collective-permute-start.3
  12.8 2.5 collective-permute-start.4
  16.4 1.5 collective-permute-start
  17.9 2.1 collective-permute-start.1
  19.9 7.1 %collective-permute-done.3 = bf16[288,1024]{1,0:T(8,128)(2,1)S(1)} collective-permute-done((bf16[288,1024]{1,0:T(8,128)(2,1)S(1)}, bf16[288,1024]{1,0:T(8,128)(2,1)S(1)}, u32[]{:S(2)}, u32[]{:S(2)}) %collective-permute-start.3) | collective-permute-done | bytes 589856 | tf_op jit(solution)/shard_map/ppermute | solution.py:160
  27.9 3.0 %collective-permute-start.2 = (bf16[288,1024]{1,0:T(8,128)(2,1)S(1)}, bf16[288,1024]{1,0:T(8,128)(2,1)}, u32[]{:S(2)}, u32[]{:S(2)}) collective-permute-start(bf16[288,1024]{1,0:T(8,128)(2,1)S(1)} %get-tuple-element.41), channel_id=1, source_target_pairs={{0,8},{1,9},{2,10},{3,11},{4,12},{5,13},{6,14},{7,15},{8,0},{9,1},... | collective-permute-start | bytes 1769480 | tf_op jit(solution)/shard_map/ppermute | solution.py:156
  35.3 5.3 %collective-permute-done.4 = bf16[288,1024]{1,0:T(8,128)(2,1)} collective-permute-done((bf16[288,1024]{1,0:T(8,128)(2,1)}, bf16[288,1024]{1,0:T(8,128)(2,1)}, u32[]{:S(2)}, u32[]{:S(2)}) %collective-permute-start.4) | collective-permute-done | bytes 589856 | tf_op jit(solution)/shard_map/ppermute | solution.py:160
  40.6 1.6 collective-permute-done.5
  42.1 1.8 add_convert_fusion.2
  44.0 2.0 collective-permute-done.1
  46.0 1.7 add_convert_fusion.3
  47.8 2.2 collective-permute-start.10
  50.3 2.5 collective-permute-start.7
  52.8 1.3 collective-permute-start.8
  54.6 1.6 collective-permute-start.9
  56.2 1.7 collective-permute-done.11.b3
  57.9 1.6 collective-permute-done.8.a3
  60.1 2.3 collective-permute-start.15
  62.4 2.3 collective-permute-start.16
  66.2 3.9 %collective-permute-start.13 = (bf16[72,1024]{1,0:T(8,128)(2,1)S(1)}, bf16[72,1024]{1,0:T(8,128)(2,1)S(1)}, u32[]{:S(2)}, u32[]{:S(2)}) collective-permute-start(bf16[72,1024]{1,0:T(8,128)(2,1)S(1)} %get-tuple-element.94), channel_id=1, source_target_pairs={{0,2},{1,3},{2,0},{3,1},{4,6},{5,7},{6,4},{7,5},{8,10},{9,11},{10,... | collective-permute-start | bytes 442376 | tf_op jit(solution)/shard_map/ppermute | solution.py:160
  71.1 3.6 %collective-permute-done.13 = bf16[72,1024]{1,0:T(8,128)(2,1)S(1)} collective-permute-done((bf16[72,1024]{1,0:T(8,128)(2,1)S(1)}, bf16[72,1024]{1,0:T(8,128)(2,1)S(1)}, u32[]{:S(2)}, u32[]{:S(2)}) %collective-permute-start.13) | collective-permute-done | bytes 147488 | tf_op jit(solution)/shard_map/ppermute | solution.py:160
  74.7 1.7 collective-permute-done.14
  76.6 4.7 %collective-permute-start.19 = (bf16[4,72,1024]{2,1,0:T(8,128)(2,1)S(1)}, bf16[4,72,1024]{2,1,0:T(8,128)(2,1)S(1)}, u32[]{:S(2)}, u32[]{:S(2)}) collective-permute-start(bf16[4,72,1024]{2,1,0:T(8,128)(2,1)S(1)} %pad_maximum_fusion.1.refs_0_), channel_id=1, source_target_pairs={{0,8},{1,9},{2,10},{3,11},{4,12},{5,13},{6,14},{7,15},{8,0},{9,1},... | collective-permute-start | bytes 1769480 | tf_op jit(solution)/shard_map/ppermute | solution.py:156
  81.3 2.3 collective-permute-start.22
  83.5 9.3 %collective-permute-done.18.refs_1_ = bf16[4,72,1024]{2,1,0:T(8,128)(2,1)S(1)} collective-permute-done((bf16[4,72,1024]{2,1,0:T(8,128)(2,1)S(1)}, bf16[4,72,1024]{2,1,0:T(8,128)(2,1)S(1)}, u32[]{:S(2)}, u32[]{:S(2)}) %collective-permute-start.18) | collective-permute-done | bytes 589856 | tf_op jit(solution)/shard_map/ppermute | solution.py:156
  93.6 6.4 %collective-permute-done.19.refs_2_ = bf16[4,72,1024]{2,1,0:T(8,128)(2,1)S(1)} collective-permute-done((bf16[4,72,1024]{2,1,0:T(8,128)(2,1)S(1)}, bf16[4,72,1024]{2,1,0:T(8,128)(2,1)S(1)}, u32[]{:S(2)}, u32[]{:S(2)}) %collective-permute-start.19) | collective-permute-done | bytes 589856 | tf_op jit(solution)/shard_map/ppermute | solution.py:156
  100.0 2.5 collective-permute-done.20.refs_3_
  103.4 6.3 %collective-permute-done.23.refs_7_ = bf16[4,72,1024]{2,1,0:T(8,128)(2,1)S(1)} collective-permute-done((bf16[4,72,1024]{2,1,0:T(8,128)(2,1)S(1)}, bf16[4,72,1024]{2,1,0:T(8,128)(2,1)S(1)}, u32[]{:S(2)}, u32[]{:S(2)}) %collective-permute-start.23) | collective-permute-done | bytes 589856 | tf_op jit(solution)/shard_map/ppermute | solution.py:160
  110.6 5.7 %pick.1 = bf16[8,16,8,2048]{3,2,1,0:T(8,128)(2,1)} custom-call(s32[1]{0:T(128)} %bitcast.mine, bf16[4,72,1024]{2,1,0:T(8,128)(2,1)} %copy-done, bf16[4,72,1024]{2,1,0:T(8,128)(2,1)} %copy-done.3, bf16[4,72,1024]{2,1,0:T(8,128)(2,1)} %copy-done.11, bf16[4,72,1024]{2,1,0:T(8,128)(2,1)} %copy-done.12, bf16[4,72,1024]{2,1,0:T(8,128)(2,1)} %copy-done.10, ...), custom_call_target="tpu_custom_call" | custom-call | tf_op jit(solution)/shard_map/pick/pallas_call | solution.py:270
  116.3 5.0 %all-to-all-start = ((bf16[8,128,2048]{2,1,0:T(8,128)(2,1)}), bf16[8,128,2048]{2,1,0:T(8,128)(2,1)}, u32[]{:S(2)}, u32[]{:S(2)}) async-start(bf16[8,128,2048]{2,1,0:T(8,128)(2,1)} %bitcast.81), calls=%async_computation | async-start | bytes 8388608 | tf_op jit(solution)/shard_map/all_to_all | solution.py:411
  121.4 10.8 %shared_expert.1 = (bf16[288,1024]{1,0:T(8,128)(2,1)S(1)}, bf16[288,1024]{1,0:T(8,128)(2,1)S(1)}, bf16[288,1024]{1,0:T(8,128)(2,1)S(1)}, bf16[288,1024]{1,0:T(8,...) custom-call(bf16[288,1024]{1,0:T(8,128)(2,1)S(1)} %bitcast.77, ...), custom_call_target="tpu_custom_call" | custom-call | flops 4982833152 | bytes 13762560 | tf_op jit(solution)/shard_map/shared_expert/pallas_call | solution.py:334
  132.2 1.5 collective-permute-start.28
  133.8 2.5 collective-permute-start.29
  137.6 10.8 %collective-permute-done.27 = bf16[288,1024]{1,0:T(8,128)(2,1)S(1)} collective-permute-done((bf16[288,1024]{1,0:T(8,128)(2,1)S(1)}, bf16[288,1024]{1,0:T(8,128)(2,1)S(1)}, u32[]{:S(2)}, u32[]{:S(2)}) %collective-permute-start.27) | collective-permute-done | bytes 589856 | tf_op jit(solution)/shard_map/ppermute | solution.py:160
  148.5 13.0 %collective-permute-done.28 = bf16[288,1024]{1,0:T(8,128)(2,1)S(1)} collective-permute-done((bf16[288,1024]{1,0:T(8,128)(2,1)S(1)}, bf16[288,1024]{1,0:T(8,128)(2,1)S(1)}, u32[]{:S(2)}, u32[]{:S(2)}) %collective-permute-start.28) | collective-permute-done | bytes 589856 | tf_op jit(solution)/shard_map/ppermute | solution.py:160
  162.0 2.7 %collective-permute-done.25 = bf16[288,1024]{1,0:T(8,128)(2,1)S(1)} collective-permute-done((bf16[288,1024]{1,0:T(8,128)(2,1)S(1)}, bf16[288,1024]{1,0:T(8,128)(2,1)S(1)}, u32[]{:S(2)}, u32[]{:S(2)}) %collective-permute-start.25) | collective-permute-done | bytes 589856 | tf_op jit(solution)/shard_map/ppermute | solution.py:156
  165.6 1.5 collective-permute-start.31
  167.1 2.3 collective-permute-start.32
  171.3 2.2 collective-permute-start.35
  174.6 1.8 collective-permute-done.34
  176.4 1.6 collective-permute-done.35
  178.0 1.8 copy-done.9
  179.8 14.6 %experts.1 = bf16[1024,2048]{1,0:T(8,128)(2,1)} custom-call(bf16[1024,2048]{1,0:T(8,128)(2,1)} %bitcast.39.rows, bf16[1,2,704,2048]{3,2,1,0:T(8,128)(2,1)} %bitcast.97, bf16[1,704,2048]{2,1,0:T(8,128)(2,1)S(1)} %copy-done.9), custom_call_target="tpu_custom_call" | custom-call | flops 8858370048 | bytes 17039360 | tf_op jit(solution)/shard_map/experts/pallas_call | solution.py:291
  194.5 7.4 %all-to-all-start.1 = ((bf16[128,8,2048]{2,1,0:T(8,128)(2,1)}), bf16[128,8,2048]{2,1,0:T(8,128)(2,1)}, u32[]{:S(2)}, u32[]{:S(2)}) async-start(bf16[128,8,2048]{2,1,0:T(8,128)(2,1)} %bitcast.82), calls=%async_computation.1 | async-start | bytes 8388608 | tf_op jit(solution)/shard_map/all_to_all | solution.py:422
  202.6 50.4 %all-to-all-done.1 = bf16[128,8,2048]{2,1,0:T(8,128)(2,1)} async-done(((bf16[128,8,2048]{2,1,0:T(8,128)(2,1)}), bf16[128,8,2048]{2,1,0:T(8,128)(2,1)}, u32[]{:S(2)}, u32[]{:S(2)}) %all-to-all-start.1) | async-done | bytes 4194336 | tf_op jit(solution)/shard_map/all_to_all | solution.py:422
  253.0 3.0 %fusion = f32[144,2048]{1,0:T(8,128)S(1)} fusion(bf16[128,8,2048]{2,1,0:T(8,128)(2,1)} %all-to-all-done.1, bf16[72,1024]{1,0:T(8,128)(2,1)S(1)} %get-tuple-element.71, bf16[72,1024]{1,0:T(8,128)(2,1)S(1)} %get-tuple-element.72), kind=kOutput, calls=%fused_computation | convolution fusion | flops 604569600 | bytes 5668864 | tf_op jit(solution)/shard_map/dot_general | solution.py:28
  (107 shorter events, 24.7 us)
Async XLA Ops:
  7.6 23.3 %copy-start.17 = (s32[65,4]{0,1:T(4,128)S(1)}, s32[65,4]{0,1:T(4,128)}, u32[]{:S(2)}) copy-start(s32[65,4]{0,1:T(4,128)} %param.26) | copy-start | bytes 3124
  10.9 16.2 %collective-permute-start.3 = (bf16[288,1024]{1,0:T(8,128)(2,1)S(1)}, bf16[288,1024]{1,0:T(8,128)(2,1)S(1)}, u32[]{:S(2)}, u32[]{:S(2)}) collective-permute-start(bf16[288,1024]{1,0:T(8,128)(2,1)S(1)} %get-tuple-element.43), channel_id=1, source_target_pairs={{0,1},{1,0},{2,3},{3,2},{4,5},{5,4},{6,7},{7,6},{8,9},{9,8},{10,11... | collective-permute-start | bytes 1769480 | tf_op jit(solution)/shard_map/ppermute | solution.py:160
  12.8 27.8 %collective-permute-start.4 = (bf16[288,1024]{1,0:T(8,128)(2,1)}, bf16[288,1024]{1,0:T(8,128)(2,1)}, u32[]{:S(2)}, u32[]{:S(2)}) collective-permute-start(bf16[288,1024]{1,0:T(8,128)(2,1)} %get-tuple-element.44), channel_id=1, source_target_pairs={{0,3},{1,2},{2,1},{3,0},{4,7},{5,6},{6,5},{7,4},{8,11},{9,10},{10,... | collective-permute-start | bytes 1769480 | tf_op jit(solution)/shard_map/ppermute | solution.py:160
  15.3 26.9 %collective-permute-start.5 = (bf16[288,1024]{1,0:T(8,128)(2,1)}, bf16[288,1024]{1,0:T(8,128)(2,1)}, u32[]{:S(2)}, u32[]{:S(2)}) collective-permute-start(bf16[288,1024]{1,0:T(8,128)(2,1)} %get-tuple-element.45), channel_id=1, source_target_pairs={{0,2},{1,3},{2,0},{3,1},{4,6},{5,7},{6,4},{7,5},{8,10},{9,11},{10,... | collective-permute-start | bytes 1769480 | tf_op jit(solution)/shard_map/ppermute | solution.py:160
  16.4 27.6 %collective-permute-start = (bf16[288,1024]{1,0:T(8,128)(2,1)S(1)}, bf16[288,1024]{1,0:T(8,128)(2,1)S(1)}, u32[]{:S(2)}, u32[]{:S(2)}) collective-permute-start(bf16[288,1024]{1,0:T(8,128)(2,1)S(1)} %get-tuple-element.39), channel_id=1, source_target_pairs={{0,4},{1,5},{2,6},{3,7},{4,0},{5,1},{6,2},{7,3},{8,12},{9,13},{10,... | collective-permute-start | bytes 1769480 | tf_op jit(solution)/shard_map/ppermute | solution.py:156
  17.9 28.2 %collective-permute-start.1 = (bf16[288,1024]{1,0:T(8,128)(2,1)S(1)}, bf16[288,1024]{1,0:T(8,128)(2,1)}, u32[]{:S(2)}, u32[]{:S(2)}) collective-permute-start(bf16[288,1024]{1,0:T(8,128)(2,1)S(1)} %get-tuple-element.40), channel_id=1, source_target_pairs={{0,12},{1,13},{2,14},{3,15},{4,8},{5,9},{6,10},{7,11},{8,4},{9,5},... | collective-permute-start | bytes 1769480 | tf_op jit(solution)/shard_map/ppermute | solution.py:156
  27.9 18.2 %collective-permute-start.2 = (bf16[288,1024]{1,0:T(8,128)(2,1)S(1)}, bf16[288,1024]{1,0:T(8,128)(2,1)}, u32[]{:S(2)}, u32[]{:S(2)}) collective-permute-start(bf16[288,1024]{1,0:T(8,128)(2,1)S(1)} %get-tuple-element.41), channel_id=1, source_target_pairs={{0,8},{1,9},{2,10},{3,11},{4,12},{5,13},{6,14},{7,15},{8,0},{9,1},... | collective-permute-start | bytes 1769480 | tf_op jit(solution)/shard_map/ppermute | solution.py:156
  47.7 12.0 %copy-start.8 = (f32[2048]{0:T(1024)S(1)}, f32[2048]{0:T(1024)}, u32[]{:S(2)}) copy-start(f32[2048]{0:T(1024)} %param.22) | copy-start | bytes 24580
  47.8 6.8 %collective-permute-start.10 = (bf16[72,1024]{1,0:T(8,128)(2,1)S(1)}, bf16[72,1024]{1,0:T(8,128)(2,1)S(1)}, u32[]{:S(2)}, u32[]{:S(2)}) collective-permute-start(bf16[72,1024]{1,0:T(8,128)(2,1)S(1)} %get-tuple-element.84), channel_id=1, source_target_pairs={{0,12},{1,13},{2,14},{3,15},{4,8},{5,9},{6,10},{7,11},{8,4},{9,5},... | collective-permute-start | bytes 442376 | tf_op jit(solution)/shard_map/ppermute | solution.py:156
  49.9 7.9 %collective-permute-start.11 = (bf16[72,1024]{1,0:T(8,128)(2,1)S(1)}, bf16[72,1024]{1,0:T(8,128)(2,1)S(1)}, u32[]{:S(2)}, u32[]{:S(2)}) collective-permute-start(bf16[72,1024]{1,0:T(8,128)(2,1)S(1)} %get-tuple-element.83), channel_id=1, source_target_pairs={{0,8},{1,9},{2,10},{3,11},{4,12},{5,13},{6,14},{7,15},{8,0},{9,1},... | collective-permute-start | bytes 442376 | tf_op jit(solution)/shard_map/ppermute | solution.py:156
  50.0 7.9 %collective-permute-start.6 = (bf16[72,1024]{1,0:T(8,128)(2,1)S(1)}, bf16[72,1024]{1,0:T(8,128)(2,1)S(1)}, u32[]{:S(2)}, u32[]{:S(2)}) collective-permute-start(bf16[72,1024]{1,0:T(8,128)(2,1)S(1)} %get-tuple-element.89), channel_id=1, source_target_pairs={{0,1},{1,0},{2,3},{3,2},{4,5},{5,4},{6,7},{7,6},{8,9},{9,8},{10,11... | collective-permute-start | bytes 442376 | tf_op jit(solution)/shard_map/ppermute | solution.py:160
  50.3 7.6 %collective-permute-start.7 = (bf16[72,1024]{1,0:T(8,128)(2,1)S(1)}, bf16[72,1024]{1,0:T(8,128)(2,1)S(1)}, u32[]{:S(2)}, u32[]{:S(2)}) collective-permute-start(bf16[72,1024]{1,0:T(8,128)(2,1)S(1)} %get-tuple-element.88), channel_id=1, source_target_pairs={{0,3},{1,2},{2,1},{3,0},{4,7},{5,6},{6,5},{7,4},{8,11},{9,10},{10,... | collective-permute-start | bytes 442376 | tf_op jit(solution)/shard_map/ppermute | solution.py:160
  52.8 6.6 %collective-permute-start.8 = (bf16[72,1024]{1,0:T(8,128)(2,1)S(1)}, bf16[72,1024]{1,0:T(8,128)(2,1)S(1)}, u32[]{:S(2)}, u32[]{:S(2)}) collective-permute-start(bf16[72,1024]{1,0:T(8,128)(2,1)S(1)} %get-tuple-element.87), channel_id=1, source_target_pairs={{0,2},{1,3},{2,0},{3,1},{4,6},{5,7},{6,4},{7,5},{8,10},{9,11},{10,... | collective-permute-start | bytes 442376 | tf_op jit(solution)/shard_map/ppermute | solution.py:160
  54.6 5.1 %collective-permute-start.9 = (bf16[72,1024]{1,0:T(8,128)(2,1)S(1)}, bf16[72,1024]{1,0:T(8,128)(2,1)S(1)}, u32[]{:S(2)}, u32[]{:S(2)}) collective-permute-start(bf16[72,1024]{1,0:T(8,128)(2,1)S(1)} %get-tuple-element.85), channel_id=1, source_target_pairs={{0,4},{1,5},{2,6},{3,7},{4,0},{5,1},{6,2},{7,3},{8,12},{9,13},{10,... | collective-permute-start | bytes 442376 | tf_op jit(solution)/shard_map/ppermute | solution.py:156
  60.1 9.9 %collective-permute-start.15 = (bf16[72,1024]{1,0:T(8,128)(2,1)S(1)}, bf16[72,1024]{1,0:T(8,128)(2,1)S(1)}, u32[]{:S(2)}, u32[]{:S(2)}) collective-permute-start(bf16[72,1024]{1,0:T(8,128)(2,1)S(1)} %get-tuple-element.93), channel_id=1, source_target_pairs={{0,4},{1,5},{2,6},{3,7},{4,0},{5,1},{6,2},{7,3},{8,12},{9,13},{10,... | collective-permute-start | bytes 442376 | tf_op jit(solution)/shard_map/ppermute | solution.py:156
  62.4 7.6 %collective-permute-start.16 = (bf16[72,1024]{1,0:T(8,128)(2,1)S(1)}, bf16[72,1024]{1,0:T(8,128)(2,1)S(1)}, u32[]{:S(2)}, u32[]{:S(2)}) collective-permute-start(bf16[72,1024]{1,0:T(8,128)(2,1)S(1)} %get-tuple-element.93), channel_id=1, source_target_pairs={{0,8},{1,9},{2,10},{3,11},{4,12},{5,13},{6,14},{7,15},{8,0},{9,1},... | collective-permute-start | bytes 442376 | tf_op jit(solution)/shard_map/ppermute | solution.py:156
  64.7 6.4 %collective-permute-start.17 = (bf16[72,1024]{1,0:T(8,128)(2,1)S(1)}, bf16[72,1024]{1,0:T(8,128)(2,1)S(1)}, u32[]{:S(2)}, u32[]{:S(2)}) collective-permute-start(bf16[72,1024]{1,0:T(8,128)(2,1)S(1)} %get-tuple-element.93), channel_id=1, source_target_pairs={{0,12},{1,13},{2,14},{3,15},{4,8},{5,9},{6,10},{7,11},{8,4},{9,5},... | collective-permute-start | bytes 442376 | tf_op jit(solution)/shard_map/ppermute | solution.py:156
  65.2 5.9 %collective-permute-start.12 = (bf16[72,1024]{1,0:T(8,128)(2,1)S(1)}, bf16[72,1024]{1,0:T(8,128)(2,1)S(1)}, u32[]{:S(2)}, u32[]{:S(2)}) collective-permute-start(bf16[72,1024]{1,0:T(8,128)(2,1)S(1)} %get-tuple-element.94), channel_id=1, source_target_pairs={{0,1},{1,0},{2,3},{3,2},{4,5},{5,4},{6,7},{7,6},{8,9},{9,8},{10,11... | collective-permute-start | bytes 442376 | tf_op jit(solution)/shard_map/ppermute | solution.py:160
  66.2 8.6 %collective-permute-start.13 = (bf16[72,1024]{1,0:T(8,128)(2,1)S(1)}, bf16[72,1024]{1,0:T(8,128)(2,1)S(1)}, u32[]{:S(2)}, u32[]{:S(2)}) collective-permute-start(bf16[72,1024]{1,0:T(8,128)(2,1)S(1)} %get-tuple-element.94), channel_id=1, source_target_pairs={{0,2},{1,3},{2,0},{3,1},{4,6},{5,7},{6,4},{7,5},{8,10},{9,11},{10,... | collective-permute-start | bytes 442376 | tf_op jit(solution)/shard_map/ppermute | solution.py:160
  70.0 6.4 %collective-permute-start.14 = (bf16[72,1024]{1,0:T(8,128)(2,1)S(1)}, bf16[72,1024]{1,0:T(8,128)(2,1)S(1)}, u32[]{:S(2)}, u32[]{:S(2)}) collective-permute-start(bf16[72,1024]{1,0:T(8,128)(2,1)S(1)} %get-tuple-element.94), channel_id=1, source_target_pairs={{0,3},{1,2},{2,1},{3,0},{4,7},{5,6},{6,5},{7,4},{8,11},{9,10},{10,... | collective-permute-start | bytes 442376 | tf_op jit(solution)/shard_map/ppermute | solution.py:160
  71.1 38.6 %copy-start.10 = (bf16[4,72,1024]{2,1,0:T(8,128)(2,1)}, bf16[4,72,1024]{2,1,0:T(8,128)(2,1)S(1)}, u32[]{:S(2)}) copy-start(bf16[4,72,1024]{2,1,0:T(8,128)(2,1)S(1)} %pad_maximum_fusion.2.refs_4_) | copy-start | bytes 1769476
  76.5 33.2 %copy-start = (bf16[4,72,1024]{2,1,0:T(8,128)(2,1)}, bf16[4,72,1024]{2,1,0:T(8,128)(2,1)S(1)}, u32[]{:S(2)}) copy-start(bf16[4,72,1024]{2,1,0:T(8,128)(2,1)S(1)} %pad_maximum_fusion.1.refs_0_) | copy-start | bytes 1769476
  76.5 16.3 %collective-permute-start.18 = (bf16[4,72,1024]{2,1,0:T(8,128)(2,1)S(1)}, bf16[4,72,1024]{2,1,0:T(8,128)(2,1)S(1)}, u32[]{:S(2)}, u32[]{:S(2)}) collective-permute-start(bf16[4,72,1024]{2,1,0:T(8,128)(2,1)S(1)} %pad_maximum_fusion.1.refs_0_), channel_id=1, source_target_pairs={{0,4},{1,5},{2,6},{3,7},{4,0},{5,1},{6,2},{7,3},{8,12},{9,13},{10,... | collective-permute-start | bytes 1769480 | tf_op jit(solution)/shard_map/ppermute | solution.py:156
  76.6 23.5 %collective-permute-start.19 = (bf16[4,72,1024]{2,1,0:T(8,128)(2,1)S(1)}, bf16[4,72,1024]{2,1,0:T(8,128)(2,1)S(1)}, u32[]{:S(2)}, u32[]{:S(2)}) collective-permute-start(bf16[4,72,1024]{2,1,0:T(8,128)(2,1)S(1)} %pad_maximum_fusion.1.refs_0_), channel_id=1, source_target_pairs={{0,8},{1,9},{2,10},{3,11},{4,12},{5,13},{6,14},{7,15},{8,0},{9,1},... | collective-permute-start | bytes 1769480 | tf_op jit(solution)/shard_map/ppermute | solution.py:156
  81.3 21.3 %collective-permute-start.20 = (bf16[4,72,1024]{2,1,0:T(8,128)(2,1)S(1)}, bf16[4,72,1024]{2,1,0:T(8,128)(2,1)S(1)}, u32[]{:S(2)}, u32[]{:S(2)}) collective-permute-start(bf16[4,72,1024]{2,1,0:T(8,128)(2,1)S(1)} %pad_maximum_fusion.1.refs_0_), channel_id=1, source_target_pairs={{0,12},{1,13},{2,14},{3,15},{4,8},{5,9},{6,10},{7,11},{8,4},{9,5},... | collective-permute-start | bytes 1769480 | tf_op jit(solution)/shard_map/ppermute | solution.py:156
  81.3 21.3 %collective-permute-start.21 = (bf16[4,72,1024]{2,1,0:T(8,128)(2,1)S(1)}, bf16[4,72,1024]{2,1,0:T(8,128)(2,1)S(1)}, u32[]{:S(2)}, u32[]{:S(2)}) collective-permute-start(bf16[4,72,1024]{2,1,0:T(8,128)(2,1)S(1)} %pad_maximum_fusion.2.refs_4_), channel_id=1, source_target_pairs={{0,1},{1,0},{2,3},{3,2},{4,5},{5,4},{6,7},{7,6},{8,9},{9,8},{10,11... | collective-permute-start | bytes 1769480 | tf_op jit(solution)/shard_map/ppermute | solution.py:160
  81.3 22.2 %collective-permute-start.22 = (bf16[4,72,1024]{2,1,0:T(8,128)(2,1)S(1)}, bf16[4,72,1024]{2,1,0:T(8,128)(2,1)S(1)}, u32[]{:S(2)}, u32[]{:S(2)}) collective-permute-start(bf16[4,72,1024]{2,1,0:T(8,128)(2,1)S(1)} %pad_maximum_fusion.2.refs_4_), channel_id=1, source_target_pairs={{0,2},{1,3},{2,0},{3,1},{4,6},{5,7},{6,4},{7,5},{8,10},{9,11},{10,... | collective-permute-start | bytes 1769480 | tf_op jit(solution)/shard_map/ppermute | solution.py:160
  92.8 16.9 %copy-start.3 = (bf16[4,72,1024]{2,1,0:T(8,128)(2,1)}, bf16[4,72,1024]{2,1,0:T(8,128)(2,1)S(1)}, u32[]{:S(2)}) copy-start(bf16[4,72,1024]{2,1,0:T(8,128)(2,1)S(1)} %collective-permute-done.18.refs_1_) | copy-start | bytes 1769476
  92.8 16.9 %collective-permute-start.23 = (bf16[4,72,1024]{2,1,0:T(8,128)(2,1)S(1)}, bf16[4,72,1024]{2,1,0:T(8,128)(2,1)S(1)}, u32[]{:S(2)}, u32[]{:S(2)}) collective-permute-start(bf16[4,72,1024]{2,1,0:T(8,128)(2,1)S(1)} %pad_maximum_fusion.2.refs_4_), channel_id=1, source_target_pairs={{0,3},{1,2},{2,1},{3,0},{4,7},{5,6},{6,5},{7,4},{8,11},{9,10},{10,... | collective-permute-start | bytes 1769480 | tf_op jit(solution)/shard_map/ppermute | solution.py:160
  100.0 9.7 %copy-start.11 = (bf16[4,72,1024]{2,1,0:T(8,128)(2,1)}, bf16[4,72,1024]{2,1,0:T(8,128)(2,1)S(1)}, u32[]{:S(2)}) copy-start(bf16[4,72,1024]{2,1,0:T(8,128)(2,1)S(1)} %collective-permute-done.19.refs_2_) | copy-start | bytes 1769476
  102.6 7.2 %copy-start.12 = (bf16[4,72,1024]{2,1,0:T(8,128)(2,1)}, bf16[4,72,1024]{2,1,0:T(8,128)(2,1)S(1)}, u32[]{:S(2)}) copy-start(bf16[4,72,1024]{2,1,0:T(8,128)(2,1)S(1)} %collective-permute-done.20.refs_3_) | copy-start | bytes 1769476
  102.6 7.2 %copy-start.13 = (bf16[4,72,1024]{2,1,0:T(8,128)(2,1)}, bf16[4,72,1024]{2,1,0:T(8,128)(2,1)S(1)}, u32[]{:S(2)}) copy-start(bf16[4,72,1024]{2,1,0:T(8,128)(2,1)S(1)} %collective-permute-done.21.refs_5_) | copy-start | bytes 1769476
  116.3 61.7 %all-to-all-start = ((bf16[8,128,2048]{2,1,0:T(8,128)(2,1)}), bf16[8,128,2048]{2,1,0:T(8,128)(2,1)}, u32[]{:S(2)}, u32[]{:S(2)}) async-start(bf16[8,128,2048]{2,1,0:T(8,128)(2,1)} %bitcast.81), calls=%async_computation | async-start | bytes 8388608 | tf_op jit(solution)/shard_map/all_to_all | solution.py:411
  132.1 16.3 %collective-permute-start.27 = (bf16[288,1024]{1,0:T(8,128)(2,1)S(1)}, bf16[288,1024]{1,0:T(8,128)(2,1)S(1)}, u32[]{:S(2)}, u32[]{:S(2)}) collective-permute-start(bf16[288,1024]{1,0:T(8,128)(2,1)S(1)} %get-tuple-element.57), channel_id=1, source_target_pairs={{0,1},{1,0},{2,3},{3,2},{4,5},{5,4},{6,7},{7,6},{8,9},{9,8},{10,11... | collective-permute-start | bytes 1769480 | tf_op jit(solution)/shard_map/ppermute | solution.py:160
  132.2 29.3 %collective-permute-start.28 = (bf16[288,1024]{1,0:T(8,128)(2,1)S(1)}, bf16[288,1024]{1,0:T(8,128)(2,1)S(1)}, u32[]{:S(2)}, u32[]{:S(2)}) collective-permute-start(bf16[288,1024]{1,0:T(8,128)(2,1)S(1)} %get-tuple-element.58), channel_id=1, source_target_pairs={{0,3},{1,2},{2,1},{3,0},{4,7},{5,6},{6,5},{7,4},{8,11},{9,10},{10,... | collective-permute-start | bytes 1769480 | tf_op jit(solution)/shard_map/ppermute | solution.py:160
  133.8 27.8 %collective-permute-start.29 = (bf16[288,1024]{1,0:T(8,128)(2,1)S(1)}, bf16[288,1024]{1,0:T(8,128)(2,1)S(1)}, u32[]{:S(2)}, u32[]{:S(2)}) collective-permute-start(bf16[288,1024]{1,0:T(8,128)(2,1)S(1)} %get-tuple-element.59), channel_id=1, source_target_pairs={{0,2},{1,3},{2,0},{3,1},{4,6},{5,7},{6,4},{7,5},{8,10},{9,11},{10,... | collective-permute-start | bytes 1769480 | tf_op jit(solution)/shard_map/ppermute | solution.py:160
  136.3 25.7 %collective-permute-start.24 = (bf16[288,1024]{1,0:T(8,128)(2,1)S(1)}, bf16[288,1024]{1,0:T(8,128)(2,1)S(1)}, u32[]{:S(2)}, u32[]{:S(2)}) collective-permute-start(bf16[288,1024]{1,0:T(8,128)(2,1)S(1)} %get-tuple-element.53), channel_id=1, source_target_pairs={{0,4},{1,5},{2,6},{3,7},{4,0},{5,1},{6,2},{7,3},{8,12},{9,13},{10,... | collective-permute-start | bytes 1769480 | tf_op jit(solution)/shard_map/ppermute | solution.py:156
  136.3 28.4 %collective-permute-start.25 = (bf16[288,1024]{1,0:T(8,128)(2,1)S(1)}, bf16[288,1024]{1,0:T(8,128)(2,1)S(1)}, u32[]{:S(2)}, u32[]{:S(2)}) collective-permute-start(bf16[288,1024]{1,0:T(8,128)(2,1)S(1)} %get-tuple-element.54), channel_id=1, source_target_pairs={{0,12},{1,13},{2,14},{3,15},{4,8},{5,9},{6,10},{7,11},{8,4},{9,5},... | collective-permute-start | bytes 1769480 | tf_op jit(solution)/shard_map/ppermute | solution.py:156
  148.4 16.3 %collective-permute-start.26 = (bf16[288,1024]{1,0:T(8,128)(2,1)S(1)}, bf16[288,1024]{1,0:T(8,128)(2,1)S(1)}, u32[]{:S(2)}, u32[]{:S(2)}) collective-permute-start(bf16[288,1024]{1,0:T(8,128)(2,1)S(1)} %get-tuple-element.55), channel_id=1, source_target_pairs={{0,8},{1,9},{2,10},{3,11},{4,12},{5,13},{6,14},{7,15},{8,0},{9,1},... | collective-permute-start | bytes 1769480 | tf_op jit(solution)/shard_map/ppermute | solution.py:156
  165.2 6.2 %collective-permute-start.30 = (bf16[72,1024]{1,0:T(8,128)(2,1)S(1)}, bf16[72,1024]{1,0:T(8,128)(2,1)S(1)}, u32[]{:S(2)}, u32[]{:S(2)}) collective-permute-start(bf16[72,1024]{1,0:T(8,128)(2,1)S(1)} %get-tuple-element.81), channel_id=1, source_target_pairs={{0,1},{1,0},{2,3},{3,2},{4,5},{5,4},{6,7},{7,6},{8,9},{9,8},{10,11... | collective-permute-start | bytes 442376 | tf_op jit(solution)/shard_map/ppermute | solution.py:160
  165.6 8.4 %collective-permute-start.31 = (bf16[72,1024]{1,0:T(8,128)(2,1)S(1)}, bf16[72,1024]{1,0:T(8,128)(2,1)S(1)}, u32[]{:S(2)}, u32[]{:S(2)}) collective-permute-start(bf16[72,1024]{1,0:T(8,128)(2,1)S(1)} %get-tuple-element.80), channel_id=1, source_target_pairs={{0,3},{1,2},{2,1},{3,0},{4,7},{5,6},{6,5},{7,4},{8,11},{9,10},{10,... | collective-permute-start | bytes 442376 | tf_op jit(solution)/shard_map/ppermute | solution.py:160
  167.1 6.9 %collective-permute-start.32 = (bf16[72,1024]{1,0:T(8,128)(2,1)S(1)}, bf16[72,1024]{1,0:T(8,128)(2,1)S(1)}, u32[]{:S(2)}, u32[]{:S(2)}) collective-permute-start(bf16[72,1024]{1,0:T(8,128)(2,1)S(1)} %get-tuple-element.79), channel_id=1, source_target_pairs={{0,2},{1,3},{2,0},{3,1},{4,6},{5,7},{6,4},{7,5},{8,10},{9,11},{10,... | collective-permute-start | bytes 442376 | tf_op jit(solution)/shard_map/ppermute | solution.py:160
  169.4 5.2 %collective-permute-start.33 = (bf16[72,1024]{1,0:T(8,128)(2,1)S(1)}, bf16[72,1024]{1,0:T(8,128)(2,1)S(1)}, u32[]{:S(2)}, u32[]{:S(2)}) collective-permute-start(bf16[72,1024]{1,0:T(8,128)(2,1)S(1)} %get-tuple-element.77), channel_id=1, source_target_pairs={{0,4},{1,5},{2,6},{3,7},{4,0},{5,1},{6,2},{7,3},{8,12},{9,13},{10,... | collective-permute-start | bytes 442376 | tf_op jit(solution)/shard_map/ppermute | solution.py:156
  170.0 6.4 %collective-permute-start.34 = (bf16[72,1024]{1,0:T(8,128)(2,1)S(1)}, bf16[72,1024]{1,0:T(8,128)(2,1)S(1)}, u32[]{:S(2)}, u32[]{:S(2)}) collective-permute-start(bf16[72,1024]{1,0:T(8,128)(2,1)S(1)} %get-tuple-element.76), channel_id=1, source_target_pairs={{0,12},{1,13},{2,14},{3,15},{4,8},{5,9},{6,10},{7,11},{8,4},{9,5},... | collective-permute-start | bytes 442376 | tf_op jit(solution)/shard_map/ppermute | solution.py:156
  171.3 6.6 %collective-permute-start.35 = (bf16[72,1024]{1,0:T(8,128)(2,1)S(1)}, bf16[72,1024]{1,0:T(8,128)(2,1)S(1)}, u32[]{:S(2)}, u32[]{:S(2)}) collective-permute-start(bf16[72,1024]{1,0:T(8,128)(2,1)S(1)} %get-tuple-element.75), channel_id=1, source_target_pairs={{0,8},{1,9},{2,10},{3,11},{4,12},{5,13},{6,14},{7,15},{8,0},{9,1},... | collective-permute-start | bytes 442376 | tf_op jit(solution)/shard_map/ppermute | solution.py:156
  194.5 7.5 %copy-start.18 = (bf16[2048]{0:T(1024)(128)(2,1)S(1)}, bf16[2048]{0:T(1024)(128)(2,1)}, u32[]{:S(2)}) copy-start(bf16[2048]{0:T(1024)(128)(2,1)} %param.25) | copy-start | bytes 12292
  194.5 7.5 %copy-start.19 = (f32[65,4]{0,1:T(4,128)S(1)}, f32[65,4]{0,1:T(4,128)}, u32[]{:S(2)}) copy-start(f32[65,4]{0,1:T(4,128)} %param.27) | copy-start | bytes 3124
  194.5 58.6 %all-to-all-start.1 = ((bf16[128,8,2048]{2,1,0:T(8,128)(2,1)}), bf16[128,8,2048]{2,1,0:T(8,128)(2,1)}, u32[]{:S(2)}, u32[]{:S(2)}) async-start(bf16[128,8,2048]{2,1,0:T(8,128)(2,1)} %bitcast.82), calls=%async_computation.1 | async-start | bytes 8388608 | tf_op jit(solution)/shard_map/all_to_all | solution.py:422
  (10 other events, 23.5 us)

commit v4 on v3

--- a/solution.py
+++ b/solution.py
@@ -56,8 +56,12 @@
             out[r * span + h * part : r * span + (h + 1) * part, :] = dot(w, v).astype(BF)
     requests, entries = table.shape
     pages, page = keys.shape[0], keys.shape[1]
+    row = lax.broadcasted_iota(jnp.int32, (requests, entries), 0)
+    held = jnp.zeros((requests, entries), jnp.int32)
+    for i in range(requests):
+        held = jnp.where(row == i, lens[i], held)
     held = jnp.clip(
-        lens[...] - page * lax.broadcasted_iota(jnp.int32, (requests, entries), 1), 0, page
+        held - page * lax.broadcasted_iota(jnp.int32, (requests, entries), 1), 0, page
     )
     ids = table[...]
     lane = lax.broadcasted_iota(jnp.int32, (requests, page), 1)
@@ -110,7 +114,7 @@
     return pl.pallas_call(
         attention_kernel,
         out_shape=jax.ShapeDtypeStruct((rows, HD), BF),
-        in_specs=[whole, whole, whole, whole, pl.BlockSpec(memory_space=pl.ANY)],
+        in_specs=[pl.BlockSpec(memory_space=pltpu.SMEM), whole, whole, whole, pl.BlockSpec(memory_space=pl.ANY)],
         out_specs=whole,
         scratch_shapes=[
             pltpu.VMEM((pages, page, HD), BF),
@@ -118,9 +122,9 @@
             pltpu.VMEM((requests, pages * page), F32),
             pltpu.SemaphoreType.DMA((2,)),
         ],
-        compiler_params=vmem(48),
+        compiler_params=vmem(56),
         name="attention",
-    )(cache_len[:, None], page_table, prefill_qkv, decode_qkv.transpose(1, 0, 2), cache_pool)
+    )(cache_len, page_table, prefill_qkv, decode_qkv.transpose(1, 0, 2), cache_pool)
 
 
 def project_kernel(mine, blocks, weight, *outs):
@@ -147,7 +151,7 @@
         out_shape=[jax.ShapeDtypeStruct((SIDE * ROWS, half), BF)] * (2 * SIDE),
         in_specs=[pl.BlockSpec(memory_space=pltpu.SMEM), whole, whole],
         out_specs=[whole] * (2 * SIDE),
-        compiler_params=vmem(32),
+        compiler_params=vmem(56),
         name="project",
     )(mine, blocks, out_weight)
 
@@ -216,22 +220,22 @@
     normed[...] = rows.astype(BF)
     count, lanes = tags.shape
     is_tag = lax.broadcasted_iota(jnp.int32, (count, lanes), 0) >= TOKENS
-    normed[:, :lanes] = jnp.where(is_tag, tags[...], rows[:, :lanes]).astype(BF)
-
-
-def chosen_rows(mine, rows_a, columns, capacity):
+    for at in (0, rows.shape[1] // 2):
+        normed[:, at : at + lanes] = jnp.where(is_tag, tags[...], rows[:, at : at + lanes]).astype(BF)
+
+
+def chosen_rows(mine, tags, columns, capacity):
     shape = (columns, LANES)
     expert = lax.broadcasted_iota(jnp.int32, shape, 0) * (SIDE * SIDE // 2) + mine // 2
     expert = expert.astype(F32)
     hits = []
-    for x in range(SIDE):
-        for z in range(SIDE):
-            tags = rows_a[x][z][:, :LANES].astype(F32)
-            hit = jnp.zeros(shape, F32)
-            for k in range(ROUTES):
-                named = jnp.broadcast_to(tags[TOKENS + k : TOKENS + k + 1, :], shape)
-                hit = jnp.where(named == expert, 1.0, hit)
-            hits.append(hit)
+    for block in tags:
+        wide = block.astype(F32)
+        hit = jnp.zeros(shape, F32)
+        for k in range(ROUTES):
+            named = jnp.broadcast_to(wide[TOKENS + k : TOKENS + k + 1, :], shape)
+            hit = jnp.where(named == expert, 1.0, hit)
+        hits.append(hit)
     hits = jnp.concatenate(hits, axis=0)
     before = lax.broadcasted_iota(jnp.int32, (LANES, LANES), 0) < lax.broadcasted_iota(
         jnp.int32, (LANES, LANES), 1
@@ -240,7 +244,7 @@
     rank = jnp.where(hits > 0.0, rank, -1.0)
     slot = lax.broadcasted_iota(jnp.int32, (columns, capacity, LANES), 1).astype(F32)
     chosen = []
-    for i in range(SIDE * SIDE):
+    for i in range(len(tags)):
         here = rank[i * columns : (i + 1) * columns, :]
         here = jnp.broadcast_to(here[:, None, :], (columns, capacity, LANES))
         here = jnp.where(here == slot, 1.0, 0.0).reshape(columns * capacity, LANES)
@@ -248,64 +252,86 @@
     return chosen
 
 
-def pick_kernel(mine, *refs):
-    rows_a, rows_b, out = refs[:SIDE], refs[SIDE : 2 * SIDE], refs[-1]
-    columns, _, capacity, width = out.shape
-    half = width // 2
-    chosen = chosen_rows(mine[0], rows_a, columns, capacity)
-    for x in range(SIDE):
-        for z in range(SIDE):
-            block = jnp.bitwise_xor(mine[0], x * SIDE + z)
-            pick = chosen[x * SIDE + z]
-            a = dot(pick, rows_a[x][z]).reshape(columns, capacity, half).astype(BF)
-            b = dot(pick, rows_b[z][x]).reshape(columns, capacity, half).astype(BF)
+def pick_kernel(start, mine, *refs):
+    rows_a, rows_b, out = refs[:2], refs[2:4], refs[4]
+    columns, _, _, capacity, _ = out.shape
+    own = range(start, start + 2)
+    pairs = [(x, z) for x in range(SIDE) for z in range(SIDE) if x in own or z in own]
+    tags = [
+        rows_a[x - start][z][:, :LANES] if x in own else rows_b[z - start][x][:, :LANES]
+        for x, z in pairs
+    ]
+    for (x, z), pick in zip(pairs, chosen_rows(mine[0], tags, columns, capacity)):
+        if x in own:
+            a = dot(pick, rows_a[x - start][z]).reshape(columns, capacity, -1).astype(BF)
             for r in range(columns):
-                out[r, block, :, :half] = a[r]
-                out[r, block, :, half:] = b[r]
-
-
-def pick(mine, rows_a, rows_b, columns, capacity):
-    width = 2 * rows_a[0].shape[-1]
+                out[r, 0, (x - start) * SIDE + z] = a[r]
+        if z in own:
+            b = dot(pick, rows_b[z - start][x]).reshape(columns, capacity, -1).astype(BF)
+            for r in range(columns):
+                out[r, 1, x * 2 + z - start] = b[r]
+
+
+def pick(start, mine, rows, columns, capacity):
     whole = pl.BlockSpec(memory_space=pltpu.VMEM)
+    half = rows[0].shape[-1]
     return pl.pallas_call(
-        pick_kernel,
-        out_shape=jax.ShapeDtypeStruct((columns, SIDE * SIDE, capacity, width), BF),
-        in_specs=[pl.BlockSpec(memory_space=pltpu.SMEM)] + [whole] * (2 * SIDE),
+        functools.partial(pick_kernel, start),
+        out_shape=jax.ShapeDtypeStruct((columns, 2, 2 * SIDE, capacity, half), BF),
+        in_specs=[pl.BlockSpec(memory_space=pltpu.SMEM)] + [whole] * 4,
         out_specs=whole,
         compiler_params=vmem(56),
         name="pick",
-    )(mine, *rows_a, *rows_b)
-
-
-def expert_kernel(rows, gate_up, down, out):
-    x = rows[...]
-    gate = dot_nt(x, gate_up[0, 0])
-    up = dot_nt(x, gate_up[0, 1])
+    )(mine, *rows)
+
+
+def expert_kernel(mine, first, second, gate_up, down, out):
+    step, _, height, half = first.shape
+    piece = height // SIDE
+    a, b = [], []
+    for i in range(step):
+        a += [first[i, 0], second[i, 0]]
+        for x in range(SIDE):
+            b += [first[i, 1, x * piece : (x + 1) * piece], second[i, 1, x * piece : (x + 1) * piece]]
+    a = jnp.concatenate(a, axis=0)
+    b = jnp.concatenate(b, axis=0)
+    gate = dot_nt(a, gate_up[0, 0, :, :half]) + dot_nt(b, gate_up[0, 0, :, half:])
+    up = dot_nt(a, gate_up[0, 1, :, :half]) + dot_nt(b, gate_up[0, 1, :, half:])
     hidden = (gate / (1.0 + jnp.exp(-gate)) * up).astype(BF)
-    out[...] = dot(hidden, down[0]).astype(BF)
-
-
-def experts(rows, gate_up, down):
-    count, width = rows.shape
-    step = 256
+    _, blocks, capacity, width = out.shape
+    answer = dot(hidden, down[0]).reshape(step, blocks, capacity, width)
+    for i in range(step):
+        for d in range(blocks):
+            out[i, jnp.bitwise_xor(mine[0], d)] = answer[i, d].astype(BF)
+
+
+def experts(mine, first, second, gate_up, down, capacity):
+    count, _, height, half = first.shape
+    step = 4
+    width = 2 * half
+    blocks = 2 * height // capacity
+    rows = count * blocks * capacity
+    tile = pl.BlockSpec((step, 2, height, half), lambda i: (i, 0, 0, 0))
     return pl.pallas_call(
         expert_kernel,
         grid=(count // step,),
-        out_shape=jax.ShapeDtypeStruct((count, width), BF),
+        out_shape=jax.ShapeDtypeStruct((count, blocks, capacity, width), BF),
         in_specs=[
-            pl.BlockSpec((step, width), lambda i: (i, 0)),
+            pl.BlockSpec(memory_space=pltpu.SMEM),
+            tile,
+            tile,
             pl.BlockSpec(gate_up.shape, lambda i: (0, 0, 0, 0)),
             pl.BlockSpec(down.shape, lambda i: (0, 0, 0)),
         ],
-        out_specs=pl.BlockSpec((step, width), lambda i: (i, 0)),
+        out_specs=pl.BlockSpec((step, blocks, capacity, width), lambda i: (i, 0, 0, 0)),
         compiler_params=vmem(50),
         cost_estimate=pl.CostEstimate(
-            flops=6 * count * width * down.shape[1],
-            bytes_accessed=2 * (2 * count * width + 3 * width * down.shape[1]),
-            transcendentals=count * down.shape[1],
+            flops=6 * rows * width * down.shape[1],
+            bytes_accessed=2 * (2 * rows * width + 3 * width * down.shape[1]),
+            transcendentals=rows * down.shape[1],
         ),
         name="experts",
-    )(rows, gate_up, down)
+    )(mine, first, second, gate_up, down)
 
 
 def shared_kernel(*refs):
@@ -407,18 +433,23 @@
         tags,
     )
     rows_a, rows_b = gather(normed)
-    outgoing = pick(mine[None], rows_a, rows_b, lax.axis_size("req"), capacity)
-    arrived = lax.all_to_all(
-        outgoing.reshape(lax.axis_size("req"), groups * capacity, width),
-        "req",
-        split_axis=0,
-        concat_axis=0,
-        tiled=True,
-    )
+    req = lax.axis_size("req")
+
+    def exchange(picked):
+        picked = picked.reshape(req, groups * capacity, width // 2)
+        picked = lax.all_to_all(picked, "req", split_axis=0, concat_axis=0, tiled=True)
+        return picked.reshape(req, 2, -1, width // 2)
+
+    first = pick(0, mine[None], [*rows_a[:2], *rows_b[:2]], req, capacity)
+    first, *late = lax.optimization_barrier((first, *rows_a[2:], *rows_b[2:]))
+    first = exchange(first)
+    second = exchange(pick(2, mine[None], late, req, capacity))
+    rows_a, rows_b = [*rows_a[:2], *late[:2]], [*rows_b[:2], *late[2:]]
     sums = sum_first(shared_expert(rows_a, rows_b, shared_gate_up.transpose(0, 2, 1), shared_down))
-    got_a, got_b = sum_second(*lax.optimization_barrier(sums))
-    arrived, got_a, got_b = lax.optimization_barrier((arrived, got_a, got_b))
-    answer = experts(arrived.reshape(devices * capacity, width), expert_gate_up.transpose(0, 1, 3, 2), expert_down)
+    answer = experts(
+        mine[None], first, second, expert_gate_up.transpose(0, 1, 3, 2), expert_down, capacity
+    )
+    answer, *sums = lax.optimization_barrier((answer, *sums))
     returned = lax.all_to_all(
         answer.reshape(devices, capacity, width),
         ("req", "exp"),
@@ -426,6 +457,7 @@
         concat_axis=0,
         tiled=True,
     )
+    got_a, got_b = sum_second(*sums)
     shared = jnp.concatenate([add_up(got_a), add_up(got_b)], axis=1)
     shared_scale = jax.nn.sigmoid(dot(normed, shared_gate))
     routed = dot(mix, returned.reshape(devices * capacity, width))

time: 260 us -> 279 us (1.073)
  blocking collectives: 0 us -> 31.1 us
  waiting for transfers between devices: 133 us -> 118 us
  Pallas kernels: 38 us -> 44.3 us
  starting transfers between devices: 64.3 us -> 68.6 us
  local copies, waits for them, and re-layouts: 12.3 us -> 8.86 us
    all_to_all x1, waiting for transfers between devices: 50.4 us -> 0.01 us  [on_device(): lax.all_to_all(answer.reshape(devices, capacity, width), ('req', 'exp'),...]
    ppermute x18, waiting for transfers between devices: 52.1 us -> 93.1 us  [along_z(): return lax.ppermute(a, 'exp', [(i, i ^ d) for i in range(SIDE * SIDE)])]
    all_to_all x0 -> x1, blocking collectives: none -> 31.1 us  [exchange(): lax.all_to_all(picked, 'req', split_axis=0, concat_axis=0, tiled=True)]
    ppermute x18, waiting for transfers between devices: 30.3 us -> 24.4 us  [along_x(): lax.ppermute(a, 'exp', [(i, i ^ d * SIDE) for i in range(SIDE * SIDE)])]
    ppermute x18, starting transfers between devices: 25.8 us -> 30.7 us  [along_x(): lax.ppermute(a, 'exp', [(i, i ^ d * SIDE) for i in range(SIDE * SIDE)])]
    unnamed x42 -> x40, local copies, waits for them, and re-layouts: 7.68 us -> 3.33 us
    pallas_call x1 -> x2, Pallas kernels: 5.71 us -> 7.56 us  [pick(): pl.pallas_call(functools.partial(pick_kernel, start), out_shape=jax.Shape...]
  transfers between devices with their start and end apart: 38 -> 38, of which waited for: 24 -> 22; matrix products, arithmetic and copies ran while one was open for 3% -> 3% of each run, Pallas kernels for 4% -> 5%
where the time goes in v4:
time: 279 us; the launch traced here: 278 us
  waiting for transfers between devices  118 us (42%)
  starting transfers between devices  68.6 us (25%)
  Pallas kernels  44.3 us (16%)
  blocking collectives  31.1 us (11%)
  local copies, waits for them, and re-layouts  8.86 us (3%)
  other arithmetic  4.38 us (2%)
  matrix products  3.16 us (1%)
    ppermute x18, waiting for transfers between devices, along_z(): return lax.ppermute(a, 'exp', [(i, i ^ d) for i in range(SIDE * SIDE)])  93.1 us
    all_to_all x1, blocking collectives, exchange(): lax.all_to_all(picked, 'req', split_axis=0, concat_axis=0, tiled=True)  31.1 us
    ppermute x18, starting transfers between devices, along_x(): lax.ppermute(a, 'exp', [(i, i ^ d * SIDE) for i in range(SIDE * SIDE)])  30.7 us
    ppermute x18, starting transfers between devices, along_z(): return lax.ppermute(a, 'exp', [(i, i ^ d) for i in range(SIDE * SIDE)])  26.4 us
    ppermute x18, waiting for transfers between devices, along_x(): lax.ppermute(a, 'exp', [(i, i ^ d * SIDE) for i in range(SIDE * SIDE)])  24.4 us
    pallas_call x1, Pallas kernels, experts(): pl.pallas_call(expert_kernel, grid=(count // step,), out_shape=jax.ShapeD...  15.4 us
    pallas_call x1, Pallas kernels, shared_expert(): pl.pallas_call(shared_kernel, out_shape=[jax.ShapeDtypeStruct((SIDE * ROW...  10.8 us
    pallas_call x2, Pallas kernels, pick(): pl.pallas_call(functools.partial(pick_kernel, start), out_shape=jax.Shape...  7.56 us
  transfers between devices with their start and end apart: 38, of which 22 were waited for; matrix products, arithmetic and copies ran while one was open for 3% of the time, Pallas kernels for 5%

profile of v4, /device:TPU:8, one launch (start us, length us, event | category | flops | bytes accessed | tf_op | source)
XLA Modules:
  0.0 278.3 jit_solution(731976312194258964)
XLA Ops:
  0.0 6.1 %attention.1 = bf16[1040,128]{1,0:T(8,128)(2,1)} custom-call(s32[16]{0:T(128)} %lens.1, s32[16,64]{1,0:T(8,128)} %table.1, bf16[2,3,512,128]{3,2,1,0:T(8,128)(2,1)} %pre.1, bf16[3,16,128]{2,1,0:T(8,128)(2,1)} %bitcast.102, bf16[2,124,128,128]{3,2,1,0:T(8,128)(2,1)} %pool.1), custom_call_target="tpu_custom_call" | custom-call | tf_op jit(solution)/shard_map/attention/pallas_call | solution.py:114
  8.0 4.0 %project.1 = (bf16[288,1024]{1,0:T(8,128)(2,1)}, bf16[288,1024]{1,0:T(8,128)(2,1)}, bf16[288,1024]{1,0:T(8,128)(2,1)}, bf16[288,1024]{1,0:T(8,128)(2,1)}, bf16[2...) custom-call(s32[1]{0:T(128)} %bitcast.mine, ...), custom_call_target="tpu_custom_call" | custom-call | tf_op jit(solution)/shard_map/project/pallas_call | solution.py:149
  12.0 1.9 collective-permute-start.3
  13.9 2.5 collective-permute-start.4
  17.5 1.5 collective-permute-start
  19.0 2.1 collective-permute-start.1
  21.1 7.3 %collective-permute-done.3 = bf16[288,1024]{1,0:T(8,128)(2,1)S(1)} collective-permute-done((bf16[288,1024]{1,0:T(8,128)(2,1)}, bf16[288,1024]{1,0:T(8,128)(2,1)S(1)}, u32[]{:S(2)}, u32[]{:S(2)}) %collective-permute-start.3) | collective-permute-done | bytes 589856 | tf_op jit(solution)/shard_map/ppermute | solution.py:164
  28.4 3.0 %collective-permute-start.2 = (bf16[288,1024]{1,0:T(8,128)(2,1)}, bf16[288,1024]{1,0:T(8,128)(2,1)S(1)}, u32[]{:S(2)}, u32[]{:S(2)}) collective-permute-start(bf16[288,1024]{1,0:T(8,128)(2,1)} %get-tuple-element.38), channel_id=1, source_target_pairs={{0,8},{1,9},{2,10},{3,11},{4,12},{5,13},{6,14},{7,15},{8,0},{9,1},... | collective-permute-start | bytes 1769480 | tf_op jit(solution)/shard_map/ppermute | solution.py:160
  35.8 5.9 %collective-permute-done.4 = bf16[288,1024]{1,0:T(8,128)(2,1)S(1)} collective-permute-done((bf16[288,1024]{1,0:T(8,128)(2,1)}, bf16[288,1024]{1,0:T(8,128)(2,1)S(1)}, u32[]{:S(2)}, u32[]{:S(2)}) %collective-permute-start.4) | collective-permute-done | bytes 589856 | tf_op jit(solution)/shard_map/ppermute | solution.py:164
  41.7 1.7 collective-permute-done.5
  43.4 1.5 add_convert_fusion.2
  45.0 2.3 collective-permute-done.1
  47.8 2.2 collective-permute-start.10
  50.3 2.5 collective-permute-start.7
  52.8 1.3 collective-permute-start.8
  54.6 1.6 collective-permute-start.9
  56.2 2.0 collective-permute-done.11.b3
  60.1 2.0 collective-permute-start.15
  62.2 4.0 %collective-permute-start.16 = (bf16[72,1024]{1,0:T(8,128)(2,1)S(1)}, bf16[72,1024]{1,0:T(8,128)(2,1)S(1)}, u32[]{:S(2)}, u32[]{:S(2)}) collective-permute-start(bf16[72,1024]{1,0:T(8,128)(2,1)S(1)} %get-tuple-element.85), channel_id=1, source_target_pairs={{0,8},{1,9},{2,10},{3,11},{4,12},{5,13},{6,14},{7,15},{8,0},{9,1},... | collective-permute-start | bytes 442376 | tf_op jit(solution)/shard_map/ppermute | solution.py:160
  66.4 4.0 %collective-permute-start.13 = (bf16[72,1024]{1,0:T(8,128)(2,1)S(1)}, bf16[72,1024]{1,0:T(8,128)(2,1)S(1)}, u32[]{:S(2)}, u32[]{:S(2)}) collective-permute-start(bf16[72,1024]{1,0:T(8,128)(2,1)S(1)} %get-tuple-element.86), channel_id=1, source_target_pairs={{0,2},{1,3},{2,0},{3,1},{4,6},{5,7},{6,4},{7,5},{8,10},{9,11},{10,... | collective-permute-start | bytes 442376 | tf_op jit(solution)/shard_map/ppermute | solution.py:164
  70.9 1.6 collective-permute-done.17
  72.6 3.2 %collective-permute-done.13 = bf16[72,1024]{1,0:T(8,128)(2,1)S(1)} collective-permute-done((bf16[72,1024]{1,0:T(8,128)(2,1)S(1)}, bf16[72,1024]{1,0:T(8,128)(2,1)S(1)}, u32[]{:S(2)}, u32[]{:S(2)}) %collective-permute-start.13) | collective-permute-done | bytes 147488 | tf_op jit(solution)/shard_map/ppermute | solution.py:164
  77.5 5.3 %collective-permute-start.20 = (bf16[4,72,1024]{2,1,0:T(8,128)(2,1)S(1)}, bf16[4,72,1024]{2,1,0:T(8,128)(2,1)S(1)}, u32[]{:S(2)}, u32[]{:S(2)}) collective-permute-start(bf16[4,72,1024]{2,1,0:T(8,128)(2,1)S(1)} %pad_maximum_fusion.1.refs_0_), channel_id=1, source_target_pairs={{0,8},{1,9},{2,10},{3,11},{4,12},{5,13},{6,14},{7,15},{8,0},{9,1},... | collective-permute-start | bytes 1769480 | tf_op jit(solution)/shard_map/ppermute | solution.py:160
  82.8 1.7 collective-permute-start.22
  84.5 8.0 %collective-permute-done.18.refs_1_ = bf16[4,72,1024]{2,1,0:T(8,128)(2,1)S(1)} collective-permute-done((bf16[4,72,1024]{2,1,0:T(8,128)(2,1)S(1)}, bf16[4,72,1024]{2,1,0:T(8,128)(2,1)S(1)}, u32[]{:S(2)}, u32[]{:S(2)}) %collective-permute-start.18) | collective-permute-done | bytes 589856 | tf_op jit(solution)/shard_map/ppermute | solution.py:160
  94.4 3.8 %pick.2 = bf16[8,2,8,8,1024]{4,3,2,1,0:T(8,128)(2,1)} custom-call(s32[1]{0:T(128)} %bitcast.mine, bf16[4,72,1024]{2,1,0:T(8,128)(2,1)} %copy-done, bf16[4,72,1024]{2,1,0:T(8,128)(2,1)} %copy-done.2, bf16[4,72,1024]{2,1,0:T(8,128)(2,1)} %copy-done.9, bf16[4,72,1024]{2,1,0:T(8,128)(2,1)} %copy-done.10), custom_call_target="tpu_custom_call" | custom-call | tf_op jit(solution)/shard_map/pick/pallas_call | solution.py:278
  98.9 2.5 collective-permute-done.21.refs_1_
  101.5 6.4 %collective-permute-done.23.refs_3_.refs_7_ = bf16[4,72,1024]{2,1,0:T(8,128)(2,1)S(1)} collective-permute-done((bf16[4,72,1024]{2,1,0:T(8,128)(2,1)S(1)}, bf16[4,72,1024]{2,1,0:T(8,128)(2,1)S(1)}, u32[]{:S(2)}, u32[]{:S(2)}) %collective-permute-start.23) | collective-permute-done | bytes 589856 | tf_op jit(solution)/shard_map/ppermute | solution.py:164
  108.7 3.8 %pick.3 = bf16[8,2,8,8,1024]{4,3,2,1,0:T(8,128)(2,1)} custom-call(s32[1]{0:T(128)} %bitcast.mine, bf16[4,72,1024]{2,1,0:T(8,128)(2,1)} %copy-done.11, bf16[4,72,1024]{2,1,0:T(8,128)(2,1)} %copy-done.12, bf16[4,72,1024]{2,1,0:T(8,128)(2,1)} %copy-done.13, bf16[4,72,1024]{2,1,0:T(8,128)(2,1)} %copy-done.14), custom_call_target="tpu_custom_call" | custom-call | tf_op jit(solution)/shard_map/pick/pallas_call | solution.py:278
  112.4 31.1 %all_to_all.15 = bf16[8,128,1024]{2,1,0:T(8,128)(2,1)} all-to-all(bf16[8,128,1024]{2,1,0:T(8,128)(2,1)} %bitcast.85), channel_id=1, replica_groups=mesh['req'=8,'exp'=16] {'req'}, dimensions={0} | all-to-all | bytes 4194304 | tf_op jit(solution)/shard_map/all_to_all | solution.py:440
  143.5 5.1 %all-to-all-start = ((bf16[8,128,1024]{2,1,0:T(8,128)(2,1)}), bf16[8,128,1024]{2,1,0:T(8,128)(2,1)S(1)}, u32[]{:S(2)}, u32[]{:S(2)}) async-start(bf16[8,128,1024]{2,1,0:T(8,128)(2,1)} %bitcast.84), calls=%async_computation | async-start | bytes 4194304 | tf_op jit(solution)/shard_map/all_to_all | solution.py:440
  148.6 10.8 %shared_expert.1 = (bf16[288,1024]{1,0:T(8,128)(2,1)S(1)}, bf16[288,1024]{1,0:T(8,128)(2,1)S(1)}, bf16[288,1024]{1,0:T(8,128)(2,1)S(1)}, bf16[288,1024]{1,0:T(8,...) custom-call(bf16[288,1024]{1,0:T(8,128)(2,1)S(1)} %bitcast.80, ...), custom_call_target="tpu_custom_call" | custom-call | flops 4982833152 | bytes 13762560 | tf_op jit(solution)/shard_map/shared_expert/pallas_call | solution.py:360
  159.5 1.3 collective-permute-start.28
  160.8 2.8 collective-permute-start.29
  163.6 2.0 collective-permute-start.25
  165.7 10.0 %collective-permute-done.27 = bf16[288,1024]{1,0:T(8,128)(2,1)S(1)} collective-permute-done((bf16[288,1024]{1,0:T(8,128)(2,1)S(1)}, bf16[288,1024]{1,0:T(8,128)(2,1)S(1)}, u32[]{:S(2)}, u32[]{:S(2)}) %collective-permute-start.27) | collective-permute-done | bytes 589856 | tf_op jit(solution)/shard_map/ppermute | solution.py:164
  176.3 12.5 %collective-permute-done.28 = bf16[288,1024]{1,0:T(8,128)(2,1)S(1)} collective-permute-done((bf16[288,1024]{1,0:T(8,128)(2,1)S(1)}, bf16[288,1024]{1,0:T(8,128)(2,1)S(1)}, u32[]{:S(2)}, u32[]{:S(2)}) %collective-permute-start.28) | collective-permute-done | bytes 589856 | tf_op jit(solution)/shard_map/ppermute | solution.py:164
  190.4 1.9 collective-permute-done.26
  192.7 15.4 %experts.1 = bf16[8,16,8,2048]{3,2,1,0:T(8,128)(2,1)} custom-call(s32[1]{0:T(128)} %bitcast.mine, bf16[8,2,64,1024]{3,2,1,0:T(8,128)(2,1)S(1)} %bitcast.81, bf16[8,2,64,1024]{3,2,1,0:T(8,128)(2,1)} %bitcast.93, bf16[1,2,704,2048]{3,2,1,0:T(8,128)(2,1)} %bitcast.104, bf16[1,704,2048]{2,1,0:T(8,128)(2,1)} %down.1), custom_call_target="tpu_custom_call" | custom-call | flops 8858370048 | bytes 17039360 | tf_op jit(solution)/shard_map/experts/pallas_call | solution.py:315
  208.2 6.4 %all-to-all-start.2 = ((bf16[128,8,2048]{2,1,0:T(8,128)(2,1)}), bf16[128,8,2048]{2,1,0:T(8,128)(2,1)}, u32[]{:S(2)}, u32[]{:S(2)}) async-start(bf16[128,8,2048]{2,1,0:T(8,128)(2,1)} %bitcast.86), calls=%async_computation.2 | async-start | bytes 8388608 | tf_op jit(solution)/shard_map/all_to_all | solution.py:453
  215.1 1.7 collective-permute-start.30
  216.9 2.3 collective-permute-start.31
  220.1 1.6 collective-permute-start.33
  221.7 2.1 collective-permute-start.34
  223.8 42.4 %collective-permute-done.30 = bf16[72,1024]{1,0:T(8,128)(2,1)S(1)} collective-permute-done((bf16[72,1024]{1,0:T(8,128)(2,1)S(1)}, bf16[72,1024]{1,0:T(8,128)(2,1)S(1)}, u32[]{:S(2)}, u32[]{:S(2)}) %collective-permute-start.30) | collective-permute-done | bytes 147488 | tf_op jit(solution)/shard_map/ppermute | solution.py:164
  266.2 2.5 collective-permute-start.35
  269.9 3.5 %collective-permute-done.35 = bf16[72,1024]{1,0:T(8,128)(2,1)S(1)} collective-permute-done((bf16[72,1024]{1,0:T(8,128)(2,1)S(1)}, bf16[72,1024]{1,0:T(8,128)(2,1)S(1)}, u32[]{:S(2)}, u32[]{:S(2)}) %collective-permute-start.35) | collective-permute-done | bytes 147488 | tf_op jit(solution)/shard_map/ppermute | solution.py:160
  273.5 3.0 %fusion = f32[144,2048]{1,0:T(8,128)S(1)} fusion(bf16[128,8,2048]{2,1,0:T(8,128)(2,1)} %all-to-all-done.2, bf16[72,1024]{1,0:T(8,128)(2,1)S(1)} %get-tuple-element.65, bf16[72,1024]{1,0:T(8,128)(2,1)S(1)} %get-tuple-element.66), kind=kOutput, calls=%fused_computation | convolution fusion | flops 604569600 | bytes 5668864 | tf_op jit(solution)/shard_map/dot_general | solution.py:28
  (107 shorter events, 23.4 us)
Async XLA Ops:
  6.1 25.3 %copy-start.16 = (s32[65,4]{0,1:T(4,128)S(1)}, s32[65,4]{0,1:T(4,128)}, u32[]{:S(2)}) copy-start(s32[65,4]{0,1:T(4,128)} %param.26) | copy-start | bytes 3124
  12.0 16.4 %collective-permute-start.3 = (bf16[288,1024]{1,0:T(8,128)(2,1)}, bf16[288,1024]{1,0:T(8,128)(2,1)S(1)}, u32[]{:S(2)}, u32[]{:S(2)}) collective-permute-start(bf16[288,1024]{1,0:T(8,128)(2,1)} %get-tuple-element.40), channel_id=1, source_target_pairs={{0,1},{1,0},{2,3},{3,2},{4,5},{5,4},{6,7},{7,6},{8,9},{9,8},{10,11... | collective-permute-start | bytes 1769480 | tf_op jit(solution)/shard_map/ppermute | solution.py:164
  13.9 27.8 %collective-permute-start.4 = (bf16[288,1024]{1,0:T(8,128)(2,1)}, bf16[288,1024]{1,0:T(8,128)(2,1)S(1)}, u32[]{:S(2)}, u32[]{:S(2)}) collective-permute-start(bf16[288,1024]{1,0:T(8,128)(2,1)} %get-tuple-element.41), channel_id=1, source_target_pairs={{0,3},{1,2},{2,1},{3,0},{4,7},{5,6},{6,5},{7,4},{8,11},{9,10},{10,... | collective-permute-start | bytes 1769480 | tf_op jit(solution)/shard_map/ppermute | solution.py:164
  16.4 27.0 %collective-permute-start.5 = (bf16[288,1024]{1,0:T(8,128)(2,1)}, bf16[288,1024]{1,0:T(8,128)(2,1)S(1)}, u32[]{:S(2)}, u32[]{:S(2)}) collective-permute-start(bf16[288,1024]{1,0:T(8,128)(2,1)} %get-tuple-element.42), channel_id=1, source_target_pairs={{0,2},{1,3},{2,0},{3,1},{4,6},{5,7},{6,4},{7,5},{8,10},{9,11},{10,... | collective-permute-start | bytes 1769480 | tf_op jit(solution)/shard_map/ppermute | solution.py:164
  17.5 27.4 %collective-permute-start = (bf16[288,1024]{1,0:T(8,128)(2,1)}, bf16[288,1024]{1,0:T(8,128)(2,1)S(1)}, u32[]{:S(2)}, u32[]{:S(2)}) collective-permute-start(bf16[288,1024]{1,0:T(8,128)(2,1)} %get-tuple-element.36), channel_id=1, source_target_pairs={{0,4},{1,5},{2,6},{3,7},{4,0},{5,1},{6,2},{7,3},{8,12},{9,13},{10,... | collective-permute-start | bytes 1769480 | tf_op jit(solution)/shard_map/ppermute | solution.py:160
  19.0 28.3 %collective-permute-start.1 = (bf16[288,1024]{1,0:T(8,128)(2,1)}, bf16[288,1024]{1,0:T(8,128)(2,1)S(1)}, u32[]{:S(2)}, u32[]{:S(2)}) collective-permute-start(bf16[288,1024]{1,0:T(8,128)(2,1)} %get-tuple-element.37), channel_id=1, source_target_pairs={{0,12},{1,13},{2,14},{3,15},{4,8},{5,9},{6,10},{7,11},{8,4},{9,5},... | collective-permute-start | bytes 1769480 | tf_op jit(solution)/shard_map/ppermute | solution.py:160
  28.4 18.9 %collective-permute-start.2 = (bf16[288,1024]{1,0:T(8,128)(2,1)}, bf16[288,1024]{1,0:T(8,128)(2,1)S(1)}, u32[]{:S(2)}, u32[]{:S(2)}) collective-permute-start(bf16[288,1024]{1,0:T(8,128)(2,1)} %get-tuple-element.38), channel_id=1, source_target_pairs={{0,8},{1,9},{2,10},{3,11},{4,12},{5,13},{6,14},{7,15},{8,0},{9,1},... | collective-permute-start | bytes 1769480 | tf_op jit(solution)/shard_map/ppermute | solution.py:160
  47.7 12.0 %copy-start.8 = (f32[2048]{0:T(1024)S(1)}, f32[2048]{0:T(1024)}, u32[]{:S(2)}) copy-start(f32[2048]{0:T(1024)} %param.22) | copy-start | bytes 24580
  47.8 6.8 %collective-permute-start.10 = (bf16[72,1024]{1,0:T(8,128)(2,1)S(1)}, bf16[72,1024]{1,0:T(8,128)(2,1)S(1)}, u32[]{:S(2)}, u32[]{:S(2)}) collective-permute-start(bf16[72,1024]{1,0:T(8,128)(2,1)S(1)} %get-tuple-element.76), channel_id=1, source_target_pairs={{0,12},{1,13},{2,14},{3,15},{4,8},{5,9},{6,10},{7,11},{8,4},{9,5},... | collective-permute-start | bytes 442376 | tf_op jit(solution)/shard_map/ppermute | solution.py:160
  50.0 8.2 %collective-permute-start.11 = (bf16[72,1024]{1,0:T(8,128)(2,1)S(1)}, bf16[72,1024]{1,0:T(8,128)(2,1)S(1)}, u32[]{:S(2)}, u32[]{:S(2)}) collective-permute-start(bf16[72,1024]{1,0:T(8,128)(2,1)S(1)} %get-tuple-element.75), channel_id=1, source_target_pairs={{0,8},{1,9},{2,10},{3,11},{4,12},{5,13},{6,14},{7,15},{8,0},{9,1},... | collective-permute-start | bytes 442376 | tf_op jit(solution)/shard_map/ppermute | solution.py:160
  50.0 8.2 %collective-permute-start.6 = (bf16[72,1024]{1,0:T(8,128)(2,1)S(1)}, bf16[72,1024]{1,0:T(8,128)(2,1)S(1)}, u32[]{:S(2)}, u32[]{:S(2)}) collective-permute-start(bf16[72,1024]{1,0:T(8,128)(2,1)S(1)} %get-tuple-element.81), channel_id=1, source_target_pairs={{0,1},{1,0},{2,3},{3,2},{4,5},{5,4},{6,7},{7,6},{8,9},{9,8},{10,11... | collective-permute-start | bytes 442376 | tf_op jit(solution)/shard_map/ppermute | solution.py:164
  50.3 7.9 %collective-permute-start.7 = (bf16[72,1024]{1,0:T(8,128)(2,1)S(1)}, bf16[72,1024]{1,0:T(8,128)(2,1)S(1)}, u32[]{:S(2)}, u32[]{:S(2)}) collective-permute-start(bf16[72,1024]{1,0:T(8,128)(2,1)S(1)} %get-tuple-element.80), channel_id=1, source_target_pairs={{0,3},{1,2},{2,1},{3,0},{4,7},{5,6},{6,5},{7,4},{8,11},{9,10},{10,... | collective-permute-start | bytes 442376 | tf_op jit(solution)/shard_map/ppermute | solution.py:164
  52.8 6.6 %collective-permute-start.8 = (bf16[72,1024]{1,0:T(8,128)(2,1)S(1)}, bf16[72,1024]{1,0:T(8,128)(2,1)S(1)}, u32[]{:S(2)}, u32[]{:S(2)}) collective-permute-start(bf16[72,1024]{1,0:T(8,128)(2,1)S(1)} %get-tuple-element.79), channel_id=1, source_target_pairs={{0,2},{1,3},{2,0},{3,1},{4,6},{5,7},{6,4},{7,5},{8,10},{9,11},{10,... | collective-permute-start | bytes 442376 | tf_op jit(solution)/shard_map/ppermute | solution.py:164
  54.6 5.1 %collective-permute-start.9 = (bf16[72,1024]{1,0:T(8,128)(2,1)S(1)}, bf16[72,1024]{1,0:T(8,128)(2,1)S(1)}, u32[]{:S(2)}, u32[]{:S(2)}) collective-permute-start(bf16[72,1024]{1,0:T(8,128)(2,1)S(1)} %get-tuple-element.77), channel_id=1, source_target_pairs={{0,4},{1,5},{2,6},{3,7},{4,0},{5,1},{6,2},{7,3},{8,12},{9,13},{10,... | collective-permute-start | bytes 442376 | tf_op jit(solution)/shard_map/ppermute | solution.py:160
  60.1 17.1 %copy-start.4 = (bf16[72,2048]{1,0:T(8,128)(2,1)}, bf16[72,2048]{1,0:T(8,128)(2,1)S(1)}, u32[]{:S(2)}) copy-start(bf16[72,2048]{1,0:T(8,128)(2,1)S(1)} %get-tuple-element.45) | copy-start | bytes 884740
  60.1 17.1 %copy-start.6 = (bf16[72,2048]{1,0:T(8,128)(2,1)}, bf16[72,2048]{1,0:T(8,128)(2,1)S(1)}, u32[]{:S(2)}) copy-start(bf16[72,2048]{1,0:T(8,128)(2,1)S(1)} %get-tuple-element.46) | copy-start | bytes 884740
  60.1 10.2 %collective-permute-start.15 = (bf16[72,1024]{1,0:T(8,128)(2,1)S(1)}, bf16[72,1024]{1,0:T(8,128)(2,1)S(1)}, u32[]{:S(2)}, u32[]{:S(2)}) collective-permute-start(bf16[72,1024]{1,0:T(8,128)(2,1)S(1)} %get-tuple-element.85), channel_id=1, source_target_pairs={{0,4},{1,5},{2,6},{3,7},{4,0},{5,1},{6,2},{7,3},{8,12},{9,13},{10,... | collective-permute-start | bytes 442376 | tf_op jit(solution)/shard_map/ppermute | solution.py:160
  62.2 8.7 %collective-permute-start.16 = (bf16[72,1024]{1,0:T(8,128)(2,1)S(1)}, bf16[72,1024]{1,0:T(8,128)(2,1)S(1)}, u32[]{:S(2)}, u32[]{:S(2)}) collective-permute-start(bf16[72,1024]{1,0:T(8,128)(2,1)S(1)} %get-tuple-element.85), channel_id=1, source_target_pairs={{0,8},{1,9},{2,10},{3,11},{4,12},{5,13},{6,14},{7,15},{8,0},{9,1},... | collective-permute-start | bytes 442376 | tf_op jit(solution)/shard_map/ppermute | solution.py:160
  66.2 6.4 %collective-permute-start.17 = (bf16[72,1024]{1,0:T(8,128)(2,1)S(1)}, bf16[72,1024]{1,0:T(8,128)(2,1)S(1)}, u32[]{:S(2)}, u32[]{:S(2)}) collective-permute-start(bf16[72,1024]{1,0:T(8,128)(2,1)S(1)} %get-tuple-element.85), channel_id=1, source_target_pairs={{0,12},{1,13},{2,14},{3,15},{4,8},{5,9},{6,10},{7,11},{8,4},{9,5},... | collective-permute-start | bytes 442376 | tf_op jit(solution)/shard_map/ppermute | solution.py:160
  66.2 6.4 %collective-permute-start.12 = (bf16[72,1024]{1,0:T(8,128)(2,1)S(1)}, bf16[72,1024]{1,0:T(8,128)(2,1)S(1)}, u32[]{:S(2)}, u32[]{:S(2)}) collective-permute-start(bf16[72,1024]{1,0:T(8,128)(2,1)S(1)} %get-tuple-element.86), channel_id=1, source_target_pairs={{0,1},{1,0},{2,3},{3,2},{4,5},{5,4},{6,7},{7,6},{8,9},{9,8},{10,11... | collective-permute-start | bytes 442376 | tf_op jit(solution)/shard_map/ppermute | solution.py:164
  66.4 9.4 %collective-permute-start.13 = (bf16[72,1024]{1,0:T(8,128)(2,1)S(1)}, bf16[72,1024]{1,0:T(8,128)(2,1)S(1)}, u32[]{:S(2)}, u32[]{:S(2)}) collective-permute-start(bf16[72,1024]{1,0:T(8,128)(2,1)S(1)} %get-tuple-element.86), channel_id=1, source_target_pairs={{0,2},{1,3},{2,0},{3,1},{4,6},{5,7},{6,4},{7,5},{8,10},{9,11},{10,... | collective-permute-start | bytes 442376 | tf_op jit(solution)/shard_map/ppermute | solution.py:164
  70.4 6.7 %collective-permute-start.14 = (bf16[72,1024]{1,0:T(8,128)(2,1)S(1)}, bf16[72,1024]{1,0:T(8,128)(2,1)S(1)}, u32[]{:S(2)}, u32[]{:S(2)}) collective-permute-start(bf16[72,1024]{1,0:T(8,128)(2,1)S(1)} %get-tuple-element.86), channel_id=1, source_target_pairs={{0,3},{1,2},{2,1},{3,0},{4,7},{5,6},{6,5},{7,4},{8,11},{9,10},{10,... | collective-permute-start | bytes 442376 | tf_op jit(solution)/shard_map/ppermute | solution.py:164
  72.6 20.9 %copy-start.9 = (bf16[4,72,1024]{2,1,0:T(8,128)(2,1)}, bf16[4,72,1024]{2,1,0:T(8,128)(2,1)S(1)}, u32[]{:S(2)}) copy-start(bf16[4,72,1024]{2,1,0:T(8,128)(2,1)S(1)} %pad_maximum_fusion.2.refs_2_.refs_4_) | copy-start | bytes 1769476
  77.2 16.3 %copy-start = (bf16[4,72,1024]{2,1,0:T(8,128)(2,1)}, bf16[4,72,1024]{2,1,0:T(8,128)(2,1)S(1)}, u32[]{:S(2)}) copy-start(bf16[4,72,1024]{2,1,0:T(8,128)(2,1)S(1)} %pad_maximum_fusion.1.refs_0_) | copy-start | bytes 1769476
  77.2 15.4 %collective-permute-start.18 = (bf16[4,72,1024]{2,1,0:T(8,128)(2,1)S(1)}, bf16[4,72,1024]{2,1,0:T(8,128)(2,1)S(1)}, u32[]{:S(2)}, u32[]{:S(2)}) collective-permute-start(bf16[4,72,1024]{2,1,0:T(8,128)(2,1)S(1)} %pad_maximum_fusion.1.refs_0_), channel_id=1, source_target_pairs={{0,4},{1,5},{2,6},{3,7},{4,0},{5,1},{6,2},{7,3},{8,12},{9,13},{10,... | collective-permute-start | bytes 1769480 | tf_op jit(solution)/shard_map/ppermute | solution.py:160
  77.3 16.2 %collective-permute-start.19 = (bf16[4,72,1024]{2,1,0:T(8,128)(2,1)S(1)}, bf16[4,72,1024]{2,1,0:T(8,128)(2,1)S(1)}, u32[]{:S(2)}, u32[]{:S(2)}) collective-permute-start(bf16[4,72,1024]{2,1,0:T(8,128)(2,1)S(1)} %pad_maximum_fusion.2.refs_2_.refs_4_), channel_id=1, source_target_pairs={{0,1},{1,0},{2,3},{3,2},{4,5},{5,4},{6,7},{7,6},{8,9},{9,8},{10,11... | collective-permute-start | bytes 1769480 | tf_op jit(solution)/shard_map/ppermute | solution.py:164
  77.5 21.4 %collective-permute-start.20 = (bf16[4,72,1024]{2,1,0:T(8,128)(2,1)S(1)}, bf16[4,72,1024]{2,1,0:T(8,128)(2,1)S(1)}, u32[]{:S(2)}, u32[]{:S(2)}) collective-permute-start(bf16[4,72,1024]{2,1,0:T(8,128)(2,1)S(1)} %pad_maximum_fusion.1.refs_0_), channel_id=1, source_target_pairs={{0,8},{1,9},{2,10},{3,11},{4,12},{5,13},{6,14},{7,15},{8,0},{9,1},... | collective-permute-start | bytes 1769480 | tf_op jit(solution)/shard_map/ppermute | solution.py:160
  82.8 18.6 %collective-permute-start.21 = (bf16[4,72,1024]{2,1,0:T(8,128)(2,1)S(1)}, bf16[4,72,1024]{2,1,0:T(8,128)(2,1)S(1)}, u32[]{:S(2)}, u32[]{:S(2)}) collective-permute-start(bf16[4,72,1024]{2,1,0:T(8,128)(2,1)S(1)} %pad_maximum_fusion.1.refs_0_), channel_id=1, source_target_pairs={{0,12},{1,13},{2,14},{3,15},{4,8},{5,9},{6,10},{7,11},{8,4},{9,5},... | collective-permute-start | bytes 1769480 | tf_op jit(solution)/shard_map/ppermute | solution.py:160
  82.8 18.6 %collective-permute-start.22 = (bf16[4,72,1024]{2,1,0:T(8,128)(2,1)S(1)}, bf16[4,72,1024]{2,1,0:T(8,128)(2,1)S(1)}, u32[]{:S(2)}, u32[]{:S(2)}) collective-permute-start(bf16[4,72,1024]{2,1,0:T(8,128)(2,1)S(1)} %pad_maximum_fusion.2.refs_2_.refs_4_), channel_id=1, source_target_pairs={{0,2},{1,3},{2,0},{3,1},{4,6},{5,7},{6,4},{7,5},{8,10},{9,11},{10,... | collective-permute-start | bytes 1769480 | tf_op jit(solution)/shard_map/ppermute | solution.py:164
  92.5 15.3 %collective-permute-start.23 = (bf16[4,72,1024]{2,1,0:T(8,128)(2,1)S(1)}, bf16[4,72,1024]{2,1,0:T(8,128)(2,1)S(1)}, u32[]{:S(2)}, u32[]{:S(2)}) collective-permute-start(bf16[4,72,1024]{2,1,0:T(8,128)(2,1)S(1)} %pad_maximum_fusion.2.refs_2_.refs_4_), channel_id=1, source_target_pairs={{0,3},{1,2},{2,1},{3,0},{4,7},{5,6},{6,5},{7,4},{8,11},{9,10},{10,... | collective-permute-start | bytes 1769480 | tf_op jit(solution)/shard_map/ppermute | solution.py:164
  98.9 8.9 %copy-start.11 = (bf16[4,72,1024]{2,1,0:T(8,128)(2,1)}, bf16[4,72,1024]{2,1,0:T(8,128)(2,1)S(1)}, u32[]{:S(2)}) copy-start(bf16[4,72,1024]{2,1,0:T(8,128)(2,1)S(1)} %collective-permute-done.20.refs_0_) | copy-start | bytes 1769476
  143.5 49.2 %all-to-all-start = ((bf16[8,128,1024]{2,1,0:T(8,128)(2,1)}), bf16[8,128,1024]{2,1,0:T(8,128)(2,1)S(1)}, u32[]{:S(2)}, u32[]{:S(2)}) async-start(bf16[8,128,1024]{2,1,0:T(8,128)(2,1)} %bitcast.84), calls=%async_computation | async-start | bytes 4194304 | tf_op jit(solution)/shard_map/all_to_all | solution.py:440
  159.4 16.3 %collective-permute-start.27 = (bf16[288,1024]{1,0:T(8,128)(2,1)S(1)}, bf16[288,1024]{1,0:T(8,128)(2,1)S(1)}, u32[]{:S(2)}, u32[]{:S(2)}) collective-permute-start(bf16[288,1024]{1,0:T(8,128)(2,1)S(1)} %get-tuple-element.59), channel_id=1, source_target_pairs={{0,1},{1,0},{2,3},{3,2},{4,5},{5,4},{6,7},{7,6},{8,9},{9,8},{10,11... | collective-permute-start | bytes 1769480 | tf_op jit(solution)/shard_map/ppermute | solution.py:164
  159.5 29.3 %collective-permute-start.28 = (bf16[288,1024]{1,0:T(8,128)(2,1)S(1)}, bf16[288,1024]{1,0:T(8,128)(2,1)S(1)}, u32[]{:S(2)}, u32[]{:S(2)}) collective-permute-start(bf16[288,1024]{1,0:T(8,128)(2,1)S(1)} %get-tuple-element.60), channel_id=1, source_target_pairs={{0,3},{1,2},{2,1},{3,0},{4,7},{5,6},{6,5},{7,4},{8,11},{9,10},{10,... | collective-permute-start | bytes 1769480 | tf_op jit(solution)/shard_map/ppermute | solution.py:164
  160.8 28.0 %collective-permute-start.29 = (bf16[288,1024]{1,0:T(8,128)(2,1)S(1)}, bf16[288,1024]{1,0:T(8,128)(2,1)S(1)}, u32[]{:S(2)}, u32[]{:S(2)}) collective-permute-start(bf16[288,1024]{1,0:T(8,128)(2,1)S(1)} %get-tuple-element.61), channel_id=1, source_target_pairs={{0,2},{1,3},{2,0},{3,1},{4,6},{5,7},{6,4},{7,5},{8,10},{9,11},{10,... | collective-permute-start | bytes 1769480 | tf_op jit(solution)/shard_map/ppermute | solution.py:164
  163.6 25.7 %collective-permute-start.24 = (bf16[288,1024]{1,0:T(8,128)(2,1)S(1)}, bf16[288,1024]{1,0:T(8,128)(2,1)S(1)}, u32[]{:S(2)}, u32[]{:S(2)}) collective-permute-start(bf16[288,1024]{1,0:T(8,128)(2,1)S(1)} %get-tuple-element.55), channel_id=1, source_target_pairs={{0,4},{1,5},{2,6},{3,7},{4,0},{5,1},{6,2},{7,3},{8,12},{9,13},{10,... | collective-permute-start | bytes 1769480 | tf_op jit(solution)/shard_map/ppermute | solution.py:160
  163.6 26.8 %collective-permute-start.25 = (bf16[288,1024]{1,0:T(8,128)(2,1)S(1)}, bf16[288,1024]{1,0:T(8,128)(2,1)S(1)}, u32[]{:S(2)}, u32[]{:S(2)}) collective-permute-start(bf16[288,1024]{1,0:T(8,128)(2,1)S(1)} %get-tuple-element.56), channel_id=1, source_target_pairs={{0,12},{1,13},{2,14},{3,15},{4,8},{5,9},{6,10},{7,11},{8,4},{9,5},... | collective-permute-start | bytes 1769480 | tf_op jit(solution)/shard_map/ppermute | solution.py:160
  175.7 16.6 %collective-permute-start.26 = (bf16[288,1024]{1,0:T(8,128)(2,1)S(1)}, bf16[288,1024]{1,0:T(8,128)(2,1)S(1)}, u32[]{:S(2)}, u32[]{:S(2)}) collective-permute-start(bf16[288,1024]{1,0:T(8,128)(2,1)S(1)} %get-tuple-element.57), channel_id=1, source_target_pairs={{0,8},{1,9},{2,10},{3,11},{4,12},{5,13},{6,14},{7,15},{8,0},{9,1},... | collective-permute-start | bytes 1769480 | tf_op jit(solution)/shard_map/ppermute | solution.py:160
  208.2 6.4 %copy-start.17 = (bf16[2048]{0:T(1024)(128)(2,1)S(1)}, bf16[2048]{0:T(1024)(128)(2,1)}, u32[]{:S(2)}) copy-start(bf16[2048]{0:T(1024)(128)(2,1)} %param.25) | copy-start | bytes 12292
  208.2 6.5 %copy-start.18 = (f32[65,4]{0,1:T(4,128)S(1)}, f32[65,4]{0,1:T(4,128)}, u32[]{:S(2)}) copy-start(f32[65,4]{0,1:T(4,128)} %param.27) | copy-start | bytes 3124
  208.2 6.7 %copy-start.7 = (bf16[72,2048]{1,0:T(8,128)(2,1)S(1)}, bf16[72,2048]{1,0:T(8,128)(2,1)}, u32[]{:S(2)}) copy-start(bf16[72,2048]{1,0:T(8,128)(2,1)} %copy-done.6) | copy-start | bytes 884740
  208.2 65.3 %all-to-all-start.2 = ((bf16[128,8,2048]{2,1,0:T(8,128)(2,1)}), bf16[128,8,2048]{2,1,0:T(8,128)(2,1)}, u32[]{:S(2)}, u32[]{:S(2)}) async-start(bf16[128,8,2048]{2,1,0:T(8,128)(2,1)} %bitcast.86), calls=%async_computation.2 | async-start | bytes 8388608 | tf_op jit(solution)/shard_map/all_to_all | solution.py:453
  215.1 51.1 %collective-permute-start.30 = (bf16[72,1024]{1,0:T(8,128)(2,1)S(1)}, bf16[72,1024]{1,0:T(8,128)(2,1)S(1)}, u32[]{:S(2)}, u32[]{:S(2)}) collective-permute-start(bf16[72,1024]{1,0:T(8,128)(2,1)S(1)} %get-tuple-element.69), channel_id=1, source_target_pairs={{0,1},{1,0},{2,3},{3,2},{4,5},{5,4},{6,7},{7,6},{8,9},{9,8},{10,11... | collective-permute-start | bytes 442376 | tf_op jit(solution)/shard_map/ppermute | solution.py:164
  216.9 51.9 %collective-permute-start.31 = (bf16[72,1024]{1,0:T(8,128)(2,1)S(1)}, bf16[72,1024]{1,0:T(8,128)(2,1)S(1)}, u32[]{:S(2)}, u32[]{:S(2)}) collective-permute-start(bf16[72,1024]{1,0:T(8,128)(2,1)S(1)} %get-tuple-element.71), channel_id=1, source_target_pairs={{0,3},{1,2},{2,1},{3,0},{4,7},{5,6},{6,5},{7,4},{8,11},{9,10},{10,... | collective-permute-start | bytes 442376 | tf_op jit(solution)/shard_map/ppermute | solution.py:164
  219.2 50.6 %collective-permute-start.32 = (bf16[72,1024]{1,0:T(8,128)(2,1)S(1)}, bf16[72,1024]{1,0:T(8,128)(2,1)S(1)}, u32[]{:S(2)}, u32[]{:S(2)}) collective-permute-start(bf16[72,1024]{1,0:T(8,128)(2,1)S(1)} %get-tuple-element.70), channel_id=1, source_target_pairs={{0,2},{1,3},{2,0},{3,1},{4,6},{5,7},{6,4},{7,5},{8,10},{9,11},{10,... | collective-permute-start | bytes 442376 | tf_op jit(solution)/shard_map/ppermute | solution.py:164
  220.1 49.8 %collective-permute-start.33 = (bf16[72,1024]{1,0:T(8,128)(2,1)S(1)}, bf16[72,1024]{1,0:T(8,128)(2,1)S(1)}, u32[]{:S(2)}, u32[]{:S(2)}) collective-permute-start(bf16[72,1024]{1,0:T(8,128)(2,1)S(1)} %get-tuple-element.72), channel_id=1, source_target_pairs={{0,4},{1,5},{2,6},{3,7},{4,0},{5,1},{6,2},{7,3},{8,12},{9,13},{10,... | collective-permute-start | bytes 442376 | tf_op jit(solution)/shard_map/ppermute | solution.py:160
  221.7 48.2 %collective-permute-start.34 = (bf16[72,1024]{1,0:T(8,128)(2,1)S(1)}, bf16[72,1024]{1,0:T(8,128)(2,1)S(1)}, u32[]{:S(2)}, u32[]{:S(2)}) collective-permute-start(bf16[72,1024]{1,0:T(8,128)(2,1)S(1)} %get-tuple-element.74), channel_id=1, source_target_pairs={{0,12},{1,13},{2,14},{3,15},{4,8},{5,9},{6,10},{7,11},{8,4},{9,5},... | collective-permute-start | bytes 442376 | tf_op jit(solution)/shard_map/ppermute | solution.py:160
  266.2 7.2 %collective-permute-start.35 = (bf16[72,1024]{1,0:T(8,128)(2,1)S(1)}, bf16[72,1024]{1,0:T(8,128)(2,1)S(1)}, u32[]{:S(2)}, u32[]{:S(2)}) collective-permute-start(bf16[72,1024]{1,0:T(8,128)(2,1)S(1)} %get-tuple-element.73), channel_id=1, source_target_pairs={{0,8},{1,9},{2,10},{3,11},{4,12},{5,13},{6,14},{7,15},{8,0},{9,1},... | collective-permute-start | bytes 442376 | tf_op jit(solution)/shard_map/ppermute | solution.py:160
  (9 other events, 30.5 us)

commit v5 on v3

--- a/solution.py
+++ b/solution.py
@@ -13,6 +13,7 @@
 ROWS = 72
 LANES = 128
 ROUTES = 4
+PIECES = 5
 NEG_FILL = -1e30
 MIB = 1 << 20
 BF = jnp.bfloat16
@@ -56,8 +57,12 @@
             out[r * span + h * part : r * span + (h + 1) * part, :] = dot(w, v).astype(BF)
     requests, entries = table.shape
     pages, page = keys.shape[0], keys.shape[1]
+    row = lax.broadcasted_iota(jnp.int32, (requests, entries), 0)
+    held = jnp.zeros((requests, entries), jnp.int32)
+    for i in range(requests):
+        held = jnp.where(row == i, lens[i], held)
     held = jnp.clip(
-        lens[...] - page * lax.broadcasted_iota(jnp.int32, (requests, entries), 1), 0, page
+        held - page * lax.broadcasted_iota(jnp.int32, (requests, entries), 1), 0, page
     )
     ids = table[...]
     lane = lax.broadcasted_iota(jnp.int32, (requests, page), 1)
@@ -110,7 +115,7 @@
     return pl.pallas_call(
         attention_kernel,
         out_shape=jax.ShapeDtypeStruct((rows, HD), BF),
-        in_specs=[whole, whole, whole, whole, pl.BlockSpec(memory_space=pl.ANY)],
+        in_specs=[pl.BlockSpec(memory_space=pltpu.SMEM), whole, whole, whole, pl.BlockSpec(memory_space=pl.ANY)],
         out_specs=whole,
         scratch_shapes=[
             pltpu.VMEM((pages, page, HD), BF),
@@ -120,7 +125,7 @@
         ],
         compiler_params=vmem(48),
         name="attention",
-    )(cache_len[:, None], page_table, prefill_qkv, decode_qkv.transpose(1, 0, 2), cache_pool)
+    )(cache_len, page_table, prefill_qkv, decode_qkv.transpose(1, 0, 2), cache_pool)
 
 
 def project_kernel(mine, blocks, weight, *outs):
@@ -167,12 +172,22 @@
     return total
 
 
+def ring_sum(parts, along):
+    half = parts[0].shape[0] // 2
+    near = along(parts[2][:half], 1)
+    far = along(parts[2][half:], 3)
+    one = jnp.concatenate([parts[1][:half], add_up([parts[1][half:], far]).astype(BF)], axis=0)
+    three = jnp.concatenate([add_up([parts[3][:half], near]).astype(BF), parts[3][half:]], axis=0)
+    return one, three
+
+
 def sum_first(parts):
     parts_a, parts_b = parts[:SIDE], parts[SIDE:]
-    got_a, got_b = [parts_a[0]], [parts_b[0]]
-    for d in (1, 3, 2):
-        got_a.append(along_x(parts_a[d], d))
-        got_b.append(along_z(parts_b[d], d))
+    one_a, three_a = ring_sum(parts_a, along_x)
+    one_b, three_b = ring_sum(parts_b, along_z)
+    one_a, three_a, one_b, three_b = lax.optimization_barrier((one_a, three_a, one_b, three_b))
+    got_a = [parts_a[0], along_x(one_a, 1), along_x(three_a, 3)]
+    got_b = [parts_b[0], along_z(one_b, 1), along_z(three_b, 3)]
     sum_a = add_up(got_a).astype(BF).reshape(SIDE, ROWS, -1)
     sum_b = add_up(got_b).astype(BF).reshape(SIDE, ROWS, -1)
     return sum_a, sum_b
@@ -196,11 +211,19 @@
     rows_a = jnp.stack([got_a[d] for d in range(SIDE)])
     rows_b = jnp.stack([got_b[d] for d in range(SIDE)])
     rows_a, rows_b = lax.optimization_barrier((rows_a, rows_b))
-    got_a, got_b = {0: rows_a}, {0: rows_b}
-    for d in (1, 3, 2):
-        got_a[d] = along_x(rows_a, d)
-        got_b[d] = along_z(rows_b, d)
-    return [got_a[d] for d in range(SIDE)], [got_b[d] for d in range(SIDE)]
+    one_a, one_b = along_x(rows_a, 1), along_z(rows_b, 1)
+    three_a, three_b = along_x(rows_a, 3), along_z(rows_b, 3)
+    half = SIDE // 2
+    return (
+        [rows_a, one_a, three_a, along_x(three_a[:half], 1), along_x(one_a[half:], 3)],
+        [rows_b, one_b, three_b, along_z(three_b[:half], 1), along_z(one_b[half:], 3)],
+    )
+
+
+def block_of(pieces, d, i):
+    if d == 2:
+        return pieces[3][i] if i < SIDE // 2 else pieces[4][i - SIDE // 2]
+    return pieces[{0: 0, 1: 1, 3: 2}[d]][i]
 
 
 def token_kernel(a0, a1, a2, a3, b0, b1, b2, b3, residual, gain, tags, stream, normed):
@@ -226,7 +249,7 @@
     hits = []
     for x in range(SIDE):
         for z in range(SIDE):
-            tags = rows_a[x][z][:, :LANES].astype(F32)
+            tags = block_of(rows_a, x, z)[:, :LANES].astype(F32)
             hit = jnp.zeros(shape, F32)
             for k in range(ROUTES):
                 named = jnp.broadcast_to(tags[TOKENS + k : TOKENS + k + 1, :], shape)
@@ -249,7 +272,7 @@
 
 
 def pick_kernel(mine, *refs):
-    rows_a, rows_b, out = refs[:SIDE], refs[SIDE : 2 * SIDE], refs[-1]
+    rows_a, rows_b, out = refs[:PIECES], refs[PIECES : 2 * PIECES], refs[-1]
     columns, _, capacity, width = out.shape
     half = width // 2
     chosen = chosen_rows(mine[0], rows_a, columns, capacity)
@@ -257,8 +280,8 @@
         for z in range(SIDE):
             block = jnp.bitwise_xor(mine[0], x * SIDE + z)
             pick = chosen[x * SIDE + z]
-            a = dot(pick, rows_a[x][z]).reshape(columns, capacity, half).astype(BF)
-            b = dot(pick, rows_b[z][x]).reshape(columns, capacity, half).astype(BF)
+            a = dot(pick, block_of(rows_a, x, z)).reshape(columns, capacity, half).astype(BF)
+            b = dot(pick, block_of(rows_b, z, x)).reshape(columns, capacity, half).astype(BF)
             for r in range(columns):
                 out[r, block, :, :half] = a[r]
                 out[r, block, :, half:] = b[r]
@@ -270,7 +293,7 @@
     return pl.pallas_call(
         pick_kernel,
         out_shape=jax.ShapeDtypeStruct((columns, SIDE * SIDE, capacity, width), BF),
-        in_specs=[pl.BlockSpec(memory_space=pltpu.SMEM)] + [whole] * (2 * SIDE),
+        in_specs=[pl.BlockSpec(memory_space=pltpu.SMEM)] + [whole] * (2 * PIECES),
         out_specs=whole,
         compiler_params=vmem(56),
         name="pick",
@@ -287,7 +310,7 @@
 
 def experts(rows, gate_up, down):
     count, width = rows.shape
-    step = 256
+    step = 512
     return pl.pallas_call(
         expert_kernel,
         grid=(count // step,),
@@ -298,7 +321,7 @@
             pl.BlockSpec(down.shape, lambda i: (0, 0, 0)),
         ],
         out_specs=pl.BlockSpec((step, width), lambda i: (i, 0)),
-        compiler_params=vmem(50),
+        compiler_params=vmem(56),
         cost_estimate=pl.CostEstimate(
             flops=6 * count * width * down.shape[1],
             bytes_accessed=2 * (2 * count * width + 3 * width * down.shape[1]),
@@ -309,15 +332,18 @@
 
 
 def shared_kernel(*refs):
-    rows_a, rows_b = refs[:SIDE], refs[SIDE : 2 * SIDE]
-    gate_up, down = refs[2 * SIDE : 2 * SIDE + 2]
-    outs, hidden = refs[2 * SIDE + 2 : -1], refs[-1]
+    rows_a, rows_b = refs[:PIECES], refs[PIECES : 2 * PIECES]
+    gate_up, down = refs[2 * PIECES : 2 * PIECES + 2]
+    outs, hidden = refs[2 * PIECES + 2 : -1], refs[-1]
     half = down.shape[1] // 2
     for x in range(SIDE):
-        a = rows_a[x][...]
-        b = jnp.concatenate(
-            [rows_b[z][x].astype(F32) for z in range(SIDE)], axis=0
-        ).astype(BF)
+        a, b = (
+            jnp.concatenate(blocks, axis=0).astype(BF)
+            for blocks in (
+                [block_of(rows_a, x, z).astype(F32) for z in range(SIDE)],
+                [block_of(rows_b, z, x).astype(F32) for z in range(SIDE)],
+            )
+        )
         gate = dot_nt(a, gate_up[0, :, :half]) + dot_nt(b, gate_up[0, :, half:])
         up = dot_nt(a, gate_up[1, :, :half]) + dot_nt(b, gate_up[1, :, half:])
         hidden[x] = (gate / (1.0 + jnp.exp(-gate)) * up).reshape(SIDE, ROWS, -1)
@@ -342,7 +368,7 @@
             transcendentals=count * down.shape[0],
         ),
         name="shared_expert",
-    )(*[a.reshape(SIDE * ROWS, half) for a in rows_a], *rows_b, gate_up, down)
+    )(*rows_a, *rows_b, gate_up, down)
 
 
 def on_device(

time: 260 us -> 249 us (0.958)
  waiting for transfers between devices: 133 us -> 118 us
  starting transfers between devices: 64.3 us -> 67.9 us
    ppermute x18 -> x21, waiting for transfers between devices: 52.1 us -> 40.9 us  [along_z(): return lax.ppermute(a, 'exp', [(i, i ^ d) for i in range(SIDE * SIDE)])]
    ppermute x18 -> x21, waiting for transfers between devices: 30.3 us -> 27 us  [along_x(): lax.ppermute(a, 'exp', [(i, i ^ d * SIDE) for i in range(SIDE * SIDE)])]
    unnamed x42 -> x48, local copies, waits for them, and re-layouts: 7.68 us -> 5.58 us
    ppermute x18 -> x21, starting transfers between devices: 25.8 us -> 27.5 us  [along_x(): lax.ppermute(a, 'exp', [(i, i ^ d * SIDE) for i in range(SIDE * SIDE)])]
    ppermute x18 -> x21, starting transfers between devices: 25.9 us -> 27.5 us  [along_z(): return lax.ppermute(a, 'exp', [(i, i ^ d) for i in range(SIDE * SIDE)])]
  transfers between devices with their start and end apart: 38 -> 44, of which waited for: 24 -> 28; matrix products, arithmetic and copies ran while one was open for 3% -> 3% of each run, Pallas kernels for 4% -> 4%
where the time goes in v5:
time: 249 us; the launch traced here: 246 us
  waiting for transfers between devices  118 us (47%)
  starting transfers between devices  67.9 us (27%)
  Pallas kernels  39.5 us (16%)
  local copies, waits for them, and re-layouts  9.86 us (4%)
  other arithmetic  6.26 us (3%)
  matrix products  3.15 us (1%)
    all_to_all x1, waiting for transfers between devices, on_device(): lax.all_to_all(answer.reshape(devices, capacity, width), ('req', 'exp'),...  50.4 us
    ppermute x21, waiting for transfers between devices, along_z(): return lax.ppermute(a, 'exp', [(i, i ^ d) for i in range(SIDE * SIDE)])  40.9 us
    ppermute x21, starting transfers between devices, along_z(): return lax.ppermute(a, 'exp', [(i, i ^ d) for i in range(SIDE * SIDE)])  27.5 us
    ppermute x21, starting transfers between devices, along_x(): lax.ppermute(a, 'exp', [(i, i ^ d * SIDE) for i in range(SIDE * SIDE)])  27.5 us
    ppermute x21, waiting for transfers between devices, along_x(): lax.ppermute(a, 'exp', [(i, i ^ d * SIDE) for i in range(SIDE * SIDE)])  27 us
    pallas_call x1, Pallas kernels, experts(): pl.pallas_call(expert_kernel, grid=(count // step,), out_shape=jax.ShapeD...  15.7 us
    pallas_call x1, Pallas kernels, shared_expert(): pl.pallas_call(shared_kernel, out_shape=[jax.ShapeDtypeStruct((SIDE * ROW...  10.8 us
    all_to_all x1, starting transfers between devices, on_device(): lax.all_to_all(answer.reshape(devices, capacity, width), ('req', 'exp'),...  7.78 us
  transfers between devices with their start and end apart: 44, of which 28 were waited for; matrix products, arithmetic and copies ran while one was open for 3% of the time, Pallas kernels for 4%

profile of v5, /device:TPU:8, one launch (start us, length us, event | category | flops | bytes accessed | tf_op | source)
XLA Modules:
  0.0 245.7 jit_solution(14766628807394394835)
XLA Ops:
  3.2 5.6 %attention.1 = bf16[1040,128]{1,0:T(8,128)(2,1)S(1)} custom-call(s32[16]{0:T(128)S(1)} %copy-done.13, s32[16,64]{1,0:T(8,128)S(1)} %copy-done.12, bf16[2,3,512,128]{3,2,1,0:T(8,128)(2,1)S(1)} %copy-done, bf16[3,16,128]{2,1,0:T(8,128)(2,1)S(1)} %bitcast.72, bf16[2,124,128,128]{3,2,1,0:T(8,128)(2,1)} %pool.1), custom_call_target="tpu_custom_call" | custom-call | tf_op jit(solution)/shard_map/attention/pallas_call | solution.py:115
  9.8 1.4 project.1
  11.2 2.0 collective-permute-start.3
  13.2 2.5 %collective-permute-start.2 = (bf16[144,1024]{1,0:T(8,128)(2,1)S(1)}, bf16[144,1024]{1,0:T(8,128)(2,1)S(1)}, u32[]{:S(2)}, u32[]{:S(2)}) collective-permute-start(bf16[144,1024]{1,0:T(8,128)(2,1)S(1)} %get-tuple-element.112), channel_id=1, source_target_pairs={{0,3},{1,2},{2,1},{3,0},{4,7},{5,6},{6,5},{7,4},{8,11},{9,10},{10,... | collective-permute-start | bytes 884744 | tf_op jit(solution)/shard_map/ppermute | solution.py:165
  15.8 1.6 collective-permute-start.1
  17.4 2.1 collective-permute-start
  20.3 2.6 %collective-permute-done.2 = bf16[144,1024]{1,0:T(8,128)(2,1)S(1)} collective-permute-done((bf16[144,1024]{1,0:T(8,128)(2,1)S(1)}, bf16[144,1024]{1,0:T(8,128)(2,1)S(1)}, u32[]{:S(2)}, u32[]{:S(2)}) %collective-permute-start.2) | collective-permute-done | bytes 294944 | tf_op jit(solution)/shard_map/ppermute | solution.py:165
  24.3 2.2 collective-permute-done
  28.6 2.1 collective-permute-start.5
  35.1 5.0 %collective-permute-done.6 = bf16[288,1024]{1,0:T(8,128)(2,1)} collective-permute-done((bf16[288,1024]{1,0:T(8,128)(2,1)S(1)}, bf16[288,1024]{1,0:T(8,128)(2,1)}, u32[]{:S(2)}, u32[]{:S(2)}) %collective-permute-start.6) | collective-permute-done | bytes 589856 | tf_op jit(solution)/shard_map/ppermute | solution.py:165
  40.1 1.9 collective-permute-done.7
  42.1 1.5 add_convert_fusion.2
  43.6 1.5 add_convert_fusion.3
  47.2 2.1 collective-permute-start.12
  49.3 1.5 collective-permute-start.13
  53.1 1.7 collective-permute-start.9
  56.0 3.5 %collective-permute-done.9.a2 = bf16[72,1024]{1,0:T(8,128)(2,1)S(1)} collective-permute-done((bf16[72,1024]{1,0:T(8,128)(2,1)S(1)}, bf16[72,1024]{1,0:T(8,128)(2,1)S(1)}, u32[]{:S(2)}, u32[]{:S(2)}) %collective-permute-start.9) | collective-permute-done | bytes 147488 | tf_op jit(solution)/shard_map/ppermute | solution.py:165
  60.3 3.2 %collective-permute-start.18 = (bf16[72,1024]{1,0:T(8,128)(2,1)S(1)}, bf16[72,1024]{1,0:T(8,128)(2,1)S(1)}, u32[]{:S(2)}, u32[]{:S(2)}) collective-permute-start(bf16[72,1024]{1,0:T(8,128)(2,1)S(1)} %get-tuple-element.117), channel_id=1, source_target_pairs={{0,8},{1,9},{2,10},{3,11},{4,12},{5,13},{6,14},{7,15},{8,0},{9,1},... | collective-permute-start | bytes 442376 | tf_op jit(solution)/shard_map/ppermute | solution.py:161
  64.6 3.2 %collective-permute-start.15 = (bf16[72,1024]{1,0:T(8,128)(2,1)S(1)}, bf16[72,1024]{1,0:T(8,128)(2,1)S(1)}, u32[]{:S(2)}, u32[]{:S(2)}) collective-permute-start(bf16[72,1024]{1,0:T(8,128)(2,1)S(1)} %get-tuple-element.118), channel_id=1, source_target_pairs={{0,2},{1,3},{2,0},{3,1},{4,6},{5,7},{6,4},{7,5},{8,10},{9,11},{10,... | collective-permute-start | bytes 442376 | tf_op jit(solution)/shard_map/ppermute | solution.py:165
  67.8 1.5 collective-permute-start.16
  69.9 2.6 %collective-permute-done.15 = bf16[72,1024]{1,0:T(8,128)(2,1)S(1)} collective-permute-done((bf16[72,1024]{1,0:T(8,128)(2,1)S(1)}, bf16[72,1024]{1,0:T(8,128)(2,1)S(1)}, u32[]{:S(2)}, u32[]{:S(2)}) %collective-permute-start.15) | collective-permute-done | bytes 147488 | tf_op jit(solution)/shard_map/ppermute | solution.py:165
  72.5 3.1 %collective-permute-done.16 = bf16[72,1024]{1,0:T(8,128)(2,1)S(1)} collective-permute-done((bf16[72,1024]{1,0:T(8,128)(2,1)S(1)}, bf16[72,1024]{1,0:T(8,128)(2,1)S(1)}, u32[]{:S(2)}, u32[]{:S(2)}) %collective-permute-start.16) | collective-permute-done | bytes 147488 | tf_op jit(solution)/shard_map/ppermute | solution.py:165
  75.7 2.3 collective-permute-start.21
  78.0 1.5 collective-permute-start.25
  79.5 10.5 %collective-permute-done.21.refs_2_ = bf16[4,72,1024]{2,1,0:T(8,128)(2,1)S(1)} collective-permute-done((bf16[4,72,1024]{2,1,0:T(8,128)(2,1)S(1)}, bf16[4,72,1024]{2,1,0:T(8,128)(2,1)S(1)}, u32[]{:S(2)}, u32[]{:S(2)}) %collective-permute-start.21) | collective-permute-done | bytes 589856 | tf_op jit(solution)/shard_map/ppermute | solution.py:161
  90.2 2.3 collective-permute-start.23
  92.7 1.7 collective-permute-start.27
  94.4 2.5 %collective-permute-done.22.refs_3_ = bf16[2,72,1024]{2,1,0:T(8,128)(2,1)S(1)} collective-permute-done((bf16[2,72,1024]{2,1,0:T(8,128)(2,1)S(1)}, bf16[2,72,1024]{2,1,0:T(8,128)(2,1)S(1)}, u32[]{:S(2)}, u32[]{:S(2)}) %collective-permute-start.22) | collective-permute-done | bytes 294944 | tf_op jit(solution)/shard_map/ppermute | solution.py:161
  99.3 1.4 collective-permute-done.27.refs_9_
  101.5 5.7 %pick.1 = bf16[8,16,8,2048]{3,2,1,0:T(8,128)(2,1)} custom-call(s32[1]{0:T(128)} %bitcast.mine, bf16[4,72,1024]{2,1,0:T(8,128)(2,1)} %copy-done.15, bf16[4,72,1024]{2,1,0:T(8,128)(2,1)} %copy-done.17, bf16[4,72,1024]{2,1,0:T(8,128)(2,1)} %copy-done.16, bf16[2,72,1024]{2,1,0:T(8,128)(2,1)} %copy-done.2, bf16[2,72,1024]{2,1,0:T(8,128)(2,1)} %copy-done.4, ...), custom_call_target="tpu_custom_call" | custom-call | tf_op jit(solution)/shard_map/pick/pallas_call | solution.py:293
  107.2 5.1 %all-to-all-start = ((bf16[8,128,2048]{2,1,0:T(8,128)(2,1)}), bf16[8,128,2048]{2,1,0:T(8,128)(2,1)}, u32[]{:S(2)}, u32[]{:S(2)}) async-start(bf16[8,128,2048]{2,1,0:T(8,128)(2,1)} %bitcast.74), calls=%async_computation | async-start | bytes 8388608 | tf_op jit(solution)/shard_map/all_to_all | solution.py:437
  112.3 10.8 %shared_expert.1 = (bf16[288,1024]{1,0:T(8,128)(2,1)S(1)}, bf16[288,1024]{1,0:T(8,128)(2,1)S(1)}, bf16[288,1024]{1,0:T(8,128)(2,1)S(1)}, bf16[288,1024]{1,0:T(8,...) custom-call(bf16[4,72,1024]{2,1,0:T(8,128)(2,1)} %copy-done.15, ...), custom_call_target="tpu_custom_call" | custom-call | flops 4982833152 | bytes 13762560 | tf_op jit(solution)/shard_map/shared_expert/pallas_call | solution.py:360
  124.0 1.5 collective-permute-start.30
  125.6 1.9 collective-permute-start.29
  128.7 3.6 %collective-permute-done.31 = bf16[144,1024]{1,0:T(8,128)(2,1)S(1)} collective-permute-done((bf16[144,1024]{1,0:T(8,128)(2,1)S(1)}, bf16[144,1024]{1,0:T(8,128)(2,1)S(1)}, u32[]{:S(2)}, u32[]{:S(2)}) %collective-permute-start.31) | collective-permute-done | bytes 294944 | tf_op jit(solution)/shard_map/ppermute | solution.py:165
  132.4 1.6 collective-permute-done.30
  134.5 2.8 %collective-permute-done.28 = bf16[144,1024]{1,0:T(8,128)(2,1)S(1)} collective-permute-done((bf16[144,1024]{1,0:T(8,128)(2,1)S(1)}, bf16[144,1024]{1,0:T(8,128)(2,1)S(1)}, u32[]{:S(2)}, u32[]{:S(2)}) %collective-permute-start.28) | collective-permute-done | bytes 294944 | tf_op jit(solution)/shard_map/ppermute | solution.py:161
  138.1 1.7 collective-permute-start.35
  140.8 10.3 %collective-permute-done.34 = bf16[288,1024]{1,0:T(8,128)(2,1)S(1)} collective-permute-done((bf16[288,1024]{1,0:T(8,128)(2,1)S(1)}, bf16[288,1024]{1,0:T(8,128)(2,1)S(1)}, u32[]{:S(2)}, u32[]{:S(2)}) %collective-permute-start.34) | collective-permute-done | bytes 589856 | tf_op jit(solution)/shard_map/ppermute | solution.py:165
  151.1 1.5 collective-permute-done.35
  155.3 1.5 collective-permute-start.37
  156.8 1.7 collective-permute-start.38
  160.2 2.6 %collective-permute-start.41 = (bf16[72,1024]{1,0:T(8,128)(2,1)S(1)}, bf16[72,1024]{1,0:T(8,128)(2,1)S(1)}, u32[]{:S(2)}, u32[]{:S(2)}) collective-permute-start(bf16[72,1024]{1,0:T(8,128)(2,1)S(1)} %get-tuple-element.91), channel_id=1, source_target_pairs={{0,8},{1,9},{2,10},{3,11},{4,12},{5,13},{6,14},{7,15},{8,0},{9,1},... | collective-permute-start | bytes 442376 | tf_op jit(solution)/shard_map/ppermute | solution.py:161
  163.9 3.3 %collective-permute-done.40 = bf16[72,1024]{1,0:T(8,128)(2,1)S(1)} collective-permute-done((bf16[72,1024]{1,0:T(8,128)(2,1)S(1)}, bf16[72,1024]{1,0:T(8,128)(2,1)S(1)}, u32[]{:S(2)}, u32[]{:S(2)}) %collective-permute-start.40) | collective-permute-done | bytes 147488 | tf_op jit(solution)/shard_map/ppermute | solution.py:161
  167.2 15.7 %experts.1 = bf16[1024,2048]{1,0:T(8,128)(2,1)} custom-call(bf16[1024,2048]{1,0:T(8,128)(2,1)} %bitcast.34.rows, bf16[1,2,704,2048]{3,2,1,0:T(8,128)(2,1)} %bitcast.87, bf16[1,704,2048]{2,1,0:T(8,128)(2,1)} %down.1), custom_call_target="tpu_custom_call" | custom-call | flops 8858370048 | bytes 17039360 | tf_op jit(solution)/shard_map/experts/pallas_call | solution.py:314
  182.9 7.8 %all-to-all-start.1 = ((bf16[128,8,2048]{2,1,0:T(8,128)(2,1)}), bf16[128,8,2048]{2,1,0:T(8,128)(2,1)}, u32[]{:S(2)}, u32[]{:S(2)}) async-start(bf16[128,8,2048]{2,1,0:T(8,128)(2,1)} %bitcast.75), calls=%async_computation.1 | async-start | bytes 8388608 | tf_op jit(solution)/shard_map/all_to_all | solution.py:448
  191.4 50.4 %all-to-all-done.1 = bf16[128,8,2048]{2,1,0:T(8,128)(2,1)} async-done(((bf16[128,8,2048]{2,1,0:T(8,128)(2,1)}), bf16[128,8,2048]{2,1,0:T(8,128)(2,1)}, u32[]{:S(2)}, u32[]{:S(2)}) %all-to-all-start.1) | async-done | bytes 4194336 | tf_op jit(solution)/shard_map/all_to_all | solution.py:448
  241.8 3.0 %fusion = f32[144,2048]{1,0:T(8,128)S(1)} fusion(bf16[128,8,2048]{2,1,0:T(8,128)(2,1)} %all-to-all-done.1, bf16[72,1024]{1,0:T(8,128)(2,1)S(1)} %get-tuple-element.87, bf16[72,1024]{1,0:T(8,128)(2,1)S(1)} %get-tuple-element.88), kind=kOutput, calls=%fused_computation | convolution fusion | flops 604569600 | bytes 5668864 | tf_op jit(solution)/shard_map/dot_general | solution.py:29
  (156 shorter events, 35.9 us)
Async XLA Ops:
  11.2 9.0 %collective-permute-start.3 = (bf16[144,1024]{1,0:T(8,128)(2,1)S(1)}, bf16[144,1024]{1,0:T(8,128)(2,1)S(1)}, u32[]{:S(2)}, u32[]{:S(2)}) collective-permute-start(bf16[144,1024]{1,0:T(8,128)(2,1)S(1)} %get-tuple-element.111), channel_id=1, source_target_pairs={{0,1},{1,0},{2,3},{3,2},{4,5},{5,4},{6,7},{7,6},{8,9},{9,8},{10,11... | collective-permute-start | bytes 884744 | tf_op jit(solution)/shard_map/ppermute | solution.py:165
  13.2 9.7 %collective-permute-start.2 = (bf16[144,1024]{1,0:T(8,128)(2,1)S(1)}, bf16[144,1024]{1,0:T(8,128)(2,1)S(1)}, u32[]{:S(2)}, u32[]{:S(2)}) collective-permute-start(bf16[144,1024]{1,0:T(8,128)(2,1)S(1)} %get-tuple-element.112), channel_id=1, source_target_pairs={{0,3},{1,2},{2,1},{3,0},{4,7},{5,6},{6,5},{7,4},{8,11},{9,10},{10,... | collective-permute-start | bytes 884744 | tf_op jit(solution)/shard_map/ppermute | solution.py:165
  15.8 8.3 %collective-permute-start.1 = (bf16[144,1024]{1,0:T(8,128)(2,1)S(1)}, bf16[144,1024]{1,0:T(8,128)(2,1)S(1)}, u32[]{:S(2)}, u32[]{:S(2)}) collective-permute-start(bf16[144,1024]{1,0:T(8,128)(2,1)S(1)} %get-tuple-element.113), channel_id=1, source_target_pairs={{0,4},{1,5},{2,6},{3,7},{4,0},{5,1},{6,2},{7,3},{8,12},{9,13},{10,... | collective-permute-start | bytes 884744 | tf_op jit(solution)/shard_map/ppermute | solution.py:161
  17.4 9.1 %collective-permute-start = (bf16[144,1024]{1,0:T(8,128)(2,1)S(1)}, bf16[144,1024]{1,0:T(8,128)(2,1)S(1)}, u32[]{:S(2)}, u32[]{:S(2)}) collective-permute-start(bf16[144,1024]{1,0:T(8,128)(2,1)S(1)} %get-tuple-element.114), channel_id=1, source_target_pairs={{0,12},{1,13},{2,14},{3,15},{4,8},{5,9},{6,10},{7,11},{8,4},{9,5},... | collective-permute-start | bytes 884744 | tf_op jit(solution)/shard_map/ppermute | solution.py:161
  26.6 13.5 %collective-permute-start.6 = (bf16[288,1024]{1,0:T(8,128)(2,1)S(1)}, bf16[288,1024]{1,0:T(8,128)(2,1)}, u32[]{:S(2)}, u32[]{:S(2)}) collective-permute-start(bf16[288,1024]{1,0:T(8,128)(2,1)S(1)} %pad_maximum_fusion.3), channel_id=1, source_target_pairs={{0,1},{1,0},{2,3},{3,2},{4,5},{5,4},{6,7},{7,6},{8,9},{9,8},{10,11... | collective-permute-start | bytes 1769480 | tf_op jit(solution)/shard_map/ppermute | solution.py:165
  27.7 14.3 %collective-permute-start.7 = (bf16[288,1024]{1,0:T(8,128)(2,1)S(1)}, bf16[288,1024]{1,0:T(8,128)(2,1)}, u32[]{:S(2)}, u32[]{:S(2)}) collective-permute-start(bf16[288,1024]{1,0:T(8,128)(2,1)S(1)} %pad_maximum_fusion.4), channel_id=1, source_target_pairs={{0,3},{1,2},{2,1},{3,0},{4,7},{5,6},{6,5},{7,4},{8,11},{9,10},{10,... | collective-permute-start | bytes 1769480 | tf_op jit(solution)/shard_map/ppermute | solution.py:165
  28.6 15.0 %collective-permute-start.4 = (bf16[288,1024]{1,0:T(8,128)(2,1)S(1)}, bf16[288,1024]{1,0:T(8,128)(2,1)}, u32[]{:S(2)}, u32[]{:S(2)}) collective-permute-start(bf16[288,1024]{1,0:T(8,128)(2,1)S(1)} %pad_maximum_fusion.1), channel_id=1, source_target_pairs={{0,4},{1,5},{2,6},{3,7},{4,0},{5,1},{6,2},{7,3},{8,12},{9,13},{10,... | collective-permute-start | bytes 1769480 | tf_op jit(solution)/shard_map/ppermute | solution.py:161
  28.6 15.0 %collective-permute-start.5 = (bf16[288,1024]{1,0:T(8,128)(2,1)S(1)}, bf16[288,1024]{1,0:T(8,128)(2,1)}, u32[]{:S(2)}, u32[]{:S(2)}) collective-permute-start(bf16[288,1024]{1,0:T(8,128)(2,1)S(1)} %pad_maximum_fusion.2), channel_id=1, source_target_pairs={{0,12},{1,13},{2,14},{3,15},{4,8},{5,9},{6,10},{7,11},{8,4},{9,5},... | collective-permute-start | bytes 1769480 | tf_op jit(solution)/shard_map/ppermute | solution.py:161
  45.2 14.2 %copy-start.11 = (f32[2048]{0:T(1024)S(1)}, f32[2048]{0:T(1024)}, u32[]{:S(2)}) copy-start(f32[2048]{0:T(1024)} %param.22) | copy-start | bytes 24580
  45.3 7.8 %collective-permute-start.10 = (bf16[72,1024]{1,0:T(8,128)(2,1)S(1)}, bf16[72,1024]{1,0:T(8,128)(2,1)S(1)}, u32[]{:S(2)}, u32[]{:S(2)}) collective-permute-start(bf16[72,1024]{1,0:T(8,128)(2,1)S(1)} %get-tuple-element.107), channel_id=1, source_target_pairs={{0,2},{1,3},{2,0},{3,1},{4,6},{5,7},{6,4},{7,5},{8,10},{9,11},{10,... | collective-permute-start | bytes 442376 | tf_op jit(solution)/shard_map/ppermute | solution.py:165
  46.6 8.2 %collective-permute-start.11 = (bf16[72,1024]{1,0:T(8,128)(2,1)S(1)}, bf16[72,1024]{1,0:T(8,128)(2,1)S(1)}, u32[]{:S(2)}, u32[]{:S(2)}) collective-permute-start(bf16[72,1024]{1,0:T(8,128)(2,1)S(1)} %get-tuple-element.105), channel_id=1, source_target_pairs={{0,4},{1,5},{2,6},{3,7},{4,0},{5,1},{6,2},{7,3},{8,12},{9,13},{10,... | collective-permute-start | bytes 442376 | tf_op jit(solution)/shard_map/ppermute | solution.py:161
  47.2 7.6 %collective-permute-start.12 = (bf16[72,1024]{1,0:T(8,128)(2,1)S(1)}, bf16[72,1024]{1,0:T(8,128)(2,1)S(1)}, u32[]{:S(2)}, u32[]{:S(2)}) collective-permute-start(bf16[72,1024]{1,0:T(8,128)(2,1)S(1)} %get-tuple-element.104), channel_id=1, source_target_pairs={{0,12},{1,13},{2,14},{3,15},{4,8},{5,9},{6,10},{7,11},{8,4},{9,5},... | collective-permute-start | bytes 442376 | tf_op jit(solution)/shard_map/ppermute | solution.py:161
  49.3 6.6 %collective-permute-start.13 = (bf16[72,1024]{1,0:T(8,128)(2,1)S(1)}, bf16[72,1024]{1,0:T(8,128)(2,1)S(1)}, u32[]{:S(2)}, u32[]{:S(2)}) collective-permute-start(bf16[72,1024]{1,0:T(8,128)(2,1)S(1)} %get-tuple-element.103), channel_id=1, source_target_pairs={{0,8},{1,9},{2,10},{3,11},{4,12},{5,13},{6,14},{7,15},{8,0},{9,1},... | collective-permute-start | bytes 442376 | tf_op jit(solution)/shard_map/ppermute | solution.py:161
  50.8 5.2 %collective-permute-start.8 = (bf16[72,1024]{1,0:T(8,128)(2,1)S(1)}, bf16[72,1024]{1,0:T(8,128)(2,1)S(1)}, u32[]{:S(2)}, u32[]{:S(2)}) collective-permute-start(bf16[72,1024]{1,0:T(8,128)(2,1)S(1)} %get-tuple-element.109), channel_id=1, source_target_pairs={{0,1},{1,0},{2,3},{3,2},{4,5},{5,4},{6,7},{7,6},{8,9},{9,8},{10,11... | collective-permute-start | bytes 442376 | tf_op jit(solution)/shard_map/ppermute | solution.py:165
  53.1 6.4 %collective-permute-start.9 = (bf16[72,1024]{1,0:T(8,128)(2,1)S(1)}, bf16[72,1024]{1,0:T(8,128)(2,1)S(1)}, u32[]{:S(2)}, u32[]{:S(2)}) collective-permute-start(bf16[72,1024]{1,0:T(8,128)(2,1)S(1)} %get-tuple-element.108), channel_id=1, source_target_pairs={{0,3},{1,2},{2,1},{3,0},{4,7},{5,6},{6,5},{7,4},{8,11},{9,10},{10,... | collective-permute-start | bytes 442376 | tf_op jit(solution)/shard_map/ppermute | solution.py:165
  59.9 8.0 %collective-permute-start.17 = (bf16[72,1024]{1,0:T(8,128)(2,1)S(1)}, bf16[72,1024]{1,0:T(8,128)(2,1)S(1)}, u32[]{:S(2)}, u32[]{:S(2)}) collective-permute-start(bf16[72,1024]{1,0:T(8,128)(2,1)S(1)} %get-tuple-element.117), channel_id=1, source_target_pairs={{0,4},{1,5},{2,6},{3,7},{4,0},{5,1},{6,2},{7,3},{8,12},{9,13},{10,... | collective-permute-start | bytes 442376 | tf_op jit(solution)/shard_map/ppermute | solution.py:161
  60.3 9.0 %collective-permute-start.18 = (bf16[72,1024]{1,0:T(8,128)(2,1)S(1)}, bf16[72,1024]{1,0:T(8,128)(2,1)S(1)}, u32[]{:S(2)}, u32[]{:S(2)}) collective-permute-start(bf16[72,1024]{1,0:T(8,128)(2,1)S(1)} %get-tuple-element.117), channel_id=1, source_target_pairs={{0,8},{1,9},{2,10},{3,11},{4,12},{5,13},{6,14},{7,15},{8,0},{9,1},... | collective-permute-start | bytes 442376 | tf_op jit(solution)/shard_map/ppermute | solution.py:161
  63.5 6.4 %collective-permute-start.19 = (bf16[72,1024]{1,0:T(8,128)(2,1)S(1)}, bf16[72,1024]{1,0:T(8,128)(2,1)S(1)}, u32[]{:S(2)}, u32[]{:S(2)}) collective-permute-start(bf16[72,1024]{1,0:T(8,128)(2,1)S(1)} %get-tuple-element.117), channel_id=1, source_target_pairs={{0,12},{1,13},{2,14},{3,15},{4,8},{5,9},{6,10},{7,11},{8,4},{9,5},... | collective-permute-start | bytes 442376 | tf_op jit(solution)/shard_map/ppermute | solution.py:161
  64.6 5.3 %collective-permute-start.14 = (bf16[72,1024]{1,0:T(8,128)(2,1)S(1)}, bf16[72,1024]{1,0:T(8,128)(2,1)S(1)}, u32[]{:S(2)}, u32[]{:S(2)}) collective-permute-start(bf16[72,1024]{1,0:T(8,128)(2,1)S(1)} %get-tuple-element.118), channel_id=1, source_target_pairs={{0,1},{1,0},{2,3},{3,2},{4,5},{5,4},{6,7},{7,6},{8,9},{9,8},{10,11... | collective-permute-start | bytes 442376 | tf_op jit(solution)/shard_map/ppermute | solution.py:165
  64.6 7.9 %collective-permute-start.15 = (bf16[72,1024]{1,0:T(8,128)(2,1)S(1)}, bf16[72,1024]{1,0:T(8,128)(2,1)S(1)}, u32[]{:S(2)}, u32[]{:S(2)}) collective-permute-start(bf16[72,1024]{1,0:T(8,128)(2,1)S(1)} %get-tuple-element.118), channel_id=1, source_target_pairs={{0,2},{1,3},{2,0},{3,1},{4,6},{5,7},{6,4},{7,5},{8,10},{9,11},{10,... | collective-permute-start | bytes 442376 | tf_op jit(solution)/shard_map/ppermute | solution.py:165
  67.8 7.8 %collective-permute-start.16 = (bf16[72,1024]{1,0:T(8,128)(2,1)S(1)}, bf16[72,1024]{1,0:T(8,128)(2,1)S(1)}, u32[]{:S(2)}, u32[]{:S(2)}) collective-permute-start(bf16[72,1024]{1,0:T(8,128)(2,1)S(1)} %get-tuple-element.118), channel_id=1, source_target_pairs={{0,3},{1,2},{2,1},{3,0},{4,7},{5,6},{6,5},{7,4},{8,11},{9,10},{10,... | collective-permute-start | bytes 442376 | tf_op jit(solution)/shard_map/ppermute | solution.py:165
  69.9 20.3 %copy-start.14 = (bf16[4,72,1024]{2,1,0:T(8,128)(2,1)}, bf16[4,72,1024]{2,1,0:T(8,128)(2,1)S(1)}, u32[]{:S(2)}) copy-start(bf16[4,72,1024]{2,1,0:T(8,128)(2,1)S(1)} %pad_maximum_fusion.6.refs_5_) | copy-start | bytes 1769476
  75.7 17.0 %copy-start.15 = (bf16[4,72,1024]{2,1,0:T(8,128)(2,1)}, bf16[4,72,1024]{2,1,0:T(8,128)(2,1)S(1)}, u32[]{:S(2)}) copy-start(bf16[4,72,1024]{2,1,0:T(8,128)(2,1)S(1)} %pad_maximum_fusion.5.refs_0_) | copy-start | bytes 1769476
  75.7 14.3 %collective-permute-start.21 = (bf16[4,72,1024]{2,1,0:T(8,128)(2,1)S(1)}, bf16[4,72,1024]{2,1,0:T(8,128)(2,1)S(1)}, u32[]{:S(2)}, u32[]{:S(2)}) collective-permute-start(bf16[4,72,1024]{2,1,0:T(8,128)(2,1)S(1)} %pad_maximum_fusion.5.refs_0_), channel_id=1, source_target_pairs={{0,12},{1,13},{2,14},{3,15},{4,8},{5,9},{6,10},{7,11},{8,4},{9,5},... | collective-permute-start | bytes 1769480 | tf_op jit(solution)/shard_map/ppermute | solution.py:161
  78.0 12.2 %collective-permute-start.20 = (bf16[4,72,1024]{2,1,0:T(8,128)(2,1)S(1)}, bf16[4,72,1024]{2,1,0:T(8,128)(2,1)S(1)}, u32[]{:S(2)}, u32[]{:S(2)}) collective-permute-start(bf16[4,72,1024]{2,1,0:T(8,128)(2,1)S(1)} %pad_maximum_fusion.5.refs_0_), channel_id=1, source_target_pairs={{0,4},{1,5},{2,6},{3,7},{4,0},{5,1},{6,2},{7,3},{8,12},{9,13},{10,... | collective-permute-start | bytes 1769480 | tf_op jit(solution)/shard_map/ppermute | solution.py:161
  78.0 14.5 %collective-permute-start.25 = (bf16[4,72,1024]{2,1,0:T(8,128)(2,1)S(1)}, bf16[4,72,1024]{2,1,0:T(8,128)(2,1)S(1)}, u32[]{:S(2)}, u32[]{:S(2)}) collective-permute-start(bf16[4,72,1024]{2,1,0:T(8,128)(2,1)S(1)} %pad_maximum_fusion.6.refs_5_), channel_id=1, source_target_pairs={{0,3},{1,2},{2,1},{3,0},{4,7},{5,6},{6,5},{7,4},{8,11},{9,10},{10,... | collective-permute-start | bytes 1769480 | tf_op jit(solution)/shard_map/ppermute | solution.py:165
  79.5 13.1 %collective-permute-start.24 = (bf16[4,72,1024]{2,1,0:T(8,128)(2,1)S(1)}, bf16[4,72,1024]{2,1,0:T(8,128)(2,1)S(1)}, u32[]{:S(2)}, u32[]{:S(2)}) collective-permute-start(bf16[4,72,1024]{2,1,0:T(8,128)(2,1)S(1)} %pad_maximum_fusion.6.refs_5_), channel_id=1, source_target_pairs={{0,1},{1,0},{2,3},{3,2},{4,5},{5,4},{6,7},{7,6},{8,9},{9,8},{10,11... | collective-permute-start | bytes 1769480 | tf_op jit(solution)/shard_map/ppermute | solution.py:165
  90.1 6.8 %collective-permute-start.22 = (bf16[2,72,1024]{2,1,0:T(8,128)(2,1)S(1)}, bf16[2,72,1024]{2,1,0:T(8,128)(2,1)S(1)}, u32[]{:S(2)}, u32[]{:S(2)}) collective-permute-start(bf16[2,72,1024]{2,1,0:T(8,128)(2,1)S(1)} %slice.197), channel_id=1, source_target_pairs={{0,4},{1,5},{2,6},{3,7},{4,0},{5,1},{6,2},{7,3},{8,12},{9,13},{10,... | collective-permute-start | bytes 884744 | tf_op jit(solution)/shard_map/ppermute | solution.py:161
  90.2 10.5 %copy-start.17 = (bf16[4,72,1024]{2,1,0:T(8,128)(2,1)}, bf16[4,72,1024]{2,1,0:T(8,128)(2,1)S(1)}, u32[]{:S(2)}) copy-start(bf16[4,72,1024]{2,1,0:T(8,128)(2,1)S(1)} %collective-permute-done.20.refs_1_) | copy-start | bytes 1769476
  90.2 8.0 %collective-permute-start.23 = (bf16[2,72,1024]{2,1,0:T(8,128)(2,1)S(1)}, bf16[2,72,1024]{2,1,0:T(8,128)(2,1)S(1)}, u32[]{:S(2)}, u32[]{:S(2)}) collective-permute-start(bf16[2,72,1024]{2,1,0:T(8,128)(2,1)S(1)} %slice.198), channel_id=1, source_target_pairs={{0,12},{1,13},{2,14},{3,15},{4,8},{5,9},{6,10},{7,11},{8,4},{9,5},... | collective-permute-start | bytes 884744 | tf_op jit(solution)/shard_map/ppermute | solution.py:161
  92.5 6.8 %collective-permute-start.26 = (bf16[2,72,1024]{2,1,0:T(8,128)(2,1)S(1)}, bf16[2,72,1024]{2,1,0:T(8,128)(2,1)S(1)}, u32[]{:S(2)}, u32[]{:S(2)}) collective-permute-start(bf16[2,72,1024]{2,1,0:T(8,128)(2,1)S(1)} %slice.199), channel_id=1, source_target_pairs={{0,1},{1,0},{2,3},{3,2},{4,5},{5,4},{6,7},{7,6},{8,9},{9,8},{10,11... | collective-permute-start | bytes 884744 | tf_op jit(solution)/shard_map/ppermute | solution.py:165
  92.7 8.0 %collective-permute-start.27 = (bf16[2,72,1024]{2,1,0:T(8,128)(2,1)S(1)}, bf16[2,72,1024]{2,1,0:T(8,128)(2,1)S(1)}, u32[]{:S(2)}, u32[]{:S(2)}) collective-permute-start(bf16[2,72,1024]{2,1,0:T(8,128)(2,1)S(1)} %slice.200), channel_id=1, source_target_pairs={{0,3},{1,2},{2,1},{3,0},{4,7},{5,6},{6,5},{7,4},{8,11},{9,10},{10,... | collective-permute-start | bytes 884744 | tf_op jit(solution)/shard_map/ppermute | solution.py:165
  107.2 60.0 %all-to-all-start = ((bf16[8,128,2048]{2,1,0:T(8,128)(2,1)}), bf16[8,128,2048]{2,1,0:T(8,128)(2,1)}, u32[]{:S(2)}, u32[]{:S(2)}) async-start(bf16[8,128,2048]{2,1,0:T(8,128)(2,1)} %bitcast.74), calls=%async_computation | async-start | bytes 8388608 | tf_op jit(solution)/shard_map/all_to_all | solution.py:437
  123.1 9.1 %collective-permute-start.31 = (bf16[144,1024]{1,0:T(8,128)(2,1)S(1)}, bf16[144,1024]{1,0:T(8,128)(2,1)S(1)}, u32[]{:S(2)}, u32[]{:S(2)}) collective-permute-start(bf16[144,1024]{1,0:T(8,128)(2,1)S(1)} %get-tuple-element.99), channel_id=1, source_target_pairs={{0,1},{1,0},{2,3},{3,2},{4,5},{5,4},{6,7},{7,6},{8,9},{9,8},{10,11... | collective-permute-start | bytes 884744 | tf_op jit(solution)/shard_map/ppermute | solution.py:165
  124.0 10.0 %collective-permute-start.30 = (bf16[144,1024]{1,0:T(8,128)(2,1)S(1)}, bf16[144,1024]{1,0:T(8,128)(2,1)S(1)}, u32[]{:S(2)}, u32[]{:S(2)}) collective-permute-start(bf16[144,1024]{1,0:T(8,128)(2,1)S(1)} %get-tuple-element.100), channel_id=1, source_target_pairs={{0,3},{1,2},{2,1},{3,0},{4,7},{5,6},{6,5},{7,4},{8,11},{9,10},{10,... | collective-permute-start | bytes 884744 | tf_op jit(solution)/shard_map/ppermute | solution.py:165
  125.6 8.6 %collective-permute-start.29 = (bf16[144,1024]{1,0:T(8,128)(2,1)S(1)}, bf16[144,1024]{1,0:T(8,128)(2,1)S(1)}, u32[]{:S(2)}, u32[]{:S(2)}) collective-permute-start(bf16[144,1024]{1,0:T(8,128)(2,1)S(1)} %get-tuple-element.101), channel_id=1, source_target_pairs={{0,4},{1,5},{2,6},{3,7},{4,0},{5,1},{6,2},{7,3},{8,12},{9,13},{10,... | collective-permute-start | bytes 884744 | tf_op jit(solution)/shard_map/ppermute | solution.py:161
  127.5 9.7 %collective-permute-start.28 = (bf16[144,1024]{1,0:T(8,128)(2,1)S(1)}, bf16[144,1024]{1,0:T(8,128)(2,1)S(1)}, u32[]{:S(2)}, u32[]{:S(2)}) collective-permute-start(bf16[144,1024]{1,0:T(8,128)(2,1)S(1)} %get-tuple-element.102), channel_id=1, source_target_pairs={{0,12},{1,13},{2,14},{3,15},{4,8},{5,9},{6,10},{7,11},{8,4},{9,5},... | collective-permute-start | bytes 884744 | tf_op jit(solution)/shard_map/ppermute | solution.py:161
  137.4 13.7 %collective-permute-start.34 = (bf16[288,1024]{1,0:T(8,128)(2,1)S(1)}, bf16[288,1024]{1,0:T(8,128)(2,1)S(1)}, u32[]{:S(2)}, u32[]{:S(2)}) collective-permute-start(bf16[288,1024]{1,0:T(8,128)(2,1)S(1)} %pad_maximum_fusion.9), channel_id=1, source_target_pairs={{0,1},{1,0},{2,3},{3,2},{4,5},{5,4},{6,7},{7,6},{8,9},{9,8},{10,11... | collective-permute-start | bytes 1769480 | tf_op jit(solution)/shard_map/ppermute | solution.py:165
  138.1 14.6 %collective-permute-start.35 = (bf16[288,1024]{1,0:T(8,128)(2,1)S(1)}, bf16[288,1024]{1,0:T(8,128)(2,1)S(1)}, u32[]{:S(2)}, u32[]{:S(2)}) collective-permute-start(bf16[288,1024]{1,0:T(8,128)(2,1)S(1)} %pad_maximum_fusion.10), channel_id=1, source_target_pairs={{0,3},{1,2},{2,1},{3,0},{4,7},{5,6},{6,5},{7,4},{8,11},{9,10},{10,... | collective-permute-start | bytes 1769480 | tf_op jit(solution)/shard_map/ppermute | solution.py:165
  139.8 13.2 %collective-permute-start.32 = (bf16[288,1024]{1,0:T(8,128)(2,1)S(1)}, bf16[288,1024]{1,0:T(8,128)(2,1)S(1)}, u32[]{:S(2)}, u32[]{:S(2)}) collective-permute-start(bf16[288,1024]{1,0:T(8,128)(2,1)S(1)} %pad_maximum_fusion.7), channel_id=1, source_target_pairs={{0,4},{1,5},{2,6},{3,7},{4,0},{5,1},{6,2},{7,3},{8,12},{9,13},{10,... | collective-permute-start | bytes 1769480 | tf_op jit(solution)/shard_map/ppermute | solution.py:161
  139.8 14.3 %collective-permute-start.33 = (bf16[288,1024]{1,0:T(8,128)(2,1)S(1)}, bf16[288,1024]{1,0:T(8,128)(2,1)S(1)}, u32[]{:S(2)}, u32[]{:S(2)}) collective-permute-start(bf16[288,1024]{1,0:T(8,128)(2,1)S(1)} %pad_maximum_fusion.8), channel_id=1, source_target_pairs={{0,12},{1,13},{2,14},{3,15},{4,8},{5,9},{6,10},{7,11},{8,4},{9,5},... | collective-permute-start | bytes 1769480 | tf_op jit(solution)/shard_map/ppermute | solution.py:161
  154.4 5.8 %collective-permute-start.36 = (bf16[72,1024]{1,0:T(8,128)(2,1)S(1)}, bf16[72,1024]{1,0:T(8,128)(2,1)S(1)}, u32[]{:S(2)}, u32[]{:S(2)}) collective-permute-start(bf16[72,1024]{1,0:T(8,128)(2,1)S(1)} %get-tuple-element.97), channel_id=1, source_target_pairs={{0,1},{1,0},{2,3},{3,2},{4,5},{5,4},{6,7},{7,6},{8,9},{9,8},{10,11... | collective-permute-start | bytes 442376 | tf_op jit(solution)/shard_map/ppermute | solution.py:165
  155.3 7.5 %collective-permute-start.37 = (bf16[72,1024]{1,0:T(8,128)(2,1)S(1)}, bf16[72,1024]{1,0:T(8,128)(2,1)S(1)}, u32[]{:S(2)}, u32[]{:S(2)}) collective-permute-start(bf16[72,1024]{1,0:T(8,128)(2,1)S(1)} %get-tuple-element.96), channel_id=1, source_target_pairs={{0,3},{1,2},{2,1},{3,0},{4,7},{5,6},{6,5},{7,4},{8,11},{9,10},{10,... | collective-permute-start | bytes 442376 | tf_op jit(solution)/shard_map/ppermute | solution.py:165
  156.8 6.6 %collective-permute-start.38 = (bf16[72,1024]{1,0:T(8,128)(2,1)S(1)}, bf16[72,1024]{1,0:T(8,128)(2,1)S(1)}, u32[]{:S(2)}, u32[]{:S(2)}) collective-permute-start(bf16[72,1024]{1,0:T(8,128)(2,1)S(1)} %get-tuple-element.95), channel_id=1, source_target_pairs={{0,2},{1,3},{2,0},{3,1},{4,6},{5,7},{6,4},{7,5},{8,10},{9,11},{10,... | collective-permute-start | bytes 442376 | tf_op jit(solution)/shard_map/ppermute | solution.py:165
  158.6 5.2 %collective-permute-start.39 = (bf16[72,1024]{1,0:T(8,128)(2,1)S(1)}, bf16[72,1024]{1,0:T(8,128)(2,1)S(1)}, u32[]{:S(2)}, u32[]{:S(2)}) collective-permute-start(bf16[72,1024]{1,0:T(8,128)(2,1)S(1)} %get-tuple-element.93), channel_id=1, source_target_pairs={{0,4},{1,5},{2,6},{3,7},{4,0},{5,1},{6,2},{7,3},{8,12},{9,13},{10,... | collective-permute-start | bytes 442376 | tf_op jit(solution)/shard_map/ppermute | solution.py:161
  159.3 7.9 %collective-permute-start.40 = (bf16[72,1024]{1,0:T(8,128)(2,1)S(1)}, bf16[72,1024]{1,0:T(8,128)(2,1)S(1)}, u32[]{:S(2)}, u32[]{:S(2)}) collective-permute-start(bf16[72,1024]{1,0:T(8,128)(2,1)S(1)} %get-tuple-element.92), channel_id=1, source_target_pairs={{0,12},{1,13},{2,14},{3,15},{4,8},{5,9},{6,10},{7,11},{8,4},{9,5},... | collective-permute-start | bytes 442376 | tf_op jit(solution)/shard_map/ppermute | solution.py:161
  160.2 6.9 %collective-permute-start.41 = (bf16[72,1024]{1,0:T(8,128)(2,1)S(1)}, bf16[72,1024]{1,0:T(8,128)(2,1)S(1)}, u32[]{:S(2)}, u32[]{:S(2)}) collective-permute-start(bf16[72,1024]{1,0:T(8,128)(2,1)S(1)} %get-tuple-element.91), channel_id=1, source_target_pairs={{0,8},{1,9},{2,10},{3,11},{4,12},{5,13},{6,14},{7,15},{8,0},{9,1},... | collective-permute-start | bytes 442376 | tf_op jit(solution)/shard_map/ppermute | solution.py:161
  182.9 58.9 %all-to-all-start.1 = ((bf16[128,8,2048]{2,1,0:T(8,128)(2,1)}), bf16[128,8,2048]{2,1,0:T(8,128)(2,1)}, u32[]{:S(2)}, u32[]{:S(2)}) async-start(bf16[128,8,2048]{2,1,0:T(8,128)(2,1)} %bitcast.75), calls=%async_computation.1 | async-start | bytes 8388608 | tf_op jit(solution)/shard_map/all_to_all | solution.py:448
  (19 other events, 74.0 us)

commit v6 on v5

--- a/solution.py
+++ b/solution.py
@@ -33,13 +33,20 @@
     return lax.dot_general(a, b, NT, preferred_element_type=F32)
 
 
-def attention_kernel(lens, table, pre, dec, pool, out, keys, values, scores, sems):
+def attention_kernel(mine, *refs):
+    given, outs, held_in = refs[:6], refs[6 : 6 + 2 * SIDE], refs[6 + 2 * SIDE : 13 + 2 * SIDE]
+    scores, mixed_rows, blocks, made, sems = refs[13 + 2 * SIDE :]
     scale = HD ** (-0.5)
+    pool = given[5]
+    sources = [*given[:5], pool.at[0], pool.at[1]]
     copies = [
-        pltpu.make_async_copy(pool.at[i], buf, sems.at[i]) for i, buf in enumerate((keys, values))
+        pltpu.make_async_copy(source, buf, sems.at[i])
+        for i, (source, buf) in enumerate(zip(sources, held_in))
     ]
     for c in copies:
         c.start()
+    pre, lens, table, dec, weight, keys, values = held_in
+    copies[0].wait()
     spans, _, span, _ = pre.shape
     part = span // 2
     for r in range(spans):
@@ -48,21 +55,24 @@
             q = pre[r, 0, h * part : (h + 1) * part, :]
             k = pre[r, 1, :width, :]
             v = pre[r, 2, :width, :]
-            s = lax.dot_general(q, k, NT, preferred_element_type=F32) * scale
+            s = dot_nt(q, k) * scale
             row = lax.broadcasted_iota(jnp.int32, s.shape, 0) + h * part
             col = lax.broadcasted_iota(jnp.int32, s.shape, 1)
             s = jnp.where(col <= row, s, NEG_FILL)
             p = jnp.exp(s - jnp.max(s, axis=-1, keepdims=True))
             w = (p / jnp.sum(p, axis=-1, keepdims=True)).astype(BF)
-            out[r * span + h * part : r * span + (h + 1) * part, :] = dot(w, v).astype(BF)
+            at = r * span + h * part
+            mixed_rows[at : at + part, :] = dot(w, v).astype(BF).astype(F32)
+    for c in copies[1:5]:
+        c.wait()
     requests, entries = table.shape
     pages, page = keys.shape[0], keys.shape[1]
-    row = lax.broadcasted_iota(jnp.int32, (requests, entries), 0)
-    held = jnp.zeros((requests, entries), jnp.int32)
-    for i in range(requests):
-        held = jnp.where(row == i, lens[i], held)
+    square = (requests, requests)
+    diagonal = lax.broadcasted_iota(jnp.int32, square, 0) == lax.broadcasted_iota(jnp.int32, square, 1)
+    lengths = jnp.where(diagonal, jnp.broadcast_to(lens[...], square), 0).astype(F32)
+    lengths = jnp.sum(lengths, axis=1, keepdims=True).astype(jnp.int32)
     held = jnp.clip(
-        held - page * lax.broadcasted_iota(jnp.int32, (requests, entries), 1), 0, page
+        lengths - page * lax.broadcasted_iota(jnp.int32, (requests, entries), 1), 0, page
     )
     ids = table[...]
     lane = lax.broadcasted_iota(jnp.int32, (requests, page), 1)
@@ -73,11 +83,11 @@
     own = jnp.sum(q.astype(F32) * dec[1].astype(F32), axis=-1, keepdims=True) * scale
     group = 4
     wide = group * page
-    copies[0].wait()
+    copies[5].wait()
     top = jnp.full((requests, wide), NEG_FILL, F32)
     for c in range(pages // group):
         k = keys[c * group : (c + 1) * group].reshape(wide, HD)
-        s = lax.dot_general(q, k, NT, preferred_element_type=F32) * scale
+        s = dot_nt(q, k) * scale
         s = jnp.concatenate(
             [
                 jnp.where(
@@ -99,62 +109,67 @@
         total = total + p
     own = jnp.exp(own - top)
     total = jnp.sum(total, axis=-1, keepdims=True) + own
-    copies[1].wait()
+    copies[6].wait()
     mixed = (own / total).astype(BF).astype(F32) * dec[2].astype(F32)
     for c in range(pages // group):
         w = (scores[:, c * wide : (c + 1) * wide] / total).astype(BF)
         mixed = mixed + dot(w, values[c * group : (c + 1) * group].reshape(wide, HD))
-    out[spans * span : spans * span + requests, :] = mixed.astype(BF)
-
-
-def attention(prefill_qkv, decode_qkv, cache_pool, page_table, cache_len):
+    mixed_rows[spans * span : spans * span + requests, :] = mixed.astype(BF).astype(F32)
+
+    real = lax.broadcasted_iota(jnp.int32, (ROWS, HD), 0) < TOKENS
+    for i in range(SIDE * SIDE):
+        blocks[i] = jnp.where(real, mixed_rows[i * TOKENS : i * TOKENS + ROWS, :], 0.0)
+    half = weight.shape[1] // 2
+    at_x, at_z = mine[0] // SIDE, mine[0] % SIDE
+
+    def rows(picked):
+        return jnp.concatenate([blocks[i] for i in picked], axis=0).astype(BF)
+
+    xs = [jnp.bitwise_xor(at_x, d) * SIDE for d in range(SIDE)]
+    zs = [jnp.bitwise_xor(at_z, d) for d in range(SIDE)]
+    leaving = [
+        pltpu.make_async_copy(made.at[i], out, sems.at[len(copies) + i]) for i, out in enumerate(outs)
+    ]
+    for d in (2, 1, 3, 0):
+        made[d] = dot(rows([xs[d] + z for z in zs]), weight[:, :half]).astype(BF)
+        leaving[d].start()
+        made[SIDE + d] = dot(rows([x + zs[d] for x in xs]), weight[:, half:]).astype(BF)
+        leaving[SIDE + d].start()
+    for c in leaving:
+        c.wait()
+
+
+def attention(mine, prefill_qkv, decode_qkv, cache_pool, page_table, cache_len, out_weight):
     requests = decode_qkv.shape[0]
     pages, page = cache_pool.shape[1:3]
-    rows = prefill_qkv.shape[0] * prefill_qkv.shape[2] + requests
-    whole = pl.BlockSpec(memory_space=pltpu.VMEM)
+    half = out_weight.shape[1] // 2
+    given = [
+        prefill_qkv,
+        cache_len[None, :],
+        page_table,
+        decode_qkv.transpose(1, 0, 2),
+        out_weight,
+        cache_pool,
+    ]
     return pl.pallas_call(
         attention_kernel,
-        out_shape=jax.ShapeDtypeStruct((rows, HD), BF),
-        in_specs=[pl.BlockSpec(memory_space=pltpu.SMEM), whole, whole, whole, pl.BlockSpec(memory_space=pl.ANY)],
-        out_specs=whole,
-        scratch_shapes=[
+        out_shape=[jax.ShapeDtypeStruct((SIDE * ROWS, half), BF)] * (2 * SIDE),
+        in_specs=[pl.BlockSpec(memory_space=pltpu.SMEM)]
+        + [pl.BlockSpec(memory_space=pltpu.HBM)] * len(given),
+        out_specs=[pl.BlockSpec(memory_space=pltpu.HBM)] * (2 * SIDE),
+        scratch_shapes=[pltpu.VMEM(a.shape, a.dtype) for a in given[:5]]
+        + [
             pltpu.VMEM((pages, page, HD), BF),
             pltpu.VMEM((pages, page, HD), BF),
             pltpu.VMEM((requests, pages * page), F32),
-            pltpu.SemaphoreType.DMA((2,)),
+            pltpu.VMEM((SIDE * SIDE * TOKENS + 8, HD), F32),
+            pltpu.VMEM((SIDE * SIDE, ROWS, HD), F32),
+            pltpu.VMEM((2 * SIDE, SIDE * ROWS, half), BF),
+            pltpu.SemaphoreType.DMA((7 + 2 * SIDE,)),
         ],
-        compiler_params=vmem(48),
+        compiler_params=vmem(56),
         name="attention",
-    )(cache_len, page_table, prefill_qkv, decode_qkv.transpose(1, 0, 2), cache_pool)
-
-
-def project_kernel(mine, blocks, weight, *outs):
-    half = weight.shape[1] // 2
-    at_x, at_z = mine[0] // SIDE, mine[0] % SIDE
-
-    def rows(picked):
-        return jnp.concatenate([blocks[i].astype(F32) for i in picked], axis=0).astype(BF)
-
-    xs = [jnp.bitwise_xor(at_x, d) * SIDE for d in range(SIDE)]
-    zs = [jnp.bitwise_xor(at_z, d) for d in range(SIDE)]
-    for d in range(SIDE):
-        outs[d][...] = dot(rows([xs[d] + z for z in zs]), weight[:, :half]).astype(BF)
-        outs[SIDE + d][...] = dot(rows([x + zs[d] for x in xs]), weight[:, half:]).astype(BF)
-
-
-def project(attended, out_weight, mine):
-    blocks = attended.reshape(SIDE * SIDE, -1, HD)
-    blocks = jnp.pad(blocks, ((0, 0), (0, ROWS - blocks.shape[1]), (0, 0)))
-    half = out_weight.shape[1] // 2
-    whole = pl.BlockSpec(memory_space=pltpu.VMEM)
-    return pl.pallas_call(
-        project_kernel,
-        out_shape=[jax.ShapeDtypeStruct((SIDE * ROWS, half), BF)] * (2 * SIDE),
-        in_specs=[pl.BlockSpec(memory_space=pltpu.SMEM), whole, whole],
-        out_specs=[whole] * (2 * SIDE),
-        compiler_params=vmem(32),
-        name="project",
-    )(mine, blocks, out_weight)
+    )(mine, *given)
 
 
 def along_x(a, d):
@@ -300,12 +315,35 @@
     )(mine, *rows_a, *rows_b)
 
 
-def expert_kernel(rows, gate_up, down, out):
+def expert_kernel(rows, gate_up, down, out, gate_held, up_held, down_held, sems):
+    sources = (gate_up.at[0, 0], gate_up.at[0, 1], down.at[0])
+    copies = [
+        pltpu.make_async_copy(source, buf, sems.at[i])
+        for i, (source, buf) in enumerate(zip(sources, (gate_held, up_held, down_held)))
+    ]
+    first = pl.program_id(0) == 0
+
+    @pl.when(first)
+    def _():
+        for c in copies:
+            c.start()
+        copies[0].wait()
+
     x = rows[...]
-    gate = dot_nt(x, gate_up[0, 0])
-    up = dot_nt(x, gate_up[0, 1])
+    gate = dot_nt(x, gate_held[...])
+
+    @pl.when(first)
+    def _():
+        copies[1].wait()
+
+    up = dot_nt(x, up_held[...])
     hidden = (gate / (1.0 + jnp.exp(-gate)) * up).astype(BF)
-    out[...] = dot(hidden, down[0]).astype(BF)
+
+    @pl.when(first)
+    def _():
+        copies[2].wait()
+
+    out[...] = dot(hidden, down_held[...]).astype(BF)
 
 
 def experts(rows, gate_up, down):
@@ -317,10 +355,16 @@
         out_shape=jax.ShapeDtypeStruct((count, width), BF),
         in_specs=[
             pl.BlockSpec((step, width), lambda i: (i, 0)),
-            pl.BlockSpec(gate_up.shape, lambda i: (0, 0, 0, 0)),
-            pl.BlockSpec(down.shape, lambda i: (0, 0, 0)),
+            pl.BlockSpec(memory_space=pltpu.HBM),
+            pl.BlockSpec(memory_space=pltpu.HBM),
         ],
         out_specs=pl.BlockSpec((step, width), lambda i: (i, 0)),
+        scratch_shapes=[
+            pltpu.VMEM(gate_up.shape[2:], BF),
+            pltpu.VMEM(gate_up.shape[2:], BF),
+            pltpu.VMEM(down.shape[1:], BF),
+            pltpu.SemaphoreType.DMA((3,)),
+        ],
         compiler_params=vmem(56),
         cost_estimate=pl.CostEstimate(
             flops=6 * count * width * down.shape[1],
@@ -329,6 +373,30 @@
         ),
         name="experts",
     )(rows, gate_up, down)
+
+
+def result_kernel(mix, rows, base, out):
+    routed = dot(mix[...], rows[...])
+    total = routed[:ROWS] + routed[ROWS:] + base[...]
+    out[...] = total[: out.shape[0]].astype(BF)
+
+
+def result(mix, rows, base, tok_rows):
+    count, width = rows.shape
+    step = 512
+    return pl.pallas_call(
+        result_kernel,
+        grid=(width // step,),
+        out_shape=jax.ShapeDtypeStruct((tok_rows, width), BF),
+        in_specs=[
+            pl.BlockSpec(mix.shape, lambda i: (0, 0)),
+            pl.BlockSpec((count, step), lambda i: (0, i)),
+            pl.BlockSpec((ROWS, step), lambda i: (0, i)),
+        ],
+        out_specs=pl.BlockSpec((tok_rows, step), lambda i: (0, i)),
+        compiler_params=vmem(32),
+        name="result",
+    )(mix, rows, base)
 
 
 def shared_kernel(*refs):
@@ -417,8 +485,10 @@
     mix_low = (mix - mix_high.astype(F32)).astype(BF)
     mix = jnp.concatenate([mix_high, mix_low], axis=0)
 
-    attended = attention(prefill_qkv, decode_qkv, cache_pool, page_table, cache_len)
-    sums = sum_first(project(attended, out_weight, mine[None]))
+    parts = attention(
+        mine[None], prefill_qkv, decode_qkv, cache_pool, page_table, cache_len, out_weight
+    )
+    sums = sum_first(parts)
     got_a, got_b = sum_second(*lax.optimization_barrier(sums))
     stream, normed = pl.pallas_call(
         token_kernel,
@@ -454,10 +524,8 @@
     )
     shared = jnp.concatenate([add_up(got_a), add_up(got_b)], axis=1)
     shared_scale = jax.nn.sigmoid(dot(normed, shared_gate))
-    routed = dot(mix, returned.reshape(devices * capacity, width))
-    routed = routed[:ROWS] + routed[ROWS:]
-    result = stream.astype(F32) + routed + shared_scale[:, None] * shared
-    return result[:tok_rows].astype(BF)
+    base = stream.astype(F32) + shared_scale[:, None] * shared
+    return result(mix, returned.reshape(devices * capacity, width), base, tok_rows)
 
 
 def solution(mesh):

time: 249 us -> 249 us (level)
  Pallas kernels: 39.5 us -> 47.4 us
  local copies, waits for them, and re-layouts: 9.86 us -> 5.79 us
  matrix products: 3.15 us -> 0.19 us
    pallas_call x2, Pallas kernels: 6.94 us -> 12.6 us  [the longest x1 8.15 us: attention(): pl.pallas_call(attention_kernel, out_shape=[jax.ShapeDtypeStruct((SIDE *...]
    unnamed x48 -> x54, local copies, waits for them, and re-layouts: 5.58 us -> 1.53 us
    dot_general x2 -> x1, matrix products: 3.15 us -> 0.19 us  [dot(): return jnp.dot(a, b, preferred_element_type=F32)]
where the time goes in v6:
time: 249 us; the launch traced here: 247 us
  waiting for transfers between devices  119 us (48%)
  starting transfers between devices  68.1 us (27%)
  Pallas kernels  47.4 us (19%)
  local copies, waits for them, and re-layouts  5.79 us (2%)
  other arithmetic  5.43 us (2%)
    all_to_all x1, waiting for transfers between devices, on_device(): lax.all_to_all(answer.reshape(devices, capacity, width), ('req', 'exp'),...  50.3 us
    ppermute x21, waiting for transfers between devices, along_z(): return lax.ppermute(a, 'exp', [(i, i ^ d) for i in range(SIDE * SIDE)])  41.9 us
    ppermute x21, starting transfers between devices, along_x(): lax.ppermute(a, 'exp', [(i, i ^ d * SIDE) for i in range(SIDE * SIDE)])  27.8 us
    ppermute x21, starting transfers between devices, along_z(): return lax.ppermute(a, 'exp', [(i, i ^ d) for i in range(SIDE * SIDE)])  27.4 us
    ppermute x21, waiting for transfers between devices, along_x(): lax.ppermute(a, 'exp', [(i, i ^ d * SIDE) for i in range(SIDE * SIDE)])  26.7 us
    pallas_call x1, Pallas kernels, experts(): pl.pallas_call(expert_kernel, grid=(count // step,), out_shape=jax.ShapeD...  18 us
    pallas_call x1, Pallas kernels, shared_expert(): pl.pallas_call(shared_kernel, out_shape=[jax.ShapeDtypeStruct((SIDE * ROW...  10.8 us
    pallas_call x1, Pallas kernels, attention(): pl.pallas_call(attention_kernel, out_shape=[jax.ShapeDtypeStruct((SIDE *...  8.15 us
  transfers between devices with their start and end apart: 44, of which 28 were waited for; matrix products, arithmetic and copies ran while one was open for 3% of the time, Pallas kernels for 4%

profile of v6, /device:TPU:8, one launch (start us, length us, event | category | flops | bytes accessed | tf_op | source)
XLA Modules:
  0.0 246.6 jit_solution(3253723909254845997)
XLA Ops:
  0.0 8.2 %attention.1 = (bf16[288,1024]{1,0:T(8,128)(2,1)}, bf16[288,1024]{1,0:T(8,128)(2,1)}, bf16[288,1024]{1,0:T(8,128)(2,1)}, bf16[288,1024]{1,0:T(8,128)(2,1)}, bf16...) custom-call(s32[1]{0:T(128)} %bitcast.mine, ...), custom_call_target="tpu_custom_call" | custom-call | tf_op jit(solution)/shard_map/attention/pallas_call | solution.py:154
  9.4 2.0 collective-permute-start.3
  11.4 2.5 %collective-permute-start.2 = (bf16[144,1024]{1,0:T(8,128)(2,1)S(1)}, bf16[144,1024]{1,0:T(8,128)(2,1)S(1)}, u32[]{:S(2)}, u32[]{:S(2)}) collective-permute-start(bf16[144,1024]{1,0:T(8,128)(2,1)S(1)} %get-tuple-element.110), channel_id=1, source_target_pairs={{0,3},{1,2},{2,1},{3,0},{4,7},{5,6},{6,5},{7,4},{8,11},{9,10},{10,... | collective-permute-start | bytes 884744 | tf_op jit(solution)/shard_map/ppermute | solution.py:180
  13.9 1.6 collective-permute-start.1
  15.5 2.1 collective-permute-start
  18.5 2.6 %collective-permute-done.2 = bf16[144,1024]{1,0:T(8,128)(2,1)S(1)} collective-permute-done((bf16[144,1024]{1,0:T(8,128)(2,1)S(1)}, bf16[144,1024]{1,0:T(8,128)(2,1)S(1)}, u32[]{:S(2)}, u32[]{:S(2)}) %collective-permute-start.2) | collective-permute-done | bytes 294944 | tf_op jit(solution)/shard_map/ppermute | solution.py:180
  22.5 2.2 collective-permute-done
  26.8 2.1 collective-permute-start.5
  32.2 6.0 %collective-permute-done.6 = bf16[288,1024]{1,0:T(8,128)(2,1)} collective-permute-done((bf16[288,1024]{1,0:T(8,128)(2,1)S(1)}, bf16[288,1024]{1,0:T(8,128)(2,1)}, u32[]{:S(2)}, u32[]{:S(2)}) %collective-permute-start.6) | collective-permute-done | bytes 589856 | tf_op jit(solution)/shard_map/ppermute | solution.py:180
  38.2 2.0 collective-permute-done.7
  40.2 1.6 add_convert_fusion.2
  41.9 1.4 add_convert_fusion.3
  45.2 2.1 collective-permute-start.12
  47.3 1.4 collective-permute-start.13
  51.1 1.6 collective-permute-start.9
  53.9 3.5 %collective-permute-done.9.a2 = bf16[72,1024]{1,0:T(8,128)(2,1)S(1)} collective-permute-done((bf16[72,1024]{1,0:T(8,128)(2,1)S(1)}, bf16[72,1024]{1,0:T(8,128)(2,1)S(1)}, u32[]{:S(2)}, u32[]{:S(2)}) %collective-permute-start.9) | collective-permute-done | bytes 147488 | tf_op jit(solution)/shard_map/ppermute | solution.py:180
  58.3 3.2 %collective-permute-start.18 = (bf16[72,1024]{1,0:T(8,128)(2,1)S(1)}, bf16[72,1024]{1,0:T(8,128)(2,1)S(1)}, u32[]{:S(2)}, u32[]{:S(2)}) collective-permute-start(bf16[72,1024]{1,0:T(8,128)(2,1)S(1)} %get-tuple-element.115), channel_id=1, source_target_pairs={{0,8},{1,9},{2,10},{3,11},{4,12},{5,13},{6,14},{7,15},{8,0},{9,1},... | collective-permute-start | bytes 442376 | tf_op jit(solution)/shard_map/ppermute | solution.py:176
  62.7 3.1 %collective-permute-start.15 = (bf16[72,1024]{1,0:T(8,128)(2,1)S(1)}, bf16[72,1024]{1,0:T(8,128)(2,1)S(1)}, u32[]{:S(2)}, u32[]{:S(2)}) collective-permute-start(bf16[72,1024]{1,0:T(8,128)(2,1)S(1)} %get-tuple-element.116), channel_id=1, source_target_pairs={{0,2},{1,3},{2,0},{3,1},{4,6},{5,7},{6,4},{7,5},{8,10},{9,11},{10,... | collective-permute-start | bytes 442376 | tf_op jit(solution)/shard_map/ppermute | solution.py:180
  65.8 1.6 collective-permute-start.16
  68.0 2.5 collective-permute-done.15
  70.5 3.1 %collective-permute-done.16 = bf16[72,1024]{1,0:T(8,128)(2,1)S(1)} collective-permute-done((bf16[72,1024]{1,0:T(8,128)(2,1)S(1)}, bf16[72,1024]{1,0:T(8,128)(2,1)S(1)}, u32[]{:S(2)}, u32[]{:S(2)}) %collective-permute-start.16) | collective-permute-done | bytes 147488 | tf_op jit(solution)/shard_map/ppermute | solution.py:180
  73.6 2.4 collective-permute-start.21
  76.0 1.6 collective-permute-start.25
  77.6 10.4 %collective-permute-done.21.refs_2_ = bf16[4,72,1024]{2,1,0:T(8,128)(2,1)S(1)} collective-permute-done((bf16[4,72,1024]{2,1,0:T(8,128)(2,1)S(1)}, bf16[4,72,1024]{2,1,0:T(8,128)(2,1)S(1)}, u32[]{:S(2)}, u32[]{:S(2)}) %collective-permute-start.21) | collective-permute-done | bytes 589856 | tf_op jit(solution)/shard_map/ppermute | solution.py:176
  88.1 2.4 collective-permute-start.23
  90.7 1.7 collective-permute-start.27
  92.4 2.4 collective-permute-done.22.refs_3_
  94.8 1.4 collective-permute-done.23.refs_4_
  97.3 1.4 collective-permute-done.27.refs_9_
  99.4 5.7 %pick.1 = bf16[8,16,8,2048]{3,2,1,0:T(8,128)(2,1)} custom-call(s32[1]{0:T(128)} %bitcast.mine, bf16[4,72,1024]{2,1,0:T(8,128)(2,1)} %copy-done.10, bf16[4,72,1024]{2,1,0:T(8,128)(2,1)} %copy-done.12, bf16[4,72,1024]{2,1,0:T(8,128)(2,1)} %copy-done.11, bf16[2,72,1024]{2,1,0:T(8,128)(2,1)} %copy-done, bf16[2,72,1024]{2,1,0:T(8,128)(2,1)} %copy-done.2, ...), custom_call_target="tpu_custom_call" | custom-call | tf_op jit(solution)/shard_map/pick/pallas_call | solution.py:308
  105.2 5.1 %all-to-all-start = ((bf16[8,128,2048]{2,1,0:T(8,128)(2,1)}), bf16[8,128,2048]{2,1,0:T(8,128)(2,1)}, u32[]{:S(2)}, u32[]{:S(2)}) async-start(bf16[8,128,2048]{2,1,0:T(8,128)(2,1)} %bitcast.71), calls=%async_computation | async-start | bytes 8388608 | tf_op jit(solution)/shard_map/all_to_all | solution.py:507
  110.3 10.8 %shared_expert.1 = (bf16[288,1024]{1,0:T(8,128)(2,1)S(1)}, bf16[288,1024]{1,0:T(8,128)(2,1)S(1)}, bf16[288,1024]{1,0:T(8,128)(2,1)S(1)}, bf16[288,1024]{1,0:T(8,...) custom-call(bf16[4,72,1024]{2,1,0:T(8,128)(2,1)} %copy-done.10, ...), custom_call_target="tpu_custom_call" | custom-call | flops 4982833152 | bytes 13762560 | tf_op jit(solution)/shard_map/shared_expert/pallas_call | solution.py:428
  122.0 1.6 collective-permute-start.30
  123.6 1.9 collective-permute-start.29
  126.7 3.5 %collective-permute-done.31 = bf16[144,1024]{1,0:T(8,128)(2,1)S(1)} collective-permute-done((bf16[144,1024]{1,0:T(8,128)(2,1)S(1)}, bf16[144,1024]{1,0:T(8,128)(2,1)S(1)}, u32[]{:S(2)}, u32[]{:S(2)}) %collective-permute-start.31) | collective-permute-done | bytes 294944 | tf_op jit(solution)/shard_map/ppermute | solution.py:180
  130.3 1.6 collective-permute-done.30
  132.5 2.8 %collective-permute-done.28 = bf16[144,1024]{1,0:T(8,128)(2,1)S(1)} collective-permute-done((bf16[144,1024]{1,0:T(8,128)(2,1)S(1)}, bf16[144,1024]{1,0:T(8,128)(2,1)S(1)}, u32[]{:S(2)}, u32[]{:S(2)}) %collective-permute-start.28) | collective-permute-done | bytes 294944 | tf_op jit(solution)/shard_map/ppermute | solution.py:176
  136.1 1.6 collective-permute-start.35
  138.8 10.3 %collective-permute-done.34 = bf16[288,1024]{1,0:T(8,128)(2,1)S(1)} collective-permute-done((bf16[288,1024]{1,0:T(8,128)(2,1)S(1)}, bf16[288,1024]{1,0:T(8,128)(2,1)S(1)}, u32[]{:S(2)}, u32[]{:S(2)}) %collective-permute-start.34) | collective-permute-done | bytes 589856 | tf_op jit(solution)/shard_map/ppermute | solution.py:180
  149.1 1.5 collective-permute-done.35
  153.3 1.6 collective-permute-start.37
  154.9 1.7 collective-permute-start.38
  158.2 2.5 %collective-permute-start.41 = (bf16[72,1024]{1,0:T(8,128)(2,1)S(1)}, bf16[72,1024]{1,0:T(8,128)(2,1)S(1)}, u32[]{:S(2)}, u32[]{:S(2)}) collective-permute-start(bf16[72,1024]{1,0:T(8,128)(2,1)S(1)} %get-tuple-element.89), channel_id=1, source_target_pairs={{0,8},{1,9},{2,10},{3,11},{4,12},{5,13},{6,14},{7,15},{8,0},{9,1},... | collective-permute-start | bytes 442376 | tf_op jit(solution)/shard_map/ppermute | solution.py:176
  161.8 3.3 %collective-permute-done.40 = bf16[72,1024]{1,0:T(8,128)(2,1)S(1)} collective-permute-done((bf16[72,1024]{1,0:T(8,128)(2,1)S(1)}, bf16[72,1024]{1,0:T(8,128)(2,1)S(1)}, u32[]{:S(2)}, u32[]{:S(2)}) %collective-permute-start.40) | collective-permute-done | bytes 147488 | tf_op jit(solution)/shard_map/ppermute | solution.py:176
  165.1 18.0 %experts.1 = bf16[1024,2048]{1,0:T(8,128)(2,1)} custom-call(bf16[1024,2048]{1,0:T(8,128)(2,1)} %bitcast.35.rows, bf16[1,2,704,2048]{3,2,1,0:T(8,128)(2,1)} %bitcast.85, bf16[1,704,2048]{2,1,0:T(8,128)(2,1)} %down.1), custom_call_target="tpu_custom_call" | custom-call | flops 8858370048 | bytes 17039360 | tf_op jit(solution)/shard_map/experts/pallas_call | solution.py:352
  183.2 7.8 %all-to-all-start.1 = ((bf16[128,8,2048]{2,1,0:T(8,128)(2,1)}), bf16[128,8,2048]{2,1,0:T(8,128)(2,1)}, u32[]{:S(2)}, u32[]{:S(2)}) async-start(bf16[128,8,2048]{2,1,0:T(8,128)(2,1)} %bitcast.72), calls=%async_computation.1 | async-start | bytes 8388608 | tf_op jit(solution)/shard_map/all_to_all | solution.py:518
  191.9 50.3 %all-to-all-done.1 = bf16[128,8,2048]{2,1,0:T(8,128)(2,1)} async-done(((bf16[128,8,2048]{2,1,0:T(8,128)(2,1)}), bf16[128,8,2048]{2,1,0:T(8,128)(2,1)}, u32[]{:S(2)}, u32[]{:S(2)}) %all-to-all-start.1) | async-done | bytes 4194336 | tf_op jit(solution)/shard_map/all_to_all | solution.py:518
  242.2 4.5 %result.1 = bf16[65,2048]{1,0:T(8,128)(2,1)} custom-call(bf16[144,1024]{1,0:T(8,128)(2,1)S(1)} %pad_maximum_fusion.10.mix, bf16[1024,2048]{1,0:T(8,128)(2,1)} %bitcast.38.rows, f32[72,2048]{1,0:T(8,128)S(1)} %fusion.4.base), custom_call_target="tpu_custom_call" | custom-call | tf_op jit(solution)/shard_map/result/pallas_call | solution.py:387
  (159 shorter events, 29.9 us)
Async XLA Ops:
  9.4 9.0 %collective-permute-start.3 = (bf16[144,1024]{1,0:T(8,128)(2,1)S(1)}, bf16[144,1024]{1,0:T(8,128)(2,1)S(1)}, u32[]{:S(2)}, u32[]{:S(2)}) collective-permute-start(bf16[144,1024]{1,0:T(8,128)(2,1)S(1)} %get-tuple-element.109), channel_id=1, source_target_pairs={{0,1},{1,0},{2,3},{3,2},{4,5},{5,4},{6,7},{7,6},{8,9},{9,8},{10,11... | collective-permute-start | bytes 884744 | tf_op jit(solution)/shard_map/ppermute | solution.py:180
  11.4 9.7 %collective-permute-start.2 = (bf16[144,1024]{1,0:T(8,128)(2,1)S(1)}, bf16[144,1024]{1,0:T(8,128)(2,1)S(1)}, u32[]{:S(2)}, u32[]{:S(2)}) collective-permute-start(bf16[144,1024]{1,0:T(8,128)(2,1)S(1)} %get-tuple-element.110), channel_id=1, source_target_pairs={{0,3},{1,2},{2,1},{3,0},{4,7},{5,6},{6,5},{7,4},{8,11},{9,10},{10,... | collective-permute-start | bytes 884744 | tf_op jit(solution)/shard_map/ppermute | solution.py:180
  13.9 8.3 %collective-permute-start.1 = (bf16[144,1024]{1,0:T(8,128)(2,1)S(1)}, bf16[144,1024]{1,0:T(8,128)(2,1)S(1)}, u32[]{:S(2)}, u32[]{:S(2)}) collective-permute-start(bf16[144,1024]{1,0:T(8,128)(2,1)S(1)} %get-tuple-element.111), channel_id=1, source_target_pairs={{0,4},{1,5},{2,6},{3,7},{4,0},{5,1},{6,2},{7,3},{8,12},{9,13},{10,... | collective-permute-start | bytes 884744 | tf_op jit(solution)/shard_map/ppermute | solution.py:176
  15.5 9.1 %collective-permute-start = (bf16[144,1024]{1,0:T(8,128)(2,1)S(1)}, bf16[144,1024]{1,0:T(8,128)(2,1)S(1)}, u32[]{:S(2)}, u32[]{:S(2)}) collective-permute-start(bf16[144,1024]{1,0:T(8,128)(2,1)S(1)} %get-tuple-element.112), channel_id=1, source_target_pairs={{0,12},{1,13},{2,14},{3,15},{4,8},{5,9},{6,10},{7,11},{8,4},{9,5},... | collective-permute-start | bytes 884744 | tf_op jit(solution)/shard_map/ppermute | solution.py:176
  22.5 17.8 %copy-start.21 = (bf16[288,1024]{1,0:T(8,128)(2,1)S(1)}, bf16[288,1024]{1,0:T(8,128)(2,1)}, u32[]{:S(2)}) copy-start(bf16[288,1024]{1,0:T(8,128)(2,1)} %get-tuple-element.55) | copy-start | bytes 1769476
  24.8 13.5 %collective-permute-start.6 = (bf16[288,1024]{1,0:T(8,128)(2,1)S(1)}, bf16[288,1024]{1,0:T(8,128)(2,1)}, u32[]{:S(2)}, u32[]{:S(2)}) collective-permute-start(bf16[288,1024]{1,0:T(8,128)(2,1)S(1)} %pad_maximum_fusion.2), channel_id=1, source_target_pairs={{0,1},{1,0},{2,3},{3,2},{4,5},{5,4},{6,7},{7,6},{8,9},{9,8},{10,11... | collective-permute-start | bytes 1769480 | tf_op jit(solution)/shard_map/ppermute | solution.py:180
  25.9 14.3 %collective-permute-start.7 = (bf16[288,1024]{1,0:T(8,128)(2,1)S(1)}, bf16[288,1024]{1,0:T(8,128)(2,1)}, u32[]{:S(2)}, u32[]{:S(2)}) collective-permute-start(bf16[288,1024]{1,0:T(8,128)(2,1)S(1)} %pad_maximum_fusion.3), channel_id=1, source_target_pairs={{0,3},{1,2},{2,1},{3,0},{4,7},{5,6},{6,5},{7,4},{8,11},{9,10},{10,... | collective-permute-start | bytes 1769480 | tf_op jit(solution)/shard_map/ppermute | solution.py:180
  26.8 15.1 %collective-permute-start.4 = (bf16[288,1024]{1,0:T(8,128)(2,1)S(1)}, bf16[288,1024]{1,0:T(8,128)(2,1)S(1)}, u32[]{:S(2)}, u32[]{:S(2)}) collective-permute-start(bf16[288,1024]{1,0:T(8,128)(2,1)S(1)} %pad_maximum_fusion), channel_id=1, source_target_pairs={{0,4},{1,5},{2,6},{3,7},{4,0},{5,1},{6,2},{7,3},{8,12},{9,13},{10,... | collective-permute-start | bytes 1769480 | tf_op jit(solution)/shard_map/ppermute | solution.py:176
  26.8 15.1 %collective-permute-start.5 = (bf16[288,1024]{1,0:T(8,128)(2,1)S(1)}, bf16[288,1024]{1,0:T(8,128)(2,1)}, u32[]{:S(2)}, u32[]{:S(2)}) collective-permute-start(bf16[288,1024]{1,0:T(8,128)(2,1)S(1)} %pad_maximum_fusion.1), channel_id=1, source_target_pairs={{0,12},{1,13},{2,14},{3,15},{4,8},{5,9},{6,10},{7,11},{8,4},{9,5},... | collective-permute-start | bytes 1769480 | tf_op jit(solution)/shard_map/ppermute | solution.py:176
  43.3 14.1 %copy-start.8 = (f32[2048]{0:T(1024)S(1)}, f32[2048]{0:T(1024)}, u32[]{:S(2)}) copy-start(f32[2048]{0:T(1024)} %param.22) | copy-start | bytes 24580
  43.3 7.8 %collective-permute-start.10 = (bf16[72,1024]{1,0:T(8,128)(2,1)S(1)}, bf16[72,1024]{1,0:T(8,128)(2,1)S(1)}, u32[]{:S(2)}, u32[]{:S(2)}) collective-permute-start(bf16[72,1024]{1,0:T(8,128)(2,1)S(1)} %get-tuple-element.105), channel_id=1, source_target_pairs={{0,2},{1,3},{2,0},{3,1},{4,6},{5,7},{6,4},{7,5},{8,10},{9,11},{10,... | collective-permute-start | bytes 442376 | tf_op jit(solution)/shard_map/ppermute | solution.py:180
  44.6 8.2 %collective-permute-start.11 = (bf16[72,1024]{1,0:T(8,128)(2,1)S(1)}, bf16[72,1024]{1,0:T(8,128)(2,1)S(1)}, u32[]{:S(2)}, u32[]{:S(2)}) collective-permute-start(bf16[72,1024]{1,0:T(8,128)(2,1)S(1)} %get-tuple-element.103), channel_id=1, source_target_pairs={{0,4},{1,5},{2,6},{3,7},{4,0},{5,1},{6,2},{7,3},{8,12},{9,13},{10,... | collective-permute-start | bytes 442376 | tf_op jit(solution)/shard_map/ppermute | solution.py:176
  45.2 7.6 %collective-permute-start.12 = (bf16[72,1024]{1,0:T(8,128)(2,1)S(1)}, bf16[72,1024]{1,0:T(8,128)(2,1)S(1)}, u32[]{:S(2)}, u32[]{:S(2)}) collective-permute-start(bf16[72,1024]{1,0:T(8,128)(2,1)S(1)} %get-tuple-element.102), channel_id=1, source_target_pairs={{0,12},{1,13},{2,14},{3,15},{4,8},{5,9},{6,10},{7,11},{8,4},{9,5},... | collective-permute-start | bytes 442376 | tf_op jit(solution)/shard_map/ppermute | solution.py:176
  47.3 6.6 %collective-permute-start.13 = (bf16[72,1024]{1,0:T(8,128)(2,1)S(1)}, bf16[72,1024]{1,0:T(8,128)(2,1)S(1)}, u32[]{:S(2)}, u32[]{:S(2)}) collective-permute-start(bf16[72,1024]{1,0:T(8,128)(2,1)S(1)} %get-tuple-element.101), channel_id=1, source_target_pairs={{0,8},{1,9},{2,10},{3,11},{4,12},{5,13},{6,14},{7,15},{8,0},{9,1},... | collective-permute-start | bytes 442376 | tf_op jit(solution)/shard_map/ppermute | solution.py:176
  48.7 5.2 %collective-permute-start.8 = (bf16[72,1024]{1,0:T(8,128)(2,1)S(1)}, bf16[72,1024]{1,0:T(8,128)(2,1)S(1)}, u32[]{:S(2)}, u32[]{:S(2)}) collective-permute-start(bf16[72,1024]{1,0:T(8,128)(2,1)S(1)} %get-tuple-element.107), channel_id=1, source_target_pairs={{0,1},{1,0},{2,3},{3,2},{4,5},{5,4},{6,7},{7,6},{8,9},{9,8},{10,11... | collective-permute-start | bytes 442376 | tf_op jit(solution)/shard_map/ppermute | solution.py:180
  51.1 6.4 %collective-permute-start.9 = (bf16[72,1024]{1,0:T(8,128)(2,1)S(1)}, bf16[72,1024]{1,0:T(8,128)(2,1)S(1)}, u32[]{:S(2)}, u32[]{:S(2)}) collective-permute-start(bf16[72,1024]{1,0:T(8,128)(2,1)S(1)} %get-tuple-element.106), channel_id=1, source_target_pairs={{0,3},{1,2},{2,1},{3,0},{4,7},{5,6},{6,5},{7,4},{8,11},{9,10},{10,... | collective-permute-start | bytes 442376 | tf_op jit(solution)/shard_map/ppermute | solution.py:180
  57.9 7.9 %collective-permute-start.17 = (bf16[72,1024]{1,0:T(8,128)(2,1)S(1)}, bf16[72,1024]{1,0:T(8,128)(2,1)S(1)}, u32[]{:S(2)}, u32[]{:S(2)}) collective-permute-start(bf16[72,1024]{1,0:T(8,128)(2,1)S(1)} %get-tuple-element.115), channel_id=1, source_target_pairs={{0,4},{1,5},{2,6},{3,7},{4,0},{5,1},{6,2},{7,3},{8,12},{9,13},{10,... | collective-permute-start | bytes 442376 | tf_op jit(solution)/shard_map/ppermute | solution.py:176
  58.3 9.0 %collective-permute-start.18 = (bf16[72,1024]{1,0:T(8,128)(2,1)S(1)}, bf16[72,1024]{1,0:T(8,128)(2,1)S(1)}, u32[]{:S(2)}, u32[]{:S(2)}) collective-permute-start(bf16[72,1024]{1,0:T(8,128)(2,1)S(1)} %get-tuple-element.115), channel_id=1, source_target_pairs={{0,8},{1,9},{2,10},{3,11},{4,12},{5,13},{6,14},{7,15},{8,0},{9,1},... | collective-permute-start | bytes 442376 | tf_op jit(solution)/shard_map/ppermute | solution.py:176
  61.5 6.4 %collective-permute-start.19 = (bf16[72,1024]{1,0:T(8,128)(2,1)S(1)}, bf16[72,1024]{1,0:T(8,128)(2,1)S(1)}, u32[]{:S(2)}, u32[]{:S(2)}) collective-permute-start(bf16[72,1024]{1,0:T(8,128)(2,1)S(1)} %get-tuple-element.115), channel_id=1, source_target_pairs={{0,12},{1,13},{2,14},{3,15},{4,8},{5,9},{6,10},{7,11},{8,4},{9,5},... | collective-permute-start | bytes 442376 | tf_op jit(solution)/shard_map/ppermute | solution.py:176
  62.7 5.3 %collective-permute-start.14 = (bf16[72,1024]{1,0:T(8,128)(2,1)S(1)}, bf16[72,1024]{1,0:T(8,128)(2,1)S(1)}, u32[]{:S(2)}, u32[]{:S(2)}) collective-permute-start(bf16[72,1024]{1,0:T(8,128)(2,1)S(1)} %get-tuple-element.116), channel_id=1, source_target_pairs={{0,1},{1,0},{2,3},{3,2},{4,5},{5,4},{6,7},{7,6},{8,9},{9,8},{10,11... | collective-permute-start | bytes 442376 | tf_op jit(solution)/shard_map/ppermute | solution.py:180
  62.7 7.8 %collective-permute-start.15 = (bf16[72,1024]{1,0:T(8,128)(2,1)S(1)}, bf16[72,1024]{1,0:T(8,128)(2,1)S(1)}, u32[]{:S(2)}, u32[]{:S(2)}) collective-permute-start(bf16[72,1024]{1,0:T(8,128)(2,1)S(1)} %get-tuple-element.116), channel_id=1, source_target_pairs={{0,2},{1,3},{2,0},{3,1},{4,6},{5,7},{6,4},{7,5},{8,10},{9,11},{10,... | collective-permute-start | bytes 442376 | tf_op jit(solution)/shard_map/ppermute | solution.py:180
  65.8 7.8 %collective-permute-start.16 = (bf16[72,1024]{1,0:T(8,128)(2,1)S(1)}, bf16[72,1024]{1,0:T(8,128)(2,1)S(1)}, u32[]{:S(2)}, u32[]{:S(2)}) collective-permute-start(bf16[72,1024]{1,0:T(8,128)(2,1)S(1)} %get-tuple-element.116), channel_id=1, source_target_pairs={{0,3},{1,2},{2,1},{3,0},{4,7},{5,6},{6,5},{7,4},{8,11},{9,10},{10,... | collective-permute-start | bytes 442376 | tf_op jit(solution)/shard_map/ppermute | solution.py:180
  68.0 20.1 %copy-start.9 = (bf16[4,72,1024]{2,1,0:T(8,128)(2,1)}, bf16[4,72,1024]{2,1,0:T(8,128)(2,1)S(1)}, u32[]{:S(2)}) copy-start(bf16[4,72,1024]{2,1,0:T(8,128)(2,1)S(1)} %pad_maximum_fusion.5.refs_5_) | copy-start | bytes 1769476
  73.6 17.1 %copy-start.10 = (bf16[4,72,1024]{2,1,0:T(8,128)(2,1)}, bf16[4,72,1024]{2,1,0:T(8,128)(2,1)S(1)}, u32[]{:S(2)}) copy-start(bf16[4,72,1024]{2,1,0:T(8,128)(2,1)S(1)} %pad_maximum_fusion.4.refs_0_) | copy-start | bytes 1769476
  73.6 14.3 %collective-permute-start.21 = (bf16[4,72,1024]{2,1,0:T(8,128)(2,1)S(1)}, bf16[4,72,1024]{2,1,0:T(8,128)(2,1)S(1)}, u32[]{:S(2)}, u32[]{:S(2)}) collective-permute-start(bf16[4,72,1024]{2,1,0:T(8,128)(2,1)S(1)} %pad_maximum_fusion.4.refs_0_), channel_id=1, source_target_pairs={{0,12},{1,13},{2,14},{3,15},{4,8},{5,9},{6,10},{7,11},{8,4},{9,5},... | collective-permute-start | bytes 1769480 | tf_op jit(solution)/shard_map/ppermute | solution.py:176
  76.0 12.1 %collective-permute-start.20 = (bf16[4,72,1024]{2,1,0:T(8,128)(2,1)S(1)}, bf16[4,72,1024]{2,1,0:T(8,128)(2,1)S(1)}, u32[]{:S(2)}, u32[]{:S(2)}) collective-permute-start(bf16[4,72,1024]{2,1,0:T(8,128)(2,1)S(1)} %pad_maximum_fusion.4.refs_0_), channel_id=1, source_target_pairs={{0,4},{1,5},{2,6},{3,7},{4,0},{5,1},{6,2},{7,3},{8,12},{9,13},{10,... | collective-permute-start | bytes 1769480 | tf_op jit(solution)/shard_map/ppermute | solution.py:176
  76.0 14.5 %collective-permute-start.25 = (bf16[4,72,1024]{2,1,0:T(8,128)(2,1)S(1)}, bf16[4,72,1024]{2,1,0:T(8,128)(2,1)S(1)}, u32[]{:S(2)}, u32[]{:S(2)}) collective-permute-start(bf16[4,72,1024]{2,1,0:T(8,128)(2,1)S(1)} %pad_maximum_fusion.5.refs_5_), channel_id=1, source_target_pairs={{0,3},{1,2},{2,1},{3,0},{4,7},{5,6},{6,5},{7,4},{8,11},{9,10},{10,... | collective-permute-start | bytes 1769480 | tf_op jit(solution)/shard_map/ppermute | solution.py:180
  77.6 13.0 %collective-permute-start.24 = (bf16[4,72,1024]{2,1,0:T(8,128)(2,1)S(1)}, bf16[4,72,1024]{2,1,0:T(8,128)(2,1)S(1)}, u32[]{:S(2)}, u32[]{:S(2)}) collective-permute-start(bf16[4,72,1024]{2,1,0:T(8,128)(2,1)S(1)} %pad_maximum_fusion.5.refs_5_), channel_id=1, source_target_pairs={{0,1},{1,0},{2,3},{3,2},{4,5},{5,4},{6,7},{7,6},{8,9},{9,8},{10,11... | collective-permute-start | bytes 1769480 | tf_op jit(solution)/shard_map/ppermute | solution.py:180
  88.0 6.8 %collective-permute-start.22 = (bf16[2,72,1024]{2,1,0:T(8,128)(2,1)S(1)}, bf16[2,72,1024]{2,1,0:T(8,128)(2,1)S(1)}, u32[]{:S(2)}, u32[]{:S(2)}) collective-permute-start(bf16[2,72,1024]{2,1,0:T(8,128)(2,1)S(1)} %slice.184), channel_id=1, source_target_pairs={{0,4},{1,5},{2,6},{3,7},{4,0},{5,1},{6,2},{7,3},{8,12},{9,13},{10,... | collective-permute-start | bytes 884744 | tf_op jit(solution)/shard_map/ppermute | solution.py:176
  88.1 8.0 %collective-permute-start.23 = (bf16[2,72,1024]{2,1,0:T(8,128)(2,1)S(1)}, bf16[2,72,1024]{2,1,0:T(8,128)(2,1)S(1)}, u32[]{:S(2)}, u32[]{:S(2)}) collective-permute-start(bf16[2,72,1024]{2,1,0:T(8,128)(2,1)S(1)} %slice.185), channel_id=1, source_target_pairs={{0,12},{1,13},{2,14},{3,15},{4,8},{5,9},{6,10},{7,11},{8,4},{9,5},... | collective-permute-start | bytes 884744 | tf_op jit(solution)/shard_map/ppermute | solution.py:176
  90.5 6.8 %collective-permute-start.26 = (bf16[2,72,1024]{2,1,0:T(8,128)(2,1)S(1)}, bf16[2,72,1024]{2,1,0:T(8,128)(2,1)S(1)}, u32[]{:S(2)}, u32[]{:S(2)}) collective-permute-start(bf16[2,72,1024]{2,1,0:T(8,128)(2,1)S(1)} %slice.186), channel_id=1, source_target_pairs={{0,1},{1,0},{2,3},{3,2},{4,5},{5,4},{6,7},{7,6},{8,9},{9,8},{10,11... | collective-permute-start | bytes 884744 | tf_op jit(solution)/shard_map/ppermute | solution.py:180
  90.7 8.0 %collective-permute-start.27 = (bf16[2,72,1024]{2,1,0:T(8,128)(2,1)S(1)}, bf16[2,72,1024]{2,1,0:T(8,128)(2,1)S(1)}, u32[]{:S(2)}, u32[]{:S(2)}) collective-permute-start(bf16[2,72,1024]{2,1,0:T(8,128)(2,1)S(1)} %slice.187), channel_id=1, source_target_pairs={{0,3},{1,2},{2,1},{3,0},{4,7},{5,6},{6,5},{7,4},{8,11},{9,10},{10,... | collective-permute-start | bytes 884744 | tf_op jit(solution)/shard_map/ppermute | solution.py:180
  105.2 60.0 %all-to-all-start = ((bf16[8,128,2048]{2,1,0:T(8,128)(2,1)}), bf16[8,128,2048]{2,1,0:T(8,128)(2,1)}, u32[]{:S(2)}, u32[]{:S(2)}) async-start(bf16[8,128,2048]{2,1,0:T(8,128)(2,1)} %bitcast.71), calls=%async_computation | async-start | bytes 8388608 | tf_op jit(solution)/shard_map/all_to_all | solution.py:507
  121.1 9.1 %collective-permute-start.31 = (bf16[144,1024]{1,0:T(8,128)(2,1)S(1)}, bf16[144,1024]{1,0:T(8,128)(2,1)S(1)}, u32[]{:S(2)}, u32[]{:S(2)}) collective-permute-start(bf16[144,1024]{1,0:T(8,128)(2,1)S(1)} %get-tuple-element.97), channel_id=1, source_target_pairs={{0,1},{1,0},{2,3},{3,2},{4,5},{5,4},{6,7},{7,6},{8,9},{9,8},{10,11... | collective-permute-start | bytes 884744 | tf_op jit(solution)/shard_map/ppermute | solution.py:180
  122.0 10.0 %collective-permute-start.30 = (bf16[144,1024]{1,0:T(8,128)(2,1)S(1)}, bf16[144,1024]{1,0:T(8,128)(2,1)S(1)}, u32[]{:S(2)}, u32[]{:S(2)}) collective-permute-start(bf16[144,1024]{1,0:T(8,128)(2,1)S(1)} %get-tuple-element.98), channel_id=1, source_target_pairs={{0,3},{1,2},{2,1},{3,0},{4,7},{5,6},{6,5},{7,4},{8,11},{9,10},{10,... | collective-permute-start | bytes 884744 | tf_op jit(solution)/shard_map/ppermute | solution.py:180
  123.6 8.6 %collective-permute-start.29 = (bf16[144,1024]{1,0:T(8,128)(2,1)S(1)}, bf16[144,1024]{1,0:T(8,128)(2,1)S(1)}, u32[]{:S(2)}, u32[]{:S(2)}) collective-permute-start(bf16[144,1024]{1,0:T(8,128)(2,1)S(1)} %get-tuple-element.99), channel_id=1, source_target_pairs={{0,4},{1,5},{2,6},{3,7},{4,0},{5,1},{6,2},{7,3},{8,12},{9,13},{10,... | collective-permute-start | bytes 884744 | tf_op jit(solution)/shard_map/ppermute | solution.py:176
  125.5 9.7 %collective-permute-start.28 = (bf16[144,1024]{1,0:T(8,128)(2,1)S(1)}, bf16[144,1024]{1,0:T(8,128)(2,1)S(1)}, u32[]{:S(2)}, u32[]{:S(2)}) collective-permute-start(bf16[144,1024]{1,0:T(8,128)(2,1)S(1)} %get-tuple-element.100), channel_id=1, source_target_pairs={{0,12},{1,13},{2,14},{3,15},{4,8},{5,9},{6,10},{7,11},{8,4},{9,5},... | collective-permute-start | bytes 884744 | tf_op jit(solution)/shard_map/ppermute | solution.py:176
  135.4 13.7 %collective-permute-start.34 = (bf16[288,1024]{1,0:T(8,128)(2,1)S(1)}, bf16[288,1024]{1,0:T(8,128)(2,1)S(1)}, u32[]{:S(2)}, u32[]{:S(2)}) collective-permute-start(bf16[288,1024]{1,0:T(8,128)(2,1)S(1)} %pad_maximum_fusion.8), channel_id=1, source_target_pairs={{0,1},{1,0},{2,3},{3,2},{4,5},{5,4},{6,7},{7,6},{8,9},{9,8},{10,11... | collective-permute-start | bytes 1769480 | tf_op jit(solution)/shard_map/ppermute | solution.py:180
  136.1 14.6 %collective-permute-start.35 = (bf16[288,1024]{1,0:T(8,128)(2,1)S(1)}, bf16[288,1024]{1,0:T(8,128)(2,1)S(1)}, u32[]{:S(2)}, u32[]{:S(2)}) collective-permute-start(bf16[288,1024]{1,0:T(8,128)(2,1)S(1)} %pad_maximum_fusion.9), channel_id=1, source_target_pairs={{0,3},{1,2},{2,1},{3,0},{4,7},{5,6},{6,5},{7,4},{8,11},{9,10},{10,... | collective-permute-start | bytes 1769480 | tf_op jit(solution)/shard_map/ppermute | solution.py:180
  137.7 13.2 %collective-permute-start.32 = (bf16[288,1024]{1,0:T(8,128)(2,1)S(1)}, bf16[288,1024]{1,0:T(8,128)(2,1)S(1)}, u32[]{:S(2)}, u32[]{:S(2)}) collective-permute-start(bf16[288,1024]{1,0:T(8,128)(2,1)S(1)} %pad_maximum_fusion.6), channel_id=1, source_target_pairs={{0,4},{1,5},{2,6},{3,7},{4,0},{5,1},{6,2},{7,3},{8,12},{9,13},{10,... | collective-permute-start | bytes 1769480 | tf_op jit(solution)/shard_map/ppermute | solution.py:176
  137.7 14.3 %collective-permute-start.33 = (bf16[288,1024]{1,0:T(8,128)(2,1)S(1)}, bf16[288,1024]{1,0:T(8,128)(2,1)S(1)}, u32[]{:S(2)}, u32[]{:S(2)}) collective-permute-start(bf16[288,1024]{1,0:T(8,128)(2,1)S(1)} %pad_maximum_fusion.7), channel_id=1, source_target_pairs={{0,12},{1,13},{2,14},{3,15},{4,8},{5,9},{6,10},{7,11},{8,4},{9,5},... | collective-permute-start | bytes 1769480 | tf_op jit(solution)/shard_map/ppermute | solution.py:176
  152.4 5.9 %collective-permute-start.36 = (bf16[72,1024]{1,0:T(8,128)(2,1)S(1)}, bf16[72,1024]{1,0:T(8,128)(2,1)S(1)}, u32[]{:S(2)}, u32[]{:S(2)}) collective-permute-start(bf16[72,1024]{1,0:T(8,128)(2,1)S(1)} %get-tuple-element.95), channel_id=1, source_target_pairs={{0,1},{1,0},{2,3},{3,2},{4,5},{5,4},{6,7},{7,6},{8,9},{9,8},{10,11... | collective-permute-start | bytes 442376 | tf_op jit(solution)/shard_map/ppermute | solution.py:180
  153.3 7.5 %collective-permute-start.37 = (bf16[72,1024]{1,0:T(8,128)(2,1)S(1)}, bf16[72,1024]{1,0:T(8,128)(2,1)S(1)}, u32[]{:S(2)}, u32[]{:S(2)}) collective-permute-start(bf16[72,1024]{1,0:T(8,128)(2,1)S(1)} %get-tuple-element.94), channel_id=1, source_target_pairs={{0,3},{1,2},{2,1},{3,0},{4,7},{5,6},{6,5},{7,4},{8,11},{9,10},{10,... | collective-permute-start | bytes 442376 | tf_op jit(solution)/shard_map/ppermute | solution.py:180
  154.9 6.6 %collective-permute-start.38 = (bf16[72,1024]{1,0:T(8,128)(2,1)S(1)}, bf16[72,1024]{1,0:T(8,128)(2,1)S(1)}, u32[]{:S(2)}, u32[]{:S(2)}) collective-permute-start(bf16[72,1024]{1,0:T(8,128)(2,1)S(1)} %get-tuple-element.93), channel_id=1, source_target_pairs={{0,2},{1,3},{2,0},{3,1},{4,6},{5,7},{6,4},{7,5},{8,10},{9,11},{10,... | collective-permute-start | bytes 442376 | tf_op jit(solution)/shard_map/ppermute | solution.py:180
  156.6 5.2 %collective-permute-start.39 = (bf16[72,1024]{1,0:T(8,128)(2,1)S(1)}, bf16[72,1024]{1,0:T(8,128)(2,1)S(1)}, u32[]{:S(2)}, u32[]{:S(2)}) collective-permute-start(bf16[72,1024]{1,0:T(8,128)(2,1)S(1)} %get-tuple-element.91), channel_id=1, source_target_pairs={{0,4},{1,5},{2,6},{3,7},{4,0},{5,1},{6,2},{7,3},{8,12},{9,13},{10,... | collective-permute-start | bytes 442376 | tf_op jit(solution)/shard_map/ppermute | solution.py:176
  157.2 7.9 %collective-permute-start.40 = (bf16[72,1024]{1,0:T(8,128)(2,1)S(1)}, bf16[72,1024]{1,0:T(8,128)(2,1)S(1)}, u32[]{:S(2)}, u32[]{:S(2)}) collective-permute-start(bf16[72,1024]{1,0:T(8,128)(2,1)S(1)} %get-tuple-element.90), channel_id=1, source_target_pairs={{0,12},{1,13},{2,14},{3,15},{4,8},{5,9},{6,10},{7,11},{8,4},{9,5},... | collective-permute-start | bytes 442376 | tf_op jit(solution)/shard_map/ppermute | solution.py:176
  158.2 6.9 %collective-permute-start.41 = (bf16[72,1024]{1,0:T(8,128)(2,1)S(1)}, bf16[72,1024]{1,0:T(8,128)(2,1)S(1)}, u32[]{:S(2)}, u32[]{:S(2)}) collective-permute-start(bf16[72,1024]{1,0:T(8,128)(2,1)S(1)} %get-tuple-element.89), channel_id=1, source_target_pairs={{0,8},{1,9},{2,10},{3,11},{4,12},{5,13},{6,14},{7,15},{8,0},{9,1},... | collective-permute-start | bytes 442376 | tf_op jit(solution)/shard_map/ppermute | solution.py:176
  183.2 59.0 %all-to-all-start.1 = ((bf16[128,8,2048]{2,1,0:T(8,128)(2,1)}), bf16[128,8,2048]{2,1,0:T(8,128)(2,1)}, u32[]{:S(2)}, u32[]{:S(2)}) async-start(bf16[128,8,2048]{2,1,0:T(8,128)(2,1)} %bitcast.72), calls=%async_computation.1 | async-start | bytes 8388608 | tf_op jit(solution)/shard_map/all_to_all | solution.py:518
  (22 other events, 123.1 us)

commit v7 on v6

--- a/solution.py
+++ b/solution.py
@@ -34,8 +34,8 @@
 
 
 def attention_kernel(mine, *refs):
-    given, outs, held_in = refs[:6], refs[6 : 6 + 2 * SIDE], refs[6 + 2 * SIDE : 13 + 2 * SIDE]
-    scores, mixed_rows, blocks, made, sems = refs[13 + 2 * SIDE :]
+    given, outs, held_in = refs[:6], refs[6 : 6 + 2 * PIECES], refs[6 + 2 * PIECES : 13 + 2 * PIECES]
+    scores, mixed_rows, blocks, made, sems = refs[13 + 2 * PIECES :]
     scale = HD ** (-0.5)
     pool = given[5]
     sources = [*given[:5], pool.at[0], pool.at[1]]
@@ -127,15 +127,25 @@
 
     xs = [jnp.bitwise_xor(at_x, d) * SIDE for d in range(SIDE)]
     zs = [jnp.bitwise_xor(at_z, d) for d in range(SIDE)]
-    leaving = [
-        pltpu.make_async_copy(made.at[i], out, sems.at[len(copies) + i]) for i, out in enumerate(outs)
-    ]
+    middle = SIDE * ROWS // 2
+    sent = []
+
+    def send(at, place, out):
+        sent.append(pltpu.make_async_copy(place, out, sems.at[at]))
+        sent[-1].start()
+
     for d in (2, 1, 3, 0):
-        made[d] = dot(rows([xs[d] + z for z in zs]), weight[:, :half]).astype(BF)
-        leaving[d].start()
-        made[SIDE + d] = dot(rows([x + zs[d] for x in xs]), weight[:, half:]).astype(BF)
-        leaving[SIDE + d].start()
-    for c in leaving:
+        for f, picked in enumerate(([xs[d] + z for z in zs], [x + zs[d] for x in xs])):
+            i, first = f * SIDE + d, f * PIECES
+            made[i] = dot(rows(picked), weight[:, f * half : (f + 1) * half]).astype(BF)
+            at = len(copies) + first
+            if d == 2:
+                send(at + 3, made.at[i, pl.ds(0, middle)], outs[first + 3])
+                send(at + 4, made.at[i, pl.ds(middle, middle)], outs[first + 4])
+            else:
+                place = {0: 0, 1: 1, 3: 2}[d]
+                send(at + place, made.at[i], outs[first + place])
+    for c in sent:
         c.wait()
 
 
@@ -153,10 +163,10 @@
     ]
     return pl.pallas_call(
         attention_kernel,
-        out_shape=[jax.ShapeDtypeStruct((SIDE * ROWS, half), BF)] * (2 * SIDE),
+        out_shape=part_shapes(half) * 2,
         in_specs=[pl.BlockSpec(memory_space=pltpu.SMEM)]
         + [pl.BlockSpec(memory_space=pltpu.HBM)] * len(given),
-        out_specs=[pl.BlockSpec(memory_space=pltpu.HBM)] * (2 * SIDE),
+        out_specs=[pl.BlockSpec(memory_space=pltpu.HBM)] * (2 * PIECES),
         scratch_shapes=[pltpu.VMEM(a.shape, a.dtype) for a in given[:5]]
         + [
             pltpu.VMEM((pages, page, HD), BF),
@@ -165,7 +175,7 @@
             pltpu.VMEM((SIDE * SIDE * TOKENS + 8, HD), F32),
             pltpu.VMEM((SIDE * SIDE, ROWS, HD), F32),
             pltpu.VMEM((2 * SIDE, SIDE * ROWS, half), BF),
-            pltpu.SemaphoreType.DMA((7 + 2 * SIDE,)),
+            pltpu.SemaphoreType.DMA((7 + 2 * PIECES,)),
         ],
         compiler_params=vmem(56),
         name="attention",
@@ -187,17 +197,22 @@
     return total
 
 
+def part_shapes(half):
+    rows = SIDE * ROWS
+    return [jax.ShapeDtypeStruct((n, half), BF) for n in (rows, rows, rows, rows // 2, rows // 2)]
+
+
 def ring_sum(parts, along):
-    half = parts[0].shape[0] // 2
-    near = along(parts[2][:half], 1)
-    far = along(parts[2][half:], 3)
+    half = parts[3].shape[0]
+    near = along(parts[3], 1)
+    far = along(parts[4], 3)
     one = jnp.concatenate([parts[1][:half], add_up([parts[1][half:], far]).astype(BF)], axis=0)
-    three = jnp.concatenate([add_up([parts[3][:half], near]).astype(BF), parts[3][half:]], axis=0)
+    three = jnp.concatenate([add_up([parts[2][:half], near]).astype(BF), parts[2][half:]], axis=0)
     return one, three
 
 
 def sum_first(parts):
-    parts_a, parts_b = parts[:SIDE], parts[SIDE:]
+    parts_a, parts_b = parts[:PIECES], parts[PIECES:]
     one_a, three_a = ring_sum(parts_a, along_x)
     one_b, three_b = ring_sum(parts_b, along_z)
     one_a, three_a, one_b, three_b = lax.optimization_barrier((one_a, three_a, one_b, three_b))
@@ -315,35 +330,12 @@
     )(mine, *rows_a, *rows_b)
 
 
-def expert_kernel(rows, gate_up, down, out, gate_held, up_held, down_held, sems):
-    sources = (gate_up.at[0, 0], gate_up.at[0, 1], down.at[0])
-    copies = [
-        pltpu.make_async_copy(source, buf, sems.at[i])
-        for i, (source, buf) in enumerate(zip(sources, (gate_held, up_held, down_held)))
-    ]
-    first = pl.program_id(0) == 0
-
-    @pl.when(first)
-    def _():
-        for c in copies:
-            c.start()
-        copies[0].wait()
-
+def expert_kernel(rows, gate_up, down, out):
     x = rows[...]
-    gate = dot_nt(x, gate_held[...])
-
-    @pl.when(first)
-    def _():
-        copies[1].wait()
-
-    up = dot_nt(x, up_held[...])
+    gate = dot_nt(x, gate_up[0, 0])
+    up = dot_nt(x, gate_up[0, 1])
     hidden = (gate / (1.0 + jnp.exp(-gate)) * up).astype(BF)
-
-    @pl.when(first)
-    def _():
-        copies[2].wait()
-
-    out[...] = dot(hidden, down_held[...]).astype(BF)
+    out[...] = dot(hidden, down[0]).astype(BF)
 
 
 def experts(rows, gate_up, down):
@@ -355,16 +347,10 @@
         out_shape=jax.ShapeDtypeStruct((count, width), BF),
         in_specs=[
             pl.BlockSpec((step, width), lambda i: (i, 0)),
-            pl.BlockSpec(memory_space=pltpu.HBM),
-            pl.BlockSpec(memory_space=pltpu.HBM),
+            pl.BlockSpec(gate_up.shape, lambda i: (0, 0, 0, 0)),
+            pl.BlockSpec(down.shape, lambda i: (0, 0, 0)),
         ],
         out_specs=pl.BlockSpec((step, width), lambda i: (i, 0)),
-        scratch_shapes=[
-            pltpu.VMEM(gate_up.shape[2:], BF),
-            pltpu.VMEM(gate_up.shape[2:], BF),
-            pltpu.VMEM(down.shape[1:], BF),
-            pltpu.SemaphoreType.DMA((3,)),
-        ],
         compiler_params=vmem(56),
         cost_estimate=pl.CostEstimate(
             flops=6 * count * width * down.shape[1],
@@ -373,30 +359,6 @@
         ),
         name="experts",
     )(rows, gate_up, down)
-
-
-def result_kernel(mix, rows, base, out):
-    routed = dot(mix[...], rows[...])
-    total = routed[:ROWS] + routed[ROWS:] + base[...]
-    out[...] = total[: out.shape[0]].astype(BF)
-
-
-def result(mix, rows, base, tok_rows):
-    count, width = rows.shape
-    step = 512
-    return pl.pallas_call(
-        result_kernel,
-        grid=(width // step,),
-        out_shape=jax.ShapeDtypeStruct((tok_rows, width), BF),
-        in_specs=[
-            pl.BlockSpec(mix.shape, lambda i: (0, 0)),
-            pl.BlockSpec((count, step), lambda i: (0, i)),
-            pl.BlockSpec((ROWS, step), lambda i: (0, i)),
-        ],
-        out_specs=pl.BlockSpec((tok_rows, step), lambda i: (0, i)),
-        compiler_params=vmem(32),
-        name="result",
-    )(mix, rows, base)
 
 
 def shared_kernel(*refs):
@@ -415,11 +377,16 @@
         gate = dot_nt(a, gate_up[0, :, :half]) + dot_nt(b, gate_up[0, :, half:])
         up = dot_nt(a, gate_up[1, :, :half]) + dot_nt(b, gate_up[1, :, half:])
         hidden[x] = (gate / (1.0 + jnp.exp(-gate)) * up).reshape(SIDE, ROWS, -1)
+    middle = SIDE * ROWS // 2
     for d in range(SIDE):
-        part = hidden[d].reshape(SIDE * ROWS, -1)
-        outs[d][...] = dot(part.astype(BF), down[:, :half]).astype(BF)
-        part = hidden[:, d].reshape(SIDE * ROWS, -1)
-        outs[SIDE + d][...] = dot(part.astype(BF), down[:, half:]).astype(BF)
+        for f, part in enumerate((hidden[d], hidden[:, d])):
+            part = part.reshape(SIDE * ROWS, -1).astype(BF)
+            made = dot(part, down[:, f * half : (f + 1) * half]).astype(BF)
+            if d == 2:
+                outs[f * PIECES + 3][...] = made[:middle]
+                outs[f * PIECES + 4][...] = made[middle:]
+            else:
+                outs[f * PIECES + {0: 0, 1: 1, 3: 2}[d]][...] = made
 
 
 def shared_expert(rows_a, rows_b, gate_up, down):
@@ -427,7 +394,7 @@
     count, width = SIDE * SIDE * ROWS, down.shape[1]
     return pl.pallas_call(
         shared_kernel,
-        out_shape=[jax.ShapeDtypeStruct((SIDE * ROWS, half), BF)] * (2 * SIDE),
+        out_shape=part_shapes(half) * 2,
         scratch_shapes=[pltpu.VMEM((SIDE, SIDE, ROWS, down.shape[0]), F32)],
         compiler_params=vmem(48),
         cost_estimate=pl.CostEstimate(
@@ -524,8 +491,10 @@
     )
     shared = jnp.concatenate([add_up(got_a), add_up(got_b)], axis=1)
     shared_scale = jax.nn.sigmoid(dot(normed, shared_gate))
-    base = stream.astype(F32) + shared_scale[:, None] * shared
-    return result(mix, returned.reshape(devices * capacity, width), base, tok_rows)
+    routed = dot(mix, returned.reshape(devices * capacity, width))
+    routed = routed[:ROWS] + routed[ROWS:]
+    result = stream.astype(F32) + routed + shared_scale[:, None] * shared
+    return result[:tok_rows].astype(BF)
 
 
 def solution(mesh):

time: 249 us -> 245 us (0.984)
  Pallas kernels: 47.4 us -> 40.8 us
  matrix products: 0.19 us -> 3.15 us
    pallas_call x3 -> x2, Pallas kernels: 23.4 us -> 19 us  [the longest x1 10.8 us: shared_expert(): pl.pallas_call(shared_kernel, out_shape=part_shapes(half) * 2, scratch_sh...]
    dot_general x1 -> x2, matrix products: 0.19 us -> 3.15 us  [dot(): return jnp.dot(a, b, preferred_element_type=F32)]
  transfers between devices with their start and end apart: 44 -> 44, of which waited for: 28 -> 27; matrix products, arithmetic and copies ran while one was open for 3% -> 4% of each run, Pallas kernels for 4% -> 4%
where the time goes in v7:
time: 245 us; the launch traced here: 243 us
  waiting for transfers between devices  117 us (48%)
  starting transfers between devices  68 us (28%)
  Pallas kernels  40.8 us (17%)
  local copies, waits for them, and re-layouts  6.55 us (3%)
  other arithmetic  6.14 us (3%)
  matrix products  3.15 us (1%)
    all_to_all x1, waiting for transfers between devices, on_device(): lax.all_to_all(answer.reshape(devices, capacity, width), ('req', 'exp'),...  50.4 us
    ppermute x21, waiting for transfers between devices, along_z(): return lax.ppermute(a, 'exp', [(i, i ^ d) for i in range(SIDE * SIDE)])  40.3 us
    ppermute x21, starting transfers between devices, along_x(): lax.ppermute(a, 'exp', [(i, i ^ d * SIDE) for i in range(SIDE * SIDE)])  27.7 us
    ppermute x21, starting transfers between devices, along_z(): return lax.ppermute(a, 'exp', [(i, i ^ d) for i in range(SIDE * SIDE)])  27.5 us
    ppermute x21, waiting for transfers between devices, along_x(): lax.ppermute(a, 'exp', [(i, i ^ d * SIDE) for i in range(SIDE * SIDE)])  26.5 us
    pallas_call x1, Pallas kernels, experts(): pl.pallas_call(expert_kernel, grid=(count // step,), out_shape=jax.ShapeD...  15.7 us
    pallas_call x1, Pallas kernels, shared_expert(): pl.pallas_call(shared_kernel, out_shape=part_shapes(half) * 2, scratch_sh...  10.8 us
    pallas_call x1, Pallas kernels, attention(): pl.pallas_call(attention_kernel, out_shape=part_shapes(half) * 2, in_spec...  8.23 us
  transfers between devices with their start and end apart: 44, of which 27 were waited for; matrix products, arithmetic and copies ran while one was open for 4% of the time, Pallas kernels for 4%

profile of v7, /device:TPU:8, one launch (start us, length us, event | category | flops | bytes accessed | tf_op | source)
XLA Modules:
  0.0 242.6 jit_solution(14930080733175931316)
XLA Ops:
  0.0 8.2 %attention.1 = (bf16[288,1024]{1,0:T(8,128)(2,1)}, bf16[288,1024]{1,0:T(8,128)(2,1)}, bf16[288,1024]{1,0:T(8,128)(2,1)}, bf16[144,1024]{1,0:T(8,128)(2,1)}, bf16...) custom-call(s32[1]{0:T(128)} %bitcast.mine, ...), custom_call_target="tpu_custom_call" | custom-call | tf_op jit(solution)/shard_map/attention/pallas_call | solution.py:164
  8.3 2.0 collective-permute-start.3
  10.3 2.5 %collective-permute-start.2 = (bf16[144,1024]{1,0:T(8,128)(2,1)}, bf16[144,1024]{1,0:T(8,128)(2,1)S(1)}, u32[]{:S(2)}, u32[]{:S(2)}) collective-permute-start(bf16[144,1024]{1,0:T(8,128)(2,1)} %get-tuple-element.56), channel_id=1, source_target_pairs={{0,3},{1,2},{2,1},{3,0},{4,7},{5,6},{6,5},{7,4},{8,11},{9,10},{10,... | collective-permute-start | bytes 884744 | tf_op jit(solution)/shard_map/ppermute | solution.py:190
  12.8 1.5 collective-permute-start.1
  14.3 2.1 collective-permute-start
  18.6 1.5 collective-permute-done.2
  21.4 2.2 collective-permute-done
  25.7 2.1 collective-permute-start.5
  31.2 6.0 %collective-permute-done.6 = bf16[288,1024]{1,0:T(8,128)(2,1)} collective-permute-done((bf16[288,1024]{1,0:T(8,128)(2,1)S(1)}, bf16[288,1024]{1,0:T(8,128)(2,1)}, u32[]{:S(2)}, u32[]{:S(2)}) %collective-permute-start.6) | collective-permute-done | bytes 589856 | tf_op jit(solution)/shard_map/ppermute | solution.py:190
  37.2 2.0 collective-permute-done.7
  39.2 1.6 add_convert_fusion.2
  40.8 1.4 add_convert_fusion.3
  44.1 2.1 collective-permute-start.12
  46.2 1.4 collective-permute-start.13
  50.1 1.6 collective-permute-start.9
  52.9 3.5 %collective-permute-done.9.a2 = bf16[72,1024]{1,0:T(8,128)(2,1)S(1)} collective-permute-done((bf16[72,1024]{1,0:T(8,128)(2,1)S(1)}, bf16[72,1024]{1,0:T(8,128)(2,1)S(1)}, u32[]{:S(2)}, u32[]{:S(2)}) %collective-permute-start.9) | collective-permute-done | bytes 147488 | tf_op jit(solution)/shard_map/ppermute | solution.py:190
  57.3 3.2 %collective-permute-start.18 = (bf16[72,1024]{1,0:T(8,128)(2,1)S(1)}, bf16[72,1024]{1,0:T(8,128)(2,1)S(1)}, u32[]{:S(2)}, u32[]{:S(2)}) collective-permute-start(bf16[72,1024]{1,0:T(8,128)(2,1)S(1)} %get-tuple-element.117), channel_id=1, source_target_pairs={{0,8},{1,9},{2,10},{3,11},{4,12},{5,13},{6,14},{7,15},{8,0},{9,1},... | collective-permute-start | bytes 442376 | tf_op jit(solution)/shard_map/ppermute | solution.py:186
  61.6 3.1 %collective-permute-start.15 = (bf16[72,1024]{1,0:T(8,128)(2,1)S(1)}, bf16[72,1024]{1,0:T(8,128)(2,1)S(1)}, u32[]{:S(2)}, u32[]{:S(2)}) collective-permute-start(bf16[72,1024]{1,0:T(8,128)(2,1)S(1)} %get-tuple-element.118), channel_id=1, source_target_pairs={{0,2},{1,3},{2,0},{3,1},{4,6},{5,7},{6,4},{7,5},{8,10},{9,11},{10,... | collective-permute-start | bytes 442376 | tf_op jit(solution)/shard_map/ppermute | solution.py:190
  64.7 1.6 collective-permute-start.16
  66.9 2.5 %collective-permute-done.15 = bf16[72,1024]{1,0:T(8,128)(2,1)S(1)} collective-permute-done((bf16[72,1024]{1,0:T(8,128)(2,1)S(1)}, bf16[72,1024]{1,0:T(8,128)(2,1)S(1)}, u32[]{:S(2)}, u32[]{:S(2)}) %collective-permute-start.15) | collective-permute-done | bytes 147488 | tf_op jit(solution)/shard_map/ppermute | solution.py:190
  69.4 3.1 %collective-permute-done.16 = bf16[72,1024]{1,0:T(8,128)(2,1)S(1)} collective-permute-done((bf16[72,1024]{1,0:T(8,128)(2,1)S(1)}, bf16[72,1024]{1,0:T(8,128)(2,1)S(1)}, u32[]{:S(2)}, u32[]{:S(2)}) %collective-permute-start.16) | collective-permute-done | bytes 147488 | tf_op jit(solution)/shard_map/ppermute | solution.py:190
  72.6 2.4 collective-permute-start.21
  74.9 1.6 collective-permute-start.25
  76.5 10.4 %collective-permute-done.21.refs_2_ = bf16[4,72,1024]{2,1,0:T(8,128)(2,1)S(1)} collective-permute-done((bf16[4,72,1024]{2,1,0:T(8,128)(2,1)S(1)}, bf16[4,72,1024]{2,1,0:T(8,128)(2,1)S(1)}, u32[]{:S(2)}, u32[]{:S(2)}) %collective-permute-start.21) | collective-permute-done | bytes 589856 | tf_op jit(solution)/shard_map/ppermute | solution.py:186
  87.1 2.4 collective-permute-start.23
  89.6 1.7 collective-permute-start.27
  91.3 2.4 collective-permute-done.22.refs_3_
  93.7 1.4 collective-permute-done.23.refs_4_
  96.3 1.4 collective-permute-done.27.refs_9_
  98.4 5.7 %pick.1 = bf16[8,16,8,2048]{3,2,1,0:T(8,128)(2,1)} custom-call(s32[1]{0:T(128)} %bitcast.mine, bf16[4,72,1024]{2,1,0:T(8,128)(2,1)} %copy-done.10, bf16[4,72,1024]{2,1,0:T(8,128)(2,1)} %copy-done.12, bf16[4,72,1024]{2,1,0:T(8,128)(2,1)} %copy-done.11, bf16[2,72,1024]{2,1,0:T(8,128)(2,1)} %copy-done, bf16[2,72,1024]{2,1,0:T(8,128)(2,1)} %copy-done.2, ...), custom_call_target="tpu_custom_call" | custom-call | tf_op jit(solution)/shard_map/pick/pallas_call | solution.py:323
  104.1 5.1 %all-to-all-start = ((bf16[8,128,2048]{2,1,0:T(8,128)(2,1)}), bf16[8,128,2048]{2,1,0:T(8,128)(2,1)}, u32[]{:S(2)}, u32[]{:S(2)}) async-start(bf16[8,128,2048]{2,1,0:T(8,128)(2,1)} %bitcast.74), calls=%async_computation | async-start | bytes 8388608 | tf_op jit(solution)/shard_map/all_to_all | solution.py:474
  109.2 10.8 %shared_expert.1 = (bf16[288,1024]{1,0:T(8,128)(2,1)S(1)}, bf16[288,1024]{1,0:T(8,128)(2,1)S(1)}, bf16[288,1024]{1,0:T(8,128)(2,1)S(1)}, bf16[144,1024]{1,0:T(8,...) custom-call(bf16[4,72,1024]{2,1,0:T(8,128)(2,1)} %copy-done.10, ...), custom_call_target="tpu_custom_call" | custom-call | flops 4982833152 | bytes 13762560 | tf_op jit(solution)/shard_map/shared_expert/pallas_call | solution.py:395
  120.9 1.6 collective-permute-start.30
  122.5 1.9 collective-permute-start.29
  125.6 3.6 %collective-permute-done.31 = bf16[144,1024]{1,0:T(8,128)(2,1)S(1)} collective-permute-done((bf16[144,1024]{1,0:T(8,128)(2,1)S(1)}, bf16[144,1024]{1,0:T(8,128)(2,1)S(1)}, u32[]{:S(2)}, u32[]{:S(2)}) %collective-permute-start.31) | collective-permute-done | bytes 294944 | tf_op jit(solution)/shard_map/ppermute | solution.py:190
  129.2 1.7 collective-permute-done.30
  131.4 2.8 %collective-permute-done.28 = bf16[144,1024]{1,0:T(8,128)(2,1)S(1)} collective-permute-done((bf16[144,1024]{1,0:T(8,128)(2,1)S(1)}, bf16[144,1024]{1,0:T(8,128)(2,1)S(1)}, u32[]{:S(2)}, u32[]{:S(2)}) %collective-permute-start.28) | collective-permute-done | bytes 294944 | tf_op jit(solution)/shard_map/ppermute | solution.py:186
  135.0 1.6 collective-permute-start.35
  137.6 10.3 %collective-permute-done.34 = bf16[288,1024]{1,0:T(8,128)(2,1)S(1)} collective-permute-done((bf16[288,1024]{1,0:T(8,128)(2,1)S(1)}, bf16[288,1024]{1,0:T(8,128)(2,1)S(1)}, u32[]{:S(2)}, u32[]{:S(2)}) %collective-permute-start.34) | collective-permute-done | bytes 589856 | tf_op jit(solution)/shard_map/ppermute | solution.py:190
  148.0 1.5 collective-permute-done.35
  152.1 1.6 collective-permute-start.37
  153.7 1.7 collective-permute-start.38
  157.1 2.6 %collective-permute-start.41 = (bf16[72,1024]{1,0:T(8,128)(2,1)S(1)}, bf16[72,1024]{1,0:T(8,128)(2,1)S(1)}, u32[]{:S(2)}, u32[]{:S(2)}) collective-permute-start(bf16[72,1024]{1,0:T(8,128)(2,1)S(1)} %get-tuple-element.99), channel_id=1, source_target_pairs={{0,8},{1,9},{2,10},{3,11},{4,12},{5,13},{6,14},{7,15},{8,0},{9,1},... | collective-permute-start | bytes 442376 | tf_op jit(solution)/shard_map/ppermute | solution.py:186
  160.7 3.3 %collective-permute-done.40 = bf16[72,1024]{1,0:T(8,128)(2,1)S(1)} collective-permute-done((bf16[72,1024]{1,0:T(8,128)(2,1)S(1)}, bf16[72,1024]{1,0:T(8,128)(2,1)S(1)}, u32[]{:S(2)}, u32[]{:S(2)}) %collective-permute-start.40) | collective-permute-done | bytes 147488 | tf_op jit(solution)/shard_map/ppermute | solution.py:186
  164.0 15.7 %experts.1 = bf16[1024,2048]{1,0:T(8,128)(2,1)} custom-call(bf16[1024,2048]{1,0:T(8,128)(2,1)} %bitcast.35.rows, bf16[1,2,704,2048]{3,2,1,0:T(8,128)(2,1)} %bitcast.89, bf16[1,704,2048]{2,1,0:T(8,128)(2,1)} %down.1), custom_call_target="tpu_custom_call" | custom-call | flops 8858370048 | bytes 17039360 | tf_op jit(solution)/shard_map/experts/pallas_call | solution.py:344
  179.7 7.8 %all-to-all-start.1 = ((bf16[128,8,2048]{2,1,0:T(8,128)(2,1)}), bf16[128,8,2048]{2,1,0:T(8,128)(2,1)}, u32[]{:S(2)}, u32[]{:S(2)}) async-start(bf16[128,8,2048]{2,1,0:T(8,128)(2,1)} %bitcast.75), calls=%async_computation.1 | async-start | bytes 8388608 | tf_op jit(solution)/shard_map/all_to_all | solution.py:485
  188.3 50.4 %all-to-all-done.1 = bf16[128,8,2048]{2,1,0:T(8,128)(2,1)} async-done(((bf16[128,8,2048]{2,1,0:T(8,128)(2,1)}), bf16[128,8,2048]{2,1,0:T(8,128)(2,1)}, u32[]{:S(2)}, u32[]{:S(2)}) %all-to-all-start.1) | async-done | bytes 4194336 | tf_op jit(solution)/shard_map/all_to_all | solution.py:485
  238.7 3.0 %fusion = f32[144,2048]{1,0:T(8,128)S(1)} fusion(bf16[128,8,2048]{2,1,0:T(8,128)(2,1)} %all-to-all-done.1, bf16[72,1024]{1,0:T(8,128)(2,1)S(1)} %get-tuple-element.95, bf16[72,1024]{1,0:T(8,128)(2,1)S(1)} %get-tuple-element.96), kind=kOutput, calls=%fused_computation | convolution fusion | flops 604569600 | bytes 5668864 | tf_op jit(solution)/shard_map/dot_general | solution.py:29
  (153 shorter events, 30.5 us)
Async XLA Ops:
  8.3 10.2 %collective-permute-start.3 = (bf16[144,1024]{1,0:T(8,128)(2,1)}, bf16[144,1024]{1,0:T(8,128)(2,1)S(1)}, u32[]{:S(2)}, u32[]{:S(2)}) collective-permute-start(bf16[144,1024]{1,0:T(8,128)(2,1)} %get-tuple-element.58), channel_id=1, source_target_pairs={{0,1},{1,0},{2,3},{3,2},{4,5},{5,4},{6,7},{7,6},{8,9},{9,8},{10,11... | collective-permute-start | bytes 884744 | tf_op jit(solution)/shard_map/ppermute | solution.py:190
  10.3 9.9 %collective-permute-start.2 = (bf16[144,1024]{1,0:T(8,128)(2,1)}, bf16[144,1024]{1,0:T(8,128)(2,1)S(1)}, u32[]{:S(2)}, u32[]{:S(2)}) collective-permute-start(bf16[144,1024]{1,0:T(8,128)(2,1)} %get-tuple-element.56), channel_id=1, source_target_pairs={{0,3},{1,2},{2,1},{3,0},{4,7},{5,6},{6,5},{7,4},{8,11},{9,10},{10,... | collective-permute-start | bytes 884744 | tf_op jit(solution)/shard_map/ppermute | solution.py:190
  12.8 8.4 %collective-permute-start.1 = (bf16[144,1024]{1,0:T(8,128)(2,1)}, bf16[144,1024]{1,0:T(8,128)(2,1)S(1)}, u32[]{:S(2)}, u32[]{:S(2)}) collective-permute-start(bf16[144,1024]{1,0:T(8,128)(2,1)} %get-tuple-element.54), channel_id=1, source_target_pairs={{0,4},{1,5},{2,6},{3,7},{4,0},{5,1},{6,2},{7,3},{8,12},{9,13},{10,... | collective-permute-start | bytes 884744 | tf_op jit(solution)/shard_map/ppermute | solution.py:186
  14.3 9.3 %collective-permute-start = (bf16[144,1024]{1,0:T(8,128)(2,1)}, bf16[144,1024]{1,0:T(8,128)(2,1)S(1)}, u32[]{:S(2)}, u32[]{:S(2)}) collective-permute-start(bf16[144,1024]{1,0:T(8,128)(2,1)} %get-tuple-element.52), channel_id=1, source_target_pairs={{0,12},{1,13},{2,14},{3,15},{4,8},{5,9},{6,10},{7,11},{8,4},{9,5},... | collective-permute-start | bytes 884744 | tf_op jit(solution)/shard_map/ppermute | solution.py:186
  21.4 17.8 %copy-start.20 = (bf16[288,1024]{1,0:T(8,128)(2,1)S(1)}, bf16[288,1024]{1,0:T(8,128)(2,1)}, u32[]{:S(2)}) copy-start(bf16[288,1024]{1,0:T(8,128)(2,1)} %get-tuple-element.61) | copy-start | bytes 1769476
  23.7 13.5 %collective-permute-start.6 = (bf16[288,1024]{1,0:T(8,128)(2,1)S(1)}, bf16[288,1024]{1,0:T(8,128)(2,1)}, u32[]{:S(2)}, u32[]{:S(2)}) collective-permute-start(bf16[288,1024]{1,0:T(8,128)(2,1)S(1)} %pad_maximum_fusion.3), channel_id=1, source_target_pairs={{0,1},{1,0},{2,3},{3,2},{4,5},{5,4},{6,7},{7,6},{8,9},{9,8},{10,11... | collective-permute-start | bytes 1769480 | tf_op jit(solution)/shard_map/ppermute | solution.py:190
  24.8 14.3 %collective-permute-start.7 = (bf16[288,1024]{1,0:T(8,128)(2,1)S(1)}, bf16[288,1024]{1,0:T(8,128)(2,1)}, u32[]{:S(2)}, u32[]{:S(2)}) collective-permute-start(bf16[288,1024]{1,0:T(8,128)(2,1)S(1)} %pad_maximum_fusion.4), channel_id=1, source_target_pairs={{0,3},{1,2},{2,1},{3,0},{4,7},{5,6},{6,5},{7,4},{8,11},{9,10},{10,... | collective-permute-start | bytes 1769480 | tf_op jit(solution)/shard_map/ppermute | solution.py:190
  25.7 15.1 %collective-permute-start.4 = (bf16[288,1024]{1,0:T(8,128)(2,1)S(1)}, bf16[288,1024]{1,0:T(8,128)(2,1)S(1)}, u32[]{:S(2)}, u32[]{:S(2)}) collective-permute-start(bf16[288,1024]{1,0:T(8,128)(2,1)S(1)} %pad_maximum_fusion.1), channel_id=1, source_target_pairs={{0,4},{1,5},{2,6},{3,7},{4,0},{5,1},{6,2},{7,3},{8,12},{9,13},{10,... | collective-permute-start | bytes 1769480 | tf_op jit(solution)/shard_map/ppermute | solution.py:186
  25.7 15.1 %collective-permute-start.5 = (bf16[288,1024]{1,0:T(8,128)(2,1)S(1)}, bf16[288,1024]{1,0:T(8,128)(2,1)}, u32[]{:S(2)}, u32[]{:S(2)}) collective-permute-start(bf16[288,1024]{1,0:T(8,128)(2,1)S(1)} %pad_maximum_fusion.2), channel_id=1, source_target_pairs={{0,12},{1,13},{2,14},{3,15},{4,8},{5,9},{6,10},{7,11},{8,4},{9,5},... | collective-permute-start | bytes 1769480 | tf_op jit(solution)/shard_map/ppermute | solution.py:186
  42.3 14.1 %copy-start.8 = (f32[2048]{0:T(1024)S(1)}, f32[2048]{0:T(1024)}, u32[]{:S(2)}) copy-start(f32[2048]{0:T(1024)} %param.22) | copy-start | bytes 24580
  42.3 7.8 %collective-permute-start.10 = (bf16[72,1024]{1,0:T(8,128)(2,1)S(1)}, bf16[72,1024]{1,0:T(8,128)(2,1)S(1)}, u32[]{:S(2)}, u32[]{:S(2)}) collective-permute-start(bf16[72,1024]{1,0:T(8,128)(2,1)S(1)} %get-tuple-element.111), channel_id=1, source_target_pairs={{0,2},{1,3},{2,0},{3,1},{4,6},{5,7},{6,4},{7,5},{8,10},{9,11},{10,... | collective-permute-start | bytes 442376 | tf_op jit(solution)/shard_map/ppermute | solution.py:190
  43.5 8.2 %collective-permute-start.11 = (bf16[72,1024]{1,0:T(8,128)(2,1)S(1)}, bf16[72,1024]{1,0:T(8,128)(2,1)S(1)}, u32[]{:S(2)}, u32[]{:S(2)}) collective-permute-start(bf16[72,1024]{1,0:T(8,128)(2,1)S(1)} %get-tuple-element.109), channel_id=1, source_target_pairs={{0,4},{1,5},{2,6},{3,7},{4,0},{5,1},{6,2},{7,3},{8,12},{9,13},{10,... | collective-permute-start | bytes 442376 | tf_op jit(solution)/shard_map/ppermute | solution.py:186
  44.1 7.6 %collective-permute-start.12 = (bf16[72,1024]{1,0:T(8,128)(2,1)S(1)}, bf16[72,1024]{1,0:T(8,128)(2,1)S(1)}, u32[]{:S(2)}, u32[]{:S(2)}) collective-permute-start(bf16[72,1024]{1,0:T(8,128)(2,1)S(1)} %get-tuple-element.108), channel_id=1, source_target_pairs={{0,12},{1,13},{2,14},{3,15},{4,8},{5,9},{6,10},{7,11},{8,4},{9,5},... | collective-permute-start | bytes 442376 | tf_op jit(solution)/shard_map/ppermute | solution.py:186
  46.2 6.6 %collective-permute-start.13 = (bf16[72,1024]{1,0:T(8,128)(2,1)S(1)}, bf16[72,1024]{1,0:T(8,128)(2,1)S(1)}, u32[]{:S(2)}, u32[]{:S(2)}) collective-permute-start(bf16[72,1024]{1,0:T(8,128)(2,1)S(1)} %get-tuple-element.107), channel_id=1, source_target_pairs={{0,8},{1,9},{2,10},{3,11},{4,12},{5,13},{6,14},{7,15},{8,0},{9,1},... | collective-permute-start | bytes 442376 | tf_op jit(solution)/shard_map/ppermute | solution.py:186
  47.7 5.2 %collective-permute-start.8 = (bf16[72,1024]{1,0:T(8,128)(2,1)S(1)}, bf16[72,1024]{1,0:T(8,128)(2,1)S(1)}, u32[]{:S(2)}, u32[]{:S(2)}) collective-permute-start(bf16[72,1024]{1,0:T(8,128)(2,1)S(1)} %get-tuple-element.113), channel_id=1, source_target_pairs={{0,1},{1,0},{2,3},{3,2},{4,5},{5,4},{6,7},{7,6},{8,9},{9,8},{10,11... | collective-permute-start | bytes 442376 | tf_op jit(solution)/shard_map/ppermute | solution.py:190
  50.1 6.4 %collective-permute-start.9 = (bf16[72,1024]{1,0:T(8,128)(2,1)S(1)}, bf16[72,1024]{1,0:T(8,128)(2,1)S(1)}, u32[]{:S(2)}, u32[]{:S(2)}) collective-permute-start(bf16[72,1024]{1,0:T(8,128)(2,1)S(1)} %get-tuple-element.112), channel_id=1, source_target_pairs={{0,3},{1,2},{2,1},{3,0},{4,7},{5,6},{6,5},{7,4},{8,11},{9,10},{10,... | collective-permute-start | bytes 442376 | tf_op jit(solution)/shard_map/ppermute | solution.py:190
  56.8 7.9 %collective-permute-start.17 = (bf16[72,1024]{1,0:T(8,128)(2,1)S(1)}, bf16[72,1024]{1,0:T(8,128)(2,1)S(1)}, u32[]{:S(2)}, u32[]{:S(2)}) collective-permute-start(bf16[72,1024]{1,0:T(8,128)(2,1)S(1)} %get-tuple-element.117), channel_id=1, source_target_pairs={{0,4},{1,5},{2,6},{3,7},{4,0},{5,1},{6,2},{7,3},{8,12},{9,13},{10,... | collective-permute-start | bytes 442376 | tf_op jit(solution)/shard_map/ppermute | solution.py:186
  57.3 9.0 %collective-permute-start.18 = (bf16[72,1024]{1,0:T(8,128)(2,1)S(1)}, bf16[72,1024]{1,0:T(8,128)(2,1)S(1)}, u32[]{:S(2)}, u32[]{:S(2)}) collective-permute-start(bf16[72,1024]{1,0:T(8,128)(2,1)S(1)} %get-tuple-element.117), channel_id=1, source_target_pairs={{0,8},{1,9},{2,10},{3,11},{4,12},{5,13},{6,14},{7,15},{8,0},{9,1},... | collective-permute-start | bytes 442376 | tf_op jit(solution)/shard_map/ppermute | solution.py:186
  60.5 6.4 %collective-permute-start.19 = (bf16[72,1024]{1,0:T(8,128)(2,1)S(1)}, bf16[72,1024]{1,0:T(8,128)(2,1)S(1)}, u32[]{:S(2)}, u32[]{:S(2)}) collective-permute-start(bf16[72,1024]{1,0:T(8,128)(2,1)S(1)} %get-tuple-element.117), channel_id=1, source_target_pairs={{0,12},{1,13},{2,14},{3,15},{4,8},{5,9},{6,10},{7,11},{8,4},{9,5},... | collective-permute-start | bytes 442376 | tf_op jit(solution)/shard_map/ppermute | solution.py:186
  61.6 5.3 %collective-permute-start.14 = (bf16[72,1024]{1,0:T(8,128)(2,1)S(1)}, bf16[72,1024]{1,0:T(8,128)(2,1)S(1)}, u32[]{:S(2)}, u32[]{:S(2)}) collective-permute-start(bf16[72,1024]{1,0:T(8,128)(2,1)S(1)} %get-tuple-element.118), channel_id=1, source_target_pairs={{0,1},{1,0},{2,3},{3,2},{4,5},{5,4},{6,7},{7,6},{8,9},{9,8},{10,11... | collective-permute-start | bytes 442376 | tf_op jit(solution)/shard_map/ppermute | solution.py:190
  61.6 7.8 %collective-permute-start.15 = (bf16[72,1024]{1,0:T(8,128)(2,1)S(1)}, bf16[72,1024]{1,0:T(8,128)(2,1)S(1)}, u32[]{:S(2)}, u32[]{:S(2)}) collective-permute-start(bf16[72,1024]{1,0:T(8,128)(2,1)S(1)} %get-tuple-element.118), channel_id=1, source_target_pairs={{0,2},{1,3},{2,0},{3,1},{4,6},{5,7},{6,4},{7,5},{8,10},{9,11},{10,... | collective-permute-start | bytes 442376 | tf_op jit(solution)/shard_map/ppermute | solution.py:190
  64.7 7.8 %collective-permute-start.16 = (bf16[72,1024]{1,0:T(8,128)(2,1)S(1)}, bf16[72,1024]{1,0:T(8,128)(2,1)S(1)}, u32[]{:S(2)}, u32[]{:S(2)}) collective-permute-start(bf16[72,1024]{1,0:T(8,128)(2,1)S(1)} %get-tuple-element.118), channel_id=1, source_target_pairs={{0,3},{1,2},{2,1},{3,0},{4,7},{5,6},{6,5},{7,4},{8,11},{9,10},{10,... | collective-permute-start | bytes 442376 | tf_op jit(solution)/shard_map/ppermute | solution.py:190
  66.9 20.1 %copy-start.9 = (bf16[4,72,1024]{2,1,0:T(8,128)(2,1)}, bf16[4,72,1024]{2,1,0:T(8,128)(2,1)S(1)}, u32[]{:S(2)}) copy-start(bf16[4,72,1024]{2,1,0:T(8,128)(2,1)S(1)} %pad_maximum_fusion.6.refs_5_) | copy-start | bytes 1769476
  72.6 17.1 %copy-start.10 = (bf16[4,72,1024]{2,1,0:T(8,128)(2,1)}, bf16[4,72,1024]{2,1,0:T(8,128)(2,1)S(1)}, u32[]{:S(2)}) copy-start(bf16[4,72,1024]{2,1,0:T(8,128)(2,1)S(1)} %pad_maximum_fusion.5.refs_0_) | copy-start | bytes 1769476
  72.6 14.3 %collective-permute-start.21 = (bf16[4,72,1024]{2,1,0:T(8,128)(2,1)S(1)}, bf16[4,72,1024]{2,1,0:T(8,128)(2,1)S(1)}, u32[]{:S(2)}, u32[]{:S(2)}) collective-permute-start(bf16[4,72,1024]{2,1,0:T(8,128)(2,1)S(1)} %pad_maximum_fusion.5.refs_0_), channel_id=1, source_target_pairs={{0,12},{1,13},{2,14},{3,15},{4,8},{5,9},{6,10},{7,11},{8,4},{9,5},... | collective-permute-start | bytes 1769480 | tf_op jit(solution)/shard_map/ppermute | solution.py:186
  74.9 12.1 %collective-permute-start.20 = (bf16[4,72,1024]{2,1,0:T(8,128)(2,1)S(1)}, bf16[4,72,1024]{2,1,0:T(8,128)(2,1)S(1)}, u32[]{:S(2)}, u32[]{:S(2)}) collective-permute-start(bf16[4,72,1024]{2,1,0:T(8,128)(2,1)S(1)} %pad_maximum_fusion.5.refs_0_), channel_id=1, source_target_pairs={{0,4},{1,5},{2,6},{3,7},{4,0},{5,1},{6,2},{7,3},{8,12},{9,13},{10,... | collective-permute-start | bytes 1769480 | tf_op jit(solution)/shard_map/ppermute | solution.py:186
  74.9 14.5 %collective-permute-start.25 = (bf16[4,72,1024]{2,1,0:T(8,128)(2,1)S(1)}, bf16[4,72,1024]{2,1,0:T(8,128)(2,1)S(1)}, u32[]{:S(2)}, u32[]{:S(2)}) collective-permute-start(bf16[4,72,1024]{2,1,0:T(8,128)(2,1)S(1)} %pad_maximum_fusion.6.refs_5_), channel_id=1, source_target_pairs={{0,3},{1,2},{2,1},{3,0},{4,7},{5,6},{6,5},{7,4},{8,11},{9,10},{10,... | collective-permute-start | bytes 1769480 | tf_op jit(solution)/shard_map/ppermute | solution.py:190
  76.5 13.0 %collective-permute-start.24 = (bf16[4,72,1024]{2,1,0:T(8,128)(2,1)S(1)}, bf16[4,72,1024]{2,1,0:T(8,128)(2,1)S(1)}, u32[]{:S(2)}, u32[]{:S(2)}) collective-permute-start(bf16[4,72,1024]{2,1,0:T(8,128)(2,1)S(1)} %pad_maximum_fusion.6.refs_5_), channel_id=1, source_target_pairs={{0,1},{1,0},{2,3},{3,2},{4,5},{5,4},{6,7},{7,6},{8,9},{9,8},{10,11... | collective-permute-start | bytes 1769480 | tf_op jit(solution)/shard_map/ppermute | solution.py:190
  86.9 6.8 %collective-permute-start.22 = (bf16[2,72,1024]{2,1,0:T(8,128)(2,1)S(1)}, bf16[2,72,1024]{2,1,0:T(8,128)(2,1)S(1)}, u32[]{:S(2)}, u32[]{:S(2)}) collective-permute-start(bf16[2,72,1024]{2,1,0:T(8,128)(2,1)S(1)} %slice.165), channel_id=1, source_target_pairs={{0,4},{1,5},{2,6},{3,7},{4,0},{5,1},{6,2},{7,3},{8,12},{9,13},{10,... | collective-permute-start | bytes 884744 | tf_op jit(solution)/shard_map/ppermute | solution.py:186
  87.1 8.0 %collective-permute-start.23 = (bf16[2,72,1024]{2,1,0:T(8,128)(2,1)S(1)}, bf16[2,72,1024]{2,1,0:T(8,128)(2,1)S(1)}, u32[]{:S(2)}, u32[]{:S(2)}) collective-permute-start(bf16[2,72,1024]{2,1,0:T(8,128)(2,1)S(1)} %slice.166), channel_id=1, source_target_pairs={{0,12},{1,13},{2,14},{3,15},{4,8},{5,9},{6,10},{7,11},{8,4},{9,5},... | collective-permute-start | bytes 884744 | tf_op jit(solution)/shard_map/ppermute | solution.py:186
  89.5 6.8 %collective-permute-start.26 = (bf16[2,72,1024]{2,1,0:T(8,128)(2,1)S(1)}, bf16[2,72,1024]{2,1,0:T(8,128)(2,1)S(1)}, u32[]{:S(2)}, u32[]{:S(2)}) collective-permute-start(bf16[2,72,1024]{2,1,0:T(8,128)(2,1)S(1)} %slice.167), channel_id=1, source_target_pairs={{0,1},{1,0},{2,3},{3,2},{4,5},{5,4},{6,7},{7,6},{8,9},{9,8},{10,11... | collective-permute-start | bytes 884744 | tf_op jit(solution)/shard_map/ppermute | solution.py:190
  89.6 8.0 %collective-permute-start.27 = (bf16[2,72,1024]{2,1,0:T(8,128)(2,1)S(1)}, bf16[2,72,1024]{2,1,0:T(8,128)(2,1)S(1)}, u32[]{:S(2)}, u32[]{:S(2)}) collective-permute-start(bf16[2,72,1024]{2,1,0:T(8,128)(2,1)S(1)} %slice.168), channel_id=1, source_target_pairs={{0,3},{1,2},{2,1},{3,0},{4,7},{5,6},{6,5},{7,4},{8,11},{9,10},{10,... | collective-permute-start | bytes 884744 | tf_op jit(solution)/shard_map/ppermute | solution.py:190
  104.1 59.9 %all-to-all-start = ((bf16[8,128,2048]{2,1,0:T(8,128)(2,1)}), bf16[8,128,2048]{2,1,0:T(8,128)(2,1)}, u32[]{:S(2)}, u32[]{:S(2)}) async-start(bf16[8,128,2048]{2,1,0:T(8,128)(2,1)} %bitcast.74), calls=%async_computation | async-start | bytes 8388608 | tf_op jit(solution)/shard_map/all_to_all | solution.py:474
  120.0 9.1 %collective-permute-start.31 = (bf16[144,1024]{1,0:T(8,128)(2,1)S(1)}, bf16[144,1024]{1,0:T(8,128)(2,1)S(1)}, u32[]{:S(2)}, u32[]{:S(2)}) collective-permute-start(bf16[144,1024]{1,0:T(8,128)(2,1)S(1)} %get-tuple-element.78), channel_id=1, source_target_pairs={{0,1},{1,0},{2,3},{3,2},{4,5},{5,4},{6,7},{7,6},{8,9},{9,8},{10,11... | collective-permute-start | bytes 884744 | tf_op jit(solution)/shard_map/ppermute | solution.py:190
  120.9 10.0 %collective-permute-start.30 = (bf16[144,1024]{1,0:T(8,128)(2,1)S(1)}, bf16[144,1024]{1,0:T(8,128)(2,1)S(1)}, u32[]{:S(2)}, u32[]{:S(2)}) collective-permute-start(bf16[144,1024]{1,0:T(8,128)(2,1)S(1)} %get-tuple-element.76), channel_id=1, source_target_pairs={{0,3},{1,2},{2,1},{3,0},{4,7},{5,6},{6,5},{7,4},{8,11},{9,10},{10,... | collective-permute-start | bytes 884744 | tf_op jit(solution)/shard_map/ppermute | solution.py:190
  122.5 8.6 %collective-permute-start.29 = (bf16[144,1024]{1,0:T(8,128)(2,1)S(1)}, bf16[144,1024]{1,0:T(8,128)(2,1)S(1)}, u32[]{:S(2)}, u32[]{:S(2)}) collective-permute-start(bf16[144,1024]{1,0:T(8,128)(2,1)S(1)} %get-tuple-element.74), channel_id=1, source_target_pairs={{0,4},{1,5},{2,6},{3,7},{4,0},{5,1},{6,2},{7,3},{8,12},{9,13},{10,... | collective-permute-start | bytes 884744 | tf_op jit(solution)/shard_map/ppermute | solution.py:186
  124.4 9.7 %collective-permute-start.28 = (bf16[144,1024]{1,0:T(8,128)(2,1)S(1)}, bf16[144,1024]{1,0:T(8,128)(2,1)S(1)}, u32[]{:S(2)}, u32[]{:S(2)}) collective-permute-start(bf16[144,1024]{1,0:T(8,128)(2,1)S(1)} %get-tuple-element.72), channel_id=1, source_target_pairs={{0,12},{1,13},{2,14},{3,15},{4,8},{5,9},{6,10},{7,11},{8,4},{9,5},... | collective-permute-start | bytes 884744 | tf_op jit(solution)/shard_map/ppermute | solution.py:186
  134.3 13.7 %collective-permute-start.34 = (bf16[288,1024]{1,0:T(8,128)(2,1)S(1)}, bf16[288,1024]{1,0:T(8,128)(2,1)S(1)}, u32[]{:S(2)}, u32[]{:S(2)}) collective-permute-start(bf16[288,1024]{1,0:T(8,128)(2,1)S(1)} %pad_maximum_fusion.9), channel_id=1, source_target_pairs={{0,1},{1,0},{2,3},{3,2},{4,5},{5,4},{6,7},{7,6},{8,9},{9,8},{10,11... | collective-permute-start | bytes 1769480 | tf_op jit(solution)/shard_map/ppermute | solution.py:190
  135.0 14.6 %collective-permute-start.35 = (bf16[288,1024]{1,0:T(8,128)(2,1)S(1)}, bf16[288,1024]{1,0:T(8,128)(2,1)S(1)}, u32[]{:S(2)}, u32[]{:S(2)}) collective-permute-start(bf16[288,1024]{1,0:T(8,128)(2,1)S(1)} %pad_maximum_fusion.10), channel_id=1, source_target_pairs={{0,3},{1,2},{2,1},{3,0},{4,7},{5,6},{6,5},{7,4},{8,11},{9,10},{10,... | collective-permute-start | bytes 1769480 | tf_op jit(solution)/shard_map/ppermute | solution.py:190
  136.6 13.2 %collective-permute-start.32 = (bf16[288,1024]{1,0:T(8,128)(2,1)S(1)}, bf16[288,1024]{1,0:T(8,128)(2,1)S(1)}, u32[]{:S(2)}, u32[]{:S(2)}) collective-permute-start(bf16[288,1024]{1,0:T(8,128)(2,1)S(1)} %pad_maximum_fusion.7), channel_id=1, source_target_pairs={{0,4},{1,5},{2,6},{3,7},{4,0},{5,1},{6,2},{7,3},{8,12},{9,13},{10,... | collective-permute-start | bytes 1769480 | tf_op jit(solution)/shard_map/ppermute | solution.py:186
  136.6 14.3 %collective-permute-start.33 = (bf16[288,1024]{1,0:T(8,128)(2,1)S(1)}, bf16[288,1024]{1,0:T(8,128)(2,1)S(1)}, u32[]{:S(2)}, u32[]{:S(2)}) collective-permute-start(bf16[288,1024]{1,0:T(8,128)(2,1)S(1)} %pad_maximum_fusion.8), channel_id=1, source_target_pairs={{0,12},{1,13},{2,14},{3,15},{4,8},{5,9},{6,10},{7,11},{8,4},{9,5},... | collective-permute-start | bytes 1769480 | tf_op jit(solution)/shard_map/ppermute | solution.py:186
  151.3 5.8 %collective-permute-start.36 = (bf16[72,1024]{1,0:T(8,128)(2,1)S(1)}, bf16[72,1024]{1,0:T(8,128)(2,1)S(1)}, u32[]{:S(2)}, u32[]{:S(2)}) collective-permute-start(bf16[72,1024]{1,0:T(8,128)(2,1)S(1)} %get-tuple-element.105), channel_id=1, source_target_pairs={{0,1},{1,0},{2,3},{3,2},{4,5},{5,4},{6,7},{7,6},{8,9},{9,8},{10,11... | collective-permute-start | bytes 442376 | tf_op jit(solution)/shard_map/ppermute | solution.py:190
  152.1 7.5 %collective-permute-start.37 = (bf16[72,1024]{1,0:T(8,128)(2,1)S(1)}, bf16[72,1024]{1,0:T(8,128)(2,1)S(1)}, u32[]{:S(2)}, u32[]{:S(2)}) collective-permute-start(bf16[72,1024]{1,0:T(8,128)(2,1)S(1)} %get-tuple-element.104), channel_id=1, source_target_pairs={{0,3},{1,2},{2,1},{3,0},{4,7},{5,6},{6,5},{7,4},{8,11},{9,10},{10,... | collective-permute-start | bytes 442376 | tf_op jit(solution)/shard_map/ppermute | solution.py:190
  153.7 6.6 %collective-permute-start.38 = (bf16[72,1024]{1,0:T(8,128)(2,1)S(1)}, bf16[72,1024]{1,0:T(8,128)(2,1)S(1)}, u32[]{:S(2)}, u32[]{:S(2)}) collective-permute-start(bf16[72,1024]{1,0:T(8,128)(2,1)S(1)} %get-tuple-element.103), channel_id=1, source_target_pairs={{0,2},{1,3},{2,0},{3,1},{4,6},{5,7},{6,4},{7,5},{8,10},{9,11},{10,... | collective-permute-start | bytes 442376 | tf_op jit(solution)/shard_map/ppermute | solution.py:190
  155.5 5.2 %collective-permute-start.39 = (bf16[72,1024]{1,0:T(8,128)(2,1)S(1)}, bf16[72,1024]{1,0:T(8,128)(2,1)S(1)}, u32[]{:S(2)}, u32[]{:S(2)}) collective-permute-start(bf16[72,1024]{1,0:T(8,128)(2,1)S(1)} %get-tuple-element.101), channel_id=1, source_target_pairs={{0,4},{1,5},{2,6},{3,7},{4,0},{5,1},{6,2},{7,3},{8,12},{9,13},{10,... | collective-permute-start | bytes 442376 | tf_op jit(solution)/shard_map/ppermute | solution.py:186
  156.1 7.9 %collective-permute-start.40 = (bf16[72,1024]{1,0:T(8,128)(2,1)S(1)}, bf16[72,1024]{1,0:T(8,128)(2,1)S(1)}, u32[]{:S(2)}, u32[]{:S(2)}) collective-permute-start(bf16[72,1024]{1,0:T(8,128)(2,1)S(1)} %get-tuple-element.100), channel_id=1, source_target_pairs={{0,12},{1,13},{2,14},{3,15},{4,8},{5,9},{6,10},{7,11},{8,4},{9,5},... | collective-permute-start | bytes 442376 | tf_op jit(solution)/shard_map/ppermute | solution.py:186
  157.1 6.9 %collective-permute-start.41 = (bf16[72,1024]{1,0:T(8,128)(2,1)S(1)}, bf16[72,1024]{1,0:T(8,128)(2,1)S(1)}, u32[]{:S(2)}, u32[]{:S(2)}) collective-permute-start(bf16[72,1024]{1,0:T(8,128)(2,1)S(1)} %get-tuple-element.99), channel_id=1, source_target_pairs={{0,8},{1,9},{2,10},{3,11},{4,12},{5,13},{6,14},{7,15},{8,0},{9,1},... | collective-permute-start | bytes 442376 | tf_op jit(solution)/shard_map/ppermute | solution.py:186
  179.7 59.0 %all-to-all-start.1 = ((bf16[128,8,2048]{2,1,0:T(8,128)(2,1)}), bf16[128,8,2048]{2,1,0:T(8,128)(2,1)}, u32[]{:S(2)}, u32[]{:S(2)}) async-start(bf16[128,8,2048]{2,1,0:T(8,128)(2,1)} %bitcast.75), calls=%async_computation.1 | async-start | bytes 8388608 | tf_op jit(solution)/shard_map/all_to_all | solution.py:485
  (21 other events, 116.2 us)

commit v8 on v7

--- a/solution.py
+++ b/solution.py
@@ -302,32 +302,57 @@
 
 
 def pick_kernel(mine, *refs):
-    rows_a, rows_b, out = refs[:PIECES], refs[PIECES : 2 * PIECES], refs[-1]
-    columns, _, capacity, width = out.shape
+    given, out, held = refs[: 2 * PIECES], refs[2 * PIECES], refs[2 * PIECES + 1 : 4 * PIECES + 1]
+    made, in_sems, out_sems = refs[4 * PIECES + 1 :]
+    columns, blocks, capacity, width = out.shape
     half = width // 2
+    arriving = [
+        pltpu.make_async_copy(source, place, in_sems.at[i])
+        for i, (source, place) in enumerate(zip(given, held))
+    ]
+    for c in arriving:
+        c.start()
+    rows_a, rows_b = held[:PIECES], held[PIECES:]
+    for c in arriving[:PIECES]:
+        c.wait()
     chosen = chosen_rows(mine[0], rows_a, columns, capacity)
+    for c in arriving[PIECES:]:
+        c.wait()
+    leaving = []
     for x in range(SIDE):
         for z in range(SIDE):
-            block = jnp.bitwise_xor(mine[0], x * SIDE + z)
-            pick = chosen[x * SIDE + z]
+            d = x * SIDE + z
+            pick = chosen[d]
             a = dot(pick, block_of(rows_a, x, z)).reshape(columns, capacity, half).astype(BF)
             b = dot(pick, block_of(rows_b, z, x)).reshape(columns, capacity, half).astype(BF)
-            for r in range(columns):
-                out[r, block, :, :half] = a[r]
-                out[r, block, :, half:] = b[r]
+            made[d, :, :, :half] = a
+            made[d, :, :, half:] = b
+            place = out.at[:, jnp.bitwise_xor(mine[0], d)]
+            leaving.append(pltpu.make_async_copy(made.at[d], place, out_sems.at[d]))
+            leaving[-1].start()
+    for c in leaving:
+        c.wait()
 
 
 def pick(mine, rows_a, rows_b, columns, capacity):
     width = 2 * rows_a[0].shape[-1]
-    whole = pl.BlockSpec(memory_space=pltpu.VMEM)
+    blocks = SIDE * SIDE
+    given = [*rows_a, *rows_b]
     return pl.pallas_call(
         pick_kernel,
-        out_shape=jax.ShapeDtypeStruct((columns, SIDE * SIDE, capacity, width), BF),
-        in_specs=[pl.BlockSpec(memory_space=pltpu.SMEM)] + [whole] * (2 * PIECES),
-        out_specs=whole,
+        out_shape=jax.ShapeDtypeStruct((columns, blocks, capacity, width), BF),
+        in_specs=[pl.BlockSpec(memory_space=pltpu.SMEM)]
+        + [pl.BlockSpec(memory_space=pltpu.HBM)] * len(given),
+        out_specs=pl.BlockSpec(memory_space=pltpu.HBM),
+        scratch_shapes=[pltpu.VMEM(a.shape, BF) for a in given]
+        + [
+            pltpu.VMEM((blocks, columns, capacity, width), BF),
+            pltpu.SemaphoreType.DMA((len(given),)),
+            pltpu.SemaphoreType.DMA((blocks,)),
+        ],
         compiler_params=vmem(56),
         name="pick",
-    )(mine, *rows_a, *rows_b)
+    )(mine, *given)
 
 
 def expert_kernel(rows, gate_up, down, out):

time: 245 us -> 244 us (level)
  no operation moved by 1% of the time
where the time goes in v8:
time: 244 us; the launch traced here: 242 us
  waiting for transfers between devices  117 us (48%)
  starting transfers between devices  67.9 us (28%)
  Pallas kernels  39.8 us (16%)
  local copies, waits for them, and re-layouts  6.56 us (3%)
  other arithmetic  6.14 us (3%)
  matrix products  3.15 us (1%)
    all_to_all x1, waiting for transfers between devices, on_device(): lax.all_to_all(answer.reshape(devices, capacity, width), ('req', 'exp'),...  50.4 us
    ppermute x21, waiting for transfers between devices, along_z(): return lax.ppermute(a, 'exp', [(i, i ^ d) for i in range(SIDE * SIDE)])  40.3 us
    ppermute x21, starting transfers between devices, along_x(): lax.ppermute(a, 'exp', [(i, i ^ d * SIDE) for i in range(SIDE * SIDE)])  27.6 us
    ppermute x21, starting transfers between devices, along_z(): return lax.ppermute(a, 'exp', [(i, i ^ d) for i in range(SIDE * SIDE)])  27.4 us
    ppermute x21, waiting for transfers between devices, along_x(): lax.ppermute(a, 'exp', [(i, i ^ d * SIDE) for i in range(SIDE * SIDE)])  26.5 us
    pallas_call x1, Pallas kernels, experts(): pl.pallas_call(expert_kernel, grid=(count // step,), out_shape=jax.ShapeD...  15.7 us
    pallas_call x1, Pallas kernels, shared_expert(): pl.pallas_call(shared_kernel, out_shape=part_shapes(half) * 2, scratch_sh...  10.8 us
    pallas_call x1, Pallas kernels, attention(): pl.pallas_call(attention_kernel, out_shape=part_shapes(half) * 2, in_spec...  8.23 us
  transfers between devices with their start and end apart: 44, of which 27 were waited for; matrix products, arithmetic and copies ran while one was open for 4% of the time, Pallas kernels for 4%

profile of v8, /device:TPU:8, one launch (start us, length us, event | category | flops | bytes accessed | tf_op | source)
XLA Modules:
  0.0 241.7 jit_solution(458453998862902614)
XLA Ops:
  0.0 8.2 %attention.1 = (bf16[288,1024]{1,0:T(8,128)(2,1)}, bf16[288,1024]{1,0:T(8,128)(2,1)}, bf16[288,1024]{1,0:T(8,128)(2,1)}, bf16[144,1024]{1,0:T(8,128)(2,1)}, bf16...) custom-call(s32[1]{0:T(128)} %bitcast.mine, ...), custom_call_target="tpu_custom_call" | custom-call | tf_op jit(solution)/shard_map/attention/pallas_call | solution.py:164
  8.3 2.0 collective-permute-start.3
  10.3 2.5 %collective-permute-start.2 = (bf16[144,1024]{1,0:T(8,128)(2,1)}, bf16[144,1024]{1,0:T(8,128)(2,1)S(1)}, u32[]{:S(2)}, u32[]{:S(2)}) collective-permute-start(bf16[144,1024]{1,0:T(8,128)(2,1)} %get-tuple-element.56), channel_id=1, source_target_pairs={{0,3},{1,2},{2,1},{3,0},{4,7},{5,6},{6,5},{7,4},{8,11},{9,10},{10,... | collective-permute-start | bytes 884744 | tf_op jit(solution)/shard_map/ppermute | solution.py:190
  12.8 1.5 collective-permute-start.1
  14.3 2.1 collective-permute-start
  18.6 1.5 collective-permute-done.2
  21.4 2.2 collective-permute-done
  25.7 2.1 collective-permute-start.5
  31.2 6.0 %collective-permute-done.6 = bf16[288,1024]{1,0:T(8,128)(2,1)} collective-permute-done((bf16[288,1024]{1,0:T(8,128)(2,1)S(1)}, bf16[288,1024]{1,0:T(8,128)(2,1)}, u32[]{:S(2)}, u32[]{:S(2)}) %collective-permute-start.6) | collective-permute-done | bytes 589856 | tf_op jit(solution)/shard_map/ppermute | solution.py:190
  37.2 2.0 collective-permute-done.7
  39.2 1.6 add_convert_fusion.2
  40.8 1.4 add_convert_fusion.3
  44.1 2.1 collective-permute-start.12
  46.2 1.4 collective-permute-start.13
  50.1 1.6 collective-permute-start.9
  52.9 3.5 %collective-permute-done.9.a2 = bf16[72,1024]{1,0:T(8,128)(2,1)S(1)} collective-permute-done((bf16[72,1024]{1,0:T(8,128)(2,1)S(1)}, bf16[72,1024]{1,0:T(8,128)(2,1)S(1)}, u32[]{:S(2)}, u32[]{:S(2)}) %collective-permute-start.9) | collective-permute-done | bytes 147488 | tf_op jit(solution)/shard_map/ppermute | solution.py:190
  57.3 3.2 %collective-permute-start.18 = (bf16[72,1024]{1,0:T(8,128)(2,1)S(1)}, bf16[72,1024]{1,0:T(8,128)(2,1)S(1)}, u32[]{:S(2)}, u32[]{:S(2)}) collective-permute-start(bf16[72,1024]{1,0:T(8,128)(2,1)S(1)} %get-tuple-element.117), channel_id=1, source_target_pairs={{0,8},{1,9},{2,10},{3,11},{4,12},{5,13},{6,14},{7,15},{8,0},{9,1},... | collective-permute-start | bytes 442376 | tf_op jit(solution)/shard_map/ppermute | solution.py:186
  61.6 3.1 %collective-permute-start.15 = (bf16[72,1024]{1,0:T(8,128)(2,1)S(1)}, bf16[72,1024]{1,0:T(8,128)(2,1)S(1)}, u32[]{:S(2)}, u32[]{:S(2)}) collective-permute-start(bf16[72,1024]{1,0:T(8,128)(2,1)S(1)} %get-tuple-element.118), channel_id=1, source_target_pairs={{0,2},{1,3},{2,0},{3,1},{4,6},{5,7},{6,4},{7,5},{8,10},{9,11},{10,... | collective-permute-start | bytes 442376 | tf_op jit(solution)/shard_map/ppermute | solution.py:190
  64.7 1.6 collective-permute-start.16
  66.9 2.5 %collective-permute-done.15 = bf16[72,1024]{1,0:T(8,128)(2,1)S(1)} collective-permute-done((bf16[72,1024]{1,0:T(8,128)(2,1)S(1)}, bf16[72,1024]{1,0:T(8,128)(2,1)S(1)}, u32[]{:S(2)}, u32[]{:S(2)}) %collective-permute-start.15) | collective-permute-done | bytes 147488 | tf_op jit(solution)/shard_map/ppermute | solution.py:190
  69.4 3.1 %collective-permute-done.16 = bf16[72,1024]{1,0:T(8,128)(2,1)S(1)} collective-permute-done((bf16[72,1024]{1,0:T(8,128)(2,1)S(1)}, bf16[72,1024]{1,0:T(8,128)(2,1)S(1)}, u32[]{:S(2)}, u32[]{:S(2)}) %collective-permute-start.16) | collective-permute-done | bytes 147488 | tf_op jit(solution)/shard_map/ppermute | solution.py:190
  72.6 2.4 collective-permute-start.21
  74.9 1.6 collective-permute-start.25
  76.5 10.4 %collective-permute-done.21.refs_2_ = bf16[4,72,1024]{2,1,0:T(8,128)(2,1)S(1)} collective-permute-done((bf16[4,72,1024]{2,1,0:T(8,128)(2,1)S(1)}, bf16[4,72,1024]{2,1,0:T(8,128)(2,1)S(1)}, u32[]{:S(2)}, u32[]{:S(2)}) %collective-permute-start.21) | collective-permute-done | bytes 589856 | tf_op jit(solution)/shard_map/ppermute | solution.py:186
  87.1 2.4 collective-permute-start.23
  89.6 1.7 collective-permute-start.27
  91.3 2.4 collective-permute-done.22.refs_3_
  93.7 1.4 collective-permute-done.23.refs_4_
  96.3 1.4 collective-permute-done.27.refs_9_
  98.4 4.8 %pick.1 = bf16[8,16,8,2048]{3,2,1,0:T(8,128)(2,1)} custom-call(s32[1]{0:T(128)} %bitcast.mine, bf16[4,72,1024]{2,1,0:T(8,128)(2,1)} %copy-done.10, bf16[4,72,1024]{2,1,0:T(8,128)(2,1)} %copy-done.12, bf16[4,72,1024]{2,1,0:T(8,128)(2,1)} %copy-done.11, bf16[2,72,1024]{2,1,0:T(8,128)(2,1)} %copy-done, bf16[2,72,1024]{2,1,0:T(8,128)(2,1)} %copy-done.2, ...), custom_call_target="tpu_custom_call" | custom-call | tf_op jit(solution)/shard_map/pick/pallas_call | solution.py:341
  103.2 5.1 %all-to-all-start = ((bf16[8,128,2048]{2,1,0:T(8,128)(2,1)}), bf16[8,128,2048]{2,1,0:T(8,128)(2,1)}, u32[]{:S(2)}, u32[]{:S(2)}) async-start(bf16[8,128,2048]{2,1,0:T(8,128)(2,1)} %bitcast.74), calls=%async_computation | async-start | bytes 8388608 | tf_op jit(solution)/shard_map/all_to_all | solution.py:499
  108.3 10.8 %shared_expert.1 = (bf16[288,1024]{1,0:T(8,128)(2,1)S(1)}, bf16[288,1024]{1,0:T(8,128)(2,1)S(1)}, bf16[288,1024]{1,0:T(8,128)(2,1)S(1)}, bf16[144,1024]{1,0:T(8,...) custom-call(bf16[4,72,1024]{2,1,0:T(8,128)(2,1)} %copy-done.10, ...), custom_call_target="tpu_custom_call" | custom-call | flops 4982833152 | bytes 13762560 | tf_op jit(solution)/shard_map/shared_expert/pallas_call | solution.py:420
  119.9 1.6 collective-permute-start.30
  121.6 1.9 collective-permute-start.29
  124.6 3.6 %collective-permute-done.31 = bf16[144,1024]{1,0:T(8,128)(2,1)S(1)} collective-permute-done((bf16[144,1024]{1,0:T(8,128)(2,1)S(1)}, bf16[144,1024]{1,0:T(8,128)(2,1)S(1)}, u32[]{:S(2)}, u32[]{:S(2)}) %collective-permute-start.31) | collective-permute-done | bytes 294944 | tf_op jit(solution)/shard_map/ppermute | solution.py:190
  128.3 1.6 collective-permute-done.30
  130.4 2.8 %collective-permute-done.28 = bf16[144,1024]{1,0:T(8,128)(2,1)S(1)} collective-permute-done((bf16[144,1024]{1,0:T(8,128)(2,1)S(1)}, bf16[144,1024]{1,0:T(8,128)(2,1)S(1)}, u32[]{:S(2)}, u32[]{:S(2)}) %collective-permute-start.28) | collective-permute-done | bytes 294944 | tf_op jit(solution)/shard_map/ppermute | solution.py:186
  134.0 1.6 collective-permute-start.35
  136.7 10.4 %collective-permute-done.34 = bf16[288,1024]{1,0:T(8,128)(2,1)S(1)} collective-permute-done((bf16[288,1024]{1,0:T(8,128)(2,1)S(1)}, bf16[288,1024]{1,0:T(8,128)(2,1)S(1)}, u32[]{:S(2)}, u32[]{:S(2)}) %collective-permute-start.34) | collective-permute-done | bytes 589856 | tf_op jit(solution)/shard_map/ppermute | solution.py:190
  147.0 1.6 collective-permute-done.35
  151.2 1.6 collective-permute-start.37
  152.8 1.7 collective-permute-start.38
  156.1 2.6 %collective-permute-start.41 = (bf16[72,1024]{1,0:T(8,128)(2,1)S(1)}, bf16[72,1024]{1,0:T(8,128)(2,1)S(1)}, u32[]{:S(2)}, u32[]{:S(2)}) collective-permute-start(bf16[72,1024]{1,0:T(8,128)(2,1)S(1)} %get-tuple-element.99), channel_id=1, source_target_pairs={{0,8},{1,9},{2,10},{3,11},{4,12},{5,13},{6,14},{7,15},{8,0},{9,1},... | collective-permute-start | bytes 442376 | tf_op jit(solution)/shard_map/ppermute | solution.py:186
  159.8 3.3 %collective-permute-done.40 = bf16[72,1024]{1,0:T(8,128)(2,1)S(1)} collective-permute-done((bf16[72,1024]{1,0:T(8,128)(2,1)S(1)}, bf16[72,1024]{1,0:T(8,128)(2,1)S(1)}, u32[]{:S(2)}, u32[]{:S(2)}) %collective-permute-start.40) | collective-permute-done | bytes 147488 | tf_op jit(solution)/shard_map/ppermute | solution.py:186
  163.1 15.7 %experts.1 = bf16[1024,2048]{1,0:T(8,128)(2,1)} custom-call(bf16[1024,2048]{1,0:T(8,128)(2,1)} %bitcast.35.rows, bf16[1,2,704,2048]{3,2,1,0:T(8,128)(2,1)} %bitcast.89, bf16[1,704,2048]{2,1,0:T(8,128)(2,1)} %down.1), custom_call_target="tpu_custom_call" | custom-call | flops 8858370048 | bytes 17039360 | tf_op jit(solution)/shard_map/experts/pallas_call | solution.py:369
  178.8 7.8 %all-to-all-start.1 = ((bf16[128,8,2048]{2,1,0:T(8,128)(2,1)}), bf16[128,8,2048]{2,1,0:T(8,128)(2,1)}, u32[]{:S(2)}, u32[]{:S(2)}) async-start(bf16[128,8,2048]{2,1,0:T(8,128)(2,1)} %bitcast.75), calls=%async_computation.1 | async-start | bytes 8388608 | tf_op jit(solution)/shard_map/all_to_all | solution.py:510
  187.3 50.4 %all-to-all-done.1 = bf16[128,8,2048]{2,1,0:T(8,128)(2,1)} async-done(((bf16[128,8,2048]{2,1,0:T(8,128)(2,1)}), bf16[128,8,2048]{2,1,0:T(8,128)(2,1)}, u32[]{:S(2)}, u32[]{:S(2)}) %all-to-all-start.1) | async-done | bytes 4194336 | tf_op jit(solution)/shard_map/all_to_all | solution.py:510
  237.8 3.0 %fusion = f32[144,2048]{1,0:T(8,128)S(1)} fusion(bf16[128,8,2048]{2,1,0:T(8,128)(2,1)} %all-to-all-done.1, bf16[72,1024]{1,0:T(8,128)(2,1)S(1)} %get-tuple-element.95, bf16[72,1024]{1,0:T(8,128)(2,1)S(1)} %get-tuple-element.96), kind=kOutput, calls=%fused_computation | convolution fusion | flops 604569600 | bytes 5668864 | tf_op jit(solution)/shard_map/dot_general | solution.py:29
  (153 shorter events, 30.4 us)
Async XLA Ops:
  8.3 10.2 %collective-permute-start.3 = (bf16[144,1024]{1,0:T(8,128)(2,1)}, bf16[144,1024]{1,0:T(8,128)(2,1)S(1)}, u32[]{:S(2)}, u32[]{:S(2)}) collective-permute-start(bf16[144,1024]{1,0:T(8,128)(2,1)} %get-tuple-element.58), channel_id=1, source_target_pairs={{0,1},{1,0},{2,3},{3,2},{4,5},{5,4},{6,7},{7,6},{8,9},{9,8},{10,11... | collective-permute-start | bytes 884744 | tf_op jit(solution)/shard_map/ppermute | solution.py:190
  10.3 9.9 %collective-permute-start.2 = (bf16[144,1024]{1,0:T(8,128)(2,1)}, bf16[144,1024]{1,0:T(8,128)(2,1)S(1)}, u32[]{:S(2)}, u32[]{:S(2)}) collective-permute-start(bf16[144,1024]{1,0:T(8,128)(2,1)} %get-tuple-element.56), channel_id=1, source_target_pairs={{0,3},{1,2},{2,1},{3,0},{4,7},{5,6},{6,5},{7,4},{8,11},{9,10},{10,... | collective-permute-start | bytes 884744 | tf_op jit(solution)/shard_map/ppermute | solution.py:190
  12.8 8.4 %collective-permute-start.1 = (bf16[144,1024]{1,0:T(8,128)(2,1)}, bf16[144,1024]{1,0:T(8,128)(2,1)S(1)}, u32[]{:S(2)}, u32[]{:S(2)}) collective-permute-start(bf16[144,1024]{1,0:T(8,128)(2,1)} %get-tuple-element.54), channel_id=1, source_target_pairs={{0,4},{1,5},{2,6},{3,7},{4,0},{5,1},{6,2},{7,3},{8,12},{9,13},{10,... | collective-permute-start | bytes 884744 | tf_op jit(solution)/shard_map/ppermute | solution.py:186
  14.3 9.3 %collective-permute-start = (bf16[144,1024]{1,0:T(8,128)(2,1)}, bf16[144,1024]{1,0:T(8,128)(2,1)S(1)}, u32[]{:S(2)}, u32[]{:S(2)}) collective-permute-start(bf16[144,1024]{1,0:T(8,128)(2,1)} %get-tuple-element.52), channel_id=1, source_target_pairs={{0,12},{1,13},{2,14},{3,15},{4,8},{5,9},{6,10},{7,11},{8,4},{9,5},... | collective-permute-start | bytes 884744 | tf_op jit(solution)/shard_map/ppermute | solution.py:186
  21.4 17.8 %copy-start.20 = (bf16[288,1024]{1,0:T(8,128)(2,1)S(1)}, bf16[288,1024]{1,0:T(8,128)(2,1)}, u32[]{:S(2)}) copy-start(bf16[288,1024]{1,0:T(8,128)(2,1)} %get-tuple-element.61) | copy-start | bytes 1769476
  23.7 13.5 %collective-permute-start.6 = (bf16[288,1024]{1,0:T(8,128)(2,1)S(1)}, bf16[288,1024]{1,0:T(8,128)(2,1)}, u32[]{:S(2)}, u32[]{:S(2)}) collective-permute-start(bf16[288,1024]{1,0:T(8,128)(2,1)S(1)} %pad_maximum_fusion.3), channel_id=1, source_target_pairs={{0,1},{1,0},{2,3},{3,2},{4,5},{5,4},{6,7},{7,6},{8,9},{9,8},{10,11... | collective-permute-start | bytes 1769480 | tf_op jit(solution)/shard_map/ppermute | solution.py:190
  24.8 14.3 %collective-permute-start.7 = (bf16[288,1024]{1,0:T(8,128)(2,1)S(1)}, bf16[288,1024]{1,0:T(8,128)(2,1)}, u32[]{:S(2)}, u32[]{:S(2)}) collective-permute-start(bf16[288,1024]{1,0:T(8,128)(2,1)S(1)} %pad_maximum_fusion.4), channel_id=1, source_target_pairs={{0,3},{1,2},{2,1},{3,0},{4,7},{5,6},{6,5},{7,4},{8,11},{9,10},{10,... | collective-permute-start | bytes 1769480 | tf_op jit(solution)/shard_map/ppermute | solution.py:190
  25.7 15.1 %collective-permute-start.4 = (bf16[288,1024]{1,0:T(8,128)(2,1)S(1)}, bf16[288,1024]{1,0:T(8,128)(2,1)S(1)}, u32[]{:S(2)}, u32[]{:S(2)}) collective-permute-start(bf16[288,1024]{1,0:T(8,128)(2,1)S(1)} %pad_maximum_fusion.1), channel_id=1, source_target_pairs={{0,4},{1,5},{2,6},{3,7},{4,0},{5,1},{6,2},{7,3},{8,12},{9,13},{10,... | collective-permute-start | bytes 1769480 | tf_op jit(solution)/shard_map/ppermute | solution.py:186
  25.7 15.1 %collective-permute-start.5 = (bf16[288,1024]{1,0:T(8,128)(2,1)S(1)}, bf16[288,1024]{1,0:T(8,128)(2,1)}, u32[]{:S(2)}, u32[]{:S(2)}) collective-permute-start(bf16[288,1024]{1,0:T(8,128)(2,1)S(1)} %pad_maximum_fusion.2), channel_id=1, source_target_pairs={{0,12},{1,13},{2,14},{3,15},{4,8},{5,9},{6,10},{7,11},{8,4},{9,5},... | collective-permute-start | bytes 1769480 | tf_op jit(solution)/shard_map/ppermute | solution.py:186
  42.3 14.1 %copy-start.8 = (f32[2048]{0:T(1024)S(1)}, f32[2048]{0:T(1024)}, u32[]{:S(2)}) copy-start(f32[2048]{0:T(1024)} %param.22) | copy-start | bytes 24580
  42.3 7.8 %collective-permute-start.10 = (bf16[72,1024]{1,0:T(8,128)(2,1)S(1)}, bf16[72,1024]{1,0:T(8,128)(2,1)S(1)}, u32[]{:S(2)}, u32[]{:S(2)}) collective-permute-start(bf16[72,1024]{1,0:T(8,128)(2,1)S(1)} %get-tuple-element.111), channel_id=1, source_target_pairs={{0,2},{1,3},{2,0},{3,1},{4,6},{5,7},{6,4},{7,5},{8,10},{9,11},{10,... | collective-permute-start | bytes 442376 | tf_op jit(solution)/shard_map/ppermute | solution.py:190
  43.5 8.2 %collective-permute-start.11 = (bf16[72,1024]{1,0:T(8,128)(2,1)S(1)}, bf16[72,1024]{1,0:T(8,128)(2,1)S(1)}, u32[]{:S(2)}, u32[]{:S(2)}) collective-permute-start(bf16[72,1024]{1,0:T(8,128)(2,1)S(1)} %get-tuple-element.109), channel_id=1, source_target_pairs={{0,4},{1,5},{2,6},{3,7},{4,0},{5,1},{6,2},{7,3},{8,12},{9,13},{10,... | collective-permute-start | bytes 442376 | tf_op jit(solution)/shard_map/ppermute | solution.py:186
  44.1 7.6 %collective-permute-start.12 = (bf16[72,1024]{1,0:T(8,128)(2,1)S(1)}, bf16[72,1024]{1,0:T(8,128)(2,1)S(1)}, u32[]{:S(2)}, u32[]{:S(2)}) collective-permute-start(bf16[72,1024]{1,0:T(8,128)(2,1)S(1)} %get-tuple-element.108), channel_id=1, source_target_pairs={{0,12},{1,13},{2,14},{3,15},{4,8},{5,9},{6,10},{7,11},{8,4},{9,5},... | collective-permute-start | bytes 442376 | tf_op jit(solution)/shard_map/ppermute | solution.py:186
  46.2 6.6 %collective-permute-start.13 = (bf16[72,1024]{1,0:T(8,128)(2,1)S(1)}, bf16[72,1024]{1,0:T(8,128)(2,1)S(1)}, u32[]{:S(2)}, u32[]{:S(2)}) collective-permute-start(bf16[72,1024]{1,0:T(8,128)(2,1)S(1)} %get-tuple-element.107), channel_id=1, source_target_pairs={{0,8},{1,9},{2,10},{3,11},{4,12},{5,13},{6,14},{7,15},{8,0},{9,1},... | collective-permute-start | bytes 442376 | tf_op jit(solution)/shard_map/ppermute | solution.py:186
  47.7 5.2 %collective-permute-start.8 = (bf16[72,1024]{1,0:T(8,128)(2,1)S(1)}, bf16[72,1024]{1,0:T(8,128)(2,1)S(1)}, u32[]{:S(2)}, u32[]{:S(2)}) collective-permute-start(bf16[72,1024]{1,0:T(8,128)(2,1)S(1)} %get-tuple-element.113), channel_id=1, source_target_pairs={{0,1},{1,0},{2,3},{3,2},{4,5},{5,4},{6,7},{7,6},{8,9},{9,8},{10,11... | collective-permute-start | bytes 442376 | tf_op jit(solution)/shard_map/ppermute | solution.py:190
  50.1 6.4 %collective-permute-start.9 = (bf16[72,1024]{1,0:T(8,128)(2,1)S(1)}, bf16[72,1024]{1,0:T(8,128)(2,1)S(1)}, u32[]{:S(2)}, u32[]{:S(2)}) collective-permute-start(bf16[72,1024]{1,0:T(8,128)(2,1)S(1)} %get-tuple-element.112), channel_id=1, source_target_pairs={{0,3},{1,2},{2,1},{3,0},{4,7},{5,6},{6,5},{7,4},{8,11},{9,10},{10,... | collective-permute-start | bytes 442376 | tf_op jit(solution)/shard_map/ppermute | solution.py:190
  56.8 7.9 %collective-permute-start.17 = (bf16[72,1024]{1,0:T(8,128)(2,1)S(1)}, bf16[72,1024]{1,0:T(8,128)(2,1)S(1)}, u32[]{:S(2)}, u32[]{:S(2)}) collective-permute-start(bf16[72,1024]{1,0:T(8,128)(2,1)S(1)} %get-tuple-element.117), channel_id=1, source_target_pairs={{0,4},{1,5},{2,6},{3,7},{4,0},{5,1},{6,2},{7,3},{8,12},{9,13},{10,... | collective-permute-start | bytes 442376 | tf_op jit(solution)/shard_map/ppermute | solution.py:186
  57.3 9.0 %collective-permute-start.18 = (bf16[72,1024]{1,0:T(8,128)(2,1)S(1)}, bf16[72,1024]{1,0:T(8,128)(2,1)S(1)}, u32[]{:S(2)}, u32[]{:S(2)}) collective-permute-start(bf16[72,1024]{1,0:T(8,128)(2,1)S(1)} %get-tuple-element.117), channel_id=1, source_target_pairs={{0,8},{1,9},{2,10},{3,11},{4,12},{5,13},{6,14},{7,15},{8,0},{9,1},... | collective-permute-start | bytes 442376 | tf_op jit(solution)/shard_map/ppermute | solution.py:186
  60.5 6.4 %collective-permute-start.19 = (bf16[72,1024]{1,0:T(8,128)(2,1)S(1)}, bf16[72,1024]{1,0:T(8,128)(2,1)S(1)}, u32[]{:S(2)}, u32[]{:S(2)}) collective-permute-start(bf16[72,1024]{1,0:T(8,128)(2,1)S(1)} %get-tuple-element.117), channel_id=1, source_target_pairs={{0,12},{1,13},{2,14},{3,15},{4,8},{5,9},{6,10},{7,11},{8,4},{9,5},... | collective-permute-start | bytes 442376 | tf_op jit(solution)/shard_map/ppermute | solution.py:186
  61.6 5.3 %collective-permute-start.14 = (bf16[72,1024]{1,0:T(8,128)(2,1)S(1)}, bf16[72,1024]{1,0:T(8,128)(2,1)S(1)}, u32[]{:S(2)}, u32[]{:S(2)}) collective-permute-start(bf16[72,1024]{1,0:T(8,128)(2,1)S(1)} %get-tuple-element.118), channel_id=1, source_target_pairs={{0,1},{1,0},{2,3},{3,2},{4,5},{5,4},{6,7},{7,6},{8,9},{9,8},{10,11... | collective-permute-start | bytes 442376 | tf_op jit(solution)/shard_map/ppermute | solution.py:190
  61.6 7.8 %collective-permute-start.15 = (bf16[72,1024]{1,0:T(8,128)(2,1)S(1)}, bf16[72,1024]{1,0:T(8,128)(2,1)S(1)}, u32[]{:S(2)}, u32[]{:S(2)}) collective-permute-start(bf16[72,1024]{1,0:T(8,128)(2,1)S(1)} %get-tuple-element.118), channel_id=1, source_target_pairs={{0,2},{1,3},{2,0},{3,1},{4,6},{5,7},{6,4},{7,5},{8,10},{9,11},{10,... | collective-permute-start | bytes 442376 | tf_op jit(solution)/shard_map/ppermute | solution.py:190
  64.7 7.8 %collective-permute-start.16 = (bf16[72,1024]{1,0:T(8,128)(2,1)S(1)}, bf16[72,1024]{1,0:T(8,128)(2,1)S(1)}, u32[]{:S(2)}, u32[]{:S(2)}) collective-permute-start(bf16[72,1024]{1,0:T(8,128)(2,1)S(1)} %get-tuple-element.118), channel_id=1, source_target_pairs={{0,3},{1,2},{2,1},{3,0},{4,7},{5,6},{6,5},{7,4},{8,11},{9,10},{10,... | collective-permute-start | bytes 442376 | tf_op jit(solution)/shard_map/ppermute | solution.py:190
  66.9 20.1 %copy-start.9 = (bf16[4,72,1024]{2,1,0:T(8,128)(2,1)}, bf16[4,72,1024]{2,1,0:T(8,128)(2,1)S(1)}, u32[]{:S(2)}) copy-start(bf16[4,72,1024]{2,1,0:T(8,128)(2,1)S(1)} %pad_maximum_fusion.6.refs_5_) | copy-start | bytes 1769476
  72.6 17.1 %copy-start.10 = (bf16[4,72,1024]{2,1,0:T(8,128)(2,1)}, bf16[4,72,1024]{2,1,0:T(8,128)(2,1)S(1)}, u32[]{:S(2)}) copy-start(bf16[4,72,1024]{2,1,0:T(8,128)(2,1)S(1)} %pad_maximum_fusion.5.refs_0_) | copy-start | bytes 1769476
  72.6 14.3 %collective-permute-start.21 = (bf16[4,72,1024]{2,1,0:T(8,128)(2,1)S(1)}, bf16[4,72,1024]{2,1,0:T(8,128)(2,1)S(1)}, u32[]{:S(2)}, u32[]{:S(2)}) collective-permute-start(bf16[4,72,1024]{2,1,0:T(8,128)(2,1)S(1)} %pad_maximum_fusion.5.refs_0_), channel_id=1, source_target_pairs={{0,12},{1,13},{2,14},{3,15},{4,8},{5,9},{6,10},{7,11},{8,4},{9,5},... | collective-permute-start | bytes 1769480 | tf_op jit(solution)/shard_map/ppermute | solution.py:186
  74.9 12.1 %collective-permute-start.20 = (bf16[4,72,1024]{2,1,0:T(8,128)(2,1)S(1)}, bf16[4,72,1024]{2,1,0:T(8,128)(2,1)S(1)}, u32[]{:S(2)}, u32[]{:S(2)}) collective-permute-start(bf16[4,72,1024]{2,1,0:T(8,128)(2,1)S(1)} %pad_maximum_fusion.5.refs_0_), channel_id=1, source_target_pairs={{0,4},{1,5},{2,6},{3,7},{4,0},{5,1},{6,2},{7,3},{8,12},{9,13},{10,... | collective-permute-start | bytes 1769480 | tf_op jit(solution)/shard_map/ppermute | solution.py:186
  74.9 14.5 %collective-permute-start.25 = (bf16[4,72,1024]{2,1,0:T(8,128)(2,1)S(1)}, bf16[4,72,1024]{2,1,0:T(8,128)(2,1)S(1)}, u32[]{:S(2)}, u32[]{:S(2)}) collective-permute-start(bf16[4,72,1024]{2,1,0:T(8,128)(2,1)S(1)} %pad_maximum_fusion.6.refs_5_), channel_id=1, source_target_pairs={{0,3},{1,2},{2,1},{3,0},{4,7},{5,6},{6,5},{7,4},{8,11},{9,10},{10,... | collective-permute-start | bytes 1769480 | tf_op jit(solution)/shard_map/ppermute | solution.py:190
  76.5 13.0 %collective-permute-start.24 = (bf16[4,72,1024]{2,1,0:T(8,128)(2,1)S(1)}, bf16[4,72,1024]{2,1,0:T(8,128)(2,1)S(1)}, u32[]{:S(2)}, u32[]{:S(2)}) collective-permute-start(bf16[4,72,1024]{2,1,0:T(8,128)(2,1)S(1)} %pad_maximum_fusion.6.refs_5_), channel_id=1, source_target_pairs={{0,1},{1,0},{2,3},{3,2},{4,5},{5,4},{6,7},{7,6},{8,9},{9,8},{10,11... | collective-permute-start | bytes 1769480 | tf_op jit(solution)/shard_map/ppermute | solution.py:190
  86.9 6.8 %collective-permute-start.22 = (bf16[2,72,1024]{2,1,0:T(8,128)(2,1)S(1)}, bf16[2,72,1024]{2,1,0:T(8,128)(2,1)S(1)}, u32[]{:S(2)}, u32[]{:S(2)}) collective-permute-start(bf16[2,72,1024]{2,1,0:T(8,128)(2,1)S(1)} %slice.165), channel_id=1, source_target_pairs={{0,4},{1,5},{2,6},{3,7},{4,0},{5,1},{6,2},{7,3},{8,12},{9,13},{10,... | collective-permute-start | bytes 884744 | tf_op jit(solution)/shard_map/ppermute | solution.py:186
  87.1 8.0 %collective-permute-start.23 = (bf16[2,72,1024]{2,1,0:T(8,128)(2,1)S(1)}, bf16[2,72,1024]{2,1,0:T(8,128)(2,1)S(1)}, u32[]{:S(2)}, u32[]{:S(2)}) collective-permute-start(bf16[2,72,1024]{2,1,0:T(8,128)(2,1)S(1)} %slice.166), channel_id=1, source_target_pairs={{0,12},{1,13},{2,14},{3,15},{4,8},{5,9},{6,10},{7,11},{8,4},{9,5},... | collective-permute-start | bytes 884744 | tf_op jit(solution)/shard_map/ppermute | solution.py:186
  89.5 6.8 %collective-permute-start.26 = (bf16[2,72,1024]{2,1,0:T(8,128)(2,1)S(1)}, bf16[2,72,1024]{2,1,0:T(8,128)(2,1)S(1)}, u32[]{:S(2)}, u32[]{:S(2)}) collective-permute-start(bf16[2,72,1024]{2,1,0:T(8,128)(2,1)S(1)} %slice.167), channel_id=1, source_target_pairs={{0,1},{1,0},{2,3},{3,2},{4,5},{5,4},{6,7},{7,6},{8,9},{9,8},{10,11... | collective-permute-start | bytes 884744 | tf_op jit(solution)/shard_map/ppermute | solution.py:190
  89.6 8.0 %collective-permute-start.27 = (bf16[2,72,1024]{2,1,0:T(8,128)(2,1)S(1)}, bf16[2,72,1024]{2,1,0:T(8,128)(2,1)S(1)}, u32[]{:S(2)}, u32[]{:S(2)}) collective-permute-start(bf16[2,72,1024]{2,1,0:T(8,128)(2,1)S(1)} %slice.168), channel_id=1, source_target_pairs={{0,3},{1,2},{2,1},{3,0},{4,7},{5,6},{6,5},{7,4},{8,11},{9,10},{10,... | collective-permute-start | bytes 884744 | tf_op jit(solution)/shard_map/ppermute | solution.py:190
  103.2 59.9 %all-to-all-start = ((bf16[8,128,2048]{2,1,0:T(8,128)(2,1)}), bf16[8,128,2048]{2,1,0:T(8,128)(2,1)}, u32[]{:S(2)}, u32[]{:S(2)}) async-start(bf16[8,128,2048]{2,1,0:T(8,128)(2,1)} %bitcast.74), calls=%async_computation | async-start | bytes 8388608 | tf_op jit(solution)/shard_map/all_to_all | solution.py:499
  119.1 9.1 %collective-permute-start.31 = (bf16[144,1024]{1,0:T(8,128)(2,1)S(1)}, bf16[144,1024]{1,0:T(8,128)(2,1)S(1)}, u32[]{:S(2)}, u32[]{:S(2)}) collective-permute-start(bf16[144,1024]{1,0:T(8,128)(2,1)S(1)} %get-tuple-element.78), channel_id=1, source_target_pairs={{0,1},{1,0},{2,3},{3,2},{4,5},{5,4},{6,7},{7,6},{8,9},{9,8},{10,11... | collective-permute-start | bytes 884744 | tf_op jit(solution)/shard_map/ppermute | solution.py:190
  119.9 10.0 %collective-permute-start.30 = (bf16[144,1024]{1,0:T(8,128)(2,1)S(1)}, bf16[144,1024]{1,0:T(8,128)(2,1)S(1)}, u32[]{:S(2)}, u32[]{:S(2)}) collective-permute-start(bf16[144,1024]{1,0:T(8,128)(2,1)S(1)} %get-tuple-element.76), channel_id=1, source_target_pairs={{0,3},{1,2},{2,1},{3,0},{4,7},{5,6},{6,5},{7,4},{8,11},{9,10},{10,... | collective-permute-start | bytes 884744 | tf_op jit(solution)/shard_map/ppermute | solution.py:190
  121.6 8.6 %collective-permute-start.29 = (bf16[144,1024]{1,0:T(8,128)(2,1)S(1)}, bf16[144,1024]{1,0:T(8,128)(2,1)S(1)}, u32[]{:S(2)}, u32[]{:S(2)}) collective-permute-start(bf16[144,1024]{1,0:T(8,128)(2,1)S(1)} %get-tuple-element.74), channel_id=1, source_target_pairs={{0,4},{1,5},{2,6},{3,7},{4,0},{5,1},{6,2},{7,3},{8,12},{9,13},{10,... | collective-permute-start | bytes 884744 | tf_op jit(solution)/shard_map/ppermute | solution.py:186
  123.5 9.7 %collective-permute-start.28 = (bf16[144,1024]{1,0:T(8,128)(2,1)S(1)}, bf16[144,1024]{1,0:T(8,128)(2,1)S(1)}, u32[]{:S(2)}, u32[]{:S(2)}) collective-permute-start(bf16[144,1024]{1,0:T(8,128)(2,1)S(1)} %get-tuple-element.72), channel_id=1, source_target_pairs={{0,12},{1,13},{2,14},{3,15},{4,8},{5,9},{6,10},{7,11},{8,4},{9,5},... | collective-permute-start | bytes 884744 | tf_op jit(solution)/shard_map/ppermute | solution.py:186
  133.3 13.7 %collective-permute-start.34 = (bf16[288,1024]{1,0:T(8,128)(2,1)S(1)}, bf16[288,1024]{1,0:T(8,128)(2,1)S(1)}, u32[]{:S(2)}, u32[]{:S(2)}) collective-permute-start(bf16[288,1024]{1,0:T(8,128)(2,1)S(1)} %pad_maximum_fusion.9), channel_id=1, source_target_pairs={{0,1},{1,0},{2,3},{3,2},{4,5},{5,4},{6,7},{7,6},{8,9},{9,8},{10,11... | collective-permute-start | bytes 1769480 | tf_op jit(solution)/shard_map/ppermute | solution.py:190
  134.0 14.6 %collective-permute-start.35 = (bf16[288,1024]{1,0:T(8,128)(2,1)S(1)}, bf16[288,1024]{1,0:T(8,128)(2,1)S(1)}, u32[]{:S(2)}, u32[]{:S(2)}) collective-permute-start(bf16[288,1024]{1,0:T(8,128)(2,1)S(1)} %pad_maximum_fusion.10), channel_id=1, source_target_pairs={{0,3},{1,2},{2,1},{3,0},{4,7},{5,6},{6,5},{7,4},{8,11},{9,10},{10,... | collective-permute-start | bytes 1769480 | tf_op jit(solution)/shard_map/ppermute | solution.py:190
  135.7 13.2 %collective-permute-start.32 = (bf16[288,1024]{1,0:T(8,128)(2,1)S(1)}, bf16[288,1024]{1,0:T(8,128)(2,1)S(1)}, u32[]{:S(2)}, u32[]{:S(2)}) collective-permute-start(bf16[288,1024]{1,0:T(8,128)(2,1)S(1)} %pad_maximum_fusion.7), channel_id=1, source_target_pairs={{0,4},{1,5},{2,6},{3,7},{4,0},{5,1},{6,2},{7,3},{8,12},{9,13},{10,... | collective-permute-start | bytes 1769480 | tf_op jit(solution)/shard_map/ppermute | solution.py:186
  135.7 14.3 %collective-permute-start.33 = (bf16[288,1024]{1,0:T(8,128)(2,1)S(1)}, bf16[288,1024]{1,0:T(8,128)(2,1)S(1)}, u32[]{:S(2)}, u32[]{:S(2)}) collective-permute-start(bf16[288,1024]{1,0:T(8,128)(2,1)S(1)} %pad_maximum_fusion.8), channel_id=1, source_target_pairs={{0,12},{1,13},{2,14},{3,15},{4,8},{5,9},{6,10},{7,11},{8,4},{9,5},... | collective-permute-start | bytes 1769480 | tf_op jit(solution)/shard_map/ppermute | solution.py:186
  150.3 5.8 %collective-permute-start.36 = (bf16[72,1024]{1,0:T(8,128)(2,1)S(1)}, bf16[72,1024]{1,0:T(8,128)(2,1)S(1)}, u32[]{:S(2)}, u32[]{:S(2)}) collective-permute-start(bf16[72,1024]{1,0:T(8,128)(2,1)S(1)} %get-tuple-element.105), channel_id=1, source_target_pairs={{0,1},{1,0},{2,3},{3,2},{4,5},{5,4},{6,7},{7,6},{8,9},{9,8},{10,11... | collective-permute-start | bytes 442376 | tf_op jit(solution)/shard_map/ppermute | solution.py:190
  151.2 7.5 %collective-permute-start.37 = (bf16[72,1024]{1,0:T(8,128)(2,1)S(1)}, bf16[72,1024]{1,0:T(8,128)(2,1)S(1)}, u32[]{:S(2)}, u32[]{:S(2)}) collective-permute-start(bf16[72,1024]{1,0:T(8,128)(2,1)S(1)} %get-tuple-element.104), channel_id=1, source_target_pairs={{0,3},{1,2},{2,1},{3,0},{4,7},{5,6},{6,5},{7,4},{8,11},{9,10},{10,... | collective-permute-start | bytes 442376 | tf_op jit(solution)/shard_map/ppermute | solution.py:190
  152.8 6.6 %collective-permute-start.38 = (bf16[72,1024]{1,0:T(8,128)(2,1)S(1)}, bf16[72,1024]{1,0:T(8,128)(2,1)S(1)}, u32[]{:S(2)}, u32[]{:S(2)}) collective-permute-start(bf16[72,1024]{1,0:T(8,128)(2,1)S(1)} %get-tuple-element.103), channel_id=1, source_target_pairs={{0,2},{1,3},{2,0},{3,1},{4,6},{5,7},{6,4},{7,5},{8,10},{9,11},{10,... | collective-permute-start | bytes 442376 | tf_op jit(solution)/shard_map/ppermute | solution.py:190
  154.5 5.2 %collective-permute-start.39 = (bf16[72,1024]{1,0:T(8,128)(2,1)S(1)}, bf16[72,1024]{1,0:T(8,128)(2,1)S(1)}, u32[]{:S(2)}, u32[]{:S(2)}) collective-permute-start(bf16[72,1024]{1,0:T(8,128)(2,1)S(1)} %get-tuple-element.101), channel_id=1, source_target_pairs={{0,4},{1,5},{2,6},{3,7},{4,0},{5,1},{6,2},{7,3},{8,12},{9,13},{10,... | collective-permute-start | bytes 442376 | tf_op jit(solution)/shard_map/ppermute | solution.py:186
  155.2 7.9 %collective-permute-start.40 = (bf16[72,1024]{1,0:T(8,128)(2,1)S(1)}, bf16[72,1024]{1,0:T(8,128)(2,1)S(1)}, u32[]{:S(2)}, u32[]{:S(2)}) collective-permute-start(bf16[72,1024]{1,0:T(8,128)(2,1)S(1)} %get-tuple-element.100), channel_id=1, source_target_pairs={{0,12},{1,13},{2,14},{3,15},{4,8},{5,9},{6,10},{7,11},{8,4},{9,5},... | collective-permute-start | bytes 442376 | tf_op jit(solution)/shard_map/ppermute | solution.py:186
  156.1 7.0 %collective-permute-start.41 = (bf16[72,1024]{1,0:T(8,128)(2,1)S(1)}, bf16[72,1024]{1,0:T(8,128)(2,1)S(1)}, u32[]{:S(2)}, u32[]{:S(2)}) collective-permute-start(bf16[72,1024]{1,0:T(8,128)(2,1)S(1)} %get-tuple-element.99), channel_id=1, source_target_pairs={{0,8},{1,9},{2,10},{3,11},{4,12},{5,13},{6,14},{7,15},{8,0},{9,1},... | collective-permute-start | bytes 442376 | tf_op jit(solution)/shard_map/ppermute | solution.py:186
  178.8 59.0 %all-to-all-start.1 = ((bf16[128,8,2048]{2,1,0:T(8,128)(2,1)}), bf16[128,8,2048]{2,1,0:T(8,128)(2,1)}, u32[]{:S(2)}, u32[]{:S(2)}) async-start(bf16[128,8,2048]{2,1,0:T(8,128)(2,1)} %bitcast.75), calls=%async_computation.1 | async-start | bytes 8388608 | tf_op jit(solution)/shard_map/all_to_all | solution.py:510
  (21 other events, 116.2 us)
